TPU v7x, 32 devices: a whole 2x2x4 slice. The times are simulated.
32 devices in a mesh: rows: 16 (over z, x, core), cols: 2 (over y).
Axes of the slice: x: 2, y: 2, z: 4, core: 2. Of those that a mesh axis runs over, the one named last changes fastest.
Arguments:
- rhs: float32 [3, 32, 256, 128], P(None, 'rows', 'cols'), may hold values from -6 to 6
- diag_inv: float32 [3, 32, 256, 256], P(None, 'rows', 'cols'), may hold values from -1 to 3.1, as said below
- factor_tiles: float32 [2, 32, 8, 256, 256], P(None, 'rows', None, 'cols'), may hold values from -0.125 to 0.125
- tile_source: int32 [2, 32, 8], P(None, 'rows'), may hold values from 0 to 63, as said below
- tile_count: int32 [2, 32], P(None, 'rows'), may hold values from 1 to 8, as said below
Outputs:
- solution: float32 [3, 32, 256, 128], P(None, 'rows', 'cols')
Inputs may be any that keep to these rules, and one draw needn't show every extreme that they name: `tile_source`: each source lies at a lower level than its target; supernode g mod 32 belongs to rows index (g mod 32) // 2, and that index differs from the target's by at most 7. The 8 sources of one supernode are distinct. `tile_count`: slots at or beyond the count hold no tile of the factor. At every target level some supernode has all 8 slots live. `diag_inv`: each block is lower triangular with a positive diagonal.
All inputs are finite; a program needn't handle non-finite values.
Results may differ from a plain program's by a relative error of at most 0.0003.
Values sent between devices are 32-bit elements; how exact they have to be, the bound alone decides.
No kernel may reach another device: no remote copies, remote signals or barrier semaphores. Data moves between devices by JAX's collectives and lax.ppermute only.
A program may use at most 64 MiB of HBM per device.

v0:
```python
import jax
import jax.numpy as jnp
from jax import lax
from jax.sharding import PartitionSpec as P

KDEV = 7


def from_behind(value, axis, steps):
    count = lax.axis_size(axis)
    leading, last = (max(0, -steps), min(count, count - steps))
    return lax.ppermute(value, axis, [(source, source + steps) for source in range(leading, last)])


def local(rhs, diag_inv, factor_tiles, tile_source, tile_count):
    levels = rhs.shape[0]
    owned_count = rhs.shape[1]
    share_rows = rhs.shape[2]
    columns = rhs.shape[3]
    slot_count = tile_source.shape[2]
    reach_dev = KDEV
    window_len = 2 * reach_dev + 1
    total_sup = lax.axis_size("rows") * owned_count
    row_place = lax.axis_index("rows")
    highest = lax.Precision.HIGHEST
    slot_ids = jnp.arange(slot_count, dtype=jnp.int32)

    def window_places(sources):
        src_level = sources // total_sup
        within = sources % total_sup
        return (
            src_level * window_len + within // owned_count - row_place + reach_dev
        ) * owned_count + within % owned_count

    def live_mask(counts):
        return (slot_ids[None, :] < counts[:, None]).astype(jnp.float32)

    def full_rows(piece):
        return lax.all_gather(piece, "cols", axis=1, tiled=True)

    forward_values = []
    windows = []
    for height in range(levels):
        if height == 0:
            whole_block = full_rows(rhs[0])
        else:
            stacked = jnp.stack(windows, 0).reshape(
                height * window_len * owned_count, share_rows, columns
            )
            places = window_places(tile_source[height - 1])
            picked = (
                jnp.take(stacked, places, axis=0)
                * live_mask(tile_count[height - 1])[:, :, None, None]
            )
            partial_value = jnp.einsum(
                "skci,skcr->sir", factor_tiles[height - 1], picked, precision=highest
            )
            whole_block = full_rows(
                rhs[height]
                - lax.psum_scatter(partial_value, "cols", scatter_dimension=1, tiled=True)
            )
        values = jnp.einsum("sci,sir->scr", diag_inv[height], whole_block, precision=highest)
        forward_values.append(values)
        if height + 1 < levels:
            pieces = []
            for pull_offset in range(-reach_dev, reach_dev + 1):
                if pull_offset == 0:
                    pieces.append(values)
                else:
                    pieces.append(from_behind(values, "rows", -pull_offset))
            windows.append(jnp.stack(pieces, 0))
    carried = [jnp.zeros_like(forward_values[0]) for height in range(levels)]
    solution = [None] * levels
    for height in reversed(range(levels)):
        partial_value = jnp.einsum(
            "sci,scr->sir",
            diag_inv[height],
            forward_values[height] - carried[height],
            precision=highest,
        )
        own_share = lax.psum_scatter(partial_value, "cols", scatter_dimension=1, tiled=True)
        if height > 0:
            whole_block = lax.all_gather(own_share, "cols", axis=1, tiled=True)
        solution[height] = own_share
        if height > 0:
            term_set = jnp.einsum(
                "skci,sir->skcr", factor_tiles[height - 1], whole_block, precision=highest
            )
            term_set = term_set * live_mask(tile_count[height - 1])[:, :, None, None]
            places = window_places(tile_source[height - 1]).reshape(-1)
            targets = height * window_len * owned_count
            one_hot = (jnp.arange(targets, dtype=jnp.int32)[:, None] == places[None, :]).astype(
                jnp.float32
            )
            outgoing = jnp.einsum(
                "ms,slg->mlg",
                one_hot,
                term_set.reshape(owned_count * slot_count, share_rows, columns),
                precision=highest,
            )
            push_outgoing = outgoing.reshape(height, window_len, owned_count, share_rows, columns)
            received = push_outgoing[:, reach_dev]
            for offset in range(-reach_dev, reach_dev + 1):
                if offset != 0:
                    received = received + from_behind(
                        push_outgoing[:, reach_dev + offset], "rows", offset
                    )
            for lower_level in range(height):
                carried[lower_level] = carried[lower_level] + received[lower_level]
    return jnp.stack(solution, 0)


def solution(mesh):
    placed = (
        P(None, "rows", "cols", None),
        P(None, "rows", "cols", None),
        P(None, "rows", None, "cols", None),
        P(None, "rows", None),
        P(None, "rows"),
    )
    return jax.shard_map(
        local, mesh=mesh, in_specs=placed, out_specs=P(None, "rows", "cols", None), check_vma=False
    )
```

profile of v0, /device:TPU:0, one launch (start us, length us, event | category | flops | bytes accessed | tf_op | source)
XLA Modules:
  0.0 392.5 jit_solution(14893982344654568340)
XLA Ops:
  7.5 7.1 %all-gather = f32[1,2,256,128]{3,2,1,0:T(8,128)S(1)} all-gather(f32[1,2,128,128]{3,2,1,0:T(8,128)S(1)} %get-tuple-element.35), channel_id=2, replica_groups=mesh['rows'=16,'cols'=2] {'cols'}, dimensions={2}, use_global_device_ids=true | all-gather | bytes 393216 | tf_op jit(solution)/shard_map/all_gather | solution.py:39
  16.0 3.2 collective-permute-start
  19.2 4.5 %collective-permute-start.1 = (f32[2,128,128]{2,1,0:T(8,128)S(1)}, f32[2,128,128]{2,1,0:T(8,128)S(1)}, u32[]{:S(2)}, u32[]{:S(2)}) collective-permute-start(f32[2,128,128]{2,1,0:T(8,128)S(1)} %fusion.44), channel_id=1, source_target_pairs={{0,12},{2,14},{4,16},{6,18},{8,20},{10,22},{12,24},{14,26},{16,28}... | collective-permute-start | bytes 393224 | tf_op jit(solution)/shard_map/ppermute | solution.py:12
  27.2 3.7 collective-permute-start.4
  33.3 2.1 collective-permute-start.5
  45.3 3.5 collective-permute-done.8
  50.2 4.9 %collective-permute-done.10 = f32[2,128,128]{2,1,0:T(8,128)S(1)} collective-permute-done((f32[2,128,128]{2,1,0:T(8,128)S(1)}, f32[2,128,128]{2,1,0:T(8,128)S(1)}, u32[]{:S(2)}, u32[]{:S(2)}) %collective-permute-start.10) | collective-permute-done | bytes 131104 | tf_op jit(solution)/shard_map/ppermute | solution.py:12
  56.6 2.1 collective-permute-done.12
  58.7 2.3 collective-permute-done.13
  61.6 4.3 %fusion.18 = f32[2,256,128]{1,2,0:T(8,128)} fusion(f32[2,2,8,128,256]{4,3,2,1,0:T(8,128)} %param.7, f32[2,8,128,128]{3,2,1,0:T(8,128)S(1)} %bitcast.369, f32[2,8]{1,0:T(2,128)S(1)} %get-tuple-element.46, pred[2,8]{1,0:T(4,128)(4,1)S(1)} %get-tuple-element.39), kind=kOutput, calls=%fused_computation.21 | convolution fusion | flops 805830656 | bytes 3407952 | tf_op jit(solution)/shard_map/skci,skcr->sir/dot_general | solution.py:55
  66.1 18.7 %reduce-scatter.6.cloned.1.call-done = f32[2,128,128]{1,2,0:T(8,128)} async-done(((f32[2,256,128]{1,2,0:T(8,128)}), f32[2,128,128]{1,2,0:T(8,128)}) %reduce-scatter.6.cloned.1.call-update) | async-done | bytes 131088 | tf_op jit(solution)/shard_map/reduce_scatter | solution.py:60
  85.7 5.9 %all_gather.16 = f32[2,256,128]{1,2,0:T(8,128)S(1)} all-gather(f32[2,128,128]{1,2,0:T(8,128)S(1)} %bitcast_subtract_fusion), channel_id=1, replica_groups=mesh['rows'=16,'cols'=2] {'cols'}, dimensions={1}, use_global_device_ids=true | all-gather | bytes 393216 | tf_op jit(solution)/shard_map/all_gather | solution.py:39
  92.9 2.9 collective-permute-start.14
  96.0 4.3 %collective-permute-start.15 = (f32[2,128,128]{2,1,0:T(8,128)S(1)}, f32[2,128,128]{2,1,0:T(8,128)S(1)}, u32[]{:S(2)}, u32[]{:S(2)}) collective-permute-start(f32[2,128,128]{2,1,0:T(8,128)S(1)} %bitcast.372), channel_id=1, source_target_pairs={{0,12},{2,14},{4,16},{6,18},{8,20},{10,22},{12,24},{14,26},{16,28}... | collective-permute-start | bytes 393224 | tf_op jit(solution)/shard_map/ppermute | solution.py:12
  103.8 3.7 collective-permute-start.18
  107.5 2.1 collective-permute-start.19
  119.5 3.5 collective-permute-done.22
  124.4 4.9 %collective-permute-done.24 = f32[2,128,128]{2,1,0:T(8,128)S(1)} collective-permute-done((f32[2,128,128]{2,1,0:T(8,128)S(1)}, f32[2,128,128]{2,1,0:T(8,128)S(1)}, u32[]{:S(2)}, u32[]{:S(2)}) %collective-permute-start.24) | collective-permute-done | bytes 131104 | tf_op jit(solution)/shard_map/ppermute | solution.py:12
  130.5 4.5 %collective-permute-done.26 = f32[2,128,128]{2,1,0:T(8,128)S(1)} collective-permute-done((f32[2,128,128]{2,1,0:T(8,128)S(1)}, f32[2,128,128]{2,1,0:T(8,128)S(1)}, u32[]{:S(2)}, u32[]{:S(2)}) %collective-permute-start.26) | collective-permute-done | bytes 131104 | tf_op jit(solution)/shard_map/ppermute | solution.py:12
  136.4 2.2 pad_maximum_fusion
  138.6 2.7 gather_fusion.1
  141.4 5.9 %fusion.21 = f32[2,256,128]{2,1,0:T(8,128)} fusion(f32[2,2,8,128,256]{4,3,2,1,0:T(8,128)} %param.7, f32[2,8,128,128]{3,2,1,0:T(8,128)S(1)} %bitcast.368, f32[2,8]{1,0:T(2,128)S(1)} %compare_convert_fusion, pred[2,8]{1,0:T(4,128)(4,1)S(1)} %get-tuple-element.38), kind=kOutput, calls=%fused_computation.22 | convolution fusion | flops 805830656 | bytes 3407952 | tf_op jit(solution)/shard_map/skci,skcr->sir/dot_general | solution.py:55
  147.4 18.1 %reduce-scatter.8.cloned.1.call-done = f32[2,128,128]{2,1,0:T(8,128)} async-done(((f32[2,256,128]{2,1,0:T(8,128)}), f32[2,128,128]{2,1,0:T(8,128)}) %reduce-scatter.8.cloned.1.call-update) | async-done | bytes 131088 | tf_op jit(solution)/shard_map/reduce_scatter | solution.py:60
  166.5 5.9 %all_gather.17 = f32[2,256,128]{2,1,0:T(8,128)S(1)} all-gather(f32[2,128,128]{2,1,0:T(8,128)S(1)} %bitcast_subtract_fusion.1), channel_id=1, replica_groups=mesh['rows'=16,'cols'=2] {'cols'}, dimensions={1}, use_global_device_ids=true | all-gather | bytes 393216 | tf_op jit(solution)/shard_map/all_gather | solution.py:39
  174.4 11.5 %reduce-scatter.10.cloned.1.call-done = f32[2,128,128]{1,2,0:T(8,128)} async-done(((f32[2,256,128]{1,2,0:T(8,128)}), f32[2,128,128]{1,2,0:T(8,128)}) %reduce-scatter.10.cloned.1.call-update) | async-done | bytes 131088 | tf_op jit(solution)/shard_map/reduce_scatter | solution.py:81
  186.0 6.3 %all_gather.18 = f32[2,256,128]{1,2,0:T(8,128)S(1)} all-gather(f32[2,128,128]{1,2,0:T(8,128)} %reduce-scatter.10.cloned.1.call-done), channel_id=1, replica_groups=mesh['rows'=16,'cols'=2] {'cols'}, dimensions={1}, use_global_device_ids=true | all-gather | bytes 393216 | tf_op jit(solution)/shard_map/all_gather | solution.py:83
  192.3 3.8 fusion.15
  198.5 3.7 fusion.97
  208.7 5.6 %collective-permute-done.28 = f32[2,2,128,128]{3,2,1,0:T(8,128)S(1)} collective-permute-done((f32[2,2,128,128]{3,2,1,0:T(8,128)S(1)}, f32[2,2,128,128]{3,2,1,0:T(8,128)S(1)}, u32[]{:S(2)}, u32[]{:S(2)}) %collective-permute-start.28) | collective-permute-done | bytes 262176 | tf_op jit(solution)/shard_map/ppermute | solution.py:12
  218.9 13.5 %collective-permute-start.35 = (f32[2,2,128,128]{3,2,1,0:T(8,128)S(1)}, f32[2,2,128,128]{3,2,1,0:T(8,128)S(1)}, u32[]{:S(2)}, u32[]{:S(2)}) collective-permute-start(f32[2,2,128,128]{3,2,1,0:T(8,128)S(1)} %bitcast.394), channel_id=1, source_target_pairs={{0,2},{2,4},{4,6},{6,8},{8,10},{10,12},{12,14},{14,16},{16,18},{18... | collective-permute-start | bytes 786440 | tf_op jit(solution)/shard_map/ppermute | solution.py:12
  232.4 11.3 %collective-permute-start.36 = (f32[2,2,128,128]{3,2,1,0:T(8,128)S(1)}, f32[2,2,128,128]{3,2,1,0:T(8,128)S(1)}, u32[]{:S(2)}, u32[]{:S(2)}) collective-permute-start(f32[2,2,128,128]{3,2,1,0:T(8,128)S(1)} %bitcast.393), channel_id=1, source_target_pairs={{0,4},{2,6},{4,8},{6,10},{8,12},{10,14},{12,16},{14,18},{16,20},{1... | collective-permute-start | bytes 786440 | tf_op jit(solution)/shard_map/ppermute | solution.py:12
  243.8 6.2 %collective-permute-start.37 = (f32[2,2,128,128]{3,2,1,0:T(8,128)S(1)}, f32[2,2,128,128]{3,2,1,0:T(8,128)S(1)}, u32[]{:S(2)}, u32[]{:S(2)}) collective-permute-start(f32[2,2,128,128]{3,2,1,0:T(8,128)S(1)} %bitcast.392), channel_id=1, source_target_pairs={{0,6},{2,8},{4,10},{6,12},{8,14},{10,16},{12,18},{14,20},{16,22},{... | collective-permute-start | bytes 786440 | tf_op jit(solution)/shard_map/ppermute | solution.py:12
  251.8 7.9 %collective-permute-start.39 = (f32[2,2,128,128]{3,2,1,0:T(8,128)S(1)}, f32[2,2,128,128]{3,2,1,0:T(8,128)S(1)}, u32[]{:S(2)}, u32[]{:S(2)}) collective-permute-start(f32[2,2,128,128]{3,2,1,0:T(8,128)S(1)} %bitcast.390), channel_id=1, source_target_pairs={{0,10},{2,12},{4,14},{6,16},{8,18},{10,20},{12,22},{14,24},{16,26}... | collective-permute-start | bytes 786440 | tf_op jit(solution)/shard_map/ppermute | solution.py:12
  259.6 3.2 collective-permute-start.40
  262.8 3.6 collective-permute-start.41
  266.5 4.8 %collective-permute-done.40 = f32[2,2,128,128]{3,2,1,0:T(8,128)S(1)} collective-permute-done((f32[2,2,128,128]{3,2,1,0:T(8,128)S(1)}, f32[2,2,128,128]{3,2,1,0:T(8,128)S(1)}, u32[]{:S(2)}, u32[]{:S(2)}) %collective-permute-start.40) | collective-permute-done | bytes 262176 | tf_op jit(solution)/shard_map/ppermute | solution.py:12
  271.3 5.6 %collective-permute-done.41 = f32[2,2,128,128]{3,2,1,0:T(8,128)S(1)} collective-permute-done((f32[2,2,128,128]{3,2,1,0:T(8,128)S(1)}, f32[2,2,128,128]{3,2,1,0:T(8,128)S(1)}, u32[]{:S(2)}, u32[]{:S(2)}) %collective-permute-start.41) | collective-permute-done | bytes 262176 | tf_op jit(solution)/shard_map/ppermute | solution.py:12
  278.3 29.7 %reduce-scatter.12.cloned.1.call-done = f32[2,128,128]{1,2,0:T(8,128)} async-done(((f32[2,256,128]{1,2,0:T(8,128)}), f32[2,128,128]{1,2,0:T(8,128)}) %reduce-scatter.12.cloned.1.call-update) | async-done | bytes 131088 | tf_op jit(solution)/shard_map/reduce_scatter | solution.py:81
  308.0 6.1 %all_gather.19 = f32[2,256,128]{1,2,0:T(8,128)S(1)} all-gather(f32[2,128,128]{1,2,0:T(8,128)} %reduce-scatter.12.cloned.1.call-done), channel_id=1, replica_groups=mesh['rows'=16,'cols'=2] {'cols'}, dimensions={1}, use_global_device_ids=true | all-gather | bytes 393216 | tf_op jit(solution)/shard_map/all_gather | solution.py:83
  314.1 3.8 fusion.12
  333.0 7.7 %collective-permute-start.49 = (f32[1,2,128,128]{3,2,1,0:T(8,128)S(1)}, f32[1,2,128,128]{3,2,1,0:T(8,128)S(1)}, u32[]{:S(2)}, u32[]{:S(2)}) collective-permute-start(f32[1,2,128,128]{3,2,1,0:T(8,128)S(1)} %get-tuple-element.27), channel_id=1, source_target_pairs={{0,2},{2,4},{4,6},{6,8},{8,10},{10,12},{12,14},{14,16},{16,18},{18... | collective-permute-start | bytes 393224 | tf_op jit(solution)/shard_map/ppermute | solution.py:12
  340.8 5.7 %collective-permute-start.50 = (f32[1,2,128,128]{3,2,1,0:T(8,128)S(1)}, f32[1,2,128,128]{3,2,1,0:T(8,128)S(1)}, u32[]{:S(2)}, u32[]{:S(2)}) collective-permute-start(f32[1,2,128,128]{3,2,1,0:T(8,128)S(1)} %get-tuple-element.26), channel_id=1, source_target_pairs={{0,4},{2,6},{4,8},{6,10},{8,12},{10,14},{12,16},{14,18},{16,20},{1... | collective-permute-start | bytes 393224 | tf_op jit(solution)/shard_map/ppermute | solution.py:12
  346.5 4.1 %collective-permute-start.51 = (f32[1,2,128,128]{3,2,1,0:T(8,128)S(1)}, f32[1,2,128,128]{3,2,1,0:T(8,128)S(1)}, u32[]{:S(2)}, u32[]{:S(2)}) collective-permute-start(f32[1,2,128,128]{3,2,1,0:T(8,128)S(1)} %get-tuple-element.25), channel_id=1, source_target_pairs={{0,6},{2,8},{4,10},{6,12},{8,14},{10,16},{12,18},{14,20},{16,22},{... | collective-permute-start | bytes 393224 | tf_op jit(solution)/shard_map/ppermute | solution.py:12
  351.9 2.1 collective-permute-start.53
  354.0 3.2 collective-permute-start.54
  357.2 2.5 collective-permute-start.55
  361.2 2.3 collective-permute-done.55
  364.8 19.3 %reduce-scatter.14.cloned.1.call-done = f32[2,128,128]{1,2,0:T(8,128)} async-done(((f32[2,256,128]{1,2,0:T(8,128)}), f32[2,128,128]{1,2,0:T(8,128)}) %reduce-scatter.14.cloned.1.call-update) | async-done | bytes 131088 | tf_op jit(solution)/shard_map/reduce_scatter | solution.py:81
  (163 shorter events, 81.4 us)
Async XLA Ops:
  6.5 78.2 %reduce-scatter.6.cloned.1.call-start = ((), (), s32[]{:S(2)}) async-start(), calls=%async_computation.5 | async-start | bytes 393216 | tf_op jit(solution)/shard_map/reduce_scatter | solution.py:60
  16.0 17.3 %collective-permute-start = (f32[2,128,128]{2,1,0:T(8,128)S(1)}, f32[2,128,128]{2,1,0:T(8,128)S(1)}, u32[]{:S(2)}, u32[]{:S(2)}) collective-permute-start(f32[2,128,128]{2,1,0:T(8,128)S(1)} %fusion.44), channel_id=1, source_target_pairs={{0,14},{2,16},{4,18},{6,20},{8,22},{10,24},{12,26},{14,28},{16,30}... | collective-permute-start | bytes 393224 | tf_op jit(solution)/shard_map/ppermute | solution.py:12
  19.2 16.2 %collective-permute-start.1 = (f32[2,128,128]{2,1,0:T(8,128)S(1)}, f32[2,128,128]{2,1,0:T(8,128)S(1)}, u32[]{:S(2)}, u32[]{:S(2)}) collective-permute-start(f32[2,128,128]{2,1,0:T(8,128)S(1)} %fusion.44), channel_id=1, source_target_pairs={{0,12},{2,14},{4,16},{6,18},{8,20},{10,22},{12,24},{14,26},{16,28}... | collective-permute-start | bytes 393224 | tf_op jit(solution)/shard_map/ppermute | solution.py:12
  23.7 13.6 %collective-permute-start.2 = (f32[2,128,128]{2,1,0:T(8,128)S(1)}, f32[2,128,128]{2,1,0:T(8,128)S(1)}, u32[]{:S(2)}, u32[]{:S(2)}) collective-permute-start(f32[2,128,128]{2,1,0:T(8,128)S(1)} %fusion.44), channel_id=1, source_target_pairs={{0,10},{2,12},{4,14},{6,16},{8,18},{10,20},{12,22},{14,24},{16,26}... | collective-permute-start | bytes 393224 | tf_op jit(solution)/shard_map/ppermute | solution.py:12
  25.3 13.4 %collective-permute-start.3 = (f32[2,128,128]{2,1,0:T(8,128)S(1)}, f32[2,128,128]{2,1,0:T(8,128)S(1)}, u32[]{:S(2)}, u32[]{:S(2)}) collective-permute-start(f32[2,128,128]{2,1,0:T(8,128)S(1)} %fusion.44), channel_id=1, source_target_pairs={{0,8},{2,10},{4,12},{6,14},{8,16},{10,18},{12,20},{14,22},{16,24},... | collective-permute-start | bytes 393224 | tf_op jit(solution)/shard_map/ppermute | solution.py:12
  27.2 12.7 %collective-permute-start.4 = (f32[2,128,128]{2,1,0:T(8,128)S(1)}, f32[2,128,128]{2,1,0:T(8,128)S(1)}, u32[]{:S(2)}, u32[]{:S(2)}) collective-permute-start(f32[2,128,128]{2,1,0:T(8,128)S(1)} %fusion.44), channel_id=1, source_target_pairs={{0,6},{2,8},{4,10},{6,12},{8,14},{10,16},{12,18},{14,20},{16,22},{... | collective-permute-start | bytes 393224 | tf_op jit(solution)/shard_map/ppermute | solution.py:12
  38.6 10.2 %collective-permute-start.8 = (f32[2,128,128]{2,1,0:T(8,128)S(1)}, f32[2,128,128]{2,1,0:T(8,128)S(1)}, u32[]{:S(2)}, u32[]{:S(2)}) collective-permute-start(f32[2,128,128]{2,1,0:T(8,128)S(1)} %fusion.44), channel_id=1, source_target_pairs={{4,0},{6,2},{8,4},{10,6},{12,8},{14,10},{16,12},{18,14},{20,16},{2... | collective-permute-start | bytes 393224 | tf_op jit(solution)/shard_map/ppermute | solution.py:12
  40.0 10.2 %collective-permute-start.9 = (f32[2,128,128]{2,1,0:T(8,128)S(1)}, f32[2,128,128]{2,1,0:T(8,128)S(1)}, u32[]{:S(2)}, u32[]{:S(2)}) collective-permute-start(f32[2,128,128]{2,1,0:T(8,128)S(1)} %fusion.44), channel_id=1, source_target_pairs={{6,0},{8,2},{10,4},{12,6},{14,8},{16,10},{18,12},{20,14},{22,16},{... | collective-permute-start | bytes 393224 | tf_op jit(solution)/shard_map/ppermute | solution.py:12
  41.3 13.7 %collective-permute-start.10 = (f32[2,128,128]{2,1,0:T(8,128)S(1)}, f32[2,128,128]{2,1,0:T(8,128)S(1)}, u32[]{:S(2)}, u32[]{:S(2)}) collective-permute-start(f32[2,128,128]{2,1,0:T(8,128)S(1)} %fusion.44), channel_id=1, source_target_pairs={{8,0},{10,2},{12,4},{14,6},{16,8},{18,10},{20,12},{22,14},{24,16},... | collective-permute-start | bytes 393224 | tf_op jit(solution)/shard_map/ppermute | solution.py:12
  42.6 13.9 %collective-permute-start.11 = (f32[2,128,128]{2,1,0:T(8,128)S(1)}, f32[2,128,128]{2,1,0:T(8,128)S(1)}, u32[]{:S(2)}, u32[]{:S(2)}) collective-permute-start(f32[2,128,128]{2,1,0:T(8,128)S(1)} %fusion.44), channel_id=1, source_target_pairs={{10,0},{12,2},{14,4},{16,6},{18,8},{20,10},{22,12},{24,14},{26,16}... | collective-permute-start | bytes 393224 | tf_op jit(solution)/shard_map/ppermute | solution.py:12
  44.0 14.7 %collective-permute-start.12 = (f32[2,128,128]{2,1,0:T(8,128)S(1)}, f32[2,128,128]{2,1,0:T(8,128)S(1)}, u32[]{:S(2)}, u32[]{:S(2)}) collective-permute-start(f32[2,128,128]{2,1,0:T(8,128)S(1)} %fusion.44), channel_id=1, source_target_pairs={{12,0},{14,2},{16,4},{18,6},{20,8},{22,10},{24,12},{26,14},{28,16}... | collective-permute-start | bytes 393224 | tf_op jit(solution)/shard_map/ppermute | solution.py:12
  48.8 12.1 %collective-permute-start.13 = (f32[2,128,128]{2,1,0:T(8,128)S(1)}, f32[2,128,128]{2,1,0:T(8,128)S(1)}, u32[]{:S(2)}, u32[]{:S(2)}) collective-permute-start(f32[2,128,128]{2,1,0:T(8,128)S(1)} %fusion.44), channel_id=1, source_target_pairs={{14,0},{16,2},{18,4},{20,6},{22,8},{24,10},{26,12},{28,14},{30,16}... | collective-permute-start | bytes 393224 | tf_op jit(solution)/shard_map/ppermute | solution.py:12
  65.9 99.5 %reduce-scatter.8.cloned.1.call-start = ((), (), s32[]{:S(2)}) async-start(), calls=%async_computation.6 | async-start | bytes 393216 | tf_op jit(solution)/shard_map/reduce_scatter | solution.py:60
  92.9 14.6 %collective-permute-start.14 = (f32[2,128,128]{2,1,0:T(8,128)S(1)}, f32[2,128,128]{2,1,0:T(8,128)S(1)}, u32[]{:S(2)}, u32[]{:S(2)}) collective-permute-start(f32[2,128,128]{2,1,0:T(8,128)S(1)} %bitcast.371), channel_id=1, source_target_pairs={{0,14},{2,16},{4,18},{6,20},{8,22},{10,24},{12,26},{14,28},{16,30}... | collective-permute-start | bytes 393224 | tf_op jit(solution)/shard_map/ppermute | solution.py:12
  96.0 13.7 %collective-permute-start.15 = (f32[2,128,128]{2,1,0:T(8,128)S(1)}, f32[2,128,128]{2,1,0:T(8,128)S(1)}, u32[]{:S(2)}, u32[]{:S(2)}) collective-permute-start(f32[2,128,128]{2,1,0:T(8,128)S(1)} %bitcast.372), channel_id=1, source_target_pairs={{0,12},{2,14},{4,16},{6,18},{8,20},{10,22},{12,24},{14,26},{16,28}... | collective-permute-start | bytes 393224 | tf_op jit(solution)/shard_map/ppermute | solution.py:12
  100.3 11.3 %collective-permute-start.16 = (f32[2,128,128]{2,1,0:T(8,128)S(1)}, f32[2,128,128]{2,1,0:T(8,128)S(1)}, u32[]{:S(2)}, u32[]{:S(2)}) collective-permute-start(f32[2,128,128]{2,1,0:T(8,128)S(1)} %bitcast.373), channel_id=1, source_target_pairs={{0,10},{2,12},{4,14},{6,16},{8,18},{10,20},{12,22},{14,24},{16,26}... | collective-permute-start | bytes 393224 | tf_op jit(solution)/shard_map/ppermute | solution.py:12
  101.8 11.0 %collective-permute-start.17 = (f32[2,128,128]{2,1,0:T(8,128)S(1)}, f32[2,128,128]{2,1,0:T(8,128)S(1)}, u32[]{:S(2)}, u32[]{:S(2)}) collective-permute-start(f32[2,128,128]{2,1,0:T(8,128)S(1)} %bitcast.374), channel_id=1, source_target_pairs={{0,8},{2,10},{4,12},{6,14},{8,16},{10,18},{12,20},{14,22},{16,24},... | collective-permute-start | bytes 393224 | tf_op jit(solution)/shard_map/ppermute | solution.py:12
  103.8 10.4 %collective-permute-start.18 = (f32[2,128,128]{2,1,0:T(8,128)S(1)}, f32[2,128,128]{2,1,0:T(8,128)S(1)}, u32[]{:S(2)}, u32[]{:S(2)}) collective-permute-start(f32[2,128,128]{2,1,0:T(8,128)S(1)} %bitcast.375), channel_id=1, source_target_pairs={{0,6},{2,8},{4,10},{6,12},{8,14},{10,16},{12,18},{14,20},{16,22},{... | collective-permute-start | bytes 393224 | tf_op jit(solution)/shard_map/ppermute | solution.py:12
  112.9 10.2 %collective-permute-start.22 = (f32[2,128,128]{2,1,0:T(8,128)S(1)}, f32[2,128,128]{2,1,0:T(8,128)S(1)}, u32[]{:S(2)}, u32[]{:S(2)}) collective-permute-start(f32[2,128,128]{2,1,0:T(8,128)S(1)} %bitcast.379), channel_id=1, source_target_pairs={{4,0},{6,2},{8,4},{10,6},{12,8},{14,10},{16,12},{18,14},{20,16},{2... | collective-permute-start | bytes 393224 | tf_op jit(solution)/shard_map/ppermute | solution.py:12
  114.2 10.2 %collective-permute-start.23 = (f32[2,128,128]{2,1,0:T(8,128)S(1)}, f32[2,128,128]{2,1,0:T(8,128)S(1)}, u32[]{:S(2)}, u32[]{:S(2)}) collective-permute-start(f32[2,128,128]{2,1,0:T(8,128)S(1)} %bitcast.380), channel_id=1, source_target_pairs={{6,0},{8,2},{10,4},{12,6},{14,8},{16,10},{18,12},{20,14},{22,16},{... | collective-permute-start | bytes 393224 | tf_op jit(solution)/shard_map/ppermute | solution.py:12
  115.5 13.8 %collective-permute-start.24 = (f32[2,128,128]{2,1,0:T(8,128)S(1)}, f32[2,128,128]{2,1,0:T(8,128)S(1)}, u32[]{:S(2)}, u32[]{:S(2)}) collective-permute-start(f32[2,128,128]{2,1,0:T(8,128)S(1)} %bitcast.381), channel_id=1, source_target_pairs={{8,0},{10,2},{12,4},{14,6},{16,8},{18,10},{20,12},{22,14},{24,16},... | collective-permute-start | bytes 393224 | tf_op jit(solution)/shard_map/ppermute | solution.py:12
  116.9 13.6 %collective-permute-start.25 = (f32[2,128,128]{2,1,0:T(8,128)S(1)}, f32[2,128,128]{2,1,0:T(8,128)S(1)}, u32[]{:S(2)}, u32[]{:S(2)}) collective-permute-start(f32[2,128,128]{2,1,0:T(8,128)S(1)} %bitcast.382), channel_id=1, source_target_pairs={{10,0},{12,2},{14,4},{16,6},{18,8},{20,10},{22,12},{24,14},{26,16}... | collective-permute-start | bytes 393224 | tf_op jit(solution)/shard_map/ppermute | solution.py:12
  118.2 16.8 %collective-permute-start.26 = (f32[2,128,128]{2,1,0:T(8,128)S(1)}, f32[2,128,128]{2,1,0:T(8,128)S(1)}, u32[]{:S(2)}, u32[]{:S(2)}) collective-permute-start(f32[2,128,128]{2,1,0:T(8,128)S(1)} %bitcast.383), channel_id=1, source_target_pairs={{12,0},{14,2},{16,4},{18,6},{20,8},{22,10},{24,12},{26,14},{28,16}... | collective-permute-start | bytes 393224 | tf_op jit(solution)/shard_map/ppermute | solution.py:12
  123.1 13.3 %collective-permute-start.27 = (f32[2,128,128]{2,1,0:T(8,128)S(1)}, f32[2,128,128]{2,1,0:T(8,128)S(1)}, u32[]{:S(2)}, u32[]{:S(2)}) collective-permute-start(f32[2,128,128]{2,1,0:T(8,128)S(1)} %bitcast.384), channel_id=1, source_target_pairs={{14,0},{16,2},{18,4},{20,6},{22,8},{24,10},{26,12},{28,14},{30,16}... | collective-permute-start | bytes 393224 | tf_op jit(solution)/shard_map/ppermute | solution.py:12
  147.3 38.6 %reduce-scatter.10.cloned.1.call-start = ((), (), s32[]{:S(2)}) async-start(), calls=%async_computation.7 | async-start | bytes 393216 | tf_op jit(solution)/shard_map/reduce_scatter | solution.py:81
  174.1 133.9 %reduce-scatter.12.cloned.1.call-start = ((), (), s32[]{:S(2)}) async-start(), calls=%async_computation.8 | async-start | bytes 393216 | tf_op jit(solution)/shard_map/reduce_scatter | solution.py:81
  202.2 12.1 %collective-permute-start.28 = (f32[2,2,128,128]{3,2,1,0:T(8,128)S(1)}, f32[2,2,128,128]{3,2,1,0:T(8,128)S(1)}, u32[]{:S(2)}, u32[]{:S(2)}) collective-permute-start(f32[2,2,128,128]{3,2,1,0:T(8,128)S(1)} %bitcast.401), channel_id=1, source_target_pairs={{14,0},{16,2},{18,4},{20,6},{22,8},{24,10},{26,12},{28,14},{30,16}... | collective-permute-start | bytes 786440 | tf_op jit(solution)/shard_map/ppermute | solution.py:12
  203.5 14.1 %collective-permute-start.29 = (f32[2,2,128,128]{3,2,1,0:T(8,128)S(1)}, f32[2,2,128,128]{3,2,1,0:T(8,128)S(1)}, u32[]{:S(2)}, u32[]{:S(2)}) collective-permute-start(f32[2,2,128,128]{3,2,1,0:T(8,128)S(1)} %bitcast.400), channel_id=1, source_target_pairs={{12,0},{14,2},{16,4},{18,6},{20,8},{22,10},{24,12},{26,14},{28,16}... | collective-permute-start | bytes 786440 | tf_op jit(solution)/shard_map/ppermute | solution.py:12
  204.8 14.1 %collective-permute-start.30 = (f32[2,2,128,128]{3,2,1,0:T(8,128)S(1)}, f32[2,2,128,128]{3,2,1,0:T(8,128)S(1)}, u32[]{:S(2)}, u32[]{:S(2)}) collective-permute-start(f32[2,2,128,128]{3,2,1,0:T(8,128)S(1)} %bitcast.399), channel_id=1, source_target_pairs={{10,0},{12,2},{14,4},{16,6},{18,8},{20,10},{22,12},{24,14},{26,16}... | collective-permute-start | bytes 786440 | tf_op jit(solution)/shard_map/ppermute | solution.py:12
  206.1 26.3 %collective-permute-start.31 = (f32[2,2,128,128]{3,2,1,0:T(8,128)S(1)}, f32[2,2,128,128]{3,2,1,0:T(8,128)S(1)}, u32[]{:S(2)}, u32[]{:S(2)}) collective-permute-start(f32[2,2,128,128]{3,2,1,0:T(8,128)S(1)} %bitcast.398), channel_id=1, source_target_pairs={{8,0},{10,2},{12,4},{14,6},{16,8},{18,10},{20,12},{22,14},{24,16},... | collective-permute-start | bytes 786440 | tf_op jit(solution)/shard_map/ppermute | solution.py:12
  207.4 36.4 %collective-permute-start.32 = (f32[2,2,128,128]{3,2,1,0:T(8,128)S(1)}, f32[2,2,128,128]{3,2,1,0:T(8,128)S(1)}, u32[]{:S(2)}, u32[]{:S(2)}) collective-permute-start(f32[2,2,128,128]{3,2,1,0:T(8,128)S(1)} %bitcast.397), channel_id=1, source_target_pairs={{6,0},{8,2},{10,4},{12,6},{14,8},{16,10},{18,12},{20,14},{22,16},{... | collective-permute-start | bytes 786440 | tf_op jit(solution)/shard_map/ppermute | solution.py:12
  214.3 35.7 %collective-permute-start.33 = (f32[2,2,128,128]{3,2,1,0:T(8,128)S(1)}, f32[2,2,128,128]{3,2,1,0:T(8,128)S(1)}, u32[]{:S(2)}, u32[]{:S(2)}) collective-permute-start(f32[2,2,128,128]{3,2,1,0:T(8,128)S(1)} %bitcast.396), channel_id=1, source_target_pairs={{4,0},{6,2},{8,4},{10,6},{12,8},{14,10},{16,12},{18,14},{20,16},{2... | collective-permute-start | bytes 786440 | tf_op jit(solution)/shard_map/ppermute | solution.py:12
  217.6 34.1 %collective-permute-start.34 = (f32[2,2,128,128]{3,2,1,0:T(8,128)S(1)}, f32[2,2,128,128]{3,2,1,0:T(8,128)S(1)}, u32[]{:S(2)}, u32[]{:S(2)}) collective-permute-start(f32[2,2,128,128]{3,2,1,0:T(8,128)S(1)} %bitcast.395), channel_id=1, source_target_pairs={{2,0},{4,2},{6,4},{8,6},{10,8},{12,10},{14,12},{16,14},{18,16},{20... | collective-permute-start | bytes 786440 | tf_op jit(solution)/shard_map/ppermute | solution.py:12
  218.9 40.7 %collective-permute-start.35 = (f32[2,2,128,128]{3,2,1,0:T(8,128)S(1)}, f32[2,2,128,128]{3,2,1,0:T(8,128)S(1)}, u32[]{:S(2)}, u32[]{:S(2)}) collective-permute-start(f32[2,2,128,128]{3,2,1,0:T(8,128)S(1)} %bitcast.394), channel_id=1, source_target_pairs={{0,2},{2,4},{4,6},{6,8},{8,10},{10,12},{12,14},{14,16},{16,18},{18... | collective-permute-start | bytes 786440 | tf_op jit(solution)/shard_map/ppermute | solution.py:12
  232.4 30.4 %collective-permute-start.36 = (f32[2,2,128,128]{3,2,1,0:T(8,128)S(1)}, f32[2,2,128,128]{3,2,1,0:T(8,128)S(1)}, u32[]{:S(2)}, u32[]{:S(2)}) collective-permute-start(f32[2,2,128,128]{3,2,1,0:T(8,128)S(1)} %bitcast.393), channel_id=1, source_target_pairs={{0,4},{2,6},{4,8},{6,10},{8,12},{10,14},{12,16},{14,18},{16,20},{1... | collective-permute-start | bytes 786440 | tf_op jit(solution)/shard_map/ppermute | solution.py:12
  243.8 22.7 %collective-permute-start.37 = (f32[2,2,128,128]{3,2,1,0:T(8,128)S(1)}, f32[2,2,128,128]{3,2,1,0:T(8,128)S(1)}, u32[]{:S(2)}, u32[]{:S(2)}) collective-permute-start(f32[2,2,128,128]{3,2,1,0:T(8,128)S(1)} %bitcast.392), channel_id=1, source_target_pairs={{0,6},{2,8},{4,10},{6,12},{8,14},{10,16},{12,18},{14,20},{16,22},{... | collective-permute-start | bytes 786440 | tf_op jit(solution)/shard_map/ppermute | solution.py:12
  250.0 16.4 %collective-permute-start.38 = (f32[2,2,128,128]{3,2,1,0:T(8,128)S(1)}, f32[2,2,128,128]{3,2,1,0:T(8,128)S(1)}, u32[]{:S(2)}, u32[]{:S(2)}) collective-permute-start(f32[2,2,128,128]{3,2,1,0:T(8,128)S(1)} %bitcast.391), channel_id=1, source_target_pairs={{0,8},{2,10},{4,12},{6,14},{8,16},{10,18},{12,20},{14,22},{16,24},... | collective-permute-start | bytes 786440 | tf_op jit(solution)/shard_map/ppermute | solution.py:12
  251.8 14.7 %collective-permute-start.39 = (f32[2,2,128,128]{3,2,1,0:T(8,128)S(1)}, f32[2,2,128,128]{3,2,1,0:T(8,128)S(1)}, u32[]{:S(2)}, u32[]{:S(2)}) collective-permute-start(f32[2,2,128,128]{3,2,1,0:T(8,128)S(1)} %bitcast.390), channel_id=1, source_target_pairs={{0,10},{2,12},{4,14},{6,16},{8,18},{10,20},{12,22},{14,24},{16,26}... | collective-permute-start | bytes 786440 | tf_op jit(solution)/shard_map/ppermute | solution.py:12
  259.6 11.6 %collective-permute-start.40 = (f32[2,2,128,128]{3,2,1,0:T(8,128)S(1)}, f32[2,2,128,128]{3,2,1,0:T(8,128)S(1)}, u32[]{:S(2)}, u32[]{:S(2)}) collective-permute-start(f32[2,2,128,128]{3,2,1,0:T(8,128)S(1)} %bitcast.389), channel_id=1, source_target_pairs={{0,12},{2,14},{4,16},{6,18},{8,20},{10,22},{12,24},{14,26},{16,28}... | collective-permute-start | bytes 786440 | tf_op jit(solution)/shard_map/ppermute | solution.py:12
  262.8 14.1 %collective-permute-start.41 = (f32[2,2,128,128]{3,2,1,0:T(8,128)S(1)}, f32[2,2,128,128]{3,2,1,0:T(8,128)S(1)}, u32[]{:S(2)}, u32[]{:S(2)}) collective-permute-start(f32[2,2,128,128]{3,2,1,0:T(8,128)S(1)} %bitcast.388), channel_id=1, source_target_pairs={{0,14},{2,16},{4,18},{6,20},{8,22},{10,24},{12,26},{14,28},{16,30}... | collective-permute-start | bytes 786440 | tf_op jit(solution)/shard_map/ppermute | solution.py:12
  278.3 105.9 %reduce-scatter.14.cloned.1.call-start = ((), (), s32[]{:S(2)}) async-start(), calls=%async_computation.9 | async-start | bytes 393216 | tf_op jit(solution)/shard_map/reduce_scatter | solution.py:81
  324.4 16.4 %collective-permute-start.45 = (f32[1,2,128,128]{3,2,1,0:T(8,128)S(1)}, f32[1,2,128,128]{3,2,1,0:T(8,128)S(1)}, u32[]{:S(2)}, u32[]{:S(2)}) collective-permute-start(f32[1,2,128,128]{3,2,1,0:T(8,128)S(1)} %get-tuple-element.31), channel_id=1, source_target_pairs={{8,0},{10,2},{12,4},{14,6},{16,8},{18,10},{20,12},{22,14},{24,16},... | collective-permute-start | bytes 393224 | tf_op jit(solution)/shard_map/ppermute | solution.py:12
  325.7 20.8 %collective-permute-start.46 = (f32[1,2,128,128]{3,2,1,0:T(8,128)S(1)}, f32[1,2,128,128]{3,2,1,0:T(8,128)S(1)}, u32[]{:S(2)}, u32[]{:S(2)}) collective-permute-start(f32[1,2,128,128]{3,2,1,0:T(8,128)S(1)} %get-tuple-element.30), channel_id=1, source_target_pairs={{6,0},{8,2},{10,4},{12,6},{14,8},{16,10},{18,12},{20,14},{22,16},{... | collective-permute-start | bytes 393224 | tf_op jit(solution)/shard_map/ppermute | solution.py:12
  328.8 21.7 %collective-permute-start.47 = (f32[1,2,128,128]{3,2,1,0:T(8,128)S(1)}, f32[1,2,128,128]{3,2,1,0:T(8,128)S(1)}, u32[]{:S(2)}, u32[]{:S(2)}) collective-permute-start(f32[1,2,128,128]{3,2,1,0:T(8,128)S(1)} %get-tuple-element.29), channel_id=1, source_target_pairs={{4,0},{6,2},{8,4},{10,6},{12,8},{14,10},{16,12},{18,14},{20,16},{2... | collective-permute-start | bytes 393224 | tf_op jit(solution)/shard_map/ppermute | solution.py:12
  331.7 20.2 %collective-permute-start.48 = (f32[1,2,128,128]{3,2,1,0:T(8,128)S(1)}, f32[1,2,128,128]{3,2,1,0:T(8,128)S(1)}, u32[]{:S(2)}, u32[]{:S(2)}) collective-permute-start(f32[1,2,128,128]{3,2,1,0:T(8,128)S(1)} %get-tuple-element.28), channel_id=1, source_target_pairs={{2,0},{4,2},{6,4},{8,6},{10,8},{12,10},{14,12},{16,14},{18,16},{20... | collective-permute-start | bytes 393224 | tf_op jit(solution)/shard_map/ppermute | solution.py:12
  333.0 21.0 %collective-permute-start.49 = (f32[1,2,128,128]{3,2,1,0:T(8,128)S(1)}, f32[1,2,128,128]{3,2,1,0:T(8,128)S(1)}, u32[]{:S(2)}, u32[]{:S(2)}) collective-permute-start(f32[1,2,128,128]{3,2,1,0:T(8,128)S(1)} %get-tuple-element.27), channel_id=1, source_target_pairs={{0,2},{2,4},{4,6},{6,8},{8,10},{10,12},{12,14},{14,16},{16,18},{18... | collective-permute-start | bytes 393224 | tf_op jit(solution)/shard_map/ppermute | solution.py:12
  340.8 16.5 %collective-permute-start.50 = (f32[1,2,128,128]{3,2,1,0:T(8,128)S(1)}, f32[1,2,128,128]{3,2,1,0:T(8,128)S(1)}, u32[]{:S(2)}, u32[]{:S(2)}) collective-permute-start(f32[1,2,128,128]{3,2,1,0:T(8,128)S(1)} %get-tuple-element.26), channel_id=1, source_target_pairs={{0,4},{2,6},{4,8},{6,10},{8,12},{10,14},{12,16},{14,18},{16,20},{1... | collective-permute-start | bytes 393224 | tf_op jit(solution)/shard_map/ppermute | solution.py:12
  346.5 13.3 %collective-permute-start.51 = (f32[1,2,128,128]{3,2,1,0:T(8,128)S(1)}, f32[1,2,128,128]{3,2,1,0:T(8,128)S(1)}, u32[]{:S(2)}, u32[]{:S(2)}) collective-permute-start(f32[1,2,128,128]{3,2,1,0:T(8,128)S(1)} %get-tuple-element.25), channel_id=1, source_target_pairs={{0,6},{2,8},{4,10},{6,12},{8,14},{10,16},{12,18},{14,20},{16,22},{... | collective-permute-start | bytes 393224 | tf_op jit(solution)/shard_map/ppermute | solution.py:12
  (17 other events, 288.1 us)
Sparse Core Ops, SparseCore 0:
  66.1 18.6 reduce-scatter.5
  147.4 18.0 reduce-scatter.7
  174.3 11.6 reduce-scatter.9
  278.4 29.5 reduce-scatter.11
  364.9 19.1 reduce-scatter.13
where the time goes:
time: 395 us; the launch traced here: 393 us
  waiting for transfers between devices  153 us (39%)
  starting transfers between devices  148 us (37%)
  blocking collectives  31.3 us (8%)
  matrix products  27.5 us (7%)
  between operations  14.3 us (4%)
  local copies, waits for them, and re-layouts  12.3 us (3%)
  other arithmetic  6.86 us (2%)
    ppermute x56, starting transfers between devices, from_behind(): lax.ppermute(value, axis, [(source, source + steps) for source in range(l...  147 us
    reduce_scatter x5, waiting for transfers between devices, local(): lax.psum_scatter(partial_value, 'cols', scatter_dimension=1, tiled=True)  97.4 us
    ppermute x56, waiting for transfers between devices, from_behind(): lax.ppermute(value, axis, [(source, source + steps) for source in range(l...  55.1 us
    all_gather x3, blocking collectives, full_rows(): return lax.all_gather(piece, 'cols', axis=1, tiled=True)  18.9 us
    all_gather x2, blocking collectives, local(): whole_block = lax.all_gather(own_share, 'cols', axis=1, tiled=True)  12.4 us
    dot_general x2, matrix products, local(): jnp.einsum('skci,skcr->sir', factor_tiles[height - 1], picked, precision=...  10.2 us
  transfers between devices with their start and end apart: 61, of which 23 were waited for; matrix products, arithmetic and copies ran while one was open for 1% of the time, Pallas kernels for 0%

commit v1 on v0

--- a/solution.py
+++ b/solution.py
@@ -1,6 +1,10 @@
+import functools
+
 import jax
 import jax.numpy as jnp
 from jax import lax
+from jax.experimental import pallas as pl
+from jax.experimental.pallas import tpu as pltpu
 from jax.sharding import PartitionSpec as P
 
 KDEV = 7
@@ -12,7 +16,7 @@
     return lax.ppermute(value, axis, [(source, source + steps) for source in range(leading, last)])
 
 
-def local(rhs, diag_inv, factor_tiles, tile_source, tile_count):
+def local_any(rhs, diag_inv, factor_tiles, tile_source, tile_count):
     levels = rhs.shape[0]
     owned_count = rhs.shape[1]
     share_rows = rhs.shape[2]
@@ -110,6 +114,316 @@
     return jnp.stack(solution, 0)
 
 
+F32 = jnp.float32
+BF16 = jnp.bfloat16
+NN = (((1,), (0,)), ((), ()))
+NT = (((1,), (1,)), ((), ()))
+TN = (((0,), (0,)), ((), ()))
+PIECES = 8
+
+
+def halves(value):
+    high = value.astype(BF16)
+    return high, (value - high.astype(F32)).astype(BF16)
+
+
+def dot3(left, right, dims):
+    left_high, left_low = halves(left)
+    right_high, right_low = halves(right)
+    dot = functools.partial(lax.dot_general, dimension_numbers=dims, preferred_element_type=F32)
+    return dot(left_high, right_high) + dot(left_low, right_high) + dot(left_high, right_low)
+
+
+def ordered(mine, theirs, place, axis):
+    first = jnp.where(place == 0, mine, theirs)
+    second = jnp.where(place == 0, theirs, mine)
+    return jnp.concatenate([first, second], axis)
+
+
+def call(kernel, name, outs, args, scalars=1, scratch=()):
+    in_specs = [pl.BlockSpec(memory_space=pltpu.SMEM)] * scalars
+    in_specs += [pl.BlockSpec(memory_space=pltpu.VMEM)] * (len(args) - scalars)
+    out_shape = [jax.ShapeDtypeStruct(shape, F32) for shape in outs]
+    return pl.pallas_call(
+        kernel,
+        out_shape=out_shape,
+        in_specs=in_specs,
+        out_specs=[pl.BlockSpec(memory_space=pltpu.VMEM)] * len(outs),
+        scratch_shapes=list(scratch),
+        name=name,
+        compiler_params=pltpu.CompilerParams(vmem_limit_bytes=40 * 1024 * 1024),
+    )(*args)
+
+
+def first_values(where, rhs_own, rhs_other, diag, mine, partner):
+    core, col = where[0] % 2, where[1]
+    half = mine.shape[1]
+    for s in range(rhs_own.shape[0]):
+        rows = ordered(rhs_own[s], rhs_other[s], col, 0)
+        values = dot3(diag[s], rows, NN).T
+        low, high = values[:half], values[half:]
+        mine[s] = jnp.where(core == 0, low, high)
+        partner[s] = jnp.where(core == 0, high, low)
+
+
+def turned_rhs(where, rhs_own, rhs_other, mine, partner):
+    core, col = where[0] % 2, where[1]
+    half = mine.shape[2]
+    for l in range(mine.shape[0]):
+        for s in range(mine.shape[1]):
+            rows = ordered(rhs_own[l, s].T, rhs_other[l, s].T, col, 1)
+            low, high = rows[:half], rows[half:]
+            mine[l, s] = jnp.where(core == 0, low, high)
+            partner[l, s] = jnp.where(core == 0, high, low)
+
+
+def tile_update(places, counts, *refs):
+    tiles_own, tiles_partner = refs[:2]
+    out, window = refs[-2:]
+    pieces = refs[2:-2]
+    sups = pieces[0].shape[0]
+    for index, piece in enumerate(pieces):
+        window[index * sups : (index + 1) * sups] = piece[...]
+    slots, depth, width = tiles_own.shape[1:]
+    for s in range(sups):
+        tiles = tiles_own if s < sups // 2 else tiles_partner
+        picked = []
+        for k in range(slots):
+            value = window[places[s * slots + k]]
+            picked.append(jnp.where(k < counts[s], value, 0.0))
+        left = jnp.concatenate(picked, 1)
+        out[s] = dot3(left, tiles[s % (sups // 2)].reshape(slots * depth, width), NN)
+
+
+def level_values(rhs, mine, theirs, d_own, d_partner, d_own_other, d_partner_other, own, other):
+    sups = rhs.shape[0]
+    for s in range(sups):
+        residual = rhs[s] - (mine[s] + theirs[s])
+        a, b = (d_own, d_own_other) if s < sups // 2 else (d_partner, d_partner_other)
+        own[s] = dot3(residual, a[s % (sups // 2)], NT)
+        other[s] = dot3(residual, b[s % (sups // 2)], NT)
+
+
+def carry_products(places, counts, tiles_own, tiles_partner, totals, x, s):
+    slots, depth, width = tiles_own.shape[1:]
+    sups = totals.shape[0]
+    half = counts.shape[0] // 2
+    tiles = tiles_own if s < half else tiles_partner
+    terms = dot3(x, tiles[s % half].reshape(slots * depth, width), NT)
+    for k in range(slots):
+        place = places[s * slots + k]
+        term = terms[:, k * depth : (k + 1) * depth]
+        totals[place] = totals[place] + jnp.where(k < counts[s], term, 0.0)
+
+
+def top_carry(
+    where, places, counts, rhs, mine, theirs, d_own, d_partner, d_own_other, d_partner_other,
+    tiles_own, tiles_partner, solved_mine, solved_partner, lowest, *rest
+):
+    outs, totals = rest[:-1], rest[-1]
+    col = where[1]
+    sups = rhs.shape[0]
+    half = sups // 2
+    depth = tiles_own.shape[2]
+    totals[...] = jnp.zeros_like(totals)
+    for s in range(sups):
+        a, b = (d_own, d_own_other) if s < half else (d_partner, d_partner_other)
+        residual = rhs[s] - (mine[s] + theirs[s])
+        own = dot3(residual, a[s % half], NT)
+        other = dot3(residual, b[s % half], NT)
+        x = dot3(own, a[s % half], NN) + dot3(other, b[s % half], NN)
+        share = jnp.where(col == 0, x[:, :depth], x[:, depth:])
+        if s < half:
+            solved_mine[s] = share
+        else:
+            solved_partner[s % half] = share
+        carry_products(places, counts, tiles_own, tiles_partner, totals, x, s)
+    lowest[...] = totals[: lowest.shape[0]]
+    for index, out in enumerate(outs):
+        first = lowest.shape[0] + index * sups
+        out[...] = totals[first : first + sups]
+
+
+def middle_carry(
+    where, places, counts, carried_own, carried_other, values_own, values_other,
+    d_own, d_partner, d_own_other, d_partner_other,
+    tiles_own, tiles_partner, lowest, solved_mine, solved_partner, *rest
+):
+    outs, totals = rest[:-1], rest[-1]
+    col = where[1]
+    sups = values_own.shape[0]
+    half = sups // 2
+    depth = tiles_own.shape[2]
+    totals[...] = lowest[...]
+    for s in range(sups):
+        a, b = (d_own, d_own_other) if s < half else (d_partner, d_partner_other)
+        own = values_own[s] - carried_own[s]
+        other = values_other[s] - carried_other[s]
+        x = dot3(own, a[s % half], NN) + dot3(other, b[s % half], NN)
+        share = jnp.where(col == 0, x[:, :depth], x[:, depth:])
+        if s < half:
+            solved_mine[s] = share
+        else:
+            solved_partner[s % half] = share
+        carry_products(places, counts, tiles_own, tiles_partner, totals, x, s)
+    for index, out in enumerate(outs):
+        out[...] = totals[index * sups : (index + 1) * sups]
+
+
+def last_product(values, a, b, c, d, e, d_own, d_partner, mine, partner):
+    sups = values.shape[0]
+    half = sups // 2
+    for s in range(sups):
+        carried = a[s] + b[s] + c[s] + d[s] + e[s]
+        diag, out = (d_own, mine) if s < half else (d_partner, partner)
+        out[s % half] = dot3(values[s] - carried, diag[s % half], NN)
+
+
+def turned_solution(where, mine, partner, own, other):
+    core, col = where[0] % 2, where[1]
+    depth = own.shape[1]
+    for s in range(mine.shape[0]):
+        both = ordered(mine[s], partner[s], core, 0)
+        low, high = both[:, :depth].T, both[:, depth:].T
+        own[s] = jnp.where(col == 0, low, high)
+        other[s] = jnp.where(col == 0, high, low)
+
+
+def turned_upper(where, mine2, partner2, mine1, partner1, out):
+    core = where[0] % 2
+    for s in range(mine2.shape[0]):
+        out[0, s] = ordered(mine1[s], partner1[s], core, 0).T
+        out[1, s] = ordered(mine2[s], partner2[s], core, 0).T
+
+
+def local(rhs, diag_inv, factor_tiles, tile_source, tile_count):
+    levels, owned, share_rows, columns = rhs.shape
+    slots = tile_source.shape[2]
+    sups = 2 * owned
+    block = share_rows * 2
+    half_columns = columns // 2
+    row = lax.axis_index("rows")
+    col = lax.axis_index("cols")
+    where = jnp.stack([row, col]).astype(jnp.int32)
+    rows_total = lax.axis_size("rows")
+    total_sup = rows_total * owned
+    piece = (sups, half_columns, share_rows)
+
+    def swap_cols(value):
+        return lax.ppermute(value, "cols", [(0, 1), (1, 0)])
+
+    def swap_rows(value, bits):
+        return lax.ppermute(value, "rows", [(r, r ^ bits) for r in range(rows_total)])
+
+    def swap_core(value):
+        return swap_rows(value, 1)
+
+    def swap_x(value):
+        return swap_rows(value, 2)
+
+    def swap_far(value):
+        inner = (rows_total // 4, 3 * rows_total // 4)
+        return lax.ppermute(
+            value, "rows",
+            [(r, r ^ 12 if inner[0] <= r < inner[1] else r) for r in range(rows_total)],
+        )
+
+    def gather_pieces(value):
+        far = swap_rows(value, 8)
+        next_ = swap_rows(value, 4)
+        mid = swap_far(value)
+        beside = swap_x(value)
+        return [
+            value, beside, next_, swap_x(next_), far, swap_x(far), mid, swap_x(mid)
+        ]
+
+    def scatter_pieces(p):
+        far = swap_rows(p[4] + swap_x(p[5]), 8)
+        mid = swap_far(p[6] + swap_x(p[7]))
+        next_ = swap_rows(p[2] + swap_x(p[3]), 4)
+        beside = swap_x(p[1])
+        return [p[0], beside, next_, far, mid]
+
+    rhs_other = swap_cols(rhs[0])
+    mine, partner = call(
+        first_values, "first_values", [(owned, half_columns, share_rows)] * 2,
+        [where, rhs[0], rhs_other, diag_inv[0]],
+    )
+    values0 = jnp.concatenate([mine, swap_core(partner)], 0)
+    pieces0 = gather_pieces(values0)
+
+    source = jnp.concatenate([tile_source, swap_core(tile_source)], 1)
+    count = jnp.concatenate([tile_count, swap_core(tile_count)], 1)
+    live = jnp.arange(slots, dtype=jnp.int32)[None, None, :] < count[:, :, None]
+    within = source % total_sup
+    place = (row ^ (within // owned)) * owned + within % owned
+    place = place + source // total_sup * (PIECES * sups)
+    places = jnp.where(live, place, 0).reshape(levels - 1, sups * slots)
+    tiles_own = [factor_tiles[l] for l in range(levels - 1)]
+    tiles_partner = [swap_core(tiles) for tiles in tiles_own]
+    d_low_partner = swap_core(diag_inv[0])
+    d_own = [diag_inv[l] for l in range(1, levels)]
+    d_own_other = [swap_cols(d) for d in d_own]
+    d_partner = [swap_core(d) for d in d_own]
+    d_partner_other = [swap_core(d) for d in d_own_other]
+    upper_other = swap_cols(rhs[1:])
+    mine, partner = call(
+        turned_rhs, "turned_rhs", [(levels - 1, owned, half_columns, block)] * 2,
+        [where, rhs[1:], upper_other],
+    )
+    upper = jnp.concatenate([mine, swap_core(partner)], 1)
+
+    def diag_args(l):
+        return [d_own[l], d_partner[l], d_own_other[l], d_partner_other[l]]
+
+    def update(l, pieces):
+        return call(
+            tile_update, "tile_update", [(sups, half_columns, block)],
+            [places[l], count[l], tiles_own[l], tiles_partner[l], *pieces], 2,
+            [pltpu.VMEM((len(pieces) * sups, half_columns, share_rows), F32)],
+        )[0]
+
+    partial = update(0, pieces0)
+    values1, values1_other = call(
+        level_values, "level_values", [piece] * 2,
+        [upper[0], partial, swap_cols(partial), *diag_args(0)], 0,
+    )
+    pieces1 = gather_pieces(values1)
+
+    partial = update(1, pieces0 + pieces1)
+    window = PIECES * sups
+    shared = (owned, half_columns, share_rows)
+    mine2, partner2, lowest, *out = call(
+        top_carry, "top_carry", [shared, shared, (window, half_columns, share_rows)] + [piece] * PIECES,
+        [where, places[1], count[1], upper[1], partial, swap_cols(partial), *diag_args(1),
+         tiles_own[1], tiles_partner[1]], 3,
+        [pltpu.VMEM((2 * window, half_columns, share_rows), F32)],
+    )
+    partner2 = swap_core(partner2)
+    carried = sum(scatter_pieces(out))
+
+    mine1, partner1, *out = call(
+        middle_carry, "middle_carry", [shared, shared] + [piece] * PIECES,
+        [where, places[0], count[0], carried, swap_cols(carried), values1, values1_other,
+         *diag_args(0), tiles_own[0], tiles_partner[0], lowest], 3,
+        [pltpu.VMEM((window, half_columns, share_rows), F32)],
+    )
+    partner1 = swap_core(partner1)
+    result_upper = call(
+        turned_upper, "turned_upper", [(levels - 1, owned, share_rows, columns)],
+        [where, mine2, partner2, mine1, partner1],
+    )[0]
+    mine, partner = call(
+        last_product, "last_product", [(owned, half_columns, block)] * 2,
+        [values0, *scatter_pieces(out), diag_inv[0], d_low_partner], 0,
+    )
+    own, other = call(
+        turned_solution, "turned_solution", [(owned, share_rows, columns)] * 2,
+        [where, mine, swap_core(partner)],
+    )
+    return jnp.concatenate([(own + swap_cols(other))[None], result_upper], 0)
+
+
 def solution(mesh):
     placed = (
         P(None, "rows", "cols", None),
@@ -118,6 +432,11 @@
         P(None, "rows", None),
         P(None, "rows"),
     )
+    small = mesh.shape["rows"] == 16 and mesh.shape["cols"] == 2
     return jax.shard_map(
-        local, mesh=mesh, in_specs=placed, out_specs=P(None, "rows", "cols", None), check_vma=False
-    )
+        local if small else local_any,
+        mesh=mesh,
+        in_specs=placed,
+        out_specs=P(None, "rows", "cols", None),
+        check_vma=False,
+    )

time: 395 us -> 156 us (0.39)
  waiting for transfers between devices: 153 us -> 55.1 us
  starting transfers between devices: 148 us -> 52.4 us
  blocking collectives: 31.3 us -> 0 us
  matrix products: 27.5 us -> 0 us
  Pallas kernels: 0 us -> 22.3 us
  between operations: 14.3 us -> 0.31 us
  local copies, waits for them, and re-layouts: 12.3 us -> 23.9 us
  other arithmetic: 6.86 us -> 1.15 us
    reduce_scatter x5 -> x0, waiting for transfers between devices: 97.4 us -> none  [local(): lax.psum_scatter(partial_value, 'cols', scatter_dimension=1, tiled=True)]
    ppermute x56 -> x50, starting transfers between devices: 147 us -> 52.4 us  [the longest x38 39.3 us: swap_rows(): lax.ppermute(value, 'rows', [(r, r ^ bits) for r in range(rows_total)])]
    all_gather x5 -> x0, blocking collectives: 31.3 us -> none  [the longest x3 18.9 us: full_rows(): return lax.all_gather(piece, 'cols', axis=1, tiled=True)]
    dot_general x12 -> x0, matrix products: 27.5 us -> none  [the longest x2 10.2 us: local(): jnp.einsum('skci,skcr->sir', factor_tiles[height - 1], picked, precision=...]
    pallas_call x0 -> x10, Pallas kernels: none -> 22.3 us  [call(): pl.pallas_call(kernel, out_shape=out_shape, in_specs=in_specs, out_specs=...]
    unnamed x37 -> x56, local copies, waits for them, and re-layouts: 0.43 us -> 14.4 us
    squeeze x3 -> x7, local copies, waits for them, and re-layouts: 0.34 us -> 7.99 us  [the longest x1 4.06 us: local(): tiles_own = [factor_tiles[l] for l in range(levels - 1)]]
    slice x3 -> x2, local copies, waits for them, and re-layouts: 4.71 us -> 0.54 us  [the longest x1 0.52 us: local(): places[0]]
  transfers between devices with their start and end apart: 61 -> 50, of which waited for: 23 -> 23; matrix products, arithmetic and copies ran while one was open for 1% -> 4% of each run, Pallas kernels for 0% -> 7%
where the time goes in v1:
time: 156 us; the launch traced here: 155 us
  waiting for transfers between devices  55.1 us (35%)
  starting transfers between devices  52.4 us (34%)
  local copies, waits for them, and re-layouts  23.9 us (15%)
  Pallas kernels  22.3 us (14%)
    ppermute x38, starting transfers between devices, swap_rows(): lax.ppermute(value, 'rows', [(r, r ^ bits) for r in range(rows_total)])  39.3 us
    ppermute x38, waiting for transfers between devices, swap_rows(): lax.ppermute(value, 'rows', [(r, r ^ bits) for r in range(rows_total)])  30.4 us
    ppermute x8, waiting for transfers between devices, swap_cols(): return lax.ppermute(value, 'cols', [(0, 1), (1, 0)])  24.8 us
    pallas_call x10, Pallas kernels, call(): pl.pallas_call(kernel, out_shape=out_shape, in_specs=in_specs, out_specs=...  22.3 us
    unnamed x56, local copies, waits for them, and re-layouts  14.4 us
    ppermute x8, starting transfers between devices, swap_cols(): return lax.ppermute(value, 'cols', [(0, 1), (1, 0)])  8.96 us
    ppermute x4, starting transfers between devices, swap_far(): lax.ppermute(value, 'rows', [(r, r ^ 12 if inner[0] <= r < inner[1] else...  4.15 us
    squeeze x1, local copies, waits for them, and re-layouts, local(): tiles_own = [factor_tiles[l] for l in range(levels - 1)]  4.06 us
  transfers between devices with their start and end apart: 50, of which 23 were waited for; matrix products, arithmetic and copies ran while one was open for 4% of the time, Pallas kernels for 7%

profile of v1, /device:TPU:0, one launch (start us, length us, event | category | flops | bytes accessed | tf_op | source)
XLA Modules:
  0.0 155.2 jit_solution(16152484740232841859)
XLA Ops:
  0.0 4.1 %slice_bitcast_fusion = (f32[2,8,128,256]{3,2,1,0:T(8,128)S(1)}, f32[2,8,128,256]{3,2,1,0:T(8,128)}) fusion(f32[2,2,8,128,256]{4,3,2,1,0:T(8,128)} %param.7), kind=kLoop, calls=%fused_computation | loop fusion | bytes 8388608 | tf_op jit(solution)/shard_map/squeeze | solution.py:362
  4.5 2.6 %collective-permute-start = (f32[2,128,128]{2,1,0:T(8,128)S(1)}, f32[2,128,128]{2,1,0:T(8,128)S(1)}, u32[]{:S(2)}, u32[]{:S(2)}) collective-permute-start(f32[2,128,128]{2,1,0:T(8,128)S(1)} %slice_bitcast_fusion.7.rhs_own), channel_id=1, source_target_pairs={{0,1},{1,0},{2,3},{3,2},{4,5},{5,4},{6,7},{7,6},{8,9},{9,8},{10,11... | collective-permute-start | bytes 393224 | tf_op jit(solution)/shard_map/ppermute | solution.py:313
  7.9 1.9 %slice_bitcast_fusion.4 = (f32[2,128,256]{2,1,0:T(8,128)}, f32[2,128,256]{2,1,0:T(8,128)S(1)}, f32[2,128,256]{2,1,0:T(8,128)S(1)}) fusion(f32[3,2,128,256]{3,2,1,0:T(8,128)} %param.6), kind=kLoop, calls=%fused_computation.5 | loop fusion | bytes 1572864 | tf_op jit(solution)/shard_map/squeeze | solution.py:365
  12.3 1.2 collective-permute-done.1
  13.5 1.7 %collective-permute-start.17 = (f32[2,128,256]{2,1,0:T(8,128)S(1)}, f32[2,128,256]{2,1,0:T(8,128)S(1)}, u32[]{:S(2)}, u32[]{:S(2)}) collective-permute-start(f32[2,128,256]{2,1,0:T(8,128)S(1)} %get-tuple-element.71.d_own), channel_id=1, source_target_pairs={{0,1},{1,0},{2,3},{3,2},{4,5},{5,4},{6,7},{7,6},{8,9},{9,8},{10,11... | collective-permute-start | bytes 786440 | tf_op jit(solution)/shard_map/ppermute | solution.py:313
  15.2 2.7 %collective-permute-start.10 = (f32[4,64,128]{2,1,0:T(8,128)S(1)}, f32[4,64,128]{2,1,0:T(8,128)S(1)}, u32[]{:S(2)}, u32[]{:S(2)}) collective-permute-start(f32[4,64,128]{2,1,0:T(8,128)S(1)} %constant_dynamic-update-slice_fusion.refs_2_.values), channel_id=1, source_target_pairs={{0,16},{2,18},{4,20},{6,22},{8,24},{10,26},{12,28},{14,30},{16,0},... | collective-permute-start | bytes 393224 | tf_op jit(solution)/shard_map/ppermute | solution.py:316
  17.9 1.1 collective-permute-done.4.rhs_other
  20.2 3.8 %collective-permute-done.17.d_own_other = f32[2,128,256]{2,1,0:T(8,128)S(1)} collective-permute-done((f32[2,128,256]{2,1,0:T(8,128)S(1)}, f32[2,128,256]{2,1,0:T(8,128)S(1)}, u32[]{:S(2)}, u32[]{:S(2)}) %collective-permute-start.17) | collective-permute-done | bytes 262176 | tf_op jit(solution)/shard_map/ppermute | solution.py:313
  24.0 1.6 %collective-permute-start.8 = (f32[4,64,128]{2,1,0:T(8,128)S(1)}, f32[4,64,128]{2,1,0:T(8,128)S(1)}, u32[]{:S(2)}, u32[]{:S(2)}) collective-permute-start(f32[4,64,128]{2,1,0:T(8,128)S(1)} %constant_dynamic-update-slice_fusion.refs_2_.values), channel_id=1, source_target_pairs={{0,8},{2,10},{4,12},{6,14},{8,0},{10,2},{12,4},{14,6},{16,24},{18,... | collective-permute-start | bytes 393224 | tf_op jit(solution)/shard_map/ppermute | solution.py:316
  25.6 1.5 collective-permute-start.7
  27.7 1.4 turned_rhs.1
  29.2 2.4 %collective-permute-done.7.refs_3_ = f32[4,64,128]{2,1,0:T(8,128)S(1)} collective-permute-done((f32[4,64,128]{2,1,0:T(8,128)S(1)}, f32[4,64,128]{2,1,0:T(8,128)S(1)}, u32[]{:S(2)}, u32[]{:S(2)}) %collective-permute-start.7) | collective-permute-done | bytes 131104 | tf_op jit(solution)/shard_map/ppermute | solution.py:316
  32.2 1.5 collective-permute-start.13
  36.1 1.1 collective-permute-done.13.refs_9_
  37.9 1.0 collective-permute-done.9.refs_5_
  38.9 1.0 collective-permute-start.28
  45.3 3.0 %tile_update.2.mine = f32[4,64,256]{2,1,0:T(8,128)S(1)} custom-call(s32[32]{0:T(128)S(1)} %squeeze.45.places, s32[4]{0:T(128)S(1)} %get-tuple-element.76.counts, f32[2,8,128,256]{3,2,1,0:T(8,128)S(1)} %get-tuple-element.67.refs_0_.tiles_own, f32[2,8,128,256]{3,2,1,0:T(8,128)} %collective-permute-done.14.refs_1_.tiles_partner, ...), custom_call_target="tpu_custom_call" | custom-call | tf_op jit(solution)/shard_map/tile_update/pallas_call | solution.py:147
  48.3 1.1 collective-permute-start.15
  51.1 6.0 %collective-permute-done.15.theirs = f32[4,64,256]{2,1,0:T(8,128)S(1)} collective-permute-done((f32[4,64,256]{2,1,0:T(8,128)S(1)}, f32[4,64,256]{2,1,0:T(8,128)S(1)}, u32[]{:S(2)}, u32[]{:S(2)}) %collective-permute-start.15) | collective-permute-done | bytes 262176 | tf_op jit(solution)/shard_map/ppermute | solution.py:313
  57.1 1.3 level_values.1
  59.1 1.4 collective-permute-start.20
  60.5 2.5 %collective-permute-start.22 = (f32[4,64,128]{2,1,0:T(8,128)}, f32[4,64,128]{2,1,0:T(8,128)}, u32[]{:S(2)}, u32[]{:S(2)}) collective-permute-start(f32[4,64,128]{2,1,0:T(8,128)} %get-tuple-element.40.refs_10_.values_own), channel_id=1, source_target_pairs={{0,16},{2,18},{4,20},{6,22},{8,24},{10,26},{12,28},{14,30},{16,0},... | collective-permute-start | bytes 393224 | tf_op jit(solution)/shard_map/ppermute | solution.py:316
  63.0 2.2 %collective-permute-start.24 = (f32[4,64,128]{2,1,0:T(8,128)}, f32[4,64,128]{2,1,0:T(8,128)}, u32[]{:S(2)}, u32[]{:S(2)}) collective-permute-start(f32[4,64,128]{2,1,0:T(8,128)} %get-tuple-element.40.refs_10_.values_own), channel_id=1, source_target_pairs={{0,0},{2,2},{4,4},{6,6},{8,16},{10,18},{12,20},{14,22},{16,8},{18,... | collective-permute-start | bytes 393224 | tf_op jit(solution)/shard_map/ppermute | solution.py:326
  65.2 1.5 collective-permute-start.19
  66.9 1.3 collective-permute-start.21
  68.2 3.1 %collective-permute-start.23 = (f32[4,64,128]{2,1,0:T(8,128)}, f32[4,64,128]{2,1,0:T(8,128)}, u32[]{:S(2)}, u32[]{:S(2)}) collective-permute-start(f32[4,64,128]{2,1,0:T(8,128)} %collective-permute-done.22.refs_14_), channel_id=1, source_target_pairs={{0,4},{2,6},{4,0},{6,2},{8,12},{10,14},{12,8},{14,10},{16,20},{18,... | collective-permute-start | bytes 393224 | tf_op jit(solution)/shard_map/ppermute | solution.py:316
  72.5 2.2 %collective-permute-done.21.refs_13_ = f32[4,64,128]{2,1,0:T(8,128)} collective-permute-done((f32[4,64,128]{2,1,0:T(8,128)}, f32[4,64,128]{2,1,0:T(8,128)}, u32[]{:S(2)}, u32[]{:S(2)}) %collective-permute-start.21) | collective-permute-done | bytes 131104 | tf_op jit(solution)/shard_map/ppermute | solution.py:316
  74.7 2.3 %collective-permute-done.23.refs_15_ = f32[4,64,128]{2,1,0:T(8,128)} collective-permute-done((f32[4,64,128]{2,1,0:T(8,128)}, f32[4,64,128]{2,1,0:T(8,128)}, u32[]{:S(2)}, u32[]{:S(2)}) %collective-permute-start.23) | collective-permute-done | bytes 131104 | tf_op jit(solution)/shard_map/ppermute | solution.py:316
  77.1 1.4 collective-permute-done.25.refs_17_
  84.5 4.0 %tile_update.3.mine = f32[4,64,256]{2,1,0:T(8,128)S(1)} custom-call(s32[32]{0:T(128)S(1)} %squeeze.47.places, s32[4]{0:T(128)S(1)} %copy-done.22, f32[2,8,128,256]{3,2,1,0:T(8,128)} %get-tuple-element.68.refs_0_.tiles_own, f32[2,8,128,256]{3,2,1,0:T(8,128)} %collective-permute-done.6.refs_1_.tiles_partner, ...), custom_call_target="tpu_custom_call" | custom-call | tf_op jit(solution)/shard_map/tile_update/pallas_call | solution.py:147
  89.5 5.6 %collective-permute-done.26.theirs = f32[4,64,256]{2,1,0:T(8,128)S(1)} collective-permute-done((f32[4,64,256]{2,1,0:T(8,128)S(1)}, f32[4,64,256]{2,1,0:T(8,128)S(1)}, u32[]{:S(2)}, u32[]{:S(2)}) %collective-permute-start.26) | collective-permute-done | bytes 262176 | tf_op jit(solution)/shard_map/ppermute | solution.py:313
  95.0 5.9 %top_carry.1 = (f32[2,64,128]{2,1,0:T(8,128)S(1)}, f32[2,64,128]{2,1,0:T(8,128)S(1)}, f32[32,64,128]{2,1,0:T(8,128)S(1)}, f32[4,64,128]{2,1,0:T(8,128)S(1)}, f32...) custom-call(s32[2]{0:T(128)S(1)} %pad_add_fusion.2.where, ...), custom_call_target="tpu_custom_call" | custom-call | tf_op jit(solution)/shard_map/top_carry/pallas_call | solution.py:147
  100.9 1.6 %collective-permute-start.31 = (f32[4,64,128]{2,1,0:T(8,128)S(1)}, f32[4,64,128]{2,1,0:T(8,128)S(1)}, u32[]{:S(2)}, u32[]{:S(2)}) collective-permute-start(f32[4,64,128]{2,1,0:T(8,128)S(1)} %get-tuple-element.44), channel_id=1, source_target_pairs={{0,4},{2,6},{4,0},{6,2},{8,12},{10,14},{12,8},{14,10},{16,20},{18,... | collective-permute-start | bytes 393224 | tf_op jit(solution)/shard_map/ppermute | solution.py:316
  103.0 1.5 collective-permute-start.35
  105.0 2.4 %collective-permute-done.31 = f32[4,64,128]{2,1,0:T(8,128)S(1)} collective-permute-done((f32[4,64,128]{2,1,0:T(8,128)S(1)}, f32[4,64,128]{2,1,0:T(8,128)S(1)}, u32[]{:S(2)}, u32[]{:S(2)}) %collective-permute-start.31) | collective-permute-done | bytes 131104 | tf_op jit(solution)/shard_map/ppermute | solution.py:316
  107.4 2.0 %collective-permute-start.32 = (f32[4,64,128]{2,1,0:T(8,128)S(1)}, f32[4,64,128]{2,1,0:T(8,128)S(1)}, u32[]{:S(2)}, u32[]{:S(2)}) collective-permute-start(f32[4,64,128]{2,1,0:T(8,128)S(1)} %add.56), channel_id=1, source_target_pairs={{0,8},{2,10},{4,12},{6,14},{8,0},{10,2},{12,4},{14,6},{16,24},{18,... | collective-permute-start | bytes 393224 | tf_op jit(solution)/shard_map/ppermute | solution.py:316
  109.5 2.8 %collective-permute-start.34 = (f32[4,64,128]{2,1,0:T(8,128)S(1)}, f32[4,64,128]{2,1,0:T(8,128)S(1)}, u32[]{:S(2)}, u32[]{:S(2)}) collective-permute-start(f32[4,64,128]{2,1,0:T(8,128)S(1)} %add.58), channel_id=1, source_target_pairs={{0,16},{2,18},{4,20},{6,22},{8,24},{10,26},{12,28},{14,30},{16,0},... | collective-permute-start | bytes 393224 | tf_op jit(solution)/shard_map/ppermute | solution.py:316
  113.1 5.0 %collective-permute-done.34 = f32[4,64,128]{2,1,0:T(8,128)S(1)} collective-permute-done((f32[4,64,128]{2,1,0:T(8,128)S(1)}, f32[4,64,128]{2,1,0:T(8,128)S(1)}, u32[]{:S(2)}, u32[]{:S(2)}) %collective-permute-start.34) | collective-permute-done | bytes 131104 | tf_op jit(solution)/shard_map/ppermute | solution.py:316
  118.3 5.0 %collective-permute-done.37.carried_other = f32[4,64,128]{2,1,0:T(8,128)S(1)} collective-permute-done((f32[4,64,128]{2,1,0:T(8,128)S(1)}, f32[4,64,128]{2,1,0:T(8,128)S(1)}, u32[]{:S(2)}, u32[]{:S(2)}) %collective-permute-start.37) | collective-permute-done | bytes 131104 | tf_op jit(solution)/shard_map/ppermute | solution.py:313
  123.2 4.1 %middle_carry.1 = (f32[2,64,128]{2,1,0:T(8,128)S(1)}, f32[2,64,128]{2,1,0:T(8,128)S(1)}, f32[4,64,128]{2,1,0:T(8,128)S(1)}, f32[4,64,128]{2,1,0:T(8,128)S(1)}, f...) custom-call(s32[2]{0:T(128)S(1)} %pad_add_fusion.2.where, ...), custom_call_target="tpu_custom_call" | custom-call | tf_op jit(solution)/shard_map/middle_carry/pallas_call | solution.py:147
  127.4 1.5 collective-permute-start.43
  129.5 1.4 collective-permute-start.39
  133.1 1.9 %collective-permute-done.41 = f32[4,64,128]{2,1,0:T(8,128)S(1)} collective-permute-done((f32[4,64,128]{2,1,0:T(8,128)S(1)}, f32[4,64,128]{2,1,0:T(8,128)S(1)}, u32[]{:S(2)}, u32[]{:S(2)}) %collective-permute-start.41) | collective-permute-done | bytes 131104 | tf_op jit(solution)/shard_map/ppermute | solution.py:316
  135.0 3.5 %collective-permute-start.42 = (f32[4,64,128]{2,1,0:T(8,128)S(1)}, f32[4,64,128]{2,1,0:T(8,128)S(1)}, u32[]{:S(2)}, u32[]{:S(2)}) collective-permute-start(f32[4,64,128]{2,1,0:T(8,128)S(1)} %add.63), channel_id=1, source_target_pairs={{0,16},{2,18},{4,20},{6,22},{8,24},{10,26},{12,28},{14,30},{16,0},... | collective-permute-start | bytes 393224 | tf_op jit(solution)/shard_map/ppermute | solution.py:316
  138.5 1.9 %collective-permute-start.40 = (f32[4,64,128]{2,1,0:T(8,128)S(1)}, f32[4,64,128]{2,1,0:T(8,128)S(1)}, u32[]{:S(2)}, u32[]{:S(2)}) collective-permute-start(f32[4,64,128]{2,1,0:T(8,128)S(1)} %add.62), channel_id=1, source_target_pairs={{0,8},{2,10},{4,12},{6,14},{8,0},{10,2},{12,4},{14,6},{16,24},{18,... | collective-permute-start | bytes 393224 | tf_op jit(solution)/shard_map/ppermute | solution.py:316
  140.5 5.9 %collective-permute-done.42.d = f32[4,64,128]{2,1,0:T(8,128)S(1)} collective-permute-done((f32[4,64,128]{2,1,0:T(8,128)S(1)}, f32[4,64,128]{2,1,0:T(8,128)S(1)}, u32[]{:S(2)}, u32[]{:S(2)}) %collective-permute-start.42) | collective-permute-done | bytes 131104 | tf_op jit(solution)/shard_map/ppermute | solution.py:316
  146.8 1.3 collective-permute-done.46.partner
  151.4 3.0 %collective-permute-done.47 = f32[2,128,128]{2,1,0:T(8,128)S(1)} collective-permute-done((f32[2,128,128]{2,1,0:T(8,128)S(1)}, f32[2,128,128]{2,1,0:T(8,128)S(1)}, u32[]{:S(2)}, u32[]{:S(2)}) %collective-permute-start.47) | collective-permute-done | bytes 131104 | tf_op jit(solution)/shard_map/ppermute | solution.py:313
  (141 shorter events, 34.7 us)
Async XLA Ops:
  4.1 35.8 %collective-permute-start.14 = (f32[2,8,128,256]{3,2,1,0:T(8,128)S(1)}, f32[2,8,128,256]{3,2,1,0:T(8,128)}, u32[]{:S(2)}, u32[]{:S(2)}) collective-permute-start(f32[2,8,128,256]{3,2,1,0:T(8,128)S(1)} %get-tuple-element.67.refs_0_.tiles_own), channel_id=1, source_target_pairs={{0,2},{2,0},{4,6},{6,4},{8,10},{10,8},{12,14},{14,12},{16,18},{18,... | collective-permute-start | bytes 6291464 | tf_op jit(solution)/shard_map/ppermute | solution.py:316
  4.5 6.8 %collective-permute-start = (f32[2,128,128]{2,1,0:T(8,128)S(1)}, f32[2,128,128]{2,1,0:T(8,128)S(1)}, u32[]{:S(2)}, u32[]{:S(2)}) collective-permute-start(f32[2,128,128]{2,1,0:T(8,128)S(1)} %slice_bitcast_fusion.7.rhs_own), channel_id=1, source_target_pairs={{0,1},{1,0},{2,3},{3,2},{4,5},{5,4},{6,7},{7,6},{8,9},{9,8},{10,11... | collective-permute-start | bytes 393224 | tf_op jit(solution)/shard_map/ppermute | solution.py:313
  7.1 2.7 %collective-permute-start.2 = (s32[2,2]{1,0:T(2,128)S(1)}, s32[2,2]{1,0:T(2,128)S(1)}, u32[]{:S(2)}, u32[]{:S(2)}) collective-permute-start(s32[2,2]{1,0:T(2,128)S(1)} %copy-done.26), channel_id=1, source_target_pairs={{0,2},{2,0},{4,6},{6,4},{8,10},{10,8},{12,14},{14,12},{16,18},{18,... | collective-permute-start | bytes 56 | tf_op jit(solution)/shard_map/ppermute | solution.py:316
  7.4 7.9 %collective-permute-start.3 = (s32[2,2,8]{2,1,0:T(2,128)S(1)}, s32[2,2,8]{2,1,0:T(2,128)S(1)}, u32[]{:S(2)}, u32[]{:S(2)}) collective-permute-start(s32[2,2,8]{2,1,0:T(2,128)S(1)} %copy-done.25), channel_id=1, source_target_pairs={{0,2},{2,0},{4,6},{6,4},{8,10},{10,8},{12,14},{14,12},{16,18},{18,... | collective-permute-start | bytes 392 | tf_op jit(solution)/shard_map/ppermute | solution.py:316
  7.6 64.3 %collective-permute-start.6 = (f32[2,8,128,256]{3,2,1,0:T(8,128)}, f32[2,8,128,256]{3,2,1,0:T(8,128)}, u32[]{:S(2)}, u32[]{:S(2)}) collective-permute-start(f32[2,8,128,256]{3,2,1,0:T(8,128)} %get-tuple-element.68.refs_0_.tiles_own), channel_id=1, source_target_pairs={{0,2},{2,0},{4,6},{6,4},{8,10},{10,8},{12,14},{14,12},{16,18},{18,... | collective-permute-start | bytes 6291464 | tf_op jit(solution)/shard_map/ppermute | solution.py:316
  9.8 9.2 %collective-permute-start.4 = (f32[2,2,128,128]{3,2,1,0:T(8,128)S(1)}, f32[2,2,128,128]{3,2,1,0:T(8,128)S(1)}, u32[]{:S(2)}, u32[]{:S(2)}) collective-permute-start(f32[2,2,128,128]{3,2,1,0:T(8,128)S(1)} %slice.55.rhs_own), channel_id=1, source_target_pairs={{0,1},{1,0},{2,3},{3,2},{4,5},{5,4},{6,7},{7,6},{8,9},{9,8},{10,11... | collective-permute-start | bytes 786440 | tf_op jit(solution)/shard_map/ppermute | solution.py:313
  13.5 10.5 %collective-permute-start.17 = (f32[2,128,256]{2,1,0:T(8,128)S(1)}, f32[2,128,256]{2,1,0:T(8,128)S(1)}, u32[]{:S(2)}, u32[]{:S(2)}) collective-permute-start(f32[2,128,256]{2,1,0:T(8,128)S(1)} %get-tuple-element.71.d_own), channel_id=1, source_target_pairs={{0,1},{1,0},{2,3},{3,2},{4,5},{5,4},{6,7},{7,6},{8,9},{9,8},{10,11... | collective-permute-start | bytes 786440 | tf_op jit(solution)/shard_map/ppermute | solution.py:313
  15.2 10.3 %collective-permute-start.10 = (f32[4,64,128]{2,1,0:T(8,128)S(1)}, f32[4,64,128]{2,1,0:T(8,128)S(1)}, u32[]{:S(2)}, u32[]{:S(2)}) collective-permute-start(f32[4,64,128]{2,1,0:T(8,128)S(1)} %constant_dynamic-update-slice_fusion.refs_2_.values), channel_id=1, source_target_pairs={{0,16},{2,18},{4,20},{6,22},{8,24},{10,26},{12,28},{14,30},{16,0},... | collective-permute-start | bytes 393224 | tf_op jit(solution)/shard_map/ppermute | solution.py:316
  19.0 8.1 %collective-permute-start.12 = (f32[4,64,128]{2,1,0:T(8,128)S(1)}, f32[4,64,128]{2,1,0:T(8,128)S(1)}, u32[]{:S(2)}, u32[]{:S(2)}) collective-permute-start(f32[4,64,128]{2,1,0:T(8,128)S(1)} %constant_dynamic-update-slice_fusion.refs_2_.values), channel_id=1, source_target_pairs={{0,0},{2,2},{4,4},{6,6},{8,16},{10,18},{12,20},{14,22},{16,8},{18,... | collective-permute-start | bytes 393224 | tf_op jit(solution)/shard_map/ppermute | solution.py:326
  24.0 5.1 %collective-permute-start.8 = (f32[4,64,128]{2,1,0:T(8,128)S(1)}, f32[4,64,128]{2,1,0:T(8,128)S(1)}, u32[]{:S(2)}, u32[]{:S(2)}) collective-permute-start(f32[4,64,128]{2,1,0:T(8,128)S(1)} %constant_dynamic-update-slice_fusion.refs_2_.values), channel_id=1, source_target_pairs={{0,8},{2,10},{4,12},{6,14},{8,0},{10,2},{12,4},{14,6},{16,24},{18,... | collective-permute-start | bytes 393224 | tf_op jit(solution)/shard_map/ppermute | solution.py:316
  25.6 6.0 %collective-permute-start.7 = (f32[4,64,128]{2,1,0:T(8,128)S(1)}, f32[4,64,128]{2,1,0:T(8,128)S(1)}, u32[]{:S(2)}, u32[]{:S(2)}) collective-permute-start(f32[4,64,128]{2,1,0:T(8,128)S(1)} %constant_dynamic-update-slice_fusion.refs_2_.values), channel_id=1, source_target_pairs={{0,4},{2,6},{4,0},{6,2},{8,12},{10,14},{12,8},{14,10},{16,20},{18,... | collective-permute-start | bytes 393224 | tf_op jit(solution)/shard_map/ppermute | solution.py:316
  27.1 6.6 %collective-permute-start.11 = (f32[4,64,128]{2,1,0:T(8,128)S(1)}, f32[4,64,128]{2,1,0:T(8,128)S(1)}, u32[]{:S(2)}, u32[]{:S(2)}) collective-permute-start(f32[4,64,128]{2,1,0:T(8,128)S(1)} %collective-permute-done.10.refs_6_), channel_id=1, source_target_pairs={{0,4},{2,6},{4,0},{6,2},{8,12},{10,14},{12,8},{14,10},{16,20},{18,... | collective-permute-start | bytes 393224 | tf_op jit(solution)/shard_map/ppermute | solution.py:316
  29.2 19.2 %collective-permute-start.5 = (f32[2,2,64,256]{3,2,1,0:T(8,128)}, f32[2,2,64,256]{3,2,1,0:T(8,128)}, u32[]{:S(2)}, u32[]{:S(2)}) collective-permute-start(f32[2,2,64,256]{3,2,1,0:T(8,128)} %get-tuple-element.39), channel_id=1, source_target_pairs={{0,2},{2,0},{4,6},{6,4},{8,10},{10,8},{12,14},{14,12},{16,18},{18,... | collective-permute-start | bytes 786440 | tf_op jit(solution)/shard_map/ppermute | solution.py:316
  32.2 5.0 %collective-permute-start.13 = (f32[4,64,128]{2,1,0:T(8,128)S(1)}, f32[4,64,128]{2,1,0:T(8,128)S(1)}, u32[]{:S(2)}, u32[]{:S(2)}) collective-permute-start(f32[4,64,128]{2,1,0:T(8,128)S(1)} %collective-permute-done.12.refs_8_), channel_id=1, source_target_pairs={{0,4},{2,6},{4,0},{6,2},{8,12},{10,14},{12,8},{14,10},{16,20},{18,... | collective-permute-start | bytes 393224 | tf_op jit(solution)/shard_map/ppermute | solution.py:316
  33.7 5.1 %collective-permute-start.9 = (f32[4,64,128]{2,1,0:T(8,128)S(1)}, f32[4,64,128]{2,1,0:T(8,128)}, u32[]{:S(2)}, u32[]{:S(2)}) collective-permute-start(f32[4,64,128]{2,1,0:T(8,128)S(1)} %collective-permute-done.8.refs_4_), channel_id=1, source_target_pairs={{0,4},{2,6},{4,0},{6,2},{8,12},{10,14},{12,8},{14,10},{16,20},{18,... | collective-permute-start | bytes 393224 | tf_op jit(solution)/shard_map/ppermute | solution.py:316
  37.9 13.2 %collective-permute-start.16 = (f32[2,128,256]{2,1,0:T(8,128)S(1)}, f32[2,128,256]{2,1,0:T(8,128)S(1)}, u32[]{:S(2)}, u32[]{:S(2)}) collective-permute-start(f32[2,128,256]{2,1,0:T(8,128)S(1)} %get-tuple-element.71.d_own), channel_id=1, source_target_pairs={{0,2},{2,0},{4,6},{6,4},{8,10},{10,8},{12,14},{14,12},{16,18},{18,... | collective-permute-start | bytes 786440 | tf_op jit(solution)/shard_map/ppermute | solution.py:316
  38.9 26.3 %collective-permute-start.28 = (f32[2,128,256]{2,1,0:T(8,128)}, f32[2,128,256]{2,1,0:T(8,128)}, u32[]{:S(2)}, u32[]{:S(2)}) collective-permute-start(f32[2,128,256]{2,1,0:T(8,128)} %get-tuple-element.69.d_own), channel_id=1, source_target_pairs={{0,1},{1,0},{2,3},{3,2},{4,5},{5,4},{6,7},{7,6},{8,9},{9,8},{10,11... | collective-permute-start | bytes 786440 | tf_op jit(solution)/shard_map/ppermute | solution.py:313
  39.9 11.2 %collective-permute-start.18 = (f32[2,128,256]{2,1,0:T(8,128)S(1)}, f32[2,128,256]{2,1,0:T(8,128)S(1)}, u32[]{:S(2)}, u32[]{:S(2)}) collective-permute-start(f32[2,128,256]{2,1,0:T(8,128)S(1)} %collective-permute-done.17.d_own_other), channel_id=1, source_target_pairs={{0,2},{2,0},{4,6},{6,4},{8,10},{10,8},{12,14},{14,12},{16,18},{18,... | collective-permute-start | bytes 786440 | tf_op jit(solution)/shard_map/ppermute | solution.py:316
  48.3 8.8 %collective-permute-start.15 = (f32[4,64,256]{2,1,0:T(8,128)S(1)}, f32[4,64,256]{2,1,0:T(8,128)S(1)}, u32[]{:S(2)}, u32[]{:S(2)}) collective-permute-start(f32[4,64,256]{2,1,0:T(8,128)S(1)} %tile_update.2.mine), channel_id=1, source_target_pairs={{0,1},{1,0},{2,3},{3,2},{4,5},{5,4},{6,7},{7,6},{8,9},{9,8},{10,11... | collective-permute-start | bytes 786440 | tf_op jit(solution)/shard_map/ppermute | solution.py:313
  59.1 7.8 %collective-permute-start.20 = (f32[4,64,128]{2,1,0:T(8,128)}, f32[4,64,128]{2,1,0:T(8,128)}, u32[]{:S(2)}, u32[]{:S(2)}) collective-permute-start(f32[4,64,128]{2,1,0:T(8,128)} %get-tuple-element.40.refs_10_.values_own), channel_id=1, source_target_pairs={{0,8},{2,10},{4,12},{6,14},{8,0},{10,2},{12,4},{14,6},{16,24},{18,... | collective-permute-start | bytes 393224 | tf_op jit(solution)/shard_map/ppermute | solution.py:316
  60.5 7.7 %collective-permute-start.22 = (f32[4,64,128]{2,1,0:T(8,128)}, f32[4,64,128]{2,1,0:T(8,128)}, u32[]{:S(2)}, u32[]{:S(2)}) collective-permute-start(f32[4,64,128]{2,1,0:T(8,128)} %get-tuple-element.40.refs_10_.values_own), channel_id=1, source_target_pairs={{0,16},{2,18},{4,20},{6,22},{8,24},{10,26},{12,28},{14,30},{16,0},... | collective-permute-start | bytes 393224 | tf_op jit(solution)/shard_map/ppermute | solution.py:316
  63.0 8.3 %collective-permute-start.24 = (f32[4,64,128]{2,1,0:T(8,128)}, f32[4,64,128]{2,1,0:T(8,128)}, u32[]{:S(2)}, u32[]{:S(2)}) collective-permute-start(f32[4,64,128]{2,1,0:T(8,128)} %get-tuple-element.40.refs_10_.values_own), channel_id=1, source_target_pairs={{0,0},{2,2},{4,4},{6,6},{8,16},{10,18},{12,20},{14,22},{16,8},{18,... | collective-permute-start | bytes 393224 | tf_op jit(solution)/shard_map/ppermute | solution.py:326
  65.2 6.8 %collective-permute-start.19 = (f32[4,64,128]{2,1,0:T(8,128)}, f32[4,64,128]{2,1,0:T(8,128)}, u32[]{:S(2)}, u32[]{:S(2)}) collective-permute-start(f32[4,64,128]{2,1,0:T(8,128)} %get-tuple-element.40.refs_10_.values_own), channel_id=1, source_target_pairs={{0,4},{2,6},{4,0},{6,2},{8,12},{10,14},{12,8},{14,10},{16,20},{18,... | collective-permute-start | bytes 393224 | tf_op jit(solution)/shard_map/ppermute | solution.py:316
  66.9 7.9 %collective-permute-start.21 = (f32[4,64,128]{2,1,0:T(8,128)}, f32[4,64,128]{2,1,0:T(8,128)}, u32[]{:S(2)}, u32[]{:S(2)}) collective-permute-start(f32[4,64,128]{2,1,0:T(8,128)} %collective-permute-done.20.refs_12_), channel_id=1, source_target_pairs={{0,4},{2,6},{4,0},{6,2},{8,12},{10,14},{12,8},{14,10},{16,20},{18,... | collective-permute-start | bytes 393224 | tf_op jit(solution)/shard_map/ppermute | solution.py:316
  68.2 8.9 %collective-permute-start.23 = (f32[4,64,128]{2,1,0:T(8,128)}, f32[4,64,128]{2,1,0:T(8,128)}, u32[]{:S(2)}, u32[]{:S(2)}) collective-permute-start(f32[4,64,128]{2,1,0:T(8,128)} %collective-permute-done.22.refs_14_), channel_id=1, source_target_pairs={{0,4},{2,6},{4,0},{6,2},{8,12},{10,14},{12,8},{14,10},{16,20},{18,... | collective-permute-start | bytes 393224 | tf_op jit(solution)/shard_map/ppermute | solution.py:316
  71.3 7.2 %collective-permute-start.25 = (f32[4,64,128]{2,1,0:T(8,128)}, f32[4,64,128]{2,1,0:T(8,128)}, u32[]{:S(2)}, u32[]{:S(2)}) collective-permute-start(f32[4,64,128]{2,1,0:T(8,128)} %collective-permute-done.24.refs_16_), channel_id=1, source_target_pairs={{0,4},{2,6},{4,0},{6,2},{8,12},{10,14},{12,8},{14,10},{16,20},{18,... | collective-permute-start | bytes 393224 | tf_op jit(solution)/shard_map/ppermute | solution.py:316
  72.0 17.5 %collective-permute-start.27 = (f32[2,128,256]{2,1,0:T(8,128)}, f32[2,128,256]{2,1,0:T(8,128)S(1)}, u32[]{:S(2)}, u32[]{:S(2)}) collective-permute-start(f32[2,128,256]{2,1,0:T(8,128)} %get-tuple-element.69.d_own), channel_id=1, source_target_pairs={{0,2},{2,0},{4,6},{6,4},{8,10},{10,8},{12,14},{14,12},{16,18},{18,... | collective-permute-start | bytes 786440 | tf_op jit(solution)/shard_map/ppermute | solution.py:316
  72.0 17.5 %collective-permute-start.29 = (f32[2,128,256]{2,1,0:T(8,128)}, f32[2,128,256]{2,1,0:T(8,128)S(1)}, u32[]{:S(2)}, u32[]{:S(2)}) collective-permute-start(f32[2,128,256]{2,1,0:T(8,128)} %collective-permute-done.28.d_own_other), channel_id=1, source_target_pairs={{0,2},{2,0},{4,6},{6,4},{8,10},{10,8},{12,14},{14,12},{16,18},{18,... | collective-permute-start | bytes 786440 | tf_op jit(solution)/shard_map/ppermute | solution.py:316
  88.5 6.5 %collective-permute-start.26 = (f32[4,64,256]{2,1,0:T(8,128)S(1)}, f32[4,64,256]{2,1,0:T(8,128)S(1)}, u32[]{:S(2)}, u32[]{:S(2)}) collective-permute-start(f32[4,64,256]{2,1,0:T(8,128)S(1)} %tile_update.3.mine), channel_id=1, source_target_pairs={{0,1},{1,0},{2,3},{3,2},{4,5},{5,4},{6,7},{7,6},{8,9},{9,8},{10,11... | collective-permute-start | bytes 786440 | tf_op jit(solution)/shard_map/ppermute | solution.py:313
  100.9 6.5 %collective-permute-start.31 = (f32[4,64,128]{2,1,0:T(8,128)S(1)}, f32[4,64,128]{2,1,0:T(8,128)S(1)}, u32[]{:S(2)}, u32[]{:S(2)}) collective-permute-start(f32[4,64,128]{2,1,0:T(8,128)S(1)} %get-tuple-element.44), channel_id=1, source_target_pairs={{0,4},{2,6},{4,0},{6,2},{8,12},{10,14},{12,8},{14,10},{16,20},{18,... | collective-permute-start | bytes 393224 | tf_op jit(solution)/shard_map/ppermute | solution.py:316
  102.5 7.0 %collective-permute-start.33 = (f32[4,64,128]{2,1,0:T(8,128)S(1)}, f32[4,64,128]{2,1,0:T(8,128)S(1)}, u32[]{:S(2)}, u32[]{:S(2)}) collective-permute-start(f32[4,64,128]{2,1,0:T(8,128)S(1)} %get-tuple-element.46), channel_id=1, source_target_pairs={{0,4},{2,6},{4,0},{6,2},{8,12},{10,14},{12,8},{14,10},{16,20},{18,... | collective-permute-start | bytes 393224 | tf_op jit(solution)/shard_map/ppermute | solution.py:316
  103.0 9.3 %collective-permute-start.35 = (f32[4,64,128]{2,1,0:T(8,128)S(1)}, f32[4,64,128]{2,1,0:T(8,128)S(1)}, u32[]{:S(2)}, u32[]{:S(2)}) collective-permute-start(f32[4,64,128]{2,1,0:T(8,128)S(1)} %get-tuple-element.48), channel_id=1, source_target_pairs={{0,4},{2,6},{4,0},{6,2},{8,12},{10,14},{12,8},{14,10},{16,20},{18,... | collective-permute-start | bytes 393224 | tf_op jit(solution)/shard_map/ppermute | solution.py:316
  104.5 8.5 %collective-permute-start.30 = (f32[4,64,128]{2,1,0:T(8,128)S(1)}, f32[4,64,128]{2,1,0:T(8,128)S(1)}, u32[]{:S(2)}, u32[]{:S(2)}) collective-permute-start(f32[4,64,128]{2,1,0:T(8,128)S(1)} %get-tuple-element.42), channel_id=1, source_target_pairs={{0,4},{2,6},{4,0},{6,2},{8,12},{10,14},{12,8},{14,10},{16,20},{18,... | collective-permute-start | bytes 393224 | tf_op jit(solution)/shard_map/ppermute | solution.py:316
  107.4 5.6 %collective-permute-start.32 = (f32[4,64,128]{2,1,0:T(8,128)S(1)}, f32[4,64,128]{2,1,0:T(8,128)S(1)}, u32[]{:S(2)}, u32[]{:S(2)}) collective-permute-start(f32[4,64,128]{2,1,0:T(8,128)S(1)} %add.56), channel_id=1, source_target_pairs={{0,8},{2,10},{4,12},{6,14},{8,0},{10,2},{12,4},{14,6},{16,24},{18,... | collective-permute-start | bytes 393224 | tf_op jit(solution)/shard_map/ppermute | solution.py:316
  109.5 8.6 %collective-permute-start.34 = (f32[4,64,128]{2,1,0:T(8,128)S(1)}, f32[4,64,128]{2,1,0:T(8,128)S(1)}, u32[]{:S(2)}, u32[]{:S(2)}) collective-permute-start(f32[4,64,128]{2,1,0:T(8,128)S(1)} %add.58), channel_id=1, source_target_pairs={{0,16},{2,18},{4,20},{6,22},{8,24},{10,26},{12,28},{14,30},{16,0},... | collective-permute-start | bytes 393224 | tf_op jit(solution)/shard_map/ppermute | solution.py:316
  112.4 5.8 %collective-permute-start.36 = (f32[4,64,128]{2,1,0:T(8,128)S(1)}, f32[4,64,128]{2,1,0:T(8,128)S(1)}, u32[]{:S(2)}, u32[]{:S(2)}) collective-permute-start(f32[4,64,128]{2,1,0:T(8,128)S(1)} %add.60), channel_id=1, source_target_pairs={{0,0},{2,2},{4,4},{6,6},{8,16},{10,18},{12,20},{14,22},{16,8},{18,... | collective-permute-start | bytes 393224 | tf_op jit(solution)/shard_map/ppermute | solution.py:326
  118.2 5.0 %collective-permute-start.37 = (f32[4,64,128]{2,1,0:T(8,128)S(1)}, f32[4,64,128]{2,1,0:T(8,128)S(1)}, u32[]{:S(2)}, u32[]{:S(2)}) collective-permute-start(f32[4,64,128]{2,1,0:T(8,128)S(1)} %add_add_fusion.carried_own), channel_id=1, source_target_pairs={{0,1},{1,0},{2,3},{3,2},{4,5},{5,4},{6,7},{7,6},{8,9},{9,8},{10,11... | collective-permute-start | bytes 393224 | tf_op jit(solution)/shard_map/ppermute | solution.py:313
  127.4 5.0 %collective-permute-start.43 = (f32[4,64,128]{2,1,0:T(8,128)S(1)}, f32[4,64,128]{2,1,0:T(8,128)S(1)}, u32[]{:S(2)}, u32[]{:S(2)}) collective-permute-start(f32[4,64,128]{2,1,0:T(8,128)S(1)} %get-tuple-element.58), channel_id=1, source_target_pairs={{0,4},{2,6},{4,0},{6,2},{8,12},{10,14},{12,8},{14,10},{16,20},{18,... | collective-permute-start | bytes 393224 | tf_op jit(solution)/shard_map/ppermute | solution.py:316
  128.8 6.2 %collective-permute-start.41 = (f32[4,64,128]{2,1,0:T(8,128)S(1)}, f32[4,64,128]{2,1,0:T(8,128)S(1)}, u32[]{:S(2)}, u32[]{:S(2)}) collective-permute-start(f32[4,64,128]{2,1,0:T(8,128)S(1)} %get-tuple-element.56), channel_id=1, source_target_pairs={{0,4},{2,6},{4,0},{6,2},{8,12},{10,14},{12,8},{14,10},{16,20},{18,... | collective-permute-start | bytes 393224 | tf_op jit(solution)/shard_map/ppermute | solution.py:316
  129.5 11.0 %collective-permute-start.45 = (f32[2,128,256]{2,1,0:T(8,128)S(1)}, f32[2,128,256]{2,1,0:T(8,128)S(1)}, u32[]{:S(2)}, u32[]{:S(2)}) collective-permute-start(f32[2,128,256]{2,1,0:T(8,128)S(1)} %get-tuple-element.70.diag.d_own), channel_id=1, source_target_pairs={{0,2},{2,0},{4,6},{6,4},{8,10},{10,8},{12,14},{14,12},{16,18},{18,... | collective-permute-start | bytes 786440 | tf_op jit(solution)/shard_map/ppermute | solution.py:316
  129.5 9.0 %collective-permute-start.39 = (f32[4,64,128]{2,1,0:T(8,128)S(1)}, f32[4,64,128]{2,1,0:T(8,128)S(1)}, u32[]{:S(2)}, u32[]{:S(2)}) collective-permute-start(f32[4,64,128]{2,1,0:T(8,128)S(1)} %get-tuple-element.54), channel_id=1, source_target_pairs={{0,4},{2,6},{4,0},{6,2},{8,12},{10,14},{12,8},{14,10},{16,20},{18,... | collective-permute-start | bytes 393224 | tf_op jit(solution)/shard_map/ppermute | solution.py:316
  130.8 9.6 %collective-permute-start.38 = (f32[4,64,128]{2,1,0:T(8,128)S(1)}, f32[4,64,128]{2,1,0:T(8,128)S(1)}, u32[]{:S(2)}, u32[]{:S(2)}) collective-permute-start(f32[4,64,128]{2,1,0:T(8,128)S(1)} %get-tuple-element.52), channel_id=1, source_target_pairs={{0,4},{2,6},{4,0},{6,2},{8,12},{10,14},{12,8},{14,10},{16,20},{18,... | collective-permute-start | bytes 393224 | tf_op jit(solution)/shard_map/ppermute | solution.py:316
  132.4 8.1 %collective-permute-start.44 = (f32[4,64,128]{2,1,0:T(8,128)S(1)}, f32[4,64,128]{2,1,0:T(8,128)S(1)}, u32[]{:S(2)}, u32[]{:S(2)}) collective-permute-start(f32[4,64,128]{2,1,0:T(8,128)S(1)} %add.64), channel_id=1, source_target_pairs={{0,0},{2,2},{4,4},{6,6},{8,16},{10,18},{12,20},{14,22},{16,8},{18,... | collective-permute-start | bytes 393224 | tf_op jit(solution)/shard_map/ppermute | solution.py:326
  135.0 11.4 %collective-permute-start.42 = (f32[4,64,128]{2,1,0:T(8,128)S(1)}, f32[4,64,128]{2,1,0:T(8,128)S(1)}, u32[]{:S(2)}, u32[]{:S(2)}) collective-permute-start(f32[4,64,128]{2,1,0:T(8,128)S(1)} %add.63), channel_id=1, source_target_pairs={{0,16},{2,18},{4,20},{6,22},{8,24},{10,26},{12,28},{14,30},{16,0},... | collective-permute-start | bytes 393224 | tf_op jit(solution)/shard_map/ppermute | solution.py:316
  138.5 7.9 %collective-permute-start.40 = (f32[4,64,128]{2,1,0:T(8,128)S(1)}, f32[4,64,128]{2,1,0:T(8,128)S(1)}, u32[]{:S(2)}, u32[]{:S(2)}) collective-permute-start(f32[4,64,128]{2,1,0:T(8,128)S(1)} %add.62), channel_id=1, source_target_pairs={{0,8},{2,10},{4,12},{6,14},{8,0},{10,2},{12,4},{14,6},{16,24},{18,... | collective-permute-start | bytes 393224 | tf_op jit(solution)/shard_map/ppermute | solution.py:316
  146.7 1.4 collective-permute-start.46
  148.8 5.6 %collective-permute-start.47 = (f32[2,128,128]{2,1,0:T(8,128)S(1)}, f32[2,128,128]{2,1,0:T(8,128)S(1)}, u32[]{:S(2)}, u32[]{:S(2)}) collective-permute-start(f32[2,128,128]{2,1,0:T(8,128)S(1)} %get-tuple-element.62), channel_id=1, source_target_pairs={{0,1},{1,0},{2,3},{3,2},{4,5},{5,4},{6,7},{7,6},{8,9},{9,8},{10,11... | collective-permute-start | bytes 393224 | tf_op jit(solution)/shard_map/ppermute | solution.py:313
  149.3 1.4 collective-permute-start.49
  (29 other events, 116.9 us)

commit v2 on v1

v2 whole, which is shorter than its diff:
```python
import functools

import jax
import jax.numpy as jnp
from jax import lax
from jax.experimental import pallas as pl
from jax.experimental.pallas import tpu as pltpu
from jax.sharding import PartitionSpec as P

KDEV = 7


def from_behind(value, axis, steps):
    count = lax.axis_size(axis)
    leading, last = (max(0, -steps), min(count, count - steps))
    return lax.ppermute(value, axis, [(source, source + steps) for source in range(leading, last)])


def local_any(rhs, diag_inv, factor_tiles, tile_source, tile_count):
    levels = rhs.shape[0]
    owned_count = rhs.shape[1]
    share_rows = rhs.shape[2]
    columns = rhs.shape[3]
    slot_count = tile_source.shape[2]
    reach_dev = KDEV
    window_len = 2 * reach_dev + 1
    total_sup = lax.axis_size("rows") * owned_count
    row_place = lax.axis_index("rows")
    highest = lax.Precision.HIGHEST
    slot_ids = jnp.arange(slot_count, dtype=jnp.int32)

    def window_places(sources):
        src_level = sources // total_sup
        within = sources % total_sup
        return (
            src_level * window_len + within // owned_count - row_place + reach_dev
        ) * owned_count + within % owned_count

    def live_mask(counts):
        return (slot_ids[None, :] < counts[:, None]).astype(jnp.float32)

    def full_rows(piece):
        return lax.all_gather(piece, "cols", axis=1, tiled=True)

    forward_values = []
    windows = []
    for height in range(levels):
        if height == 0:
            whole_block = full_rows(rhs[0])
        else:
            stacked = jnp.stack(windows, 0).reshape(
                height * window_len * owned_count, share_rows, columns
            )
            places = window_places(tile_source[height - 1])
            picked = (
                jnp.take(stacked, places, axis=0)
                * live_mask(tile_count[height - 1])[:, :, None, None]
            )
            partial_value = jnp.einsum(
                "skci,skcr->sir", factor_tiles[height - 1], picked, precision=highest
            )
            whole_block = full_rows(
                rhs[height]
                - lax.psum_scatter(partial_value, "cols", scatter_dimension=1, tiled=True)
            )
        values = jnp.einsum("sci,sir->scr", diag_inv[height], whole_block, precision=highest)
        forward_values.append(values)
        if height + 1 < levels:
            pieces = []
            for pull_offset in range(-reach_dev, reach_dev + 1):
                if pull_offset == 0:
                    pieces.append(values)
                else:
                    pieces.append(from_behind(values, "rows", -pull_offset))
            windows.append(jnp.stack(pieces, 0))
    carried = [jnp.zeros_like(forward_values[0]) for height in range(levels)]
    solution = [None] * levels
    for height in reversed(range(levels)):
        partial_value = jnp.einsum(
            "sci,scr->sir",
            diag_inv[height],
            forward_values[height] - carried[height],
            precision=highest,
        )
        own_share = lax.psum_scatter(partial_value, "cols", scatter_dimension=1, tiled=True)
        if height > 0:
            whole_block = lax.all_gather(own_share, "cols", axis=1, tiled=True)
        solution[height] = own_share
        if height > 0:
            term_set = jnp.einsum(
                "skci,sir->skcr", factor_tiles[height - 1], whole_block, precision=highest
            )
            term_set = term_set * live_mask(tile_count[height - 1])[:, :, None, None]
            places = window_places(tile_source[height - 1]).reshape(-1)
            targets = height * window_len * owned_count
            one_hot = (jnp.arange(targets, dtype=jnp.int32)[:, None] == places[None, :]).astype(
                jnp.float32
            )
            outgoing = jnp.einsum(
                "ms,slg->mlg",
                one_hot,
                term_set.reshape(owned_count * slot_count, share_rows, columns),
                precision=highest,
            )
            push_outgoing = outgoing.reshape(height, window_len, owned_count, share_rows, columns)
            received = push_outgoing[:, reach_dev]
            for offset in range(-reach_dev, reach_dev + 1):
                if offset != 0:
                    received = received + from_behind(
                        push_outgoing[:, reach_dev + offset], "rows", offset
                    )
            for lower_level in range(height):
                carried[lower_level] = carried[lower_level] + received[lower_level]
    return jnp.stack(solution, 0)


F32 = jnp.float32
BF16 = jnp.bfloat16
NN = (((1,), (0,)), ((), ()))
NT = (((1,), (1,)), ((), ()))
PIECES = 8


def halves(value):
    high = value.astype(BF16)
    return high, (value - high.astype(F32)).astype(BF16)


def dot3(left, right, dims):
    left_high, left_low = halves(left)
    right_high, right_low = right if isinstance(right, tuple) else halves(right)
    dot = functools.partial(lax.dot_general, dimension_numbers=dims, preferred_element_type=F32)
    rows = left.shape[0]
    both = dot(jnp.concatenate([left_high, left_low], 0), right_high)
    return both[:rows] + both[rows:] + dot(left_high, right_low)


def ordered(mine, theirs, place, axis):
    first = jnp.where(place == 0, mine, theirs)
    second = jnp.where(place == 0, theirs, mine)
    return jnp.concatenate([first, second], axis)


def call(kernel, name, outs, args, scalars=1, scratch=()):
    in_specs = [pl.BlockSpec(memory_space=pltpu.SMEM)] * scalars
    in_specs += [pl.BlockSpec(memory_space=pltpu.VMEM)] * (len(args) - scalars)
    return pl.pallas_call(
        kernel,
        out_shape=[jax.ShapeDtypeStruct(shape, F32) for shape in outs],
        in_specs=in_specs,
        out_specs=[pl.BlockSpec(memory_space=pltpu.VMEM)] * len(outs),
        scratch_shapes=list(scratch),
        name=name,
        compiler_params=pltpu.CompilerParams(vmem_limit_bytes=VMEM_LIMIT),
    )(*args)


VMEM_LIMIT = 20 * 1024 * 1024


def split_kernel(own, partner, *outs):
    for tiles, high_out, low_out in ((own, outs[0], outs[1]), (partner, outs[2], outs[3])):
        high, low = halves(tiles[0, 0].reshape(high_out.shape[1:]))
        high_out[0] = high
        low_out[0] = low


def split_tiles(level, own, partner):
    owned, slots, depth, width = own.shape[1:]
    block_in = pl.BlockSpec((1, 1, slots, depth, width), lambda s: (level, s, 0, 0, 0))
    block_out = pl.BlockSpec((1, slots * depth, width), lambda s: (s, 0, 0))
    return pl.pallas_call(
        split_kernel,
        grid=(owned,),
        out_shape=[jax.ShapeDtypeStruct((owned, slots * depth, width), BF16)] * 4,
        in_specs=[block_in] * 2,
        out_specs=[block_out] * 4,
        name="split_tiles",
        compiler_params=pltpu.CompilerParams(vmem_limit_bytes=VMEM_LIMIT),
    )(own, partner)


def tile_of(tiles, s):
    half = tiles[0].shape[0]
    high, low = tiles[:2] if s < half else tiles[2:]
    return high[s % half], low[s % half]


def first_values(where, rhs_own, rhs_other, diag, mine, partner):
    core, col = where[0] % 2, where[1]
    half = mine.shape[1]
    for s in range(rhs_own.shape[0]):
        rows = ordered(rhs_own[s], rhs_other[s], col, 0)
        values = dot3(diag[0, s], rows, NN).T
        low, high = values[:half], values[half:]
        mine[s] = jnp.where(core == 0, low, high)
        partner[s] = jnp.where(core == 0, high, low)


def turned_rhs(where, rhs_own, rhs_other, mine, partner):
    core, col = where[0] % 2, where[1]
    half = mine.shape[2]
    for l in range(mine.shape[0]):
        for s in range(mine.shape[1]):
            rows = ordered(rhs_own[l, s].T, rhs_other[l, s].T, col, 1)
            low, high = rows[:half], rows[half:]
            mine[l, s] = jnp.where(core == 0, low, high)
            partner[l, s] = jnp.where(core == 0, high, low)


def tile_update(index, based, places, *refs):
    tiles, refs = refs[:4], refs[4:]
    if based:
        base, refs = refs[0], refs[1:]
    out, window = refs[-2:]
    pieces = refs[:-2]
    sups = pieces[0].shape[0]
    for number, piece in enumerate(pieces):
        window[number * sups : (number + 1) * sups] = piece[...]
    slots = places.shape[1] // sups
    for s in range(sups):
        picked = []
        for k in range(slots):
            place = places[index, s * slots + k]
            value = window[jnp.maximum(place, 0)]
            picked.append(jnp.where(place >= 0, value, 0.0))
        total = dot3(jnp.concatenate(picked, 1), tile_of(tiles, s), NN)
        out[s] = total + base[s] if based else total


def diag_of(level, diags, s):
    own, partner, own_other, partner_other = diags
    half = own.shape[1]
    if s < half:
        return own[level, s], own_other[level - 1, s]
    return partner[level, s % half], partner_other[level - 1, s % half]


def upper_of(level, mine, partner, s):
    half = mine.shape[1]
    return mine[level - 1, s] if s < half else partner[level - 1, s % half]


def level_values(level, rhs, rhs_partner, mine, theirs, d0, d1, d2, d3, own, other):
    for s in range(own.shape[0]):
        residual = upper_of(level, rhs, rhs_partner, s) - (mine[s] + theirs[s])
        diag, diag_other = diag_of(level, (d0, d1, d2, d3), s)
        own[s] = dot3(residual, diag, NT)
        other[s] = dot3(residual, diag_other, NT)


def add_terms(index, places, tiles, x, s, totals, depth):
    terms = dot3(x, tile_of(tiles, s), NT)
    slots = terms.shape[1] // depth
    for k in range(slots):
        place = places[index, s * slots + k]
        term = jnp.where(place >= 0, terms[:, k * depth : (k + 1) * depth], 0.0)
        place = jnp.maximum(place, 0)
        totals[place] = totals[place] + term


def share_out(col, x, s, solved_mine, solved_partner):
    depth = solved_mine.shape[2]
    half = solved_mine.shape[0]
    share = jnp.where(col == 0, x[:, :depth], x[:, depth:])
    if s < half:
        solved_mine[s] = share
    else:
        solved_partner[s % half] = share


def pieces_out(totals, outs):
    sups = outs[0].shape[0]
    for number, out in enumerate(outs):
        out[...] = totals[number * sups : (number + 1) * sups]


def top_carry(
    level, where, places, rhs, rhs_partner, mine, theirs, d0, d1, d2, d3, t0, t1, t2, t3,
    solved_mine, solved_partner, solved, *rest
):
    outs, totals = rest[:-1], rest[-1]
    totals[...] = jnp.zeros_like(totals)
    for s in range(solved.shape[0]):
        residual = upper_of(level, rhs, rhs_partner, s) - (mine[s] + theirs[s])
        diag, diag_other = diag_of(level, (d0, d1, d2, d3), s)
        own = dot3(residual, diag, NT)
        other = dot3(residual, diag_other, NT)
        x = dot3(own, diag, NN) + dot3(other, diag_other, NN)
        solved[s] = x
        share_out(where[1], x, s, solved_mine, solved_partner)
        add_terms(2, places, (t0, t1, t2, t3), x, s, totals, outs[0].shape[2])
    pieces_out(totals, outs)


def lowest_carry(places, solved, t0, t1, t2, t3, totals):
    totals[...] = jnp.zeros_like(totals)
    for s in range(solved.shape[0]):
        add_terms(1, places, (t0, t1, t2, t3), solved[s], s, totals, totals.shape[2])


def middle_carry(
    level, where, places, carried_own, carried_other, values_own, values_other,
    d0, d1, d2, d3, t0, t1, t2, t3, lowest, solved_mine, solved_partner, *rest
):
    outs, totals = rest[:-1], rest[-1]
    totals[...] = lowest[...]
    for s in range(values_own.shape[0]):
        diag, diag_other = diag_of(level, (d0, d1, d2, d3), s)
        own = values_own[s] - carried_own[s]
        other = values_other[s] - carried_other[s]
        x = dot3(own, diag, NN) + dot3(other, diag_other, NN)
        share_out(where[1], x, s, solved_mine, solved_partner)
        add_terms(0, places, (t0, t1, t2, t3), x, s, totals, outs[0].shape[2])
    pieces_out(totals, outs)


def last_product(values, a, b, c, d, e, d_own, d_partner, mine, partner):
    sups = values.shape[0]
    half = sups // 2
    for s in range(sups):
        carried = a[s] + b[s] + c[s] + d[s] + e[s]
        diag, out = (d_own, mine) if s < half else (d_partner, partner)
        out[s % half] = dot3(values[s] - carried, diag[0, s % half], NN)


def turned_solution(where, mine, partner, own, other):
    core, col = where[0] % 2, where[1]
    depth = own.shape[1]
    for s in range(mine.shape[0]):
        both = ordered(mine[s], partner[s], core, 0)
        low, high = both[:, :depth].T, both[:, depth:].T
        own[s] = jnp.where(col == 0, low, high)
        other[s] = jnp.where(col == 0, high, low)


def turned_upper(where, mine2, partner2, mine1, partner1, out):
    core = where[0] % 2
    for s in range(mine2.shape[0]):
        out[0, s] = ordered(mine1[s], partner1[s], core, 0).T
        out[1, s] = ordered(mine2[s], partner2[s], core, 0).T


def local(rhs, diag_inv, factor_tiles, tile_source, tile_count):
    levels, owned, share_rows, columns = rhs.shape
    slots = tile_source.shape[2]
    sups = 2 * owned
    block = share_rows * 2
    half_columns = columns // 2
    row = lax.axis_index("rows")
    col = lax.axis_index("cols")
    where = jnp.stack([row, col]).astype(jnp.int32)
    rows_total = lax.axis_size("rows")
    total_sup = rows_total * owned
    piece = (sups, half_columns, share_rows)
    shared = (owned, half_columns, share_rows)
    window = (PIECES * sups, half_columns, share_rows)
    after = lax.optimization_barrier

    def swap_cols(value):
        return lax.ppermute(value, "cols", [(0, 1), (1, 0)])

    def swap_rows(value, bits):
        return lax.ppermute(value, "rows", [(r, r ^ bits) for r in range(rows_total)])

    def swap_core(value):
        return swap_rows(value, 1)

    def swap_x(value):
        return swap_rows(value, 2)

    def swap_mid(value):
        low, high = rows_total // 4, 3 * rows_total // 4
        pairs = [(r, r ^ 12 if low <= r < high else r) for r in range(rows_total)]
        return lax.ppermute(value, "rows", pairs)

    def gather_pieces(value):
        far = swap_rows(value, 8)
        mid = swap_mid(value)
        near = swap_rows(value, 4)
        beside = swap_x(value)
        return [value, beside, near, swap_x(near), far, swap_x(far), mid, swap_x(mid)]

    def scatter_pieces(p):
        far = swap_rows(p[4] + swap_x(p[5]), 8)
        mid = swap_mid(p[6] + swap_x(p[7]))
        near = swap_rows(p[2] + swap_x(p[3]), 4)
        beside = swap_x(p[1])
        return [p[0], beside, near, far, mid]

    rhs0 = rhs[0]
    rhs0_other = swap_cols(rhs0)
    upper_own, d_own, rhs0 = after((rhs[1:], diag_inv[1:], rhs0))
    d_own_other = swap_cols(d_own)
    upper_other = swap_cols(upper_own)
    tiles_partner = swap_core(factor_tiles)
    d_partner = swap_core(diag_inv)
    source_partner = swap_core(tile_source)
    count_partner = swap_core(tile_count)
    mine, partner = call(
        first_values, "first_values", [shared] * 2, [where, rhs0, rhs0_other, diag_inv]
    )
    values0 = jnp.concatenate([mine, swap_core(partner)], 0)
    pieces0 = gather_pieces(values0)

    source = jnp.concatenate([tile_source, source_partner], 1)
    count = jnp.concatenate([tile_count, count_partner], 1)
    live = jnp.arange(slots, dtype=jnp.int32)[None, None, :] < count[:, :, None]
    within = source % total_sup
    place = (row ^ (within // owned)) * owned + within % owned
    lower = source // total_sup
    places = jnp.stack(
        [
            jnp.where(live[0], place[0], -1),
            jnp.where(live[1] & (lower[1] == 0), place[1], -1),
            jnp.where(live[1] & (lower[1] == 1), place[1], -1),
        ]
    ).reshape(3, sups * slots)
    tiles = [split_tiles(l, factor_tiles, tiles_partner) for l in range(levels - 1)]
    d_partner_other = swap_core(d_own_other)
    diags = [diag_inv, d_partner, d_own_other, d_partner_other]
    upper, partner = call(
        turned_rhs, "turned_rhs", [(levels - 1, owned, half_columns, block)] * 2,
        [where, upper_own, upper_other],
    )
    upper_partner = swap_core(partner)

    def update(name, index, l, pieces, base=()):
        return call(
            functools.partial(tile_update, index, len(base) > 0), name,
            [(sups, half_columns, block)],
            [places, *tiles[l], *base, *pieces], 1, [pltpu.VMEM(window, F32)],
        )[0]

    partial = update("update_middle", 0, 0, pieces0)
    values1, values1_other = call(
        functools.partial(level_values, 1), "level_values", [piece] * 2,
        [upper, upper_partner, partial, swap_cols(partial), *diags], 0,
    )
    pieces1 = gather_pieces(values1)
    base = update("update_top_low", 1, 1, pieces0)

    partial = update("update_top", 2, 1, pieces1, [base])
    mine2, partner2, solved, *out = call(
        functools.partial(top_carry, 2), "top_carry",
        [shared, shared, (sups, half_columns, block)] + [piece] * PIECES,
        [where, places, upper, upper_partner, partial, swap_cols(partial), *diags, *tiles[1]], 2,
        [pltpu.VMEM(window, F32)],
    )
    carried = sum(scatter_pieces(out))
    lowest = call(lowest_carry, "lowest_carry", [window], [places, solved, *tiles[1]])[0]
    partner2 = swap_core(partner2)

    mine1, partner1, *out = call(
        functools.partial(middle_carry, 1), "middle_carry", [shared, shared] + [piece] * PIECES,
        [where, places, carried, swap_cols(carried), values1, values1_other, *diags,
         *tiles[0], lowest], 2,
        [pltpu.VMEM(window, F32)],
    )
    partner1 = swap_core(partner1)
    result_upper = call(
        turned_upper, "turned_upper", [(levels - 1, owned, share_rows, columns)],
        [where, mine2, partner2, mine1, partner1],
    )[0]

    mine, partner = call(
        last_product, "last_product", [(owned, half_columns, block)] * 2,
        [values0, *scatter_pieces(out), diag_inv, d_partner], 0,
    )
    own, other = call(
        turned_solution, "turned_solution", [(owned, share_rows, columns)] * 2,
        [where, mine, swap_core(partner)],
    )
    return jnp.concatenate([(own + swap_cols(other))[None], result_upper], 0)


def solution(mesh):
    placed = (
        P(None, "rows", "cols", None),
        P(None, "rows", "cols", None),
        P(None, "rows", None, "cols", None),
        P(None, "rows", None),
        P(None, "rows"),
    )
    small = mesh.shape["rows"] == 16 and mesh.shape["cols"] == 2
    return jax.shard_map(
        local if small else local_any,
        mesh=mesh,
        in_specs=placed,
        out_specs=P(None, "rows", "cols", None),
        check_vma=False,
    )
```

time: 156 us -> 130 us (0.83)
  local copies, waits for them, and re-layouts: 23.9 us -> 6.21 us
  starting transfers between devices: 52.4 us -> 42.6 us
  other arithmetic: 1.15 us -> 4.66 us
  waiting for transfers between devices: 55.1 us -> 51.6 us
    unnamed x56 -> x5, local copies, waits for them, and re-layouts: 14.4 us -> 2.19 us
    squeeze x7 -> x1, local copies, waits for them, and re-layouts: 7.99 us -> 0.91 us  [local(): rhs0 = rhs[0]]
    ppermute x38 -> x34, starting transfers between devices: 39.3 us -> 33 us  [swap_rows(): lax.ppermute(value, 'rows', [(r, r ^ bits) for r in range(rows_total)])]
    ppermute x8 -> x7, waiting for transfers between devices: 24.8 us -> 19.2 us  [swap_cols(): return lax.ppermute(value, 'cols', [(0, 1), (1, 0)])]
    slice x2, local copies, waits for them, and re-layouts: 0.54 us -> 2.85 us  [local(): upper_own, d_own, rhs0 = after((rhs[1:], diag_inv[1:], rhs0))]
    ppermute x38 -> x34, waiting for transfers between devices: 30.4 us -> 32.4 us  [swap_rows(): lax.ppermute(value, 'rows', [(r, r ^ bits) for r in range(rows_total)])]
    ppermute x8 -> x7, starting transfers between devices: 8.96 us -> 6.89 us  [swap_cols(): return lax.ppermute(value, 'cols', [(0, 1), (1, 0)])]
    pallas_call x10 -> x14, Pallas kernels: 22.3 us -> 23.5 us  [the longest x12 19.8 us: call(): pl.pallas_call(kernel, out_shape=[jax.ShapeDtypeStruct(shape, F32) for sh...]
  transfers between devices with their start and end apart: 50 -> 45, of which waited for: 23 -> 22; matrix products, arithmetic and copies ran while one was open for 4% -> 6% of each run, Pallas kernels for 7% -> 9%
where the time goes in v2:
time: 130 us; the launch traced here: 129 us
  waiting for transfers between devices  51.6 us (40%)
  starting transfers between devices  42.6 us (33%)
  Pallas kernels  23.5 us (18%)
  local copies, waits for them, and re-layouts  6.21 us (5%)
  other arithmetic  4.66 us (4%)
    ppermute x34, starting transfers between devices, swap_rows(): lax.ppermute(value, 'rows', [(r, r ^ bits) for r in range(rows_total)])  33 us
    ppermute x34, waiting for transfers between devices, swap_rows(): lax.ppermute(value, 'rows', [(r, r ^ bits) for r in range(rows_total)])  32.4 us
    pallas_call x12, Pallas kernels, call(): pl.pallas_call(kernel, out_shape=[jax.ShapeDtypeStruct(shape, F32) for sh...  19.8 us
    ppermute x7, waiting for transfers between devices, swap_cols(): return lax.ppermute(value, 'cols', [(0, 1), (1, 0)])  19.2 us
    ppermute x7, starting transfers between devices, swap_cols(): return lax.ppermute(value, 'cols', [(0, 1), (1, 0)])  6.89 us
    pallas_call x2, Pallas kernels, split_tiles(): pl.pallas_call(split_kernel, grid=(owned,), out_shape=[jax.ShapeDtypeStru...  3.67 us
    slice x2, local copies, waits for them, and re-layouts, local(): upper_own, d_own, rhs0 = after((rhs[1:], diag_inv[1:], rhs0))  2.85 us
    ppermute x4, starting transfers between devices, swap_mid(): return lax.ppermute(value, 'rows', pairs)  2.65 us
  transfers between devices with their start and end apart: 45, of which 22 were waited for; matrix products, arithmetic and copies ran while one was open for 6% of the time, Pallas kernels for 9%

profile of v2, /device:TPU:0, one launch (start us, length us, event | category | flops | bytes accessed | tf_op | source)
XLA Modules:
  0.0 128.9 jit_solution(12926280759934322337)
XLA Ops:
  1.0 0.9 slice_bitcast_fusion.rhs_own
  1.9 2.6 %collective-permute-start = (f32[2,128,128]{2,1,0:T(8,128)S(1)}, f32[2,128,128]{2,1,0:T(8,128)S(1)}, u32[]{:S(2)}, u32[]{:S(2)}) collective-permute-start(f32[2,128,128]{2,1,0:T(8,128)S(1)} %slice_bitcast_fusion.rhs_own), channel_id=1, source_target_pairs={{0,1},{1,0},{2,3},{3,2},{4,5},{5,4},{6,7},{7,6},{8,9},{9,8},{10,11... | collective-permute-start | bytes 393224 | tf_op jit(solution)/shard_map/ppermute | solution.py:361
  4.5 1.0 slice.27.rhs_own
  5.4 1.9 %slice.28 = f32[2,2,128,256]{3,2,1,0:T(8,128)} slice(f32[3,2,128,256]{3,2,1,0:T(8,128)} %d_own.1), slice={[1:3], [0:2], [0:128], [0:256]} | slice | bytes 1048576 | tf_op jit(solution)/shard_map/slice | solution.py:393
  7.4 2.0 %collective-permute-start.16 = (f32[2,2,128,256]{3,2,1,0:T(8,128)}, f32[2,2,128,256]{3,2,1,0:T(8,128)S(1)}, u32[]{:S(2)}, u32[]{:S(2)}) collective-permute-start(f32[2,2,128,256]{3,2,1,0:T(8,128)} %slice.28), channel_id=1, source_target_pairs={{0,1},{1,0},{2,3},{3,2},{4,5},{5,4},{6,7},{7,6},{8,9},{9,8},{10,11... | collective-permute-start | bytes 1572872 | tf_op jit(solution)/shard_map/ppermute | solution.py:361
  11.7 1.5 %first_values.1 = (f32[2,64,128]{2,1,0:T(8,128)S(1)}, f32[2,64,128]{2,1,0:T(8,128)S(1)}) custom-call(s32[2]{0:T(128)S(1)} %pad_add_fusion.3.where, f32[2,128,128]{2,1,0:T(8,128)S(1)} %slice_bitcast_fusion.rhs_own, f32[2,128,128]{2,1,0:T(8,128)S(1)} %collective-permute-done.rhs_other, f32[3,2,128,256]{3,2,1,0:T(8,128)} %d_own.1), custom_call_target="tpu_custom_call" | custom-call | tf_op jit(solution)/shard_map/first_values/pallas_call | solution.py:147
  13.3 1.2 collective-permute-done.1
  14.5 1.5 %collective-permute-start.7 = (f32[4,64,128]{2,1,0:T(8,128)S(1)}, f32[4,64,128]{2,1,0:T(8,128)S(1)}, u32[]{:S(2)}, u32[]{:S(2)}) collective-permute-start(f32[4,64,128]{2,1,0:T(8,128)S(1)} %constant_dynamic-update-slice_fusion.refs_4_.values), channel_id=1, source_target_pairs={{0,4},{2,6},{4,0},{6,2},{8,12},{10,14},{12,8},{14,10},{16,20},{18,... | collective-permute-start | bytes 393224 | tf_op jit(solution)/shard_map/ppermute | solution.py:364
  16.0 1.6 %collective-permute-start.8 = (f32[4,64,128]{2,1,0:T(8,128)S(1)}, f32[4,64,128]{2,1,0:T(8,128)S(1)}, u32[]{:S(2)}, u32[]{:S(2)}) collective-permute-start(f32[4,64,128]{2,1,0:T(8,128)S(1)} %constant_dynamic-update-slice_fusion.refs_4_.values), channel_id=1, source_target_pairs={{0,8},{2,10},{4,12},{6,14},{8,0},{10,2},{12,4},{14,6},{16,24},{18,... | collective-permute-start | bytes 393224 | tf_op jit(solution)/shard_map/ppermute | solution.py:364
  18.3 1.7 %collective-permute-done.7.refs_5_ = f32[4,64,128]{2,1,0:T(8,128)S(1)} collective-permute-done((f32[4,64,128]{2,1,0:T(8,128)S(1)}, f32[4,64,128]{2,1,0:T(8,128)S(1)}, u32[]{:S(2)}, u32[]{:S(2)}) %collective-permute-start.7) | collective-permute-done | bytes 131104 | tf_op jit(solution)/shard_map/ppermute | solution.py:364
  20.0 2.6 %collective-permute-start.10 = (f32[4,64,128]{2,1,0:T(8,128)S(1)}, f32[4,64,128]{2,1,0:T(8,128)S(1)}, u32[]{:S(2)}, u32[]{:S(2)}) collective-permute-start(f32[4,64,128]{2,1,0:T(8,128)S(1)} %constant_dynamic-update-slice_fusion.refs_4_.values), channel_id=1, source_target_pairs={{0,16},{2,18},{4,20},{6,22},{8,24},{10,26},{12,28},{14,30},{16,0},... | collective-permute-start | bytes 393224 | tf_op jit(solution)/shard_map/ppermute | solution.py:364
  24.0 5.7 %collective-permute-done.10.refs_8_ = f32[4,64,128]{2,1,0:T(8,128)S(1)} collective-permute-done((f32[4,64,128]{2,1,0:T(8,128)S(1)}, f32[4,64,128]{2,1,0:T(8,128)S(1)}, u32[]{:S(2)}, u32[]{:S(2)}) %collective-permute-start.10) | collective-permute-done | bytes 131104 | tf_op jit(solution)/shard_map/ppermute | solution.py:364
  29.7 1.5 %collective-permute-start.9 = (f32[4,64,128]{2,1,0:T(8,128)S(1)}, f32[4,64,128]{2,1,0:T(8,128)S(1)}, u32[]{:S(2)}, u32[]{:S(2)}) collective-permute-start(f32[4,64,128]{2,1,0:T(8,128)S(1)} %collective-permute-done.8.refs_6_), channel_id=1, source_target_pairs={{0,4},{2,6},{4,0},{6,2},{8,12},{10,14},{12,8},{14,10},{16,20},{18,... | collective-permute-start | bytes 393224 | tf_op jit(solution)/shard_map/ppermute | solution.py:364
  31.7 1.5 %collective-permute-start.13 = (f32[4,64,128]{2,1,0:T(8,128)S(1)}, f32[4,64,128]{2,1,0:T(8,128)S(1)}, u32[]{:S(2)}, u32[]{:S(2)}) collective-permute-start(f32[4,64,128]{2,1,0:T(8,128)S(1)} %collective-permute-done.12.refs_10_), channel_id=1, source_target_pairs={{0,4},{2,6},{4,0},{6,2},{8,12},{10,14},{12,8},{14,10},{16,20},{18,... | collective-permute-start | bytes 393224 | tf_op jit(solution)/shard_map/ppermute | solution.py:364
  34.2 2.2 %copy-done = f32[2,2,8,128,256]{4,3,2,1,0:T(8,128)S(1)} copy-done((f32[2,2,8,128,256]{4,3,2,1,0:T(8,128)S(1)}, f32[2,2,8,128,256]{4,3,2,1,0:T(8,128)}, u32[]{:S(2)}) %copy-start) | copy-done | bytes 4194328
  36.4 1.8 %split_tiles.3 = (bf16[2,1024,256]{2,1,0:T(8,128)(2,1)S(1)}, bf16[2,1024,256]{2,1,0:T(8,128)(2,1)S(1)}, bf16[2,1024,256]{2,1,0:T(8,128)(2,1)S(1)}, bf16[2,1024,256]{2,1,0:T(8,128)(2,1)S(1)}) custom-call(f32[2,2,8,128,256]{4,3,2,1,0:T(8,128)S(1)} %copy-done, f32[2,2,8,128,256]{4,3,2,1,0:T(8,128)} %collective-permute-done.6.partner), custom_call_target="tpu_custom_call" | custom-call | tf_op jit(solution)/shard_map/split_tiles/pallas_call | solution.py:172
  38.8 1.4 %update_middle.1.mine = f32[4,64,256]{2,1,0:T(8,128)S(1)} custom-call(s32[3,32]{1,0:T(4,128)S(1)} %pad_add_fusion.1.places, bf16[2,1024,256]{2,1,0:T(8,128)(2,1)S(1)} %get-tuple-element.57.refs_0_.t0, bf16[2,1024,256]{2,1,0:T(8,128)(2,1)S(1)} %get-tuple-element.58.refs_1_.t1, bf16[2,1024,256]{2,1,0:T(8,128)(2,1)S(1)} %get-tuple-element.59.refs_2_.t2, ...), custom_call_target="tpu_custom_call" | custom-call | tf_op jit(solution)/shard_map/update_middle/pallas_call | solution.py:147
  40.8 7.7 %collective-permute-done.14.theirs = f32[4,64,256]{2,1,0:T(8,128)S(1)} collective-permute-done((f32[4,64,256]{2,1,0:T(8,128)S(1)}, f32[4,64,256]{2,1,0:T(8,128)S(1)}, u32[]{:S(2)}, u32[]{:S(2)}) %collective-permute-start.14) | collective-permute-done | bytes 262176 | tf_op jit(solution)/shard_map/ppermute | solution.py:361
  48.6 1.6 %level_values.1 = (f32[4,64,128]{2,1,0:T(8,128)S(1)}, f32[4,64,128]{2,1,0:T(8,128)S(1)}) custom-call(f32[2,2,64,256]{3,2,1,0:T(8,128)S(1)} %get-tuple-element.51.rhs, f32[2,2,64,256]{3,2,1,0:T(8,128)S(1)} %collective-permute-done.5.rhs_partner, f32[4,64,256]{2,1,0:T(8,128)S(1)} %update_middle.1.mine, f32[4,64,256]{2,1,0:T(8,128)S(1)} %collective-permute-done.14.theirs, ...), custom_call_target="tpu_custom_call" | custom-call | tf_op jit(solution)/shard_map/level_values/pallas_call | solution.py:147
  50.2 0.9 collective-permute-start.19
  51.0 2.5 %collective-permute-start.21 = (f32[4,64,128]{2,1,0:T(8,128)S(1)}, f32[4,64,128]{2,1,0:T(8,128)S(1)}, u32[]{:S(2)}, u32[]{:S(2)}) collective-permute-start(f32[4,64,128]{2,1,0:T(8,128)S(1)} %get-tuple-element.62.refs_5_.values_own), channel_id=1, source_target_pairs={{0,16},{2,18},{4,20},{6,22},{8,24},{10,26},{12,28},{14,30},{16,0},... | collective-permute-start | bytes 393224 | tf_op jit(solution)/shard_map/ppermute | solution.py:364
  54.2 1.6 %collective-permute-start.18 = (f32[4,64,128]{2,1,0:T(8,128)S(1)}, f32[4,64,128]{2,1,0:T(8,128)S(1)}, u32[]{:S(2)}, u32[]{:S(2)}) collective-permute-start(f32[4,64,128]{2,1,0:T(8,128)S(1)} %get-tuple-element.62.refs_5_.values_own), channel_id=1, source_target_pairs={{0,4},{2,6},{4,0},{6,2},{8,12},{10,14},{12,8},{14,10},{16,20},{18,... | collective-permute-start | bytes 393224 | tf_op jit(solution)/shard_map/ppermute | solution.py:364
  57.1 3.0 %collective-permute-done.21.refs_9_ = f32[4,64,128]{2,1,0:T(8,128)S(1)} collective-permute-done((f32[4,64,128]{2,1,0:T(8,128)S(1)}, f32[4,64,128]{2,1,0:T(8,128)S(1)}, u32[]{:S(2)}, u32[]{:S(2)}) %collective-permute-start.21) | collective-permute-done | bytes 131104 | tf_op jit(solution)/shard_map/ppermute | solution.py:364
  60.1 1.5 %collective-permute-start.22 = (f32[4,64,128]{2,1,0:T(8,128)S(1)}, f32[4,64,128]{2,1,0:T(8,128)S(1)}, u32[]{:S(2)}, u32[]{:S(2)}) collective-permute-start(f32[4,64,128]{2,1,0:T(8,128)S(1)} %collective-permute-done.21.refs_9_), channel_id=1, source_target_pairs={{0,4},{2,6},{4,0},{6,2},{8,12},{10,14},{12,8},{14,10},{16,20},{18,... | collective-permute-start | bytes 393224 | tf_op jit(solution)/shard_map/ppermute | solution.py:364
  62.2 1.8 %split_tiles.2 = (bf16[2,1024,256]{2,1,0:T(8,128)(2,1)S(1)}, bf16[2,1024,256]{2,1,0:T(8,128)(2,1)S(1)}, bf16[2,1024,256]{2,1,0:T(8,128)(2,1)S(1)}, bf16[2,1024,256]{2,1,0:T(8,128)(2,1)S(1)}) custom-call(f32[2,2,8,128,256]{4,3,2,1,0:T(8,128)S(1)} %copy-done.1, f32[2,2,8,128,256]{4,3,2,1,0:T(8,128)} %collective-permute-done.6.partner), custom_call_target="tpu_custom_call" | custom-call | tf_op jit(solution)/shard_map/split_tiles/pallas_call | solution.py:172
  64.0 1.4 %update_top_low.1.refs_4_ = f32[4,64,256]{2,1,0:T(8,128)S(1)} custom-call(s32[3,32]{1,0:T(4,128)S(1)} %pad_add_fusion.1.places, bf16[2,1024,256]{2,1,0:T(8,128)(2,1)S(1)} %get-tuple-element.53.refs_0_.t0, bf16[2,1024,256]{2,1,0:T(8,128)(2,1)S(1)} %get-tuple-element.54.refs_1_.t1, bf16[2,1024,256]{2,1,0:T(8,128)(2,1)S(1)} %get-tuple-element.55.refs_2_.t2, ...), custom_call_target="tpu_custom_call" | custom-call | tf_op jit(solution)/shard_map/update_top_low/pallas_call | solution.py:147
  66.2 1.4 %collective-permute-done.24.refs_12_ = f32[4,64,128]{2,1,0:T(8,128)S(1)} collective-permute-done((f32[4,64,128]{2,1,0:T(8,128)S(1)}, f32[4,64,128]{2,1,0:T(8,128)S(1)}, u32[]{:S(2)}, u32[]{:S(2)}) %collective-permute-start.24) | collective-permute-done | bytes 131104 | tf_op jit(solution)/shard_map/ppermute | solution.py:364
  67.6 1.4 %update_top.1.mine = f32[4,64,256]{2,1,0:T(8,128)S(1)} custom-call(s32[3,32]{1,0:T(4,128)S(1)} %pad_add_fusion.1.places, bf16[2,1024,256]{2,1,0:T(8,128)(2,1)S(1)} %get-tuple-element.53.refs_0_.t0, bf16[2,1024,256]{2,1,0:T(8,128)(2,1)S(1)} %get-tuple-element.54.refs_1_.t1, bf16[2,1024,256]{2,1,0:T(8,128)(2,1)S(1)} %get-tuple-element.55.refs_2_.t2, ...), custom_call_target="tpu_custom_call" | custom-call | tf_op jit(solution)/shard_map/update_top/pallas_call | solution.py:147
  69.6 6.0 %collective-permute-done.25.theirs = f32[4,64,256]{2,1,0:T(8,128)S(1)} collective-permute-done((f32[4,64,256]{2,1,0:T(8,128)S(1)}, f32[4,64,256]{2,1,0:T(8,128)S(1)}, u32[]{:S(2)}, u32[]{:S(2)}) %collective-permute-start.25) | collective-permute-done | bytes 262176 | tf_op jit(solution)/shard_map/ppermute | solution.py:361
  75.7 3.9 %top_carry.1 = (f32[2,64,128]{2,1,0:T(8,128)S(1)}, f32[2,64,128]{2,1,0:T(8,128)S(1)}, f32[4,64,256]{2,1,0:T(8,128)S(1)}, f32[4,64,128]{2,1,0:T(8,128)S(1)}, f32[...) custom-call(s32[2]{0:T(128)S(1)} %pad_add_fusion.3.where, ...), custom_call_target="tpu_custom_call" | custom-call | tf_op jit(solution)/shard_map/top_carry/pallas_call | solution.py:147
  79.9 1.8 %collective-permute-start.29 = (f32[4,64,128]{2,1,0:T(8,128)S(1)}, f32[4,64,128]{2,1,0:T(8,128)S(1)}, u32[]{:S(2)}, u32[]{:S(2)}) collective-permute-start(f32[4,64,128]{2,1,0:T(8,128)S(1)} %get-tuple-element.68), channel_id=1, source_target_pairs={{0,4},{2,6},{4,0},{6,2},{8,12},{10,14},{12,8},{14,10},{16,20},{18,... | collective-permute-start | bytes 393224 | tf_op jit(solution)/shard_map/ppermute | solution.py:364
  81.9 1.8 %collective-permute-start.26 = (f32[4,64,128]{2,1,0:T(8,128)S(1)}, f32[4,64,128]{2,1,0:T(8,128)S(1)}, u32[]{:S(2)}, u32[]{:S(2)}) collective-permute-start(f32[4,64,128]{2,1,0:T(8,128)S(1)} %get-tuple-element.64), channel_id=1, source_target_pairs={{0,4},{2,6},{4,0},{6,2},{8,12},{10,14},{12,8},{14,10},{16,20},{18,... | collective-permute-start | bytes 393224 | tf_op jit(solution)/shard_map/ppermute | solution.py:364
  83.7 2.4 %collective-permute-done.31 = f32[4,64,128]{2,1,0:T(8,128)S(1)} collective-permute-done((f32[4,64,128]{2,1,0:T(8,128)S(1)}, f32[4,64,128]{2,1,0:T(8,128)S(1)}, u32[]{:S(2)}, u32[]{:S(2)}) %collective-permute-start.31) | collective-permute-done | bytes 131104 | tf_op jit(solution)/shard_map/ppermute | solution.py:364
  86.8 1.3 %collective-permute-done.29 = f32[4,64,128]{2,1,0:T(8,128)S(1)} collective-permute-done((f32[4,64,128]{2,1,0:T(8,128)S(1)}, f32[4,64,128]{2,1,0:T(8,128)S(1)}, u32[]{:S(2)}, u32[]{:S(2)}) %collective-permute-start.29) | collective-permute-done | bytes 131104 | tf_op jit(solution)/shard_map/ppermute | solution.py:364
  88.1 3.1 %collective-permute-start.30 = (f32[4,64,128]{2,1,0:T(8,128)S(1)}, f32[4,64,128]{2,1,0:T(8,128)S(1)}, u32[]{:S(2)}, u32[]{:S(2)}) collective-permute-start(f32[4,64,128]{2,1,0:T(8,128)S(1)} %add.54), channel_id=1, source_target_pairs={{0,16},{2,18},{4,20},{6,22},{8,24},{10,26},{12,28},{14,30},{16,0},... | collective-permute-start | bytes 393224 | tf_op jit(solution)/shard_map/ppermute | solution.py:364
  91.5 5.4 %collective-permute-done.30 = f32[4,64,128]{2,1,0:T(8,128)S(1)} collective-permute-done((f32[4,64,128]{2,1,0:T(8,128)S(1)}, f32[4,64,128]{2,1,0:T(8,128)S(1)}, u32[]{:S(2)}, u32[]{:S(2)}) %collective-permute-start.30) | collective-permute-done | bytes 131104 | tf_op jit(solution)/shard_map/ppermute | solution.py:364
  97.5 2.0 %lowest_carry.1.lowest = f32[32,64,128]{2,1,0:T(8,128)S(1)} custom-call(s32[3,32]{1,0:T(4,128)S(1)} %pad_add_fusion.1.places, f32[4,64,256]{2,1,0:T(8,128)S(1)} %get-tuple-element.72.solved, bf16[2,1024,256]{2,1,0:T(8,128)(2,1)S(1)} %get-tuple-element.53.refs_0_.t0, bf16[2,1024,256]{2,1,0:T(8,128)(2,1)S(1)} %get-tuple-element.54.refs_1_.t1, ...), custom_call_target="tpu_custom_call" | custom-call | tf_op jit(solution)/shard_map/lowest_carry/pallas_call | solution.py:147
  99.5 2.4 %collective-permute-done.33.carried_other = f32[4,64,128]{2,1,0:T(8,128)S(1)} collective-permute-done((f32[4,64,128]{2,1,0:T(8,128)S(1)}, f32[4,64,128]{2,1,0:T(8,128)S(1)}, u32[]{:S(2)}, u32[]{:S(2)}) %collective-permute-start.33) | collective-permute-done | bytes 131104 | tf_op jit(solution)/shard_map/ppermute | solution.py:361
  102.0 3.1 %middle_carry.1 = (f32[2,64,128]{2,1,0:T(8,128)S(1)}, f32[2,64,128]{2,1,0:T(8,128)S(1)}, f32[4,64,128]{2,1,0:T(8,128)S(1)}, f32[4,64,128]{2,1,0:T(8,128)S(1)}, f...) custom-call(s32[2]{0:T(128)S(1)} %pad_add_fusion.3.where, ...), custom_call_target="tpu_custom_call" | custom-call | tf_op jit(solution)/shard_map/middle_carry/pallas_call | solution.py:147
  105.1 1.5 %collective-permute-start.35 = (f32[4,64,128]{2,1,0:T(8,128)S(1)}, f32[4,64,128]{2,1,0:T(8,128)S(1)}, u32[]{:S(2)}, u32[]{:S(2)}) collective-permute-start(f32[4,64,128]{2,1,0:T(8,128)S(1)} %get-tuple-element.76), channel_id=1, source_target_pairs={{0,4},{2,6},{4,0},{6,2},{8,12},{10,14},{12,8},{14,10},{16,20},{18,... | collective-permute-start | bytes 393224 | tf_op jit(solution)/shard_map/ppermute | solution.py:364
  107.2 1.5 %collective-permute-start.39 = (f32[4,64,128]{2,1,0:T(8,128)S(1)}, f32[4,64,128]{2,1,0:T(8,128)S(1)}, u32[]{:S(2)}, u32[]{:S(2)}) collective-permute-start(f32[4,64,128]{2,1,0:T(8,128)S(1)} %get-tuple-element.80), channel_id=1, source_target_pairs={{0,4},{2,6},{4,0},{6,2},{8,12},{10,14},{12,8},{14,10},{16,20},{18,... | collective-permute-start | bytes 393224 | tf_op jit(solution)/shard_map/ppermute | solution.py:364
  109.2 0.9 collective-permute-done.35
  110.1 0.8 collective-permute-start.36
  111.6 1.5 %collective-permute-start.38 = (f32[4,64,128]{2,1,0:T(8,128)S(1)}, f32[4,64,128]{2,1,0:T(8,128)S(1)}, u32[]{:S(2)}, u32[]{:S(2)}) collective-permute-start(f32[4,64,128]{2,1,0:T(8,128)S(1)} %add.59), channel_id=1, source_target_pairs={{0,16},{2,18},{4,20},{6,22},{8,24},{10,26},{12,28},{14,30},{16,0},... | collective-permute-start | bytes 393224 | tf_op jit(solution)/shard_map/ppermute | solution.py:364
  115.2 3.8 %collective-permute-done.38.d = f32[4,64,128]{2,1,0:T(8,128)S(1)} collective-permute-done((f32[4,64,128]{2,1,0:T(8,128)S(1)}, f32[4,64,128]{2,1,0:T(8,128)S(1)}, u32[]{:S(2)}, u32[]{:S(2)}) %collective-permute-start.38) | collective-permute-done | bytes 131104 | tf_op jit(solution)/shard_map/ppermute | solution.py:364
  118.9 1.4 %last_product.1 = (f32[2,64,256]{2,1,0:T(8,128)S(1)}, f32[2,64,256]{2,1,0:T(8,128)S(1)}) custom-call(f32[4,64,128]{2,1,0:T(8,128)S(1)} %constant_dynamic-update-slice_fusion.refs_4_.values, f32[4,64,128]{2,1,0:T(8,128)S(1)} %get-tuple-element.73.a, f32[4,64,128]{2,1,0:T(8,128)S(1)} %collective-permute-done.34.b, ...), custom_call_target="tpu_custom_call" | custom-call | tf_op jit(solution)/shard_map/last_product/pallas_call | solution.py:147
  120.4 1.3 %collective-permute-done.41.partner = f32[2,64,256]{2,1,0:T(8,128)S(1)} collective-permute-done((f32[2,64,256]{2,1,0:T(8,128)S(1)}, f32[2,64,256]{2,1,0:T(8,128)S(1)}, u32[]{:S(2)}, u32[]{:S(2)}) %collective-permute-start.41) | collective-permute-done | bytes 131104 | tf_op jit(solution)/shard_map/ppermute | solution.py:364
  125.1 3.0 %collective-permute-done.42 = f32[2,128,128]{2,1,0:T(8,128)S(1)} collective-permute-done((f32[2,128,128]{2,1,0:T(8,128)S(1)}, f32[2,128,128]{2,1,0:T(8,128)S(1)}, u32[]{:S(2)}, u32[]{:S(2)}) %collective-permute-start.42) | collective-permute-done | bytes 131104 | tf_op jit(solution)/shard_map/ppermute | solution.py:361
  (86 shorter events, 22.2 us)
Async XLA Ops:
  0.0 33.2 %collective-permute-start.6 = (f32[2,2,8,128,256]{4,3,2,1,0:T(8,128)}, f32[2,2,8,128,256]{4,3,2,1,0:T(8,128)}, u32[]{:S(2)}, u32[]{:S(2)}) collective-permute-start(f32[2,2,8,128,256]{4,3,2,1,0:T(8,128)} %own.3), channel_id=1, source_target_pairs={{0,2},{2,0},{4,6},{6,4},{8,10},{10,8},{12,14},{14,12},{16,18},{18,... | collective-permute-start | bytes 12582920 | tf_op jit(solution)/shard_map/ppermute | solution.py:364
  0.5 9.8 %collective-permute-start.3 = (s32[2,2,8]{2,1,0:T(2,128)}, s32[2,2,8]{2,1,0:T(2,128)S(1)}, u32[]{:S(2)}, u32[]{:S(2)}) collective-permute-start(s32[2,2,8]{2,1,0:T(2,128)} %param.8), channel_id=1, source_target_pairs={{0,2},{2,0},{4,6},{6,4},{8,10},{10,8},{12,14},{14,12},{16,18},{18,... | collective-permute-start | bytes 392 | tf_op jit(solution)/shard_map/ppermute | solution.py:364
  0.5 6.9 %collective-permute-start.2 = (s32[2,2]{1,0:T(2,128)}, s32[2,2]{1,0:T(2,128)S(1)}, u32[]{:S(2)}, u32[]{:S(2)}) collective-permute-start(s32[2,2]{1,0:T(2,128)} %param.9), channel_id=1, source_target_pairs={{0,2},{2,0},{4,6},{6,4},{8,10},{10,8},{12,14},{14,12},{16,18},{18,... | collective-permute-start | bytes 56 | tf_op jit(solution)/shard_map/ppermute | solution.py:364
  1.9 9.8 %collective-permute-start = (f32[2,128,128]{2,1,0:T(8,128)S(1)}, f32[2,128,128]{2,1,0:T(8,128)S(1)}, u32[]{:S(2)}, u32[]{:S(2)}) collective-permute-start(f32[2,128,128]{2,1,0:T(8,128)S(1)} %slice_bitcast_fusion.rhs_own), channel_id=1, source_target_pairs={{0,1},{1,0},{2,3},{3,2},{4,5},{5,4},{6,7},{7,6},{8,9},{9,8},{10,11... | collective-permute-start | bytes 393224 | tf_op jit(solution)/shard_map/ppermute | solution.py:361
  7.3 10.9 %collective-permute-start.4 = (f32[2,2,128,128]{3,2,1,0:T(8,128)S(1)}, f32[2,2,128,128]{3,2,1,0:T(8,128)S(1)}, u32[]{:S(2)}, u32[]{:S(2)}) collective-permute-start(f32[2,2,128,128]{3,2,1,0:T(8,128)S(1)} %slice.27.rhs_own), channel_id=1, source_target_pairs={{0,1},{1,0},{2,3},{3,2},{4,5},{5,4},{6,7},{7,6},{8,9},{9,8},{10,11... | collective-permute-start | bytes 786440 | tf_op jit(solution)/shard_map/ppermute | solution.py:361
  7.4 24.3 %collective-permute-start.16 = (f32[2,2,128,256]{3,2,1,0:T(8,128)}, f32[2,2,128,256]{3,2,1,0:T(8,128)S(1)}, u32[]{:S(2)}, u32[]{:S(2)}) collective-permute-start(f32[2,2,128,256]{3,2,1,0:T(8,128)} %slice.28), channel_id=1, source_target_pairs={{0,1},{1,0},{2,3},{3,2},{4,5},{5,4},{6,7},{7,6},{8,9},{9,8},{10,11... | collective-permute-start | bytes 1572872 | tf_op jit(solution)/shard_map/ppermute | solution.py:361
  13.2 1.3 %collective-permute-start.1 = (f32[2,64,128]{2,1,0:T(8,128)S(1)}, f32[2,64,128]{2,1,0:T(8,128)S(1)}, u32[]{:S(2)}, u32[]{:S(2)}) collective-permute-start(f32[2,64,128]{2,1,0:T(8,128)S(1)} %get-tuple-element.49), channel_id=1, source_target_pairs={{0,2},{2,0},{4,6},{6,4},{8,10},{10,8},{12,14},{14,12},{16,18},{18,... | collective-permute-start | bytes 196616 | tf_op jit(solution)/shard_map/ppermute | solution.py:364
  14.5 5.6 %collective-permute-start.7 = (f32[4,64,128]{2,1,0:T(8,128)S(1)}, f32[4,64,128]{2,1,0:T(8,128)S(1)}, u32[]{:S(2)}, u32[]{:S(2)}) collective-permute-start(f32[4,64,128]{2,1,0:T(8,128)S(1)} %constant_dynamic-update-slice_fusion.refs_4_.values), channel_id=1, source_target_pairs={{0,4},{2,6},{4,0},{6,2},{8,12},{10,14},{12,8},{14,10},{16,20},{18,... | collective-permute-start | bytes 393224 | tf_op jit(solution)/shard_map/ppermute | solution.py:364
  16.0 6.7 %collective-permute-start.8 = (f32[4,64,128]{2,1,0:T(8,128)S(1)}, f32[4,64,128]{2,1,0:T(8,128)S(1)}, u32[]{:S(2)}, u32[]{:S(2)}) collective-permute-start(f32[4,64,128]{2,1,0:T(8,128)S(1)} %constant_dynamic-update-slice_fusion.refs_4_.values), channel_id=1, source_target_pairs={{0,8},{2,10},{4,12},{6,14},{8,0},{10,2},{12,4},{14,6},{16,24},{18,... | collective-permute-start | bytes 393224 | tf_op jit(solution)/shard_map/ppermute | solution.py:364
  18.3 22.6 %collective-permute-start.15 = (f32[3,2,128,256]{3,2,1,0:T(8,128)}, f32[3,2,128,256]{3,2,1,0:T(8,128)S(1)}, u32[]{:S(2)}, u32[]{:S(2)}) collective-permute-start(f32[3,2,128,256]{3,2,1,0:T(8,128)} %d_own.1), channel_id=1, source_target_pairs={{0,2},{2,0},{4,6},{6,4},{8,10},{10,8},{12,14},{14,12},{16,18},{18,... | collective-permute-start | bytes 2359304 | tf_op jit(solution)/shard_map/ppermute | solution.py:364
  20.0 9.6 %collective-permute-start.10 = (f32[4,64,128]{2,1,0:T(8,128)S(1)}, f32[4,64,128]{2,1,0:T(8,128)S(1)}, u32[]{:S(2)}, u32[]{:S(2)}) collective-permute-start(f32[4,64,128]{2,1,0:T(8,128)S(1)} %constant_dynamic-update-slice_fusion.refs_4_.values), channel_id=1, source_target_pairs={{0,16},{2,18},{4,20},{6,22},{8,24},{10,26},{12,28},{14,30},{16,0},... | collective-permute-start | bytes 393224 | tf_op jit(solution)/shard_map/ppermute | solution.py:364
  22.6 8.5 %collective-permute-start.12 = (f32[4,64,128]{2,1,0:T(8,128)S(1)}, f32[4,64,128]{2,1,0:T(8,128)S(1)}, u32[]{:S(2)}, u32[]{:S(2)}) collective-permute-start(f32[4,64,128]{2,1,0:T(8,128)S(1)} %constant_dynamic-update-slice_fusion.refs_4_.values), channel_id=1, source_target_pairs={{0,0},{2,2},{4,4},{6,6},{8,16},{10,18},{12,20},{14,22},{16,8},{18,... | collective-permute-start | bytes 393224 | tf_op jit(solution)/shard_map/ppermute | solution.py:375
  29.7 8.6 %collective-permute-start.9 = (f32[4,64,128]{2,1,0:T(8,128)S(1)}, f32[4,64,128]{2,1,0:T(8,128)S(1)}, u32[]{:S(2)}, u32[]{:S(2)}) collective-permute-start(f32[4,64,128]{2,1,0:T(8,128)S(1)} %collective-permute-done.8.refs_6_), channel_id=1, source_target_pairs={{0,4},{2,6},{4,0},{6,2},{8,12},{10,14},{12,8},{14,10},{16,20},{18,... | collective-permute-start | bytes 393224 | tf_op jit(solution)/shard_map/ppermute | solution.py:364
  31.1 7.7 %collective-permute-start.11 = (f32[4,64,128]{2,1,0:T(8,128)S(1)}, f32[4,64,128]{2,1,0:T(8,128)S(1)}, u32[]{:S(2)}, u32[]{:S(2)}) collective-permute-start(f32[4,64,128]{2,1,0:T(8,128)S(1)} %collective-permute-done.10.refs_8_), channel_id=1, source_target_pairs={{0,4},{2,6},{4,0},{6,2},{8,12},{10,14},{12,8},{14,10},{16,20},{18,... | collective-permute-start | bytes 393224 | tf_op jit(solution)/shard_map/ppermute | solution.py:364
  31.7 7.1 %collective-permute-start.13 = (f32[4,64,128]{2,1,0:T(8,128)S(1)}, f32[4,64,128]{2,1,0:T(8,128)S(1)}, u32[]{:S(2)}, u32[]{:S(2)}) collective-permute-start(f32[4,64,128]{2,1,0:T(8,128)S(1)} %collective-permute-done.12.refs_10_), channel_id=1, source_target_pairs={{0,4},{2,6},{4,0},{6,2},{8,12},{10,14},{12,8},{14,10},{16,20},{18,... | collective-permute-start | bytes 393224 | tf_op jit(solution)/shard_map/ppermute | solution.py:364
  33.2 7.6 %collective-permute-start.17 = (f32[2,2,128,256]{3,2,1,0:T(8,128)S(1)}, f32[2,2,128,256]{3,2,1,0:T(8,128)S(1)}, u32[]{:S(2)}, u32[]{:S(2)}) collective-permute-start(f32[2,2,128,256]{3,2,1,0:T(8,128)S(1)} %collective-permute-done.16.d2), channel_id=1, source_target_pairs={{0,2},{2,0},{4,6},{6,4},{8,10},{10,8},{12,14},{14,12},{16,18},{18,... | collective-permute-start | bytes 1572872 | tf_op jit(solution)/shard_map/ppermute | solution.py:364
  34.2 2.2 %copy-start = (f32[2,2,8,128,256]{4,3,2,1,0:T(8,128)S(1)}, f32[2,2,8,128,256]{4,3,2,1,0:T(8,128)}, u32[]{:S(2)}) copy-start(f32[2,2,8,128,256]{4,3,2,1,0:T(8,128)} %own.3) | copy-start | bytes 12582916
  38.3 2.6 %collective-permute-start.5 = (f32[2,2,64,256]{3,2,1,0:T(8,128)S(1)}, f32[2,2,64,256]{3,2,1,0:T(8,128)S(1)}, u32[]{:S(2)}, u32[]{:S(2)}) collective-permute-start(f32[2,2,64,256]{3,2,1,0:T(8,128)S(1)} %get-tuple-element.52), channel_id=1, source_target_pairs={{0,2},{2,0},{4,6},{6,4},{8,10},{10,8},{12,14},{14,12},{16,18},{18,... | collective-permute-start | bytes 786440 | tf_op jit(solution)/shard_map/ppermute | solution.py:364
  38.8 23.3 %copy-start.1 = (f32[2,2,8,128,256]{4,3,2,1,0:T(8,128)S(1)}, f32[2,2,8,128,256]{4,3,2,1,0:T(8,128)}, u32[]{:S(2)}) copy-start(f32[2,2,8,128,256]{4,3,2,1,0:T(8,128)} %own.3) | copy-start | bytes 12582916
  40.2 8.3 %collective-permute-start.14 = (f32[4,64,256]{2,1,0:T(8,128)S(1)}, f32[4,64,256]{2,1,0:T(8,128)S(1)}, u32[]{:S(2)}, u32[]{:S(2)}) collective-permute-start(f32[4,64,256]{2,1,0:T(8,128)S(1)} %update_middle.1.mine), channel_id=1, source_target_pairs={{0,1},{1,0},{2,3},{3,2},{4,5},{5,4},{6,7},{7,6},{8,9},{9,8},{10,11... | collective-permute-start | bytes 786440 | tf_op jit(solution)/shard_map/ppermute | solution.py:361
  50.2 6.3 %collective-permute-start.19 = (f32[4,64,128]{2,1,0:T(8,128)S(1)}, f32[4,64,128]{2,1,0:T(8,128)S(1)}, u32[]{:S(2)}, u32[]{:S(2)}) collective-permute-start(f32[4,64,128]{2,1,0:T(8,128)S(1)} %get-tuple-element.62.refs_5_.values_own), channel_id=1, source_target_pairs={{0,8},{2,10},{4,12},{6,14},{8,0},{10,2},{12,4},{14,6},{16,24},{18,... | collective-permute-start | bytes 393224 | tf_op jit(solution)/shard_map/ppermute | solution.py:364
  51.0 9.1 %collective-permute-start.21 = (f32[4,64,128]{2,1,0:T(8,128)S(1)}, f32[4,64,128]{2,1,0:T(8,128)S(1)}, u32[]{:S(2)}, u32[]{:S(2)}) collective-permute-start(f32[4,64,128]{2,1,0:T(8,128)S(1)} %get-tuple-element.62.refs_5_.values_own), channel_id=1, source_target_pairs={{0,16},{2,18},{4,20},{6,22},{8,24},{10,26},{12,28},{14,30},{16,0},... | collective-permute-start | bytes 393224 | tf_op jit(solution)/shard_map/ppermute | solution.py:364
  53.5 8.1 %collective-permute-start.23 = (f32[4,64,128]{2,1,0:T(8,128)S(1)}, f32[4,64,128]{2,1,0:T(8,128)S(1)}, u32[]{:S(2)}, u32[]{:S(2)}) collective-permute-start(f32[4,64,128]{2,1,0:T(8,128)S(1)} %get-tuple-element.62.refs_5_.values_own), channel_id=1, source_target_pairs={{0,0},{2,2},{4,4},{6,6},{8,16},{10,18},{12,20},{14,22},{16,8},{18,... | collective-permute-start | bytes 393224 | tf_op jit(solution)/shard_map/ppermute | solution.py:375
  54.2 11.3 %collective-permute-start.18 = (f32[4,64,128]{2,1,0:T(8,128)S(1)}, f32[4,64,128]{2,1,0:T(8,128)S(1)}, u32[]{:S(2)}, u32[]{:S(2)}) collective-permute-start(f32[4,64,128]{2,1,0:T(8,128)S(1)} %get-tuple-element.62.refs_5_.values_own), channel_id=1, source_target_pairs={{0,4},{2,6},{4,0},{6,2},{8,12},{10,14},{12,8},{14,10},{16,20},{18,... | collective-permute-start | bytes 393224 | tf_op jit(solution)/shard_map/ppermute | solution.py:364
  56.4 9.0 %collective-permute-start.20 = (f32[4,64,128]{2,1,0:T(8,128)S(1)}, f32[4,64,128]{2,1,0:T(8,128)S(1)}, u32[]{:S(2)}, u32[]{:S(2)}) collective-permute-start(f32[4,64,128]{2,1,0:T(8,128)S(1)} %collective-permute-done.19.refs_7_), channel_id=1, source_target_pairs={{0,4},{2,6},{4,0},{6,2},{8,12},{10,14},{12,8},{14,10},{16,20},{18,... | collective-permute-start | bytes 393224 | tf_op jit(solution)/shard_map/ppermute | solution.py:364
  60.1 6.1 %collective-permute-start.22 = (f32[4,64,128]{2,1,0:T(8,128)S(1)}, f32[4,64,128]{2,1,0:T(8,128)S(1)}, u32[]{:S(2)}, u32[]{:S(2)}) collective-permute-start(f32[4,64,128]{2,1,0:T(8,128)S(1)} %collective-permute-done.21.refs_9_), channel_id=1, source_target_pairs={{0,4},{2,6},{4,0},{6,2},{8,12},{10,14},{12,8},{14,10},{16,20},{18,... | collective-permute-start | bytes 393224 | tf_op jit(solution)/shard_map/ppermute | solution.py:364
  61.6 6.0 %collective-permute-start.24 = (f32[4,64,128]{2,1,0:T(8,128)S(1)}, f32[4,64,128]{2,1,0:T(8,128)S(1)}, u32[]{:S(2)}, u32[]{:S(2)}) collective-permute-start(f32[4,64,128]{2,1,0:T(8,128)S(1)} %collective-permute-done.23.refs_11_), channel_id=1, source_target_pairs={{0,4},{2,6},{4,0},{6,2},{8,12},{10,14},{12,8},{14,10},{16,20},{18,... | collective-permute-start | bytes 393224 | tf_op jit(solution)/shard_map/ppermute | solution.py:364
  69.1 6.6 %collective-permute-start.25 = (f32[4,64,256]{2,1,0:T(8,128)S(1)}, f32[4,64,256]{2,1,0:T(8,128)S(1)}, u32[]{:S(2)}, u32[]{:S(2)}) collective-permute-start(f32[4,64,256]{2,1,0:T(8,128)S(1)} %update_top.1.mine), channel_id=1, source_target_pairs={{0,1},{1,0},{2,3},{3,2},{4,5},{5,4},{6,7},{7,6},{8,9},{9,8},{10,11... | collective-permute-start | bytes 786440 | tf_op jit(solution)/shard_map/ppermute | solution.py:361
  79.6 6.5 %collective-permute-start.31 = (f32[4,64,128]{2,1,0:T(8,128)S(1)}, f32[4,64,128]{2,1,0:T(8,128)S(1)}, u32[]{:S(2)}, u32[]{:S(2)}) collective-permute-start(f32[4,64,128]{2,1,0:T(8,128)S(1)} %get-tuple-element.70), channel_id=1, source_target_pairs={{0,4},{2,6},{4,0},{6,2},{8,12},{10,14},{12,8},{14,10},{16,20},{18,... | collective-permute-start | bytes 393224 | tf_op jit(solution)/shard_map/ppermute | solution.py:364
  79.9 8.2 %collective-permute-start.29 = (f32[4,64,128]{2,1,0:T(8,128)S(1)}, f32[4,64,128]{2,1,0:T(8,128)S(1)}, u32[]{:S(2)}, u32[]{:S(2)}) collective-permute-start(f32[4,64,128]{2,1,0:T(8,128)S(1)} %get-tuple-element.68), channel_id=1, source_target_pairs={{0,4},{2,6},{4,0},{6,2},{8,12},{10,14},{12,8},{14,10},{16,20},{18,... | collective-permute-start | bytes 393224 | tf_op jit(solution)/shard_map/ppermute | solution.py:364
  81.7 9.6 %collective-permute-start.27 = (f32[4,64,128]{2,1,0:T(8,128)S(1)}, f32[4,64,128]{2,1,0:T(8,128)S(1)}, u32[]{:S(2)}, u32[]{:S(2)}) collective-permute-start(f32[4,64,128]{2,1,0:T(8,128)S(1)} %get-tuple-element.66), channel_id=1, source_target_pairs={{0,4},{2,6},{4,0},{6,2},{8,12},{10,14},{12,8},{14,10},{16,20},{18,... | collective-permute-start | bytes 393224 | tf_op jit(solution)/shard_map/ppermute | solution.py:364
  81.9 9.6 %collective-permute-start.26 = (f32[4,64,128]{2,1,0:T(8,128)S(1)}, f32[4,64,128]{2,1,0:T(8,128)S(1)}, u32[]{:S(2)}, u32[]{:S(2)}) collective-permute-start(f32[4,64,128]{2,1,0:T(8,128)S(1)} %get-tuple-element.64), channel_id=1, source_target_pairs={{0,4},{2,6},{4,0},{6,2},{8,12},{10,14},{12,8},{14,10},{16,20},{18,... | collective-permute-start | bytes 393224 | tf_op jit(solution)/shard_map/ppermute | solution.py:364
  86.1 5.4 %collective-permute-start.32 = (f32[4,64,128]{2,1,0:T(8,128)S(1)}, f32[4,64,128]{2,1,0:T(8,128)S(1)}, u32[]{:S(2)}, u32[]{:S(2)}) collective-permute-start(f32[4,64,128]{2,1,0:T(8,128)S(1)} %add.56), channel_id=1, source_target_pairs={{0,0},{2,2},{4,4},{6,6},{8,16},{10,18},{12,20},{14,22},{16,8},{18,... | collective-permute-start | bytes 393224 | tf_op jit(solution)/shard_map/ppermute | solution.py:375
  88.1 8.8 %collective-permute-start.30 = (f32[4,64,128]{2,1,0:T(8,128)S(1)}, f32[4,64,128]{2,1,0:T(8,128)S(1)}, u32[]{:S(2)}, u32[]{:S(2)}) collective-permute-start(f32[4,64,128]{2,1,0:T(8,128)S(1)} %add.54), channel_id=1, source_target_pairs={{0,16},{2,18},{4,20},{6,22},{8,24},{10,26},{12,28},{14,30},{16,0},... | collective-permute-start | bytes 393224 | tf_op jit(solution)/shard_map/ppermute | solution.py:364
  91.3 5.6 %collective-permute-start.28 = (f32[4,64,128]{2,1,0:T(8,128)S(1)}, f32[4,64,128]{2,1,0:T(8,128)S(1)}, u32[]{:S(2)}, u32[]{:S(2)}) collective-permute-start(f32[4,64,128]{2,1,0:T(8,128)S(1)} %add.52), channel_id=1, source_target_pairs={{0,8},{2,10},{4,12},{6,14},{8,0},{10,2},{12,4},{14,6},{16,24},{18,... | collective-permute-start | bytes 393224 | tf_op jit(solution)/shard_map/ppermute | solution.py:364
  96.9 5.0 %collective-permute-start.33 = (f32[4,64,128]{2,1,0:T(8,128)S(1)}, f32[4,64,128]{2,1,0:T(8,128)S(1)}, u32[]{:S(2)}, u32[]{:S(2)}) collective-permute-start(f32[4,64,128]{2,1,0:T(8,128)S(1)} %add_add_fusion.carried_own), channel_id=1, source_target_pairs={{0,1},{1,0},{2,3},{3,2},{4,5},{5,4},{6,7},{7,6},{8,9},{9,8},{10,11... | collective-permute-start | bytes 393224 | tf_op jit(solution)/shard_map/ppermute | solution.py:361
  105.1 5.0 %collective-permute-start.35 = (f32[4,64,128]{2,1,0:T(8,128)S(1)}, f32[4,64,128]{2,1,0:T(8,128)S(1)}, u32[]{:S(2)}, u32[]{:S(2)}) collective-permute-start(f32[4,64,128]{2,1,0:T(8,128)S(1)} %get-tuple-element.76), channel_id=1, source_target_pairs={{0,4},{2,6},{4,0},{6,2},{8,12},{10,14},{12,8},{14,10},{16,20},{18,... | collective-permute-start | bytes 393224 | tf_op jit(solution)/shard_map/ppermute | solution.py:364
  106.6 5.0 %collective-permute-start.37 = (f32[4,64,128]{2,1,0:T(8,128)S(1)}, f32[4,64,128]{2,1,0:T(8,128)S(1)}, u32[]{:S(2)}, u32[]{:S(2)}) collective-permute-start(f32[4,64,128]{2,1,0:T(8,128)S(1)} %get-tuple-element.78), channel_id=1, source_target_pairs={{0,4},{2,6},{4,0},{6,2},{8,12},{10,14},{12,8},{14,10},{16,20},{18,... | collective-permute-start | bytes 393224 | tf_op jit(solution)/shard_map/ppermute | solution.py:364
  107.2 5.9 %collective-permute-start.39 = (f32[4,64,128]{2,1,0:T(8,128)S(1)}, f32[4,64,128]{2,1,0:T(8,128)S(1)}, u32[]{:S(2)}, u32[]{:S(2)}) collective-permute-start(f32[4,64,128]{2,1,0:T(8,128)S(1)} %get-tuple-element.80), channel_id=1, source_target_pairs={{0,4},{2,6},{4,0},{6,2},{8,12},{10,14},{12,8},{14,10},{16,20},{18,... | collective-permute-start | bytes 393224 | tf_op jit(solution)/shard_map/ppermute | solution.py:364
  108.6 5.8 %collective-permute-start.34 = (f32[4,64,128]{2,1,0:T(8,128)S(1)}, f32[4,64,128]{2,1,0:T(8,128)S(1)}, u32[]{:S(2)}, u32[]{:S(2)}) collective-permute-start(f32[4,64,128]{2,1,0:T(8,128)S(1)} %get-tuple-element.74), channel_id=1, source_target_pairs={{0,4},{2,6},{4,0},{6,2},{8,12},{10,14},{12,8},{14,10},{16,20},{18,... | collective-permute-start | bytes 393224 | tf_op jit(solution)/shard_map/ppermute | solution.py:364
  110.1 5.0 %collective-permute-start.36 = (f32[4,64,128]{2,1,0:T(8,128)S(1)}, f32[4,64,128]{2,1,0:T(8,128)S(1)}, u32[]{:S(2)}, u32[]{:S(2)}) collective-permute-start(f32[4,64,128]{2,1,0:T(8,128)S(1)} %add.58), channel_id=1, source_target_pairs={{0,8},{2,10},{4,12},{6,14},{8,0},{10,2},{12,4},{14,6},{16,24},{18,... | collective-permute-start | bytes 393224 | tf_op jit(solution)/shard_map/ppermute | solution.py:364
  111.6 7.3 %collective-permute-start.38 = (f32[4,64,128]{2,1,0:T(8,128)S(1)}, f32[4,64,128]{2,1,0:T(8,128)S(1)}, u32[]{:S(2)}, u32[]{:S(2)}) collective-permute-start(f32[4,64,128]{2,1,0:T(8,128)S(1)} %add.59), channel_id=1, source_target_pairs={{0,16},{2,18},{4,20},{6,22},{8,24},{10,26},{12,28},{14,30},{16,0},... | collective-permute-start | bytes 393224 | tf_op jit(solution)/shard_map/ppermute | solution.py:364
  113.1 5.8 %collective-permute-start.40 = (f32[4,64,128]{2,1,0:T(8,128)S(1)}, f32[4,64,128]{2,1,0:T(8,128)S(1)}, u32[]{:S(2)}, u32[]{:S(2)}) collective-permute-start(f32[4,64,128]{2,1,0:T(8,128)S(1)} %add.60), channel_id=1, source_target_pairs={{0,0},{2,2},{4,4},{6,6},{8,16},{10,18},{12,20},{14,22},{16,8},{18,... | collective-permute-start | bytes 393224 | tf_op jit(solution)/shard_map/ppermute | solution.py:375
  120.4 1.4 %collective-permute-start.41 = (f32[2,64,256]{2,1,0:T(8,128)S(1)}, f32[2,64,256]{2,1,0:T(8,128)S(1)}, u32[]{:S(2)}, u32[]{:S(2)}) collective-permute-start(f32[2,64,256]{2,1,0:T(8,128)S(1)} %get-tuple-element.82), channel_id=1, source_target_pairs={{0,2},{2,0},{4,6},{6,4},{8,10},{10,8},{12,14},{14,12},{16,18},{18,... | collective-permute-start | bytes 393224 | tf_op jit(solution)/shard_map/ppermute | solution.py:364
  122.5 5.6 %collective-permute-start.42 = (f32[2,128,128]{2,1,0:T(8,128)S(1)}, f32[2,128,128]{2,1,0:T(8,128)S(1)}, u32[]{:S(2)}, u32[]{:S(2)}) collective-permute-start(f32[2,128,128]{2,1,0:T(8,128)S(1)} %get-tuple-element.84), channel_id=1, source_target_pairs={{0,1},{1,0},{2,3},{3,2},{4,5},{5,4},{6,7},{7,6},{8,9},{9,8},{10,11... | collective-permute-start | bytes 393224 | tf_op jit(solution)/shard_map/ppermute | solution.py:361
  123.0 1.3 collective-permute-start.43
  123.0 1.4 %collective-permute-start.44 = (f32[2,64,128]{2,1,0:T(8,128)S(1)}, f32[2,64,128]{2,1,0:T(8,128)S(1)}, u32[]{:S(2)}, u32[]{:S(2)}) collective-permute-start(f32[2,64,128]{2,1,0:T(8,128)S(1)} %get-tuple-element.88), channel_id=1, source_target_pairs={{0,2},{2,0},{4,6},{6,4},{8,10},{10,8},{12,14},{14,12},{16,18},{18,... | collective-permute-start | bytes 196616 | tf_op jit(solution)/shard_map/ppermute | solution.py:364

commit v3 on v2

v3 whole, which is shorter than its diff:
```python
import functools

import jax
import jax.numpy as jnp
from jax import lax
from jax.experimental import pallas as pl
from jax.experimental.pallas import tpu as pltpu
from jax.sharding import PartitionSpec as P

KDEV = 7


def from_behind(value, axis, steps):
    count = lax.axis_size(axis)
    leading, last = (max(0, -steps), min(count, count - steps))
    return lax.ppermute(value, axis, [(source, source + steps) for source in range(leading, last)])


def local_any(rhs, diag_inv, factor_tiles, tile_source, tile_count):
    levels = rhs.shape[0]
    owned_count = rhs.shape[1]
    share_rows = rhs.shape[2]
    columns = rhs.shape[3]
    slot_count = tile_source.shape[2]
    reach_dev = KDEV
    window_len = 2 * reach_dev + 1
    total_sup = lax.axis_size("rows") * owned_count
    row_place = lax.axis_index("rows")
    highest = lax.Precision.HIGHEST
    slot_ids = jnp.arange(slot_count, dtype=jnp.int32)

    def window_places(sources):
        src_level = sources // total_sup
        within = sources % total_sup
        return (
            src_level * window_len + within // owned_count - row_place + reach_dev
        ) * owned_count + within % owned_count

    def live_mask(counts):
        return (slot_ids[None, :] < counts[:, None]).astype(jnp.float32)

    def full_rows(piece):
        return lax.all_gather(piece, "cols", axis=1, tiled=True)

    forward_values = []
    windows = []
    for height in range(levels):
        if height == 0:
            whole_block = full_rows(rhs[0])
        else:
            stacked = jnp.stack(windows, 0).reshape(
                height * window_len * owned_count, share_rows, columns
            )
            places = window_places(tile_source[height - 1])
            picked = (
                jnp.take(stacked, places, axis=0)
                * live_mask(tile_count[height - 1])[:, :, None, None]
            )
            partial_value = jnp.einsum(
                "skci,skcr->sir", factor_tiles[height - 1], picked, precision=highest
            )
            whole_block = full_rows(
                rhs[height]
                - lax.psum_scatter(partial_value, "cols", scatter_dimension=1, tiled=True)
            )
        values = jnp.einsum("sci,sir->scr", diag_inv[height], whole_block, precision=highest)
        forward_values.append(values)
        if height + 1 < levels:
            pieces = []
            for pull_offset in range(-reach_dev, reach_dev + 1):
                if pull_offset == 0:
                    pieces.append(values)
                else:
                    pieces.append(from_behind(values, "rows", -pull_offset))
            windows.append(jnp.stack(pieces, 0))
    carried = [jnp.zeros_like(forward_values[0]) for height in range(levels)]
    solution = [None] * levels
    for height in reversed(range(levels)):
        partial_value = jnp.einsum(
            "sci,scr->sir",
            diag_inv[height],
            forward_values[height] - carried[height],
            precision=highest,
        )
        own_share = lax.psum_scatter(partial_value, "cols", scatter_dimension=1, tiled=True)
        if height > 0:
            whole_block = lax.all_gather(own_share, "cols", axis=1, tiled=True)
        solution[height] = own_share
        if height > 0:
            term_set = jnp.einsum(
                "skci,sir->skcr", factor_tiles[height - 1], whole_block, precision=highest
            )
            term_set = term_set * live_mask(tile_count[height - 1])[:, :, None, None]
            places = window_places(tile_source[height - 1]).reshape(-1)
            targets = height * window_len * owned_count
            one_hot = (jnp.arange(targets, dtype=jnp.int32)[:, None] == places[None, :]).astype(
                jnp.float32
            )
            outgoing = jnp.einsum(
                "ms,slg->mlg",
                one_hot,
                term_set.reshape(owned_count * slot_count, share_rows, columns),
                precision=highest,
            )
            push_outgoing = outgoing.reshape(height, window_len, owned_count, share_rows, columns)
            received = push_outgoing[:, reach_dev]
            for offset in range(-reach_dev, reach_dev + 1):
                if offset != 0:
                    received = received + from_behind(
                        push_outgoing[:, reach_dev + offset], "rows", offset
                    )
            for lower_level in range(height):
                carried[lower_level] = carried[lower_level] + received[lower_level]
    return jnp.stack(solution, 0)


F32 = jnp.float32
BF16 = jnp.bfloat16
NN = (((1,), (0,)), ((), ()))
NT = (((1,), (1,)), ((), ()))
PIECES = 8


def halves(value):
    high = value.astype(BF16)
    return high, (value - high.astype(F32)).astype(BF16)


def dot3(left, right, dims):
    left_high, left_low = halves(left)
    right_high, right_low = right if isinstance(right, tuple) else halves(right)
    dot = functools.partial(lax.dot_general, dimension_numbers=dims, preferred_element_type=F32)
    rows = left.shape[0]
    both = dot(jnp.concatenate([left_high, left_low], 0), right_high)
    return both[:rows] + both[rows:] + dot(left_high, right_low)


def ordered(mine, theirs, place, axis):
    first = jnp.where(place == 0, mine, theirs)
    second = jnp.where(place == 0, theirs, mine)
    return jnp.concatenate([first, second], axis)


VMEM_LIMIT = 20 * 1024 * 1024


def options(cost):
    return dict(
        cost_estimate=pl.CostEstimate(flops=cost * 1000000, bytes_accessed=0, transcendentals=0),
        compiler_params=pltpu.CompilerParams(vmem_limit_bytes=VMEM_LIMIT),
    )


def call(kernel, name, outs, args, scalars=1, scratch=(), cost=1000):
    in_specs = [pl.BlockSpec(memory_space=pltpu.SMEM)] * scalars
    in_specs += [pl.BlockSpec(memory_space=pltpu.VMEM)] * (len(args) - scalars)
    return pl.pallas_call(
        kernel,
        out_shape=[jax.ShapeDtypeStruct(shape, F32) for shape in outs],
        in_specs=in_specs,
        out_specs=[pl.BlockSpec(memory_space=pltpu.VMEM)] * len(outs),
        scratch_shapes=list(scratch),
        name=name,
        **options(cost),
    )(*args)


def prepare(kernel, name, level, own, partner, diags, outs, cost):
    own = pltpu.with_memory_space_constraint(own, pltpu.HBM)
    owned, slots, depth, width = own.shape[1:]
    block_in = pl.BlockSpec((1, 1, slots, depth, width), lambda s: (level, s, 0, 0, 0))
    diag_in = [pl.BlockSpec((1, 1) + d.shape[2:], lambda s, at=at: (at, s, 0, 0))
               for d, at in zip(diags, (level + 1, level + 1, level, level))]
    return pl.pallas_call(
        kernel,
        grid=(owned,),
        out_shape=[jax.ShapeDtypeStruct((owned,) + shape, kind) for shape, kind in outs * 2],
        in_specs=[block_in] * 2 + diag_in,
        out_specs=[pl.BlockSpec((1,) + shape, lambda s: (s, 0, 0)) for shape, _ in outs * 2],
        name=name,
        **options(cost),
    )(own, partner, *diags)


def put_halves(value, high_out, low_out):
    high, low = halves(value)
    high_out[0] = high
    low_out[0] = low


def flat(tiles):
    return tiles[0, 0].reshape(-1, tiles.shape[-1])


def split_tiles(own, partner, *outs):
    put_halves(flat(own), *outs[:2])
    put_halves(flat(partner), *outs[2:])


def both(diag, diag_other):
    return jnp.concatenate([diag[0, 0], diag_other[0, 0]], 0)


def diag_by_tiles(own, partner, d0, d1, d2, d3, *outs):
    put_halves(dot3(both(d0, d2), flat(own), NT), *outs[:2])
    put_halves(dot3(both(d1, d3), flat(partner), NT), *outs[2:])


def gram_by_tiles(own, partner, d0, d1, d2, d3, *outs):
    for tiles, diag, out in ((own, both(d0, d2), outs[:3]), (partner, both(d1, d3), outs[3:])):
        gram = dot3(diag.T, diag, NN)
        put_halves(dot3(gram, flat(tiles), NT), *out[:2])
        out[2][0] = gram


def part_of(parts, s):
    count = len(parts) // 2
    half = parts[0].shape[0]
    chosen = parts[:count] if s < half else parts[count:]
    return tuple(part[s % half] for part in chosen)


def first_values(rhs_own, rhs_other, diag, mine, partner):
    core, col = lax.axis_index("rows") % 2, lax.axis_index("cols")
    half = mine.shape[1]
    for s in range(rhs_own.shape[0]):
        rows = ordered(rhs_own[s], rhs_other[s], col, 0)
        values = dot3(diag[0, s], rows, NN).T
        low, high = values[:half], values[half:]
        mine[s] = jnp.where(core == 0, low, high)
        partner[s] = jnp.where(core == 0, high, low)


def first_call(rhs_own, rhs_other, diag):
    owned, depth, columns = rhs_own.shape
    whole = pl.BlockSpec((owned, depth, columns), lambda i: (0, 0, 0))
    half = pl.BlockSpec((owned, columns // 2, depth), lambda i: (0, 0, 0))
    return pl.pallas_call(
        first_values,
        grid=(1,),
        out_shape=[jax.ShapeDtypeStruct((owned, columns // 2, depth), F32)] * 2,
        in_specs=[
            whole, whole,
            pl.BlockSpec((1,) + diag.shape[1:], lambda i: (0, 0, 0, 0)),
        ],
        out_specs=[half, half],
        name="first_values",
        **options(500),
    )(rhs_own, rhs_other, pltpu.with_memory_space_constraint(diag, pltpu.HBM))


def slot_places(sources, counts, places):
    row = lax.axis_index("rows")
    levels, owned, slots = sources.shape
    total = lax.axis_size("rows") * owned
    for l in range(levels):
        for s in range(owned):
            for k in range(slots):
                source = sources[l, s, k]
                live = k < counts[l, s]
                lower = jnp.where(source >= total, 1, 0)
                within = source - lower * total
                place = (row ^ (within // owned)) * owned + within % owned
                at = s * slots + k
                if l == 0:
                    places[0, at] = jnp.where(live, place, -1)
                else:
                    places[1, at] = jnp.where(live & (lower == 0), place, -1)
                    places[2, at] = jnp.where(live & (lower == 1), place, -1)


def place_of(places, index, slot, owned):
    own, partner = places
    count = own.shape[1]
    if slot < count:
        place = own[index, slot]
        return jnp.maximum(place, 0), place >= 0
    place = partner[index, slot - count]
    return jnp.where(place >= 0, place ^ owned, 0), place >= 0


def turned_rhs(rhs, mine, partner):
    core = lax.axis_index("rows") % 2
    half = mine.shape[2]
    for l in range(mine.shape[0]):
        for s in range(mine.shape[1]):
            rows = rhs[l + 1, s].T
            low, high = rows[:half], rows[half:]
            mine[l, s] = jnp.where(core == 0, low, high)
            partner[l, s] = jnp.where(core == 0, high, low)


def gathered(index, places, pieces, window):
    sups = pieces[0].shape[0]
    slots = 2 * places[0].shape[1] // sups
    for number, piece in enumerate(pieces):
        window[number * sups : (number + 1) * sups] = piece[...]
    for s in range(sups):
        picked = []
        for k in range(slots):
            place, live = place_of(places, index, s * slots + k, sups // 2)
            picked.append(jnp.where(live, window[place], 0.0))
        yield jnp.concatenate(picked, 1)


def upper_of(level, mine, partner, s):
    half = mine.shape[1]
    return mine[level - 1, s] if s < half else partner[level - 1, s % half]


def update_lower(index, level, places, places_partner, rhs, rhs_partner, *refs):
    tiles, pieces, (out, window) = refs[:4], refs[4:-2], refs[-2:]
    col = lax.axis_index("cols")
    for s, left in enumerate(gathered(index, (places, places_partner), pieces, window)):
        right = upper_of(level, rhs, rhs_partner, s)
        zero = jnp.zeros_like(right)
        base = jnp.concatenate([jnp.where(col == 0, right, zero), jnp.where(col == 0, zero, right)], 1)
        out[s] = base - dot3(left, part_of(tiles, s), NN)


def level_values(mine, theirs, d0, d1, residual, values):
    half = d0.shape[1]
    for s in range(residual.shape[0]):
        left = mine[s] + theirs[s]
        residual[s] = left
        values[s] = dot3(left, d0[1, s] if s < half else d1[1, s % half], NT)


def update_top(places, places_partner, *refs):
    tiles, base, pieces, (out, window) = refs[:4], refs[4], refs[5:-2], refs[-2:]
    for s, left in enumerate(gathered(2, (places, places_partner), pieces, window)):
        out[s] = base[s] - dot3(left, part_of(tiles, s), NN)


def add_terms(index, places, tiles, left, s, totals):
    owned = tiles[0].shape[0]
    depth = totals.shape[2]
    terms = dot3(left, part_of(tiles, s), NN)
    slots = terms.shape[1] // depth
    for k in range(slots):
        place, live = place_of(places, index, s * slots + k, owned)
        term = jnp.where(live, terms[:, k * depth : (k + 1) * depth], 0.0)
        totals[place] = totals[place] + term


def share_out(col, x, s, solved_mine, solved_partner):
    depth = solved_mine.shape[2]
    half = solved_mine.shape[0]
    share = jnp.where(col == 0, x[:, :depth], x[:, depth:])
    if s < half:
        solved_mine[s] = share
    else:
        solved_partner[s % half] = share


def pieces_out(totals, outs):
    sups = outs[0].shape[0]
    for number, out in enumerate(outs):
        out[...] = totals[number * sups : (number + 1) * sups]


def top_carry(places, places_partner, mine, theirs, t0, t1, t2, t3, residual, *rest):
    outs, totals = rest[:-1], rest[-1]
    totals[...] = jnp.zeros_like(totals)
    for s in range(residual.shape[0]):
        left = mine[s] + theirs[s]
        residual[s] = left
        add_terms(2, (places, places_partner), (t0, t1, t2, t3), left, s, totals)
    pieces_out(totals, outs)


def lowest_carry(
    places, places_partner, residual, t0, t1, t2, t3, g0, g1, middle, d2, d3,
    totals, solved_mine, solved_partner, other,
):
    totals[...] = jnp.zeros_like(totals)
    half = g0.shape[0]
    col = lax.axis_index("cols")
    for s in range(residual.shape[0]):
        gram, diag = (g0[s], d2[0, s]) if s < half else (g1[s % half], d3[0, s % half])
        share_out(col, dot3(residual[s], gram, NN), s, solved_mine, solved_partner)
        add_terms(1, (places, places_partner), (t0, t1, t2, t3), residual[s], s, totals)
        other[s] = dot3(middle[s], diag, NT)


def middle_carry(
    places, places_partner, carried_own, carried_other, values_own, values_other, t0, t1, t2, t3, lowest,
    residual, *rest
):
    outs, totals = rest[:-1], rest[-1]
    totals[...] = lowest[...]
    for s in range(values_own.shape[0]):
        left = jnp.concatenate(
            [values_own[s] - carried_own[s], values_other[s] - carried_other[s]], 1
        )
        residual[s] = left
        add_terms(0, (places, places_partner), (t0, t1, t2, t3), left, s, totals)
    pieces_out(totals, outs)


def middle_solved(residual, d0, d1, d2, d3, solved_mine, solved_partner):
    depth = solved_mine.shape[2]
    half = d0.shape[1]
    for s in range(residual.shape[0]):
        diag, diag_other = (d0[1, s], d2[0, s]) if s < half else (d1[1, s % half], d3[0, s % half])
        left = residual[s]
        x = dot3(left[:, :depth], diag, NN) + dot3(left[:, depth:], diag_other, NN)
        share_out(lax.axis_index("cols"), x, s, solved_mine, solved_partner)


def last_product(values, a, b, c, d, e, d_own, d_partner, mine, partner):
    sups = values.shape[0]
    half = sups // 2
    for s in range(sups):
        carried = a[s] + b[s] + c[s] + d[s] + e[s]
        diag, out = (d_own, mine) if s < half else (d_partner, partner)
        out[s % half] = dot3(values[s] - carried, diag[0, s % half], NN)


def turned_solution(mine, partner, own, other):
    core, col = lax.axis_index("rows") % 2, lax.axis_index("cols")
    depth = own.shape[1]
    for s in range(mine.shape[0]):
        both = ordered(mine[s], partner[s], core, 0)
        low, high = both[:, :depth].T, both[:, depth:].T
        own[s] = jnp.where(col == 0, low, high)
        other[s] = jnp.where(col == 0, high, low)


def turned_upper(mine2, partner2, mine1, partner1, out):
    core = lax.axis_index("rows") % 2
    for s in range(mine2.shape[0]):
        out[0, s] = ordered(mine1[s], partner1[s], core, 0).T
        out[1, s] = ordered(mine2[s], partner2[s], core, 0).T


def local(rhs, diag_inv, factor_tiles, tile_source, tile_count):
    levels, owned, share_rows, columns = rhs.shape
    slots = tile_source.shape[2]
    sups = 2 * owned
    block = share_rows * 2
    half_columns = columns // 2
    rows_total = lax.axis_size("rows")
    piece = (sups, half_columns, share_rows)
    shared = (owned, half_columns, share_rows)
    window = (PIECES * sups, half_columns, share_rows)
    after = lax.optimization_barrier

    def swap_cols(value):
        return lax.ppermute(value, "cols", [(0, 1), (1, 0)])

    def swap_rows(value, bits):
        return lax.ppermute(value, "rows", [(r, r ^ bits) for r in range(rows_total)])

    def swap_core(value):
        return swap_rows(value, 1)

    def swap_x(value):
        return swap_rows(value, 2)

    def swap_mid(value):
        low, high = rows_total // 4, 3 * rows_total // 4
        pairs = [(r, r ^ 12 if low <= r < high else r) for r in range(rows_total)]
        return lax.ppermute(value, "rows", pairs)

    def gather_pieces(value):
        far = swap_rows(value, 8)
        beside = swap_x(value)
        mid = swap_mid(value)
        near = swap_rows(value, 4)
        return [
            value, beside, near, swap_x(near), far, swap_x(far), mid, swap_mid(beside)
        ]

    def scatter_pieces(p):
        far = swap_rows(p[4] + swap_x(p[5]), 8)
        mid = swap_mid(p[6] + swap_x(p[7]))
        near = swap_rows(p[2] + swap_x(p[3]), 4)
        return [p[0], far, mid, near, swap_x(p[1])]

    rhs0 = rhs[0]
    rhs0_other = swap_cols(rhs0)
    tiles_partner = swap_core(factor_tiles)
    d_partner = swap_core(diag_inv)
    own_places = pl.pallas_call(
        slot_places,
        out_shape=jax.ShapeDtypeStruct((levels, owned * slots), jnp.int32),
        in_specs=[pl.BlockSpec(memory_space=pltpu.SMEM)] * 2,
        out_specs=pl.BlockSpec(memory_space=pltpu.SMEM),
        name="slot_places",
        **options(500),
    )(tile_source, tile_count)
    places = [own_places, swap_core(own_places)]
    diag, rhs0 = after((diag_inv, rhs0))
    d_other = swap_cols(diag[1:])
    rhs0, places, tiles_partner, d_partner = after((rhs0, places, tiles_partner, d_partner))
    mine, partner = first_call(rhs0, rhs0_other, diag_inv)
    values0 = jnp.concatenate([mine, swap_core(partner)], 0)
    pieces0 = gather_pieces(values0)

    reach = slots * share_rows
    tall = [((reach, block), BF16)] * 2
    wide = [((block, reach), BF16)] * 2
    rhs, _ = after((rhs, partner))
    upper, partner = call(
        turned_rhs, "turned_rhs", [(levels - 1, owned, half_columns, share_rows)] * 2, [rhs], 0
    )
    uppers = [upper, swap_core(partner)]
    low_tiles = prepare(split_tiles, "split_tiles", 0, factor_tiles, tiles_partner, [], tall, 2000)
    full = (sups, half_columns, block)
    scratch = [pltpu.VMEM(window, F32)]
    partial = call(
        functools.partial(update_lower, 0, 1), "update_middle", [full],
        [*places, *uppers, *low_tiles, *pieces0], 2, scratch,
    )[0]
    tiles, d_other, late = after((factor_tiles, d_other, partial))
    diags = [diag_inv, d_partner, d_other, swap_core(d_other)]
    low_turned = prepare(
        diag_by_tiles, "diag_by_tiles", 0, tiles, tiles_partner, diags, wide, 3000
    )
    late, low_turned = after((late, low_turned))
    middle, values1 = call(
        level_values, "level_values", [full, piece],
        [late, swap_cols(partial), diag_inv, d_partner], 0,
    )
    pieces1 = gather_pieces(values1)
    tiles, _ = after((factor_tiles, values1))
    top_tiles = prepare(split_tiles, "split_tiles", 1, tiles, tiles_partner, [], tall, 2000)
    base = call(
        functools.partial(update_lower, 1, 2), "update_top_low", [full],
        [*places, *uppers, *top_tiles, *pieces0], 2, scratch,
    )[0]

    partial = call(
        update_top, "update_top", [full], [*places, *top_tiles, base, *pieces1], 2, scratch
    )[0]
    tiles, _ = after((factor_tiles, partial))
    turned = prepare(
        gram_by_tiles, "gram_by_tiles", 1, tiles, tiles_partner, diags,
        wide + [((block, block), F32)], 3000,
    )
    top_turned, grams = turned[:2] + turned[3:5], [turned[2], turned[5]]
    residual, *out = call(
        top_carry, "top_carry", [full] + [piece] * PIECES,
        [*places, partial, swap_cols(partial), *top_turned], 2, scratch,
    )
    carried = sum(scatter_pieces(out))
    residual, _ = after((residual, carried))
    lowest, mine2, partner2, values1_other = call(
        lowest_carry, "lowest_carry", [window, shared, shared, piece],
        [*places, residual, *top_turned, *grams, middle, *diags[2:]], 2, cost=2000,
    )

    residual, *out = call(
        middle_carry, "middle_carry", [full] + [piece] * PIECES,
        [*places, carried, swap_cols(carried), values1, values1_other, *low_turned, lowest],
        2, scratch,
    )

    mine, partner = call(
        last_product, "last_product", [(owned, half_columns, block)] * 2,
        [values0, *scatter_pieces(out), diag_inv, d_partner], 0,
    )
    own, other = call(
        turned_solution, "turned_solution", [(owned, share_rows, columns)] * 2,
        [mine, swap_core(partner)], 0,
    )
    own = own + swap_cols(other)

    residual, partner2, _ = after((residual, partner2, other))
    mine1, partner1 = call(
        middle_solved, "middle_solved", [shared, shared], [residual, *diags], 0
    )
    result_upper = call(
        turned_upper, "turned_upper", [(levels - 1, owned, share_rows, columns)],
        [mine2, swap_core(partner2), mine1, swap_core(partner1)], 0,
    )[0]
    return jnp.concatenate([own[None], result_upper], 0)


def solution(mesh):
    placed = (
        P(None, "rows", "cols", None),
        P(None, "rows", "cols", None),
        P(None, "rows", None, "cols", None),
        P(None, "rows", None),
        P(None, "rows"),
    )
    small = mesh.shape["rows"] == 16 and mesh.shape["cols"] == 2
    return jax.shard_map(
        local if small else local_any,
        mesh=mesh,
        in_specs=placed,
        out_specs=P(None, "rows", "cols", None),
        check_vma=False,
    )
```

time: 130 us -> 117 us (0.900)
  waiting for transfers between devices: 51.6 us -> 34 us
  starting transfers between devices: 42.6 us -> 52.9 us
  other arithmetic: 4.66 us -> 0.93 us
  local copies, waits for them, and re-layouts: 6.21 us -> 3.37 us
  Pallas kernels: 23.5 us -> 24.8 us
    pallas_call x2 -> x6, Pallas kernels: 3.67 us -> 14.1 us  [the longest x4 11.3 us: prepare(): pl.pallas_call(kernel, grid=(owned,), out_shape=[jax.ShapeDtypeStruct((ow...]
    pallas_call x12, Pallas kernels: 19.8 us -> 10.7 us  [call(): pl.pallas_call(kernel, out_shape=[jax.ShapeDtypeStruct(shape, F32) for sh...]
    ppermute x7 -> x6, waiting for transfers between devices: 19.2 us -> 10.2 us  [swap_cols(): return lax.ppermute(value, 'cols', [(0, 1), (1, 0)])]
    ppermute x34 -> x31, waiting for transfers between devices: 32.4 us -> 23.8 us  [swap_rows(): lax.ppermute(value, 'rows', [(r, r ^ bits) for r in range(rows_total)])]
    ppermute x34 -> x31, starting transfers between devices: 33 us -> 40.1 us  [swap_rows(): lax.ppermute(value, 'rows', [(r, r ^ bits) for r in range(rows_total)])]
    ppermute x7 -> x6, starting transfers between devices: 6.89 us -> 8.85 us  [swap_cols(): return lax.ppermute(value, 'cols', [(0, 1), (1, 0)])]
    slice x2 -> x1, local copies, waits for them, and re-layouts: 2.85 us -> 1.08 us  [local(): d_other = swap_cols(diag[1:])]
    ppermute x4 -> x6, starting transfers between devices: 2.65 us -> 3.97 us  [swap_mid(): return lax.ppermute(value, 'rows', pairs)]
  transfers between devices with their start and end apart: 45 -> 43, of which waited for: 22 -> 16; matrix products, arithmetic and copies ran while one was open for 6% -> 2% of each run, Pallas kernels for 9% -> 16%
where the time goes in v3:
time: 117 us; the launch traced here: 116 us
  starting transfers between devices  52.9 us (45%)
  waiting for transfers between devices  34 us (29%)
  Pallas kernels  24.8 us (21%)
  local copies, waits for them, and re-layouts  3.37 us (3%)
    ppermute x31, starting transfers between devices, swap_rows(): lax.ppermute(value, 'rows', [(r, r ^ bits) for r in range(rows_total)])  40.1 us
    ppermute x31, waiting for transfers between devices, swap_rows(): lax.ppermute(value, 'rows', [(r, r ^ bits) for r in range(rows_total)])  23.8 us
    pallas_call x4, Pallas kernels, prepare(): pl.pallas_call(kernel, grid=(owned,), out_shape=[jax.ShapeDtypeStruct((ow...  11.3 us
    pallas_call x12, Pallas kernels, call(): pl.pallas_call(kernel, out_shape=[jax.ShapeDtypeStruct(shape, F32) for sh...  10.7 us
    ppermute x6, waiting for transfers between devices, swap_cols(): return lax.ppermute(value, 'cols', [(0, 1), (1, 0)])  10.2 us
    ppermute x6, starting transfers between devices, swap_cols(): return lax.ppermute(value, 'cols', [(0, 1), (1, 0)])  8.85 us
    ppermute x6, starting transfers between devices, swap_mid(): return lax.ppermute(value, 'rows', pairs)  3.97 us
  transfers between devices with their start and end apart: 43, of which 16 were waited for; matrix products, arithmetic and copies ran while one was open for 2% of the time, Pallas kernels for 16%

profile of v3, /device:TPU:0, one launch (start us, length us, event | category | flops | bytes accessed | tf_op | source)
XLA Modules:
  0.0 116.3 jit_solution(8148908187141962623)
XLA Ops:
  1.4 3.0 %collective-permute-start.3 = (f32[2,128,128]{2,1,0:T(8,128)S(1)}, f32[2,128,128]{2,1,0:T(8,128)S(1)}, u32[]{:S(2)}, u32[]{:S(2)}) collective-permute-start(f32[2,128,128]{2,1,0:T(8,128)S(1)} %slice_bitcast_fusion.rhs_own), channel_id=1, source_target_pairs={{0,1},{1,0},{2,3},{3,2},{4,5},{5,4},{6,7},{7,6},{8,9},{9,8},{10,11... | collective-permute-start | bytes 393224 | tf_op jit(solution)/shard_map/ppermute | solution.py:450
  5.8 1.5 %slot_places.1.places = s32[3,16]{1,0:T(4,128)S(1)} custom-call(s32[2,2,8]{2,1,0:T(2,128)S(1)} %copy-done.2, s32[2,2]{1,0:T(2,128)S(1)} %copy-done.3), custom_call_target="tpu_custom_call" | custom-call | flops 500000000 | tf_op jit(solution)/shard_map/slot_places/pallas_call | solution.py:485
  7.4 1.1 slice.7
  8.6 1.3 %first_values.1 = (f32[2,64,128]{2,1,0:T(8,128)S(1)}, f32[2,64,128]{2,1,0:T(8,128)S(1)}) custom-call(f32[2,128,128]{2,1,0:T(8,128)S(1)} %slice_bitcast_fusion.rhs_own, f32[2,128,128]{2,1,0:T(8,128)S(1)} %collective-permute-done.3.rhs_other, f32[3,2,128,256]{3,2,1,0:T(8,128)} %d0.7), custom_call_target="tpu_custom_call" | custom-call | flops 500000000 | tf_op jit(solution)/shard_map/first_values/pallas_call | solution.py:238
  11.4 3.8 %collective-permute-start.10 = (f32[4,64,128]{2,1,0:T(8,128)S(1)}, f32[4,64,128]{2,1,0:T(8,128)S(1)}, u32[]{:S(2)}, u32[]{:S(2)}) collective-permute-start(f32[4,64,128]{2,1,0:T(8,128)S(1)} %constant_dynamic-update-slice_fusion.refs_4_.values), channel_id=1, source_target_pairs={{0,16},{2,18},{4,20},{6,22},{8,24},{10,26},{12,28},{14,30},{16,0},... | collective-permute-start | bytes 393224 | tf_op jit(solution)/shard_map/ppermute | solution.py:453
  15.2 1.5 %collective-permute-start.7 = (f32[4,64,128]{2,1,0:T(8,128)S(1)}, f32[4,64,128]{2,1,0:T(8,128)S(1)}, u32[]{:S(2)}, u32[]{:S(2)}) collective-permute-start(f32[4,64,128]{2,1,0:T(8,128)S(1)} %constant_dynamic-update-slice_fusion.refs_4_.values), channel_id=1, source_target_pairs={{0,4},{2,6},{4,0},{6,2},{8,12},{10,14},{12,8},{14,10},{16,20},{18,... | collective-permute-start | bytes 393224 | tf_op jit(solution)/shard_map/ppermute | solution.py:453
  16.7 1.6 %collective-permute-start.8 = (f32[4,64,128]{2,1,0:T(8,128)S(1)}, f32[4,64,128]{2,1,0:T(8,128)S(1)}, u32[]{:S(2)}, u32[]{:S(2)}) collective-permute-start(f32[4,64,128]{2,1,0:T(8,128)S(1)} %constant_dynamic-update-slice_fusion.refs_4_.values), channel_id=1, source_target_pairs={{0,8},{2,10},{4,12},{6,14},{8,0},{10,2},{12,4},{14,6},{16,24},{18,... | collective-permute-start | bytes 393224 | tf_op jit(solution)/shard_map/ppermute | solution.py:453
  18.9 3.0 %collective-permute-done.10.refs_8_ = f32[4,64,128]{2,1,0:T(8,128)S(1)} collective-permute-done((f32[4,64,128]{2,1,0:T(8,128)S(1)}, f32[4,64,128]{2,1,0:T(8,128)S(1)}, u32[]{:S(2)}, u32[]{:S(2)}) %collective-permute-start.10) | collective-permute-done | bytes 131104 | tf_op jit(solution)/shard_map/ppermute | solution.py:453
  21.9 2.2 %collective-permute-start.11 = (f32[4,64,128]{2,1,0:T(8,128)S(1)}, f32[4,64,128]{2,1,0:T(8,128)S(1)}, u32[]{:S(2)}, u32[]{:S(2)}) collective-permute-start(f32[4,64,128]{2,1,0:T(8,128)S(1)} %collective-permute-done.10.refs_8_), channel_id=1, source_target_pairs={{0,4},{2,6},{4,0},{6,2},{8,12},{10,14},{12,8},{14,10},{16,20},{18,... | collective-permute-start | bytes 393224 | tf_op jit(solution)/shard_map/ppermute | solution.py:453
  24.9 1.9 %split_tiles.2 = (bf16[2,1024,256]{2,1,0:T(8,128)(2,1)S(1)}, bf16[2,1024,256]{2,1,0:T(8,128)(2,1)S(1)}, bf16[2,1024,256]{2,1,0:T(8,128)(2,1)S(1)}, bf16[2,1024,256]{2,1,0:T(8,128)(2,1)S(1)}) custom-call(f32[2,2,8,128,256]{4,3,2,1,0:T(8,128)} %own.4, f32[2,2,8,128,256]{4,3,2,1,0:T(8,128)S(1)} %collective-permute-done.1.partner), custom_call_target="tpu_custom_call" | custom-call | flops 2000000000 | tf_op jit(solution)/shard_map/split_tiles/pallas_call | solution.py:174
  26.8 1.6 %collective-permute-done.11.refs_9_ = f32[4,64,128]{2,1,0:T(8,128)S(1)} collective-permute-done((f32[4,64,128]{2,1,0:T(8,128)S(1)}, f32[4,64,128]{2,1,0:T(8,128)S(1)}, u32[]{:S(2)}, u32[]{:S(2)}) %collective-permute-start.11) | collective-permute-done | bytes 131104 | tf_op jit(solution)/shard_map/ppermute | solution.py:453
  28.4 1.5 %collective-permute-done.9.refs_7_ = f32[4,64,128]{2,1,0:T(8,128)S(1)} collective-permute-done((f32[4,64,128]{2,1,0:T(8,128)S(1)}, f32[4,64,128]{2,1,0:T(8,128)S(1)}, u32[]{:S(2)}, u32[]{:S(2)}) %collective-permute-start.9) | collective-permute-done | bytes 131104 | tf_op jit(solution)/shard_map/ppermute | solution.py:453
  29.9 1.5 %update_middle.1.mine = f32[4,64,256]{2,1,0:T(8,128)S(1)} custom-call(s32[3,16]{1,0:T(4,128)S(1)} %slot_places.1.places, s32[3,16]{1,0:T(4,128)S(1)} %collective-permute-done.places_partner, f32[2,2,64,128]{3,2,1,0:T(8,128)S(1)} %get-tuple-element.86.rhs, f32[2,2,64,128]{3,2,1,0:T(8,128)S(1)} %collective-permute-done.6.rhs_partner, ...), custom_call_target="tpu_custom_call" | custom-call | flops 1000000000 | tf_op jit(solution)/shard_map/update_middle/pallas_call | solution.py:157
  31.5 1.6 %collective-permute-start.15 = (f32[4,64,256]{2,1,0:T(8,128)S(1)}, f32[4,64,256]{2,1,0:T(8,128)S(1)}, u32[]{:S(2)}, u32[]{:S(2)}) collective-permute-start(f32[4,64,256]{2,1,0:T(8,128)S(1)} %update_middle.1.mine), channel_id=1, source_target_pairs={{0,1},{1,0},{2,3},{3,2},{4,5},{5,4},{6,7},{7,6},{8,9},{9,8},{10,11... | collective-permute-start | bytes 786440 | tf_op jit(solution)/shard_map/ppermute | solution.py:450
  33.4 3.4 %diag_by_tiles.1 = (bf16[2,256,1024]{2,1,0:T(8,128)(2,1)S(1)}, bf16[2,256,1024]{2,1,0:T(8,128)(2,1)S(1)}, bf16[2,256,1024]{2,1,0:T(8,128)(2,1)S(1)}, bf16[2,256,1024]{2,1,0:T(8,128)(2,1)S(1)}) custom-call(f32[2,2,8,128,256]{4,3,2,1,0:T(8,128)} %own.4, f32[2,2,8,128,256]{4,3,2,1,0:T(8,128)S(1)} %collective-permute-done.1.partner, ...), custom_call_target="tpu_custom_call" | custom-call | flops 3000000000 | tf_op jit(solution)/shard_map/diag_by_tiles/pallas_call | solution.py:174
  36.7 3.5 %collective-permute-done.15.theirs = f32[4,64,256]{2,1,0:T(8,128)S(1)} collective-permute-done((f32[4,64,256]{2,1,0:T(8,128)S(1)}, f32[4,64,256]{2,1,0:T(8,128)S(1)}, u32[]{:S(2)}, u32[]{:S(2)}) %collective-permute-start.15) | collective-permute-done | bytes 262176 | tf_op jit(solution)/shard_map/ppermute | solution.py:450
  40.5 1.6 %collective-permute-start.17 = (f32[4,64,128]{2,1,0:T(8,128)S(1)}, f32[4,64,128]{2,1,0:T(8,128)S(1)}, u32[]{:S(2)}, u32[]{:S(2)}) collective-permute-start(f32[4,64,128]{2,1,0:T(8,128)S(1)} %get-tuple-element.102.refs_5_.values_own), channel_id=1, source_target_pairs={{0,8},{2,10},{4,12},{6,14},{8,0},{10,2},{12,4},{14,6},{16,24},{18,... | collective-permute-start | bytes 393224 | tf_op jit(solution)/shard_map/ppermute | solution.py:453
  42.1 2.7 %collective-permute-start.19 = (f32[4,64,128]{2,1,0:T(8,128)S(1)}, f32[4,64,128]{2,1,0:T(8,128)S(1)}, u32[]{:S(2)}, u32[]{:S(2)}) collective-permute-start(f32[4,64,128]{2,1,0:T(8,128)S(1)} %get-tuple-element.102.refs_5_.values_own), channel_id=1, source_target_pairs={{0,16},{2,18},{4,20},{6,22},{8,24},{10,26},{12,28},{14,30},{16,0},... | collective-permute-start | bytes 393224 | tf_op jit(solution)/shard_map/ppermute | solution.py:453
  44.9 1.4 %collective-permute-start.16 = (f32[4,64,128]{2,1,0:T(8,128)S(1)}, f32[4,64,128]{2,1,0:T(8,128)S(1)}, u32[]{:S(2)}, u32[]{:S(2)}) collective-permute-start(f32[4,64,128]{2,1,0:T(8,128)S(1)} %get-tuple-element.102.refs_5_.values_own), channel_id=1, source_target_pairs={{0,4},{2,6},{4,0},{6,2},{8,12},{10,14},{12,8},{14,10},{16,20},{18,... | collective-permute-start | bytes 393224 | tf_op jit(solution)/shard_map/ppermute | solution.py:453
  47.6 3.2 %collective-permute-done.19.refs_9_ = f32[4,64,128]{2,1,0:T(8,128)S(1)} collective-permute-done((f32[4,64,128]{2,1,0:T(8,128)S(1)}, f32[4,64,128]{2,1,0:T(8,128)S(1)}, u32[]{:S(2)}, u32[]{:S(2)}) %collective-permute-start.19) | collective-permute-done | bytes 131104 | tf_op jit(solution)/shard_map/ppermute | solution.py:453
  50.9 1.6 %collective-permute-start.20 = (f32[4,64,128]{2,1,0:T(8,128)S(1)}, f32[4,64,128]{2,1,0:T(8,128)S(1)}, u32[]{:S(2)}, u32[]{:S(2)}) collective-permute-start(f32[4,64,128]{2,1,0:T(8,128)S(1)} %collective-permute-done.19.refs_9_), channel_id=1, source_target_pairs={{0,4},{2,6},{4,0},{6,2},{8,12},{10,14},{12,8},{14,10},{16,20},{18,... | collective-permute-start | bytes 393224 | tf_op jit(solution)/shard_map/ppermute | solution.py:453
  53.1 1.9 %split_tiles.3 = (bf16[2,1024,256]{2,1,0:T(8,128)(2,1)S(1)}, bf16[2,1024,256]{2,1,0:T(8,128)(2,1)S(1)}, bf16[2,1024,256]{2,1,0:T(8,128)(2,1)S(1)}, bf16[2,1024,256]{2,1,0:T(8,128)(2,1)S(1)}) custom-call(f32[2,2,8,128,256]{4,3,2,1,0:T(8,128)} %own.4, f32[2,2,8,128,256]{4,3,2,1,0:T(8,128)S(1)} %collective-permute-done.1.partner), custom_call_target="tpu_custom_call" | custom-call | flops 2000000000 | tf_op jit(solution)/shard_map/split_tiles/pallas_call | solution.py:174
  55.0 1.5 %update_top_low.1.refs_4_ = f32[4,64,256]{2,1,0:T(8,128)S(1)} custom-call(s32[3,16]{1,0:T(4,128)S(1)} %slot_places.1.places, s32[3,16]{1,0:T(4,128)S(1)} %collective-permute-done.places_partner, f32[2,2,64,128]{3,2,1,0:T(8,128)S(1)} %get-tuple-element.86.rhs, f32[2,2,64,128]{3,2,1,0:T(8,128)S(1)} %collective-permute-done.6.rhs_partner, ...), custom_call_target="tpu_custom_call" | custom-call | flops 1000000000 | tf_op jit(solution)/shard_map/update_top_low/pallas_call | solution.py:157
  56.5 1.5 %update_top.1.mine = f32[4,64,256]{2,1,0:T(8,128)S(1)} custom-call(s32[3,16]{1,0:T(4,128)S(1)} %slot_places.1.places, s32[3,16]{1,0:T(4,128)S(1)} %collective-permute-done.places_partner, bf16[2,1024,256]{2,1,0:T(8,128)(2,1)S(1)} %get-tuple-element.104.refs_0_, bf16[2,1024,256]{2,1,0:T(8,128)(2,1)S(1)} %get-tuple-element.105.refs_1_, ...), custom_call_target="tpu_custom_call" | custom-call | flops 1000000000 | tf_op jit(solution)/shard_map/update_top/pallas_call | solution.py:157
  58.0 1.6 %collective-permute-start.23 = (f32[4,64,256]{2,1,0:T(8,128)S(1)}, f32[4,64,256]{2,1,0:T(8,128)S(1)}, u32[]{:S(2)}, u32[]{:S(2)}) collective-permute-start(f32[4,64,256]{2,1,0:T(8,128)S(1)} %update_top.1.mine), channel_id=1, source_target_pairs={{0,1},{1,0},{2,3},{3,2},{4,5},{5,4},{6,7},{7,6},{8,9},{9,8},{10,11... | collective-permute-start | bytes 786440 | tf_op jit(solution)/shard_map/ppermute | solution.py:450
  59.6 4.2 %gram_by_tiles.1 = (bf16[2,256,1024]{2,1,0:T(8,128)(2,1)S(1)}, bf16[2,256,1024]{2,1,0:T(8,128)(2,1)S(1)}, f32[2,256,256]{2,1,0:T(8,128)S(1)}, bf16[2,256,1024]{2...) custom-call(f32[2,2,8,128,256]{4,3,2,1,0:T(8,128)} %own.4, ...), custom_call_target="tpu_custom_call" | custom-call | flops 3000000000 | tf_op jit(solution)/shard_map/gram_by_tiles/pallas_call | solution.py:174
  64.4 1.6 %top_carry.1 = (f32[4,64,256]{2,1,0:T(8,128)S(1)}, f32[4,64,128]{2,1,0:T(8,128)S(1)}, f32[4,64,128]{2,1,0:T(8,128)S(1)}, f32[4,64,128]{2,1,0:T(8,128)S(1)}, f32[...) custom-call(s32[3,16]{1,0:T(4,128)S(1)} %slot_places.1.places, ...), custom_call_target="tpu_custom_call" | custom-call | flops 1000000000 | tf_op jit(solution)/shard_map/top_carry/pallas_call | solution.py:157
  66.0 1.0 collective-permute-start.24
  67.0 1.1 collective-permute-start.26
  68.1 0.9 collective-permute-start.28
  69.0 1.1 collective-permute-start.30
  70.1 2.3 %collective-permute-done.24 = f32[4,64,128]{2,1,0:T(8,128)S(1)} collective-permute-done((f32[4,64,128]{2,1,0:T(8,128)S(1)}, f32[4,64,128]{2,1,0:T(8,128)S(1)}, u32[]{:S(2)}, u32[]{:S(2)}) %collective-permute-start.24) | collective-permute-done | bytes 131104 | tf_op jit(solution)/shard_map/ppermute | solution.py:453
  72.5 3.4 %collective-permute-start.25 = (f32[4,64,128]{2,1,0:T(8,128)S(1)}, f32[4,64,128]{2,1,0:T(8,128)S(1)}, u32[]{:S(2)}, u32[]{:S(2)}) collective-permute-start(f32[4,64,128]{2,1,0:T(8,128)S(1)} %add.33), channel_id=1, source_target_pairs={{0,16},{2,18},{4,20},{6,22},{8,24},{10,26},{12,28},{14,30},{16,0},... | collective-permute-start | bytes 393224 | tf_op jit(solution)/shard_map/ppermute | solution.py:453
  76.6 3.4 %collective-permute-start.29 = (f32[4,64,128]{2,1,0:T(8,128)S(1)}, f32[4,64,128]{2,1,0:T(8,128)S(1)}, u32[]{:S(2)}, u32[]{:S(2)}) collective-permute-start(f32[4,64,128]{2,1,0:T(8,128)S(1)} %add.37), channel_id=1, source_target_pairs={{0,8},{2,10},{4,12},{6,14},{8,0},{10,2},{12,4},{14,6},{16,24},{18,... | collective-permute-start | bytes 393224 | tf_op jit(solution)/shard_map/ppermute | solution.py:453
  80.0 2.9 %collective-permute-done.29 = f32[4,64,128]{2,1,0:T(8,128)S(1)} collective-permute-done((f32[4,64,128]{2,1,0:T(8,128)S(1)}, f32[4,64,128]{2,1,0:T(8,128)S(1)}, u32[]{:S(2)}, u32[]{:S(2)}) %collective-permute-start.29) | collective-permute-done | bytes 131104 | tf_op jit(solution)/shard_map/ppermute | solution.py:453
  83.0 1.3 %collective-permute-start.31 = (f32[4,64,128]{2,1,0:T(8,128)S(1)}, f32[4,64,128]{2,1,0:T(8,128)S(1)}, u32[]{:S(2)}, u32[]{:S(2)}) collective-permute-start(f32[4,64,128]{2,1,0:T(8,128)S(1)} %add_add_fusion.carried_own), channel_id=1, source_target_pairs={{0,1},{1,0},{2,3},{3,2},{4,5},{5,4},{6,7},{7,6},{8,9},{9,8},{10,11... | collective-permute-start | bytes 393224 | tf_op jit(solution)/shard_map/ppermute | solution.py:450
  84.3 1.8 %lowest_carry.1 = (f32[32,64,128]{2,1,0:T(8,128)S(1)}, f32[2,64,128]{2,1,0:T(8,128)S(1)}, f32[2,64,128]{2,1,0:T(8,128)S(1)}, f32[4,64,128]{2,1,0:T(8,128)S(1)}) custom-call(s32[3,16]{1,0:T(4,128)S(1)} %slot_places.1.places, s32[3,16]{1,0:T(4,128)S(1)} %collective-permute-done.places_partner, f32[4,64,256]{2,1,0:T(8,128)S(1)} %get-tuple-element.122.residual, ...), custom_call_target="tpu_custom_call" | custom-call | flops 2000000000 | tf_op jit(solution)/shard_map/lowest_carry/pallas_call | solution.py:157
  86.1 1.9 %collective-permute-done.31.carried_other = f32[4,64,128]{2,1,0:T(8,128)S(1)} collective-permute-done((f32[4,64,128]{2,1,0:T(8,128)S(1)}, f32[4,64,128]{2,1,0:T(8,128)S(1)}, u32[]{:S(2)}, u32[]{:S(2)}) %collective-permute-start.31) | collective-permute-done | bytes 131104 | tf_op jit(solution)/shard_map/ppermute | solution.py:450
  88.0 1.6 %middle_carry.1 = (f32[4,64,256]{2,1,0:T(8,128)S(1)}, f32[4,64,128]{2,1,0:T(8,128)S(1)}, f32[4,64,128]{2,1,0:T(8,128)S(1)}, f32[4,64,128]{2,1,0:T(8,128)S(1)}, f...) custom-call(s32[3,16]{1,0:T(4,128)S(1)} %slot_places.1.places, ...), custom_call_target="tpu_custom_call" | custom-call | flops 1000000000 | tf_op jit(solution)/shard_map/middle_carry/pallas_call | solution.py:157
  90.0 1.7 %collective-permute-start.34 = (f32[4,64,128]{2,1,0:T(8,128)S(1)}, f32[4,64,128]{2,1,0:T(8,128)S(1)}, u32[]{:S(2)}, u32[]{:S(2)}) collective-permute-start(f32[4,64,128]{2,1,0:T(8,128)S(1)} %get-tuple-element.136), channel_id=1, source_target_pairs={{0,4},{2,6},{4,0},{6,2},{8,12},{10,14},{12,8},{14,10},{16,20},{18,... | collective-permute-start | bytes 393224 | tf_op jit(solution)/shard_map/ppermute | solution.py:453
  92.0 1.7 %collective-permute-start.38 = (f32[4,64,128]{2,1,0:T(8,128)S(1)}, f32[4,64,128]{2,1,0:T(8,128)S(1)}, u32[]{:S(2)}, u32[]{:S(2)}) collective-permute-start(f32[4,64,128]{2,1,0:T(8,128)S(1)} %get-tuple-element.139), channel_id=1, source_target_pairs={{0,4},{2,6},{4,0},{6,2},{8,12},{10,14},{12,8},{14,10},{16,20},{18,... | collective-permute-start | bytes 393224 | tf_op jit(solution)/shard_map/ppermute | solution.py:453
  93.7 0.9 collective-permute-done.36
  94.7 2.1 %collective-permute-start.37 = (f32[4,64,128]{2,1,0:T(8,128)S(1)}, f32[4,64,128]{2,1,0:T(8,128)S(1)}, u32[]{:S(2)}, u32[]{:S(2)}) collective-permute-start(f32[4,64,128]{2,1,0:T(8,128)S(1)} %add.42), channel_id=1, source_target_pairs={{0,8},{2,10},{4,12},{6,14},{8,0},{10,2},{12,4},{14,6},{16,24},{18,... | collective-permute-start | bytes 393224 | tf_op jit(solution)/shard_map/ppermute | solution.py:453
  97.5 4.1 %collective-permute-start.33 = (f32[4,64,128]{2,1,0:T(8,128)S(1)}, f32[4,64,128]{2,1,0:T(8,128)S(1)}, u32[]{:S(2)}, u32[]{:S(2)}) collective-permute-start(f32[4,64,128]{2,1,0:T(8,128)S(1)} %add.40), channel_id=1, source_target_pairs={{0,16},{2,18},{4,20},{6,22},{8,24},{10,26},{12,28},{14,30},{16,0},... | collective-permute-start | bytes 393224 | tf_op jit(solution)/shard_map/ppermute | solution.py:453
  101.6 5.6 %collective-permute-done.33.b = f32[4,64,128]{2,1,0:T(8,128)S(1)} collective-permute-done((f32[4,64,128]{2,1,0:T(8,128)S(1)}, f32[4,64,128]{2,1,0:T(8,128)S(1)}, u32[]{:S(2)}, u32[]{:S(2)}) %collective-permute-start.33) | collective-permute-done | bytes 131104 | tf_op jit(solution)/shard_map/ppermute | solution.py:453
  107.5 1.3 %collective-permute-done.39.partner = f32[2,64,256]{2,1,0:T(8,128)S(1)} collective-permute-done((f32[2,64,256]{2,1,0:T(8,128)S(1)}, f32[2,64,256]{2,1,0:T(8,128)S(1)}, u32[]{:S(2)}, u32[]{:S(2)}) %collective-permute-start.39) | collective-permute-done | bytes 131104 | tf_op jit(solution)/shard_map/ppermute | solution.py:453
  110.0 1.2 %collective-permute-start.40 = (f32[2,128,128]{2,1,0:T(8,128)S(1)}, f32[2,128,128]{2,1,0:T(8,128)S(1)}, u32[]{:S(2)}, u32[]{:S(2)}) collective-permute-start(f32[2,128,128]{2,1,0:T(8,128)S(1)} %get-tuple-element.143), channel_id=1, source_target_pairs={{0,1},{1,0},{2,3},{3,2},{4,5},{5,4},{6,7},{7,6},{8,9},{9,8},{10,11... | collective-permute-start | bytes 393224 | tf_op jit(solution)/shard_map/ppermute | solution.py:450
  111.3 4.2 %collective-permute-done.40 = f32[2,128,128]{2,1,0:T(8,128)S(1)} collective-permute-done((f32[2,128,128]{2,1,0:T(8,128)S(1)}, f32[2,128,128]{2,1,0:T(8,128)S(1)}, u32[]{:S(2)}, u32[]{:S(2)}) %collective-permute-start.40) | collective-permute-done | bytes 131104 | tf_op jit(solution)/shard_map/ppermute | solution.py:450
  (77 shorter events, 13.7 us)
Async XLA Ops:
  0.0 10.5 %copy-start.1 = (f32[3,2,128,128]{3,2,1,0:T(8,128)S(1)}, f32[3,2,128,128]{3,2,1,0:T(8,128)}, u32[]{:S(2)}) copy-start(f32[3,2,128,128]{3,2,1,0:T(8,128)} %rhs) | copy-start | bytes 1179652
  0.0 8.6 %collective-permute-start.1 = (f32[2,2,8,128,256]{4,3,2,1,0:T(8,128)}, f32[2,2,8,128,256]{4,3,2,1,0:T(8,128)S(1)}, u32[]{:S(2)}, u32[]{:S(2)}) collective-permute-start(f32[2,2,8,128,256]{4,3,2,1,0:T(8,128)} %own.4), channel_id=1, source_target_pairs={{0,2},{2,0},{4,6},{6,4},{8,10},{10,8},{12,14},{14,12},{16,18},{18,... | collective-permute-start | bytes 12582920 | tf_op jit(solution)/shard_map/ppermute | solution.py:453
  0.5 8.2 %collective-permute-start.2 = (f32[3,2,128,256]{3,2,1,0:T(8,128)}, f32[3,2,128,256]{3,2,1,0:T(8,128)S(1)}, u32[]{:S(2)}, u32[]{:S(2)}) collective-permute-start(f32[3,2,128,256]{3,2,1,0:T(8,128)} %d0.7), channel_id=1, source_target_pairs={{0,2},{2,0},{4,6},{6,4},{8,10},{10,8},{12,14},{14,12},{16,18},{18,... | collective-permute-start | bytes 2359304 | tf_op jit(solution)/shard_map/ppermute | solution.py:453
  1.4 7.2 %collective-permute-start.3 = (f32[2,128,128]{2,1,0:T(8,128)S(1)}, f32[2,128,128]{2,1,0:T(8,128)S(1)}, u32[]{:S(2)}, u32[]{:S(2)}) collective-permute-start(f32[2,128,128]{2,1,0:T(8,128)S(1)} %slice_bitcast_fusion.rhs_own), channel_id=1, source_target_pairs={{0,1},{1,0},{2,3},{3,2},{4,5},{5,4},{6,7},{7,6},{8,9},{9,8},{10,11... | collective-permute-start | bytes 393224 | tf_op jit(solution)/shard_map/ppermute | solution.py:450
  4.5 0.7 copy-start.2
  5.1 0.7 copy-start.3
  7.3 1.3 %collective-permute-start = (s32[3,16]{1,0:T(4,128)S(1)}, s32[3,16]{1,0:T(4,128)S(1)}, u32[]{:S(2)}, u32[]{:S(2)}) collective-permute-start(s32[3,16]{1,0:T(4,128)S(1)} %slot_places.1.places), channel_id=1, source_target_pairs={{0,2},{2,0},{4,6},{6,4},{8,10},{10,8},{12,14},{14,12},{16,18},{18,... | collective-permute-start | bytes 584 | tf_op jit(solution)/shard_map/ppermute | solution.py:453
  8.5 22.9 %collective-permute-start.5 = (f32[2,2,128,256]{3,2,1,0:T(8,128)S(1)}, f32[2,2,128,256]{3,2,1,0:T(8,128)S(1)}, u32[]{:S(2)}, u32[]{:S(2)}) collective-permute-start(f32[2,2,128,256]{3,2,1,0:T(8,128)S(1)} %slice.7), channel_id=1, source_target_pairs={{0,1},{1,0},{2,3},{3,2},{4,5},{5,4},{6,7},{7,6},{8,9},{9,8},{10,11... | collective-permute-start | bytes 1572872 | tf_op jit(solution)/shard_map/ppermute | solution.py:450
  9.9 1.4 %collective-permute-start.4 = (f32[2,64,128]{2,1,0:T(8,128)S(1)}, f32[2,64,128]{2,1,0:T(8,128)S(1)}, u32[]{:S(2)}, u32[]{:S(2)}) collective-permute-start(f32[2,64,128]{2,1,0:T(8,128)S(1)} %get-tuple-element.81), channel_id=1, source_target_pairs={{0,2},{2,0},{4,6},{6,4},{8,10},{10,8},{12,14},{14,12},{16,18},{18,... | collective-permute-start | bytes 196616 | tf_op jit(solution)/shard_map/ppermute | solution.py:453
  10.6 7.6 %collective-permute-start.6 = (f32[2,2,64,128]{3,2,1,0:T(8,128)S(1)}, f32[2,2,64,128]{3,2,1,0:T(8,128)S(1)}, u32[]{:S(2)}, u32[]{:S(2)}) collective-permute-start(f32[2,2,64,128]{3,2,1,0:T(8,128)S(1)} %get-tuple-element.87), channel_id=1, source_target_pairs={{0,2},{2,0},{4,6},{6,4},{8,10},{10,8},{12,14},{14,12},{16,18},{18,... | collective-permute-start | bytes 393224 | tf_op jit(solution)/shard_map/ppermute | solution.py:453
  11.4 10.5 %collective-permute-start.10 = (f32[4,64,128]{2,1,0:T(8,128)S(1)}, f32[4,64,128]{2,1,0:T(8,128)S(1)}, u32[]{:S(2)}, u32[]{:S(2)}) collective-permute-start(f32[4,64,128]{2,1,0:T(8,128)S(1)} %constant_dynamic-update-slice_fusion.refs_4_.values), channel_id=1, source_target_pairs={{0,16},{2,18},{4,20},{6,22},{8,24},{10,26},{12,28},{14,30},{16,0},... | collective-permute-start | bytes 393224 | tf_op jit(solution)/shard_map/ppermute | solution.py:453
  15.2 9.0 %collective-permute-start.7 = (f32[4,64,128]{2,1,0:T(8,128)S(1)}, f32[4,64,128]{2,1,0:T(8,128)S(1)}, u32[]{:S(2)}, u32[]{:S(2)}) collective-permute-start(f32[4,64,128]{2,1,0:T(8,128)S(1)} %constant_dynamic-update-slice_fusion.refs_4_.values), channel_id=1, source_target_pairs={{0,4},{2,6},{4,0},{6,2},{8,12},{10,14},{12,8},{14,10},{16,20},{18,... | collective-permute-start | bytes 393224 | tf_op jit(solution)/shard_map/ppermute | solution.py:453
  16.7 8.1 %collective-permute-start.8 = (f32[4,64,128]{2,1,0:T(8,128)S(1)}, f32[4,64,128]{2,1,0:T(8,128)S(1)}, u32[]{:S(2)}, u32[]{:S(2)}) collective-permute-start(f32[4,64,128]{2,1,0:T(8,128)S(1)} %constant_dynamic-update-slice_fusion.refs_4_.values), channel_id=1, source_target_pairs={{0,8},{2,10},{4,12},{6,14},{8,0},{10,2},{12,4},{14,6},{16,24},{18,... | collective-permute-start | bytes 393224 | tf_op jit(solution)/shard_map/ppermute | solution.py:453
  18.2 8.5 %collective-permute-start.12 = (f32[4,64,128]{2,1,0:T(8,128)S(1)}, f32[4,64,128]{2,1,0:T(8,128)S(1)}, u32[]{:S(2)}, u32[]{:S(2)}) collective-permute-start(f32[4,64,128]{2,1,0:T(8,128)S(1)} %constant_dynamic-update-slice_fusion.refs_4_.values), channel_id=1, source_target_pairs={{0,0},{2,2},{4,4},{6,6},{8,16},{10,18},{12,20},{14,22},{16,8},{18,... | collective-permute-start | bytes 393224 | tf_op jit(solution)/shard_map/ppermute | solution.py:464
  21.9 6.5 %collective-permute-start.11 = (f32[4,64,128]{2,1,0:T(8,128)S(1)}, f32[4,64,128]{2,1,0:T(8,128)S(1)}, u32[]{:S(2)}, u32[]{:S(2)}) collective-permute-start(f32[4,64,128]{2,1,0:T(8,128)S(1)} %collective-permute-done.10.refs_8_), channel_id=1, source_target_pairs={{0,4},{2,6},{4,0},{6,2},{8,12},{10,14},{12,8},{14,10},{16,20},{18,... | collective-permute-start | bytes 393224 | tf_op jit(solution)/shard_map/ppermute | solution.py:453
  24.1 4.3 %collective-permute-start.13 = (f32[4,64,128]{2,1,0:T(8,128)S(1)}, f32[4,64,128]{2,1,0:T(8,128)S(1)}, u32[]{:S(2)}, u32[]{:S(2)}) collective-permute-start(f32[4,64,128]{2,1,0:T(8,128)S(1)} %collective-permute-done.7.refs_5_), channel_id=1, source_target_pairs={{0,0},{2,2},{4,4},{6,6},{8,16},{10,18},{12,20},{14,22},{16,8},{18,... | collective-permute-start | bytes 393224 | tf_op jit(solution)/shard_map/ppermute | solution.py:464
  24.8 5.1 %collective-permute-start.9 = (f32[4,64,128]{2,1,0:T(8,128)S(1)}, f32[4,64,128]{2,1,0:T(8,128)S(1)}, u32[]{:S(2)}, u32[]{:S(2)}) collective-permute-start(f32[4,64,128]{2,1,0:T(8,128)S(1)} %collective-permute-done.8.refs_6_), channel_id=1, source_target_pairs={{0,4},{2,6},{4,0},{6,2},{8,12},{10,14},{12,8},{14,10},{16,20},{18,... | collective-permute-start | bytes 393224 | tf_op jit(solution)/shard_map/ppermute | solution.py:453
  26.7 6.6 %copy-start = (f32[3,2,128,256]{3,2,1,0:T(8,128)S(1)}, f32[3,2,128,256]{3,2,1,0:T(8,128)}, u32[]{:S(2)}) copy-start(f32[3,2,128,256]{3,2,1,0:T(8,128)} %d0.7) | copy-start | bytes 2359300
  31.4 2.0 %collective-permute-start.14 = (f32[2,2,128,256]{3,2,1,0:T(8,128)S(1)}, f32[2,2,128,256]{3,2,1,0:T(8,128)S(1)}, u32[]{:S(2)}, u32[]{:S(2)}) collective-permute-start(f32[2,2,128,256]{3,2,1,0:T(8,128)S(1)} %collective-permute-done.5.d2), channel_id=1, source_target_pairs={{0,2},{2,0},{4,6},{6,4},{8,10},{10,8},{12,14},{14,12},{16,18},{18,... | collective-permute-start | bytes 1572872 | tf_op jit(solution)/shard_map/ppermute | solution.py:453
  31.5 8.7 %collective-permute-start.15 = (f32[4,64,256]{2,1,0:T(8,128)S(1)}, f32[4,64,256]{2,1,0:T(8,128)S(1)}, u32[]{:S(2)}, u32[]{:S(2)}) collective-permute-start(f32[4,64,256]{2,1,0:T(8,128)S(1)} %update_middle.1.mine), channel_id=1, source_target_pairs={{0,1},{1,0},{2,3},{3,2},{4,5},{5,4},{6,7},{7,6},{8,9},{9,8},{10,11... | collective-permute-start | bytes 786440 | tf_op jit(solution)/shard_map/ppermute | solution.py:450
  40.5 6.8 %collective-permute-start.17 = (f32[4,64,128]{2,1,0:T(8,128)S(1)}, f32[4,64,128]{2,1,0:T(8,128)S(1)}, u32[]{:S(2)}, u32[]{:S(2)}) collective-permute-start(f32[4,64,128]{2,1,0:T(8,128)S(1)} %get-tuple-element.102.refs_5_.values_own), channel_id=1, source_target_pairs={{0,8},{2,10},{4,12},{6,14},{8,0},{10,2},{12,4},{14,6},{16,24},{18,... | collective-permute-start | bytes 393224 | tf_op jit(solution)/shard_map/ppermute | solution.py:453
  42.1 8.7 %collective-permute-start.19 = (f32[4,64,128]{2,1,0:T(8,128)S(1)}, f32[4,64,128]{2,1,0:T(8,128)S(1)}, u32[]{:S(2)}, u32[]{:S(2)}) collective-permute-start(f32[4,64,128]{2,1,0:T(8,128)S(1)} %get-tuple-element.102.refs_5_.values_own), channel_id=1, source_target_pairs={{0,16},{2,18},{4,20},{6,22},{8,24},{10,26},{12,28},{14,30},{16,0},... | collective-permute-start | bytes 393224 | tf_op jit(solution)/shard_map/ppermute | solution.py:453
  44.9 7.6 %collective-permute-start.16 = (f32[4,64,128]{2,1,0:T(8,128)S(1)}, f32[4,64,128]{2,1,0:T(8,128)S(1)}, u32[]{:S(2)}, u32[]{:S(2)}) collective-permute-start(f32[4,64,128]{2,1,0:T(8,128)S(1)} %get-tuple-element.102.refs_5_.values_own), channel_id=1, source_target_pairs={{0,4},{2,6},{4,0},{6,2},{8,12},{10,14},{12,8},{14,10},{16,20},{18,... | collective-permute-start | bytes 393224 | tf_op jit(solution)/shard_map/ppermute | solution.py:453
  46.3 10.2 %collective-permute-start.21 = (f32[4,64,128]{2,1,0:T(8,128)S(1)}, f32[4,64,128]{2,1,0:T(8,128)S(1)}, u32[]{:S(2)}, u32[]{:S(2)}) collective-permute-start(f32[4,64,128]{2,1,0:T(8,128)S(1)} %get-tuple-element.102.refs_5_.values_own), channel_id=1, source_target_pairs={{0,0},{2,2},{4,4},{6,6},{8,16},{10,18},{12,20},{14,22},{16,8},{18,... | collective-permute-start | bytes 393224 | tf_op jit(solution)/shard_map/ppermute | solution.py:464
  47.3 9.2 %collective-permute-start.18 = (f32[4,64,128]{2,1,0:T(8,128)S(1)}, f32[4,64,128]{2,1,0:T(8,128)S(1)}, u32[]{:S(2)}, u32[]{:S(2)}) collective-permute-start(f32[4,64,128]{2,1,0:T(8,128)S(1)} %collective-permute-done.17.refs_7_), channel_id=1, source_target_pairs={{0,4},{2,6},{4,0},{6,2},{8,12},{10,14},{12,8},{14,10},{16,20},{18,... | collective-permute-start | bytes 393224 | tf_op jit(solution)/shard_map/ppermute | solution.py:453
  50.9 5.6 %collective-permute-start.20 = (f32[4,64,128]{2,1,0:T(8,128)S(1)}, f32[4,64,128]{2,1,0:T(8,128)S(1)}, u32[]{:S(2)}, u32[]{:S(2)}) collective-permute-start(f32[4,64,128]{2,1,0:T(8,128)S(1)} %collective-permute-done.19.refs_9_), channel_id=1, source_target_pairs={{0,4},{2,6},{4,0},{6,2},{8,12},{10,14},{12,8},{14,10},{16,20},{18,... | collective-permute-start | bytes 393224 | tf_op jit(solution)/shard_map/ppermute | solution.py:453
  52.5 4.0 %collective-permute-start.22 = (f32[4,64,128]{2,1,0:T(8,128)S(1)}, f32[4,64,128]{2,1,0:T(8,128)S(1)}, u32[]{:S(2)}, u32[]{:S(2)}) collective-permute-start(f32[4,64,128]{2,1,0:T(8,128)S(1)} %collective-permute-done.16.refs_6_), channel_id=1, source_target_pairs={{0,0},{2,2},{4,4},{6,6},{8,16},{10,18},{12,20},{14,22},{16,8},{18,... | collective-permute-start | bytes 393224 | tf_op jit(solution)/shard_map/ppermute | solution.py:464
  58.0 6.4 %collective-permute-start.23 = (f32[4,64,256]{2,1,0:T(8,128)S(1)}, f32[4,64,256]{2,1,0:T(8,128)S(1)}, u32[]{:S(2)}, u32[]{:S(2)}) collective-permute-start(f32[4,64,256]{2,1,0:T(8,128)S(1)} %update_top.1.mine), channel_id=1, source_target_pairs={{0,1},{1,0},{2,3},{3,2},{4,5},{5,4},{6,7},{7,6},{8,9},{9,8},{10,11... | collective-permute-start | bytes 786440 | tf_op jit(solution)/shard_map/ppermute | solution.py:450
  66.0 6.5 %collective-permute-start.24 = (f32[4,64,128]{2,1,0:T(8,128)S(1)}, f32[4,64,128]{2,1,0:T(8,128)S(1)}, u32[]{:S(2)}, u32[]{:S(2)}) collective-permute-start(f32[4,64,128]{2,1,0:T(8,128)S(1)} %get-tuple-element.115), channel_id=1, source_target_pairs={{0,4},{2,6},{4,0},{6,2},{8,12},{10,14},{12,8},{14,10},{16,20},{18,... | collective-permute-start | bytes 393224 | tf_op jit(solution)/shard_map/ppermute | solution.py:453
  67.0 8.9 %collective-permute-start.26 = (f32[4,64,128]{2,1,0:T(8,128)S(1)}, f32[4,64,128]{2,1,0:T(8,128)S(1)}, u32[]{:S(2)}, u32[]{:S(2)}) collective-permute-start(f32[4,64,128]{2,1,0:T(8,128)S(1)} %get-tuple-element.117), channel_id=1, source_target_pairs={{0,4},{2,6},{4,0},{6,2},{8,12},{10,14},{12,8},{14,10},{16,20},{18,... | collective-permute-start | bytes 393224 | tf_op jit(solution)/shard_map/ppermute | solution.py:453
  68.1 8.5 %collective-permute-start.28 = (f32[4,64,128]{2,1,0:T(8,128)S(1)}, f32[4,64,128]{2,1,0:T(8,128)S(1)}, u32[]{:S(2)}, u32[]{:S(2)}) collective-permute-start(f32[4,64,128]{2,1,0:T(8,128)S(1)} %get-tuple-element.119), channel_id=1, source_target_pairs={{0,4},{2,6},{4,0},{6,2},{8,12},{10,14},{12,8},{14,10},{16,20},{18,... | collective-permute-start | bytes 393224 | tf_op jit(solution)/shard_map/ppermute | solution.py:453
  69.0 11.0 %collective-permute-start.30 = (f32[4,64,128]{2,1,0:T(8,128)S(1)}, f32[4,64,128]{2,1,0:T(8,128)S(1)}, u32[]{:S(2)}, u32[]{:S(2)}) collective-permute-start(f32[4,64,128]{2,1,0:T(8,128)S(1)} %get-tuple-element.120), channel_id=1, source_target_pairs={{0,4},{2,6},{4,0},{6,2},{8,12},{10,14},{12,8},{14,10},{16,20},{18,... | collective-permute-start | bytes 393224 | tf_op jit(solution)/shard_map/ppermute | solution.py:453
  72.5 7.6 %collective-permute-start.25 = (f32[4,64,128]{2,1,0:T(8,128)S(1)}, f32[4,64,128]{2,1,0:T(8,128)S(1)}, u32[]{:S(2)}, u32[]{:S(2)}) collective-permute-start(f32[4,64,128]{2,1,0:T(8,128)S(1)} %add.33), channel_id=1, source_target_pairs={{0,16},{2,18},{4,20},{6,22},{8,24},{10,26},{12,28},{14,30},{16,0},... | collective-permute-start | bytes 393224 | tf_op jit(solution)/shard_map/ppermute | solution.py:453
  75.9 4.2 %collective-permute-start.27 = (f32[4,64,128]{2,1,0:T(8,128)S(1)}, f32[4,64,128]{2,1,0:T(8,128)S(1)}, u32[]{:S(2)}, u32[]{:S(2)}) collective-permute-start(f32[4,64,128]{2,1,0:T(8,128)S(1)} %add.35), channel_id=1, source_target_pairs={{0,0},{2,2},{4,4},{6,6},{8,16},{10,18},{12,20},{14,22},{16,8},{18,... | collective-permute-start | bytes 393224 | tf_op jit(solution)/shard_map/ppermute | solution.py:464
  76.6 6.4 %collective-permute-start.29 = (f32[4,64,128]{2,1,0:T(8,128)S(1)}, f32[4,64,128]{2,1,0:T(8,128)S(1)}, u32[]{:S(2)}, u32[]{:S(2)}) collective-permute-start(f32[4,64,128]{2,1,0:T(8,128)S(1)} %add.37), channel_id=1, source_target_pairs={{0,8},{2,10},{4,12},{6,14},{8,0},{10,2},{12,4},{14,6},{16,24},{18,... | collective-permute-start | bytes 393224 | tf_op jit(solution)/shard_map/ppermute | solution.py:453
  83.0 5.0 %collective-permute-start.31 = (f32[4,64,128]{2,1,0:T(8,128)S(1)}, f32[4,64,128]{2,1,0:T(8,128)S(1)}, u32[]{:S(2)}, u32[]{:S(2)}) collective-permute-start(f32[4,64,128]{2,1,0:T(8,128)S(1)} %add_add_fusion.carried_own), channel_id=1, source_target_pairs={{0,1},{1,0},{2,3},{3,2},{4,5},{5,4},{6,7},{7,6},{8,9},{9,8},{10,11... | collective-permute-start | bytes 393224 | tf_op jit(solution)/shard_map/ppermute | solution.py:450
  89.6 5.0 %collective-permute-start.36 = (f32[4,64,128]{2,1,0:T(8,128)S(1)}, f32[4,64,128]{2,1,0:T(8,128)S(1)}, u32[]{:S(2)}, u32[]{:S(2)}) collective-permute-start(f32[4,64,128]{2,1,0:T(8,128)S(1)} %get-tuple-element.138), channel_id=1, source_target_pairs={{0,4},{2,6},{4,0},{6,2},{8,12},{10,14},{12,8},{14,10},{16,20},{18,... | collective-permute-start | bytes 393224 | tf_op jit(solution)/shard_map/ppermute | solution.py:453
  90.0 6.7 %collective-permute-start.34 = (f32[4,64,128]{2,1,0:T(8,128)S(1)}, f32[4,64,128]{2,1,0:T(8,128)S(1)}, u32[]{:S(2)}, u32[]{:S(2)}) collective-permute-start(f32[4,64,128]{2,1,0:T(8,128)S(1)} %get-tuple-element.136), channel_id=1, source_target_pairs={{0,4},{2,6},{4,0},{6,2},{8,12},{10,14},{12,8},{14,10},{16,20},{18,... | collective-permute-start | bytes 393224 | tf_op jit(solution)/shard_map/ppermute | solution.py:453
  91.7 5.8 %collective-permute-start.32 = (f32[4,64,128]{2,1,0:T(8,128)S(1)}, f32[4,64,128]{2,1,0:T(8,128)S(1)}, u32[]{:S(2)}, u32[]{:S(2)}) collective-permute-start(f32[4,64,128]{2,1,0:T(8,128)S(1)} %get-tuple-element.134), channel_id=1, source_target_pairs={{0,4},{2,6},{4,0},{6,2},{8,12},{10,14},{12,8},{14,10},{16,20},{18,... | collective-permute-start | bytes 393224 | tf_op jit(solution)/shard_map/ppermute | solution.py:453
  92.0 9.5 %collective-permute-start.38 = (f32[4,64,128]{2,1,0:T(8,128)S(1)}, f32[4,64,128]{2,1,0:T(8,128)S(1)}, u32[]{:S(2)}, u32[]{:S(2)}) collective-permute-start(f32[4,64,128]{2,1,0:T(8,128)S(1)} %get-tuple-element.139), channel_id=1, source_target_pairs={{0,4},{2,6},{4,0},{6,2},{8,12},{10,14},{12,8},{14,10},{16,20},{18,... | collective-permute-start | bytes 393224 | tf_op jit(solution)/shard_map/ppermute | solution.py:453
  94.7 6.9 %collective-permute-start.37 = (f32[4,64,128]{2,1,0:T(8,128)S(1)}, f32[4,64,128]{2,1,0:T(8,128)S(1)}, u32[]{:S(2)}, u32[]{:S(2)}) collective-permute-start(f32[4,64,128]{2,1,0:T(8,128)S(1)} %add.42), channel_id=1, source_target_pairs={{0,8},{2,10},{4,12},{6,14},{8,0},{10,2},{12,4},{14,6},{16,24},{18,... | collective-permute-start | bytes 393224 | tf_op jit(solution)/shard_map/ppermute | solution.py:453
  96.8 4.8 %collective-permute-start.35 = (f32[4,64,128]{2,1,0:T(8,128)S(1)}, f32[4,64,128]{2,1,0:T(8,128)S(1)}, u32[]{:S(2)}, u32[]{:S(2)}) collective-permute-start(f32[4,64,128]{2,1,0:T(8,128)S(1)} %add.41), channel_id=1, source_target_pairs={{0,0},{2,2},{4,4},{6,6},{8,16},{10,18},{12,20},{14,22},{16,8},{18,... | collective-permute-start | bytes 393224 | tf_op jit(solution)/shard_map/ppermute | solution.py:464
  97.5 9.7 %collective-permute-start.33 = (f32[4,64,128]{2,1,0:T(8,128)S(1)}, f32[4,64,128]{2,1,0:T(8,128)S(1)}, u32[]{:S(2)}, u32[]{:S(2)}) collective-permute-start(f32[4,64,128]{2,1,0:T(8,128)S(1)} %add.40), channel_id=1, source_target_pairs={{0,16},{2,18},{4,20},{6,22},{8,24},{10,26},{12,28},{14,30},{16,0},... | collective-permute-start | bytes 393224 | tf_op jit(solution)/shard_map/ppermute | solution.py:453
  107.5 1.4 %collective-permute-start.39 = (f32[2,64,256]{2,1,0:T(8,128)S(1)}, f32[2,64,256]{2,1,0:T(8,128)S(1)}, u32[]{:S(2)}, u32[]{:S(2)}) collective-permute-start(f32[2,64,256]{2,1,0:T(8,128)S(1)} %get-tuple-element.141), channel_id=1, source_target_pairs={{0,2},{2,0},{4,6},{6,4},{8,10},{10,8},{12,14},{14,12},{16,18},{18,... | collective-permute-start | bytes 393224 | tf_op jit(solution)/shard_map/ppermute | solution.py:453
  109.4 1.8 %collective-permute-start.42 = (f32[2,64,128]{2,1,0:T(8,128)S(1)}, f32[2,64,128]{2,1,0:T(8,128)S(1)}, u32[]{:S(2)}, u32[]{:S(2)}) collective-permute-start(f32[2,64,128]{2,1,0:T(8,128)S(1)} %get-tuple-element.150), channel_id=1, source_target_pairs={{0,2},{2,0},{4,6},{6,4},{8,10},{10,8},{12,14},{14,12},{16,18},{18,... | collective-permute-start | bytes 196616 | tf_op jit(solution)/shard_map/ppermute | solution.py:453
  109.6 1.6 %collective-permute-start.41 = (f32[2,64,128]{2,1,0:T(8,128)S(1)}, f32[2,64,128]{2,1,0:T(8,128)S(1)}, u32[]{:S(2)}, u32[]{:S(2)}) collective-permute-start(f32[2,64,128]{2,1,0:T(8,128)S(1)} %get-tuple-element.147), channel_id=1, source_target_pairs={{0,2},{2,0},{4,6},{6,4},{8,10},{10,8},{12,14},{14,12},{16,18},{18,... | collective-permute-start | bytes 196616 | tf_op jit(solution)/shard_map/ppermute | solution.py:453
  110.0 5.5 %collective-permute-start.40 = (f32[2,128,128]{2,1,0:T(8,128)S(1)}, f32[2,128,128]{2,1,0:T(8,128)S(1)}, u32[]{:S(2)}, u32[]{:S(2)}) collective-permute-start(f32[2,128,128]{2,1,0:T(8,128)S(1)} %get-tuple-element.143), channel_id=1, source_target_pairs={{0,1},{1,0},{2,3},{3,2},{4,5},{5,4},{6,7},{7,6},{8,9},{9,8},{10,11... | collective-permute-start | bytes 393224 | tf_op jit(solution)/shard_map/ppermute | solution.py:450

commit v4 on v3

--- a/solution.py
+++ b/solution.py
@@ -156,7 +156,10 @@
     in_specs += [pl.BlockSpec(memory_space=pltpu.VMEM)] * (len(args) - scalars)
     return pl.pallas_call(
         kernel,
-        out_shape=[jax.ShapeDtypeStruct(shape, F32) for shape in outs],
+        out_shape=[
+            jax.ShapeDtypeStruct(*out) if isinstance(out[0], tuple) else jax.ShapeDtypeStruct(out, F32)
+            for out in outs
+        ],
         in_specs=in_specs,
         out_specs=[pl.BlockSpec(memory_space=pltpu.VMEM)] * len(outs),
         scratch_shapes=list(scratch),
@@ -165,52 +168,60 @@
     )(*args)
 
 
-def prepare(kernel, name, level, own, partner, diags, outs, cost):
+def put_halves(value, high_out, low_out, at):
+    high, low = halves(value)
+    high_out[at] = high
+    low_out[at] = low
+
+
+def split_kernel(own, partner, *outs):
+    put_halves(own[0, 0].reshape(-1, own.shape[-1]), *outs[:2], 0)
+    put_halves(partner[0, 0].reshape(-1, own.shape[-1]), *outs[2:], 0)
+
+
+def split_tiles(level, own, partner):
     own = pltpu.with_memory_space_constraint(own, pltpu.HBM)
     owned, slots, depth, width = own.shape[1:]
     block_in = pl.BlockSpec((1, 1, slots, depth, width), lambda s: (level, s, 0, 0, 0))
-    diag_in = [pl.BlockSpec((1, 1) + d.shape[2:], lambda s, at=at: (at, s, 0, 0))
-               for d, at in zip(diags, (level + 1, level + 1, level, level))]
+    block_out = pl.BlockSpec((1, slots * depth, width), lambda s: (s, 0, 0))
     return pl.pallas_call(
-        kernel,
+        split_kernel,
         grid=(owned,),
-        out_shape=[jax.ShapeDtypeStruct((owned,) + shape, kind) for shape, kind in outs * 2],
-        in_specs=[block_in] * 2 + diag_in,
-        out_specs=[pl.BlockSpec((1,) + shape, lambda s: (s, 0, 0)) for shape, _ in outs * 2],
-        name=name,
-        **options(cost),
-    )(own, partner, *diags)
-
-
-def put_halves(value, high_out, low_out):
-    high, low = halves(value)
-    high_out[0] = high
-    low_out[0] = low
-
-
-def flat(tiles):
-    return tiles[0, 0].reshape(-1, tiles.shape[-1])
-
-
-def split_tiles(own, partner, *outs):
-    put_halves(flat(own), *outs[:2])
-    put_halves(flat(partner), *outs[2:])
-
-
-def both(diag, diag_other):
-    return jnp.concatenate([diag[0, 0], diag_other[0, 0]], 0)
-
-
-def diag_by_tiles(own, partner, d0, d1, d2, d3, *outs):
-    put_halves(dot3(both(d0, d2), flat(own), NT), *outs[:2])
-    put_halves(dot3(both(d1, d3), flat(partner), NT), *outs[2:])
-
-
-def gram_by_tiles(own, partner, d0, d1, d2, d3, *outs):
-    for tiles, diag, out in ((own, both(d0, d2), outs[:3]), (partner, both(d1, d3), outs[3:])):
+        out_shape=[jax.ShapeDtypeStruct((owned, slots * depth, width), BF16)] * 4,
+        in_specs=[block_in] * 2,
+        out_specs=[block_out] * 4,
+        name="split_tiles",
+        **options(2000),
+    )(own, partner)
+
+
+def whole_diag(level, diags, s):
+    own, partner, own_other, partner_other = diags
+    half = own.shape[1]
+    if s < half:
+        pair = own[level, s], own_other[level - 1, s]
+    else:
+        pair = partner[level, s % half], partner_other[level - 1, s % half]
+    return jnp.concatenate(pair, 0)
+
+
+def diag_by_tiles(d0, d1, d2, d3, *refs):
+    tiles, outs = refs[:4], refs[4:]
+    half = d0.shape[1]
+    for s in range(2 * half):
+        value = dot3(whole_diag(1, (d0, d1, d2, d3), s), part_of(tiles, s), NT)
+        put_halves(value, *(outs[:2] if s < half else outs[2:]), s % half)
+
+
+def gram_by_tiles(d0, d1, d2, d3, *refs):
+    tiles, grams, outs = refs[:4], refs[4], refs[5:]
+    half = d0.shape[1]
+    for s in range(2 * half):
+        diag = whole_diag(2, (d0, d1, d2, d3), s)
         gram = dot3(diag.T, diag, NN)
-        put_halves(dot3(gram, flat(tiles), NT), *out[:2])
-        out[2][0] = gram
+        grams[s] = gram
+        value = dot3(gram, part_of(tiles, s), NT)
+        put_halves(value, *(outs[:2] if s < half else outs[2:]), s % half)
 
 
 def part_of(parts, s):
@@ -308,22 +319,34 @@
     return mine[level - 1, s] if s < half else partner[level - 1, s % half]
 
 
-def update_lower(index, level, places, places_partner, rhs, rhs_partner, *refs):
-    tiles, pieces, (out, window) = refs[:4], refs[4:-2], refs[-2:]
+def lower_residuals(index, level, places, rhs, tiles, pieces, window):
     col = lax.axis_index("cols")
-    for s, left in enumerate(gathered(index, (places, places_partner), pieces, window)):
-        right = upper_of(level, rhs, rhs_partner, s)
+    for s, left in enumerate(gathered(index, places, pieces, window)):
+        right = upper_of(level, *rhs, s)
         zero = jnp.zeros_like(right)
         base = jnp.concatenate([jnp.where(col == 0, right, zero), jnp.where(col == 0, zero, right)], 1)
-        out[s] = base - dot3(left, part_of(tiles, s), NN)
-
-
-def level_values(mine, theirs, d0, d1, residual, values):
-    half = d0.shape[1]
-    for s in range(residual.shape[0]):
-        left = mine[s] + theirs[s]
-        residual[s] = left
-        values[s] = dot3(left, d0[1, s] if s < half else d1[1, s % half], NT)
+        yield base - dot3(left, part_of(tiles, s), NN)
+
+
+def update_middle(places, places_partner, rhs, rhs_partner, *refs):
+    tiles, diags, pieces, (own, other, window) = refs[:4], refs[4:8], refs[8:-3], refs[-3:]
+    depth = own.shape[2]
+    residuals = lower_residuals(
+        0, 1, (places, places_partner), (rhs, rhs_partner), tiles, pieces, window
+    )
+    for s, residual in enumerate(residuals):
+        values = dot3(residual, whole_diag(1, diags, s), NT)
+        own[s] = values[:, :depth]
+        other[s] = values[:, depth:]
+
+
+def update_top_low(places, places_partner, rhs, rhs_partner, *refs):
+    tiles, pieces, (out, window) = refs[:4], refs[4:-2], refs[-2:]
+    residuals = lower_residuals(
+        1, 2, (places, places_partner), (rhs, rhs_partner), tiles, pieces, window
+    )
+    for s, residual in enumerate(residuals):
+        out[s] = residual
 
 
 def update_top(places, places_partner, *refs):
@@ -354,9 +377,10 @@
 
 
 def pieces_out(totals, outs):
-    sups = outs[0].shape[0]
-    for number, out in enumerate(outs):
-        out[...] = totals[number * sups : (number + 1) * sups]
+    first = 0
+    for out in outs:
+        out[...] = totals[first : first + out.shape[0]]
+        first += out.shape[0]
 
 
 def top_carry(places, places_partner, mine, theirs, t0, t1, t2, t3, residual, *rest):
@@ -370,42 +394,28 @@
 
 
 def lowest_carry(
-    places, places_partner, residual, t0, t1, t2, t3, g0, g1, middle, d2, d3,
-    totals, solved_mine, solved_partner, other,
+    places, places_partner, residual, t0, t1, t2, t3, grams,
+    totals, solved_mine, solved_partner,
 ):
     totals[...] = jnp.zeros_like(totals)
-    half = g0.shape[0]
     col = lax.axis_index("cols")
     for s in range(residual.shape[0]):
-        gram, diag = (g0[s], d2[0, s]) if s < half else (g1[s % half], d3[0, s % half])
-        share_out(col, dot3(residual[s], gram, NN), s, solved_mine, solved_partner)
+        share_out(col, dot3(residual[s], grams[s], NN), s, solved_mine, solved_partner)
         add_terms(1, (places, places_partner), (t0, t1, t2, t3), residual[s], s, totals)
-        other[s] = dot3(middle[s], diag, NT)
 
 
 def middle_carry(
-    places, places_partner, carried_own, carried_other, values_own, values_other, t0, t1, t2, t3, lowest,
-    residual, *rest
+    places, places_partner, own, other, d0, d1, d2, d3, t0, t1, t2, t3,
+    lowest, solved_mine, solved_partner, *rest
 ):
     outs, totals = rest[:-1], rest[-1]
     totals[...] = lowest[...]
-    for s in range(values_own.shape[0]):
-        left = jnp.concatenate(
-            [values_own[s] - carried_own[s], values_other[s] - carried_other[s]], 1
-        )
-        residual[s] = left
+    for s in range(own.shape[0]):
+        left = jnp.concatenate([own[s], other[s]], 1)
         add_terms(0, (places, places_partner), (t0, t1, t2, t3), left, s, totals)
+        x = dot3(left, whole_diag(1, (d0, d1, d2, d3), s), NN)
+        share_out(lax.axis_index("cols"), x, s, solved_mine, solved_partner)
     pieces_out(totals, outs)
-
-
-def middle_solved(residual, d0, d1, d2, d3, solved_mine, solved_partner):
-    depth = solved_mine.shape[2]
-    half = d0.shape[1]
-    for s in range(residual.shape[0]):
-        diag, diag_other = (d0[1, s], d2[0, s]) if s < half else (d1[1, s % half], d3[0, s % half])
-        left = residual[s]
-        x = dot3(left[:, :depth], diag, NN) + dot3(left[:, depth:], diag_other, NN)
-        share_out(lax.axis_index("cols"), x, s, solved_mine, solved_partner)
 
 
 def last_product(values, a, b, c, d, e, d_own, d_partner, mine, partner):
@@ -460,7 +470,7 @@
 
     def swap_mid(value):
         low, high = rows_total // 4, 3 * rows_total // 4
-        pairs = [(r, r ^ 12 if low <= r < high else r) for r in range(rows_total)]
+        pairs = [(r, r ^ 12 if low <= r < high else r ^ 2) for r in range(rows_total)]
         return lax.ppermute(value, "rows", pairs)
 
     def gather_pieces(value):
@@ -469,19 +479,20 @@
         mid = swap_mid(value)
         near = swap_rows(value, 4)
         return [
-            value, beside, near, swap_x(near), far, swap_x(far), mid, swap_mid(beside)
+            value, beside, near, swap_rows(beside, 4), far, swap_x(far), mid, swap_mid(beside)
         ]
 
     def scatter_pieces(p):
         far = swap_rows(p[4] + swap_x(p[5]), 8)
         mid = swap_mid(p[6] + swap_x(p[7]))
-        near = swap_rows(p[2] + swap_x(p[3]), 4)
-        return [p[0], far, mid, near, swap_x(p[1])]
+        beside = swap_x(p[1] + swap_rows(p[3], 4))
+        near = swap_rows(p[2], 4)
+        return [p[0], near, far, mid, beside]
 
     rhs0 = rhs[0]
     rhs0_other = swap_cols(rhs0)
+    d_partner = swap_core(diag_inv)
     tiles_partner = swap_core(factor_tiles)
-    d_partner = swap_core(diag_inv)
     own_places = pl.pallas_call(
         slot_places,
         out_shape=jax.ShapeDtypeStruct((levels, owned * slots), jnp.int32),
@@ -499,61 +510,53 @@
     pieces0 = gather_pieces(values0)
 
     reach = slots * share_rows
-    tall = [((reach, block), BF16)] * 2
-    wide = [((block, reach), BF16)] * 2
+    wide = [((owned, block, reach), BF16)] * 4
     rhs, _ = after((rhs, partner))
     upper, partner = call(
         turned_rhs, "turned_rhs", [(levels - 1, owned, half_columns, share_rows)] * 2, [rhs], 0
     )
     uppers = [upper, swap_core(partner)]
-    low_tiles = prepare(split_tiles, "split_tiles", 0, factor_tiles, tiles_partner, [], tall, 2000)
+    low_tiles = split_tiles(0, factor_tiles, tiles_partner)
     full = (sups, half_columns, block)
     scratch = [pltpu.VMEM(window, F32)]
-    partial = call(
-        functools.partial(update_lower, 0, 1), "update_middle", [full],
-        [*places, *uppers, *low_tiles, *pieces0], 2, scratch,
-    )[0]
-    tiles, d_other, late = after((factor_tiles, d_other, partial))
+    d_other, _ = after((d_other, (low_tiles, uppers, pieces0)))
     diags = [diag_inv, d_partner, d_other, swap_core(d_other)]
-    low_turned = prepare(
-        diag_by_tiles, "diag_by_tiles", 0, tiles, tiles_partner, diags, wide, 3000
-    )
-    late, low_turned = after((late, low_turned))
-    middle, values1 = call(
-        level_values, "level_values", [full, piece],
-        [late, swap_cols(partial), diag_inv, d_partner], 0,
-    )
+    own, other = call(
+        update_middle, "update_middle", [piece] * 2,
+        [*places, *uppers, *low_tiles, *diags, *pieces0], 2, scratch,
+    )
+    values1 = own + swap_cols(other)
     pieces1 = gather_pieces(values1)
     tiles, _ = after((factor_tiles, values1))
-    top_tiles = prepare(split_tiles, "split_tiles", 1, tiles, tiles_partner, [], tall, 2000)
+    top_tiles = split_tiles(1, tiles, tiles_partner)
     base = call(
-        functools.partial(update_lower, 1, 2), "update_top_low", [full],
+        update_top_low, "update_top_low", [full],
         [*places, *uppers, *top_tiles, *pieces0], 2, scratch,
     )[0]
 
     partial = call(
         update_top, "update_top", [full], [*places, *top_tiles, base, *pieces1], 2, scratch
     )[0]
-    tiles, _ = after((factor_tiles, partial))
-    turned = prepare(
-        gram_by_tiles, "gram_by_tiles", 1, tiles, tiles_partner, diags,
-        wide + [((block, block), F32)], 3000,
-    )
-    top_turned, grams = turned[:2] + turned[3:5], [turned[2], turned[5]]
+    top_ready, _ = after((top_tiles, partial))
+    grams, *top_turned = call(
+        gram_by_tiles, "gram_by_tiles", [(sups, block, block)] + wide, [*diags, *top_ready], 0,
+        cost=3000,
+    )
     residual, *out = call(
         top_carry, "top_carry", [full] + [piece] * PIECES,
         [*places, partial, swap_cols(partial), *top_turned], 2, scratch,
     )
-    carried = sum(scatter_pieces(out))
-    residual, _ = after((residual, carried))
-    lowest, mine2, partner2, values1_other = call(
-        lowest_carry, "lowest_carry", [window, shared, shared, piece],
-        [*places, residual, *top_turned, *grams, middle, *diags[2:]], 2, cost=2000,
-    )
-
-    residual, *out = call(
-        middle_carry, "middle_carry", [full] + [piece] * PIECES,
-        [*places, carried, swap_cols(carried), values1, values1_other, *low_turned, lowest],
+    carried = values1 - functools.reduce(jnp.add, scatter_pieces(out))
+    residual, low_ready, _ = after((residual, low_tiles, carried))
+    low_turned = call(diag_by_tiles, "diag_by_tiles", wide, [*diags, *low_ready], 0, cost=3000)
+    lowest, mine2, partner2 = call(
+        lowest_carry, "lowest_carry", [window, shared, shared],
+        [*places, residual, *top_turned, grams], 2, cost=2000,
+    )
+
+    mine1, partner1, *out = call(
+        middle_carry, "middle_carry", [shared, shared] + [piece] * PIECES,
+        [*places, carried, swap_cols(carried), *diags, *low_turned, lowest],
         2, scratch,
     )
 
@@ -567,10 +570,7 @@
     )
     own = own + swap_cols(other)
 
-    residual, partner2, _ = after((residual, partner2, other))
-    mine1, partner1 = call(
-        middle_solved, "middle_solved", [shared, shared], [residual, *diags], 0
-    )
+    partner1, partner2, _ = after((partner1, partner2, mine))
     result_upper = call(
         turned_upper, "turned_upper", [(levels - 1, owned, share_rows, columns)],
         [mine2, swap_core(partner2), mine1, swap_core(partner1)], 0,

time: 117 us -> 110 us (0.940)
  starting transfers between devices: 52.9 us -> 49.6 us
  Pallas kernels: 24.8 us -> 22.5 us
    ppermute x31, starting transfers between devices: 40.1 us -> 33.1 us  [swap_rows(): lax.ppermute(value, 'rows', [(r, r ^ bits) for r in range(rows_total)])]
    ppermute x31, waiting for transfers between devices: 23.8 us -> 20 us  [swap_rows(): lax.ppermute(value, 'rows', [(r, r ^ bits) for r in range(rows_total)])]
    ppermute x6, starting transfers between devices: 3.97 us -> 6.99 us  [swap_mid(): return lax.ppermute(value, 'rows', pairs)]
    pallas_call x16 -> x14, Pallas kernels: 22 us -> 19.7 us  [the longest x12 15.8 us: call(): pl.pallas_call(kernel, out_shape=[jax.ShapeDtypeStruct(*out) if isinstanc...]
    ppermute x6, waiting for transfers between devices: 10.2 us -> 12 us  [swap_cols(): return lax.ppermute(value, 'cols', [(0, 1), (1, 0)])]
    ppermute x6, waiting for transfers between devices: 0.02 us -> 1.42 us  [swap_mid(): return lax.ppermute(value, 'rows', pairs)]
  transfers between devices with their start and end apart: 43 -> 43, of which waited for: 16 -> 19; matrix products, arithmetic and copies ran while one was open for 2% -> 2% of each run, Pallas kernels for 16% -> 13%
where the time goes in v4:
time: 110 us
  starting transfers between devices  49.6 us (45%)
  waiting for transfers between devices  33.5 us (30%)
  Pallas kernels  22.5 us (20%)
  local copies, waits for them, and re-layouts  3.36 us (3%)
    ppermute x31, starting transfers between devices, swap_rows(): lax.ppermute(value, 'rows', [(r, r ^ bits) for r in range(rows_total)])  33.1 us
    ppermute x31, waiting for transfers between devices, swap_rows(): lax.ppermute(value, 'rows', [(r, r ^ bits) for r in range(rows_total)])  20 us
    pallas_call x12, Pallas kernels, call(): pl.pallas_call(kernel, out_shape=[jax.ShapeDtypeStruct(*out) if isinstanc...  15.8 us
    ppermute x6, waiting for transfers between devices, swap_cols(): return lax.ppermute(value, 'cols', [(0, 1), (1, 0)])  12 us
    ppermute x6, starting transfers between devices, swap_cols(): return lax.ppermute(value, 'cols', [(0, 1), (1, 0)])  9.47 us
    ppermute x6, starting transfers between devices, swap_mid(): return lax.ppermute(value, 'rows', pairs)  6.99 us
    pallas_call x2, Pallas kernels, split_tiles(): pl.pallas_call(split_kernel, grid=(owned,), out_shape=[jax.ShapeDtypeStru...  3.87 us
  transfers between devices with their start and end apart: 43, of which 19 were waited for; matrix products, arithmetic and copies ran while one was open for 2% of the time, Pallas kernels for 13%

profile of v4, /device:TPU:0, one launch (start us, length us, event | category | flops | bytes accessed | tf_op | source)
XLA Modules:
  0.0 110.1 jit_solution(8610356100239362671)
XLA Ops:
  1.4 3.0 %collective-permute-start.3 = (f32[2,128,128]{2,1,0:T(8,128)S(1)}, f32[2,128,128]{2,1,0:T(8,128)S(1)}, u32[]{:S(2)}, u32[]{:S(2)}) collective-permute-start(f32[2,128,128]{2,1,0:T(8,128)S(1)} %slice_bitcast_fusion.rhs_own), channel_id=1, source_target_pairs={{0,1},{1,0},{2,3},{3,2},{4,5},{5,4},{6,7},{7,6},{8,9},{9,8},{10,11... | collective-permute-start | bytes 393224 | tf_op jit(solution)/shard_map/ppermute | solution.py:460
  7.0 1.5 %slot_places.1.places = s32[3,16]{1,0:T(4,128)S(1)} custom-call(s32[2,2,8]{2,1,0:T(2,128)S(1)} %copy-done.2, s32[2,2]{1,0:T(2,128)S(1)} %copy-done.3), custom_call_target="tpu_custom_call" | custom-call | flops 500000000 | tf_op jit(solution)/shard_map/slot_places/pallas_call | solution.py:496
  8.6 1.1 %collective-permute-done.places_partner = s32[3,16]{1,0:T(4,128)S(1)} collective-permute-done((s32[3,16]{1,0:T(4,128)S(1)}, s32[3,16]{1,0:T(4,128)S(1)}, u32[]{:S(2)}, u32[]{:S(2)}) %collective-permute-start) | collective-permute-done | bytes 224 | tf_op jit(solution)/shard_map/ppermute | solution.py:463
  9.7 1.3 %first_values.1 = (f32[2,64,128]{2,1,0:T(8,128)S(1)}, f32[2,64,128]{2,1,0:T(8,128)S(1)}) custom-call(f32[2,128,128]{2,1,0:T(8,128)S(1)} %slice_bitcast_fusion.rhs_own, f32[2,128,128]{2,1,0:T(8,128)S(1)} %collective-permute-done.3.rhs_other, f32[3,2,128,256]{3,2,1,0:T(8,128)} %d_own.1), custom_call_target="tpu_custom_call" | custom-call | flops 500000000 | tf_op jit(solution)/shard_map/first_values/pallas_call | solution.py:249
  12.3 2.0 %collective-permute-start.7 = (f32[4,64,128]{2,1,0:T(8,128)S(1)}, f32[4,64,128]{2,1,0:T(8,128)S(1)}, u32[]{:S(2)}, u32[]{:S(2)}) collective-permute-start(f32[4,64,128]{2,1,0:T(8,128)S(1)} %constant_dynamic-update-slice_fusion.refs_8_.refs_4_.values), channel_id=1, source_target_pairs={{0,4},{2,6},{4,0},{6,2},{8,12},{10,14},{12,8},{14,10},{16,20},{18,... | collective-permute-start | bytes 393224 | tf_op jit(solution)/shard_map/ppermute | solution.py:463
  14.3 2.6 %collective-permute-start.10 = (f32[4,64,128]{2,1,0:T(8,128)S(1)}, f32[4,64,128]{2,1,0:T(8,128)S(1)}, u32[]{:S(2)}, u32[]{:S(2)}) collective-permute-start(f32[4,64,128]{2,1,0:T(8,128)S(1)} %constant_dynamic-update-slice_fusion.refs_8_.refs_4_.values), channel_id=1, source_target_pairs={{0,16},{2,18},{4,20},{6,22},{8,24},{10,26},{12,28},{14,30},{16,0},... | collective-permute-start | bytes 393224 | tf_op jit(solution)/shard_map/ppermute | solution.py:463
  17.5 2.0 %collective-permute-done.6.refs_6_.d2 = f32[2,2,128,256]{3,2,1,0:T(8,128)S(1)} collective-permute-done((f32[2,2,128,256]{3,2,1,0:T(8,128)S(1)}, f32[2,2,128,256]{3,2,1,0:T(8,128)S(1)}, u32[]{:S(2)}, u32[]{:S(2)}) %collective-permute-start.6) | collective-permute-done | bytes 524320 | tf_op jit(solution)/shard_map/ppermute | solution.py:460
  19.4 1.8 %collective-permute-start.8 = (f32[4,64,128]{2,1,0:T(8,128)S(1)}, f32[4,64,128]{2,1,0:T(8,128)S(1)}, u32[]{:S(2)}, u32[]{:S(2)}) collective-permute-start(f32[4,64,128]{2,1,0:T(8,128)S(1)} %constant_dynamic-update-slice_fusion.refs_8_.refs_4_.values), channel_id=1, source_target_pairs={{0,8},{2,10},{4,12},{6,14},{8,0},{10,2},{12,4},{14,6},{16,24},{18,... | collective-permute-start | bytes 393224 | tf_op jit(solution)/shard_map/ppermute | solution.py:463
  21.2 1.5 %collective-permute-start.13 = (f32[4,64,128]{2,1,0:T(8,128)S(1)}, f32[4,64,128]{2,1,0:T(8,128)S(1)}, u32[]{:S(2)}, u32[]{:S(2)}) collective-permute-start(f32[4,64,128]{2,1,0:T(8,128)S(1)} %collective-permute-done.7.refs_9_.refs_5_), channel_id=1, source_target_pairs={{0,4},{2,6},{4,0},{6,2},{8,16},{10,18},{12,20},{14,22},{16,8},{18,... | collective-permute-start | bytes 393224 | tf_op jit(solution)/shard_map/ppermute | solution.py:474
  22.7 1.7 %collective-permute-start.9 = (f32[4,64,128]{2,1,0:T(8,128)S(1)}, f32[4,64,128]{2,1,0:T(8,128)S(1)}, u32[]{:S(2)}, u32[]{:S(2)}) collective-permute-start(f32[4,64,128]{2,1,0:T(8,128)S(1)} %collective-permute-done.7.refs_9_.refs_5_), channel_id=1, source_target_pairs={{0,8},{2,10},{4,12},{6,14},{8,0},{10,2},{12,4},{14,6},{16,24},{18,... | collective-permute-start | bytes 393224 | tf_op jit(solution)/shard_map/ppermute | solution.py:463
  24.4 1.5 %collective-permute-start.11 = (f32[4,64,128]{2,1,0:T(8,128)S(1)}, f32[4,64,128]{2,1,0:T(8,128)S(1)}, u32[]{:S(2)}, u32[]{:S(2)}) collective-permute-start(f32[4,64,128]{2,1,0:T(8,128)S(1)} %collective-permute-done.10.refs_12_.refs_8_), channel_id=1, source_target_pairs={{0,4},{2,6},{4,0},{6,2},{8,12},{10,14},{12,8},{14,10},{16,20},{18,... | collective-permute-start | bytes 393224 | tf_op jit(solution)/shard_map/ppermute | solution.py:463
  25.9 1.8 %split_tiles.2 = (bf16[2,1024,256]{2,1,0:T(8,128)(2,1)S(1)}, bf16[2,1024,256]{2,1,0:T(8,128)(2,1)S(1)}, bf16[2,1024,256]{2,1,0:T(8,128)(2,1)S(1)}, bf16[2,1024,256]{2,1,0:T(8,128)(2,1)S(1)}) custom-call(f32[2,2,8,128,256]{4,3,2,1,0:T(8,128)} %own.2, f32[2,2,8,128,256]{4,3,2,1,0:T(8,128)S(1)} %collective-permute-done.1.partner), custom_call_target="tpu_custom_call" | custom-call | flops 2000000000 | tf_op jit(solution)/shard_map/split_tiles/pallas_call | solution.py:187
  29.4 1.9 %collective-permute-done.14.refs_7_.d3 = f32[2,2,128,256]{3,2,1,0:T(8,128)S(1)} collective-permute-done((f32[2,2,128,256]{3,2,1,0:T(8,128)S(1)}, f32[2,2,128,256]{3,2,1,0:T(8,128)S(1)}, u32[]{:S(2)}, u32[]{:S(2)}) %collective-permute-start.14) | collective-permute-done | bytes 524320 | tf_op jit(solution)/shard_map/ppermute | solution.py:463
  31.3 2.7 %update_middle.1 = (f32[4,64,128]{2,1,0:T(8,128)S(1)}, f32[4,64,128]{2,1,0:T(8,128)S(1)}) custom-call(s32[3,16]{1,0:T(4,128)S(1)} %slot_places.1.places, s32[3,16]{1,0:T(4,128)S(1)} %collective-permute-done.places_partner, f32[2,2,64,128]{3,2,1,0:T(8,128)S(1)} %get-tuple-element.82.rhs, f32[2,2,64,128]{3,2,1,0:T(8,128)S(1)} %collective-permute-done.5.rhs_partner, ...), custom_call_target="tpu_custom_call" | custom-call | flops 1000000000 | tf_op jit(solution)/shard_map/update_middle/pallas_call | solution.py:157
  33.9 1.6 %collective-permute-start.15 = (f32[4,64,128]{2,1,0:T(8,128)S(1)}, f32[4,64,128]{2,1,0:T(8,128)S(1)}, u32[]{:S(2)}, u32[]{:S(2)}) collective-permute-start(f32[4,64,128]{2,1,0:T(8,128)S(1)} %get-tuple-element.93), channel_id=1, source_target_pairs={{0,1},{1,0},{2,3},{3,2},{4,5},{5,4},{6,7},{7,6},{8,9},{9,8},{10,11... | collective-permute-start | bytes 393224 | tf_op jit(solution)/shard_map/ppermute | solution.py:460
  35.5 4.0 %collective-permute-done.15 = f32[4,64,128]{2,1,0:T(8,128)S(1)} collective-permute-done((f32[4,64,128]{2,1,0:T(8,128)S(1)}, f32[4,64,128]{2,1,0:T(8,128)S(1)}, u32[]{:S(2)}, u32[]{:S(2)}) %collective-permute-start.15) | collective-permute-done | bytes 131104 | tf_op jit(solution)/shard_map/ppermute | solution.py:460
  39.6 1.6 %collective-permute-start.16 = (f32[4,64,128]{2,1,0:T(8,128)S(1)}, f32[4,64,128]{2,1,0:T(8,128)S(1)}, u32[]{:S(2)}, u32[]{:S(2)}) collective-permute-start(f32[4,64,128]{2,1,0:T(8,128)S(1)} %add.36.refs_5_), channel_id=1, source_target_pairs={{0,4},{2,6},{4,0},{6,2},{8,12},{10,14},{12,8},{14,10},{16,20},{18,... | collective-permute-start | bytes 393224 | tf_op jit(solution)/shard_map/ppermute | solution.py:463
  41.1 1.9 %collective-permute-start.19 = (f32[4,64,128]{2,1,0:T(8,128)S(1)}, f32[4,64,128]{2,1,0:T(8,128)S(1)}, u32[]{:S(2)}, u32[]{:S(2)}) collective-permute-start(f32[4,64,128]{2,1,0:T(8,128)S(1)} %add.36.refs_5_), channel_id=1, source_target_pairs={{0,16},{2,18},{4,20},{6,22},{8,24},{10,26},{12,28},{14,30},{16,0},... | collective-permute-start | bytes 393224 | tf_op jit(solution)/shard_map/ppermute | solution.py:463
  43.0 1.5 %collective-permute-start.17 = (f32[4,64,128]{2,1,0:T(8,128)S(1)}, f32[4,64,128]{2,1,0:T(8,128)S(1)}, u32[]{:S(2)}, u32[]{:S(2)}) collective-permute-start(f32[4,64,128]{2,1,0:T(8,128)S(1)} %add.36.refs_5_), channel_id=1, source_target_pairs={{0,8},{2,10},{4,12},{6,14},{8,0},{10,2},{12,4},{14,6},{16,24},{18,... | collective-permute-start | bytes 393224 | tf_op jit(solution)/shard_map/ppermute | solution.py:463
  44.4 1.5 %collective-permute-start.21 = (f32[4,64,128]{2,1,0:T(8,128)S(1)}, f32[4,64,128]{2,1,0:T(8,128)S(1)}, u32[]{:S(2)}, u32[]{:S(2)}) collective-permute-start(f32[4,64,128]{2,1,0:T(8,128)S(1)} %add.36.refs_5_), channel_id=1, source_target_pairs={{0,4},{2,6},{4,0},{6,2},{8,16},{10,18},{12,20},{14,22},{16,8},{18,... | collective-permute-start | bytes 393224 | tf_op jit(solution)/shard_map/ppermute | solution.py:474
  46.6 3.3 %collective-permute-done.19.refs_9_ = f32[4,64,128]{2,1,0:T(8,128)S(1)} collective-permute-done((f32[4,64,128]{2,1,0:T(8,128)S(1)}, f32[4,64,128]{2,1,0:T(8,128)S(1)}, u32[]{:S(2)}, u32[]{:S(2)}) %collective-permute-start.19) | collective-permute-done | bytes 131104 | tf_op jit(solution)/shard_map/ppermute | solution.py:463
  49.8 1.2 %collective-permute-start.20 = (f32[4,64,128]{2,1,0:T(8,128)S(1)}, f32[4,64,128]{2,1,0:T(8,128)S(1)}, u32[]{:S(2)}, u32[]{:S(2)}) collective-permute-start(f32[4,64,128]{2,1,0:T(8,128)S(1)} %collective-permute-done.19.refs_9_), channel_id=1, source_target_pairs={{0,4},{2,6},{4,0},{6,2},{8,12},{10,14},{12,8},{14,10},{16,20},{18,... | collective-permute-start | bytes 393224 | tf_op jit(solution)/shard_map/ppermute | solution.py:463
  51.0 2.0 %split_tiles.3 = (bf16[2,1024,256]{2,1,0:T(8,128)(2,1)S(1)}, bf16[2,1024,256]{2,1,0:T(8,128)(2,1)S(1)}, bf16[2,1024,256]{2,1,0:T(8,128)(2,1)S(1)}, bf16[2,1024,256]{2,1,0:T(8,128)(2,1)S(1)}) custom-call(f32[2,2,8,128,256]{4,3,2,1,0:T(8,128)} %own.2, f32[2,2,8,128,256]{4,3,2,1,0:T(8,128)S(1)} %collective-permute-done.1.partner), custom_call_target="tpu_custom_call" | custom-call | flops 2000000000 | tf_op jit(solution)/shard_map/split_tiles/pallas_call | solution.py:187
  53.1 1.5 %update_top_low.1.refs_4_ = f32[4,64,256]{2,1,0:T(8,128)S(1)} custom-call(s32[3,16]{1,0:T(4,128)S(1)} %slot_places.1.places, s32[3,16]{1,0:T(4,128)S(1)} %collective-permute-done.places_partner, f32[2,2,64,128]{3,2,1,0:T(8,128)S(1)} %get-tuple-element.82.rhs, f32[2,2,64,128]{3,2,1,0:T(8,128)S(1)} %collective-permute-done.5.rhs_partner, ...), custom_call_target="tpu_custom_call" | custom-call | flops 1000000000 | tf_op jit(solution)/shard_map/update_top_low/pallas_call | solution.py:157
  54.8 1.5 %update_top.1.mine = f32[4,64,256]{2,1,0:T(8,128)S(1)} custom-call(s32[3,16]{1,0:T(4,128)S(1)} %slot_places.1.places, s32[3,16]{1,0:T(4,128)S(1)} %collective-permute-done.places_partner, bf16[2,1024,256]{2,1,0:T(8,128)(2,1)S(1)} %get-tuple-element.99.refs_0_, bf16[2,1024,256]{2,1,0:T(8,128)(2,1)S(1)} %get-tuple-element.100.refs_1_, ...), custom_call_target="tpu_custom_call" | custom-call | flops 1000000000 | tf_op jit(solution)/shard_map/update_top/pallas_call | solution.py:157
  56.3 1.6 %collective-permute-start.23 = (f32[4,64,256]{2,1,0:T(8,128)S(1)}, f32[4,64,256]{2,1,0:T(8,128)S(1)}, u32[]{:S(2)}, u32[]{:S(2)}) collective-permute-start(f32[4,64,256]{2,1,0:T(8,128)S(1)} %update_top.1.mine), channel_id=1, source_target_pairs={{0,1},{1,0},{2,3},{3,2},{4,5},{5,4},{6,7},{7,6},{8,9},{9,8},{10,11... | collective-permute-start | bytes 786440 | tf_op jit(solution)/shard_map/ppermute | solution.py:460
  57.9 2.7 %gram_by_tiles.1 = (f32[4,256,256]{2,1,0:T(8,128)S(1)}, bf16[2,256,1024]{2,1,0:T(8,128)(2,1)S(1)}, bf16[2,256,1024]{2,1,0:T(8,128)(2,1)S(1)}, bf16[2,256,1024]{2,1,0:T(8,128)(2,1)S(1)}, bf16[2,256,1024]{2,1,0:T(8,128)(2,1)S(1)}) custom-call(f32[3,2,128,256]{3,2,1,0:T(8,128)S(1)} %copy-done, ...), custom_call_target="tpu_custom_call" | custom-call | flops 3000000000 | tf_op jit(solution)/shard_map/gram_by_tiles/pallas_call | solution.py:157
  60.5 2.2 %collective-permute-done.23.theirs = f32[4,64,256]{2,1,0:T(8,128)S(1)} collective-permute-done((f32[4,64,256]{2,1,0:T(8,128)S(1)}, f32[4,64,256]{2,1,0:T(8,128)S(1)}, u32[]{:S(2)}, u32[]{:S(2)}) %collective-permute-start.23) | collective-permute-done | bytes 262176 | tf_op jit(solution)/shard_map/ppermute | solution.py:460
  62.7 1.5 %top_carry.1 = (f32[4,64,256]{2,1,0:T(8,128)S(1)}, f32[4,64,128]{2,1,0:T(8,128)S(1)}, f32[4,64,128]{2,1,0:T(8,128)S(1)}, f32[4,64,128]{2,1,0:T(8,128)S(1)}, f32[...) custom-call(s32[3,16]{1,0:T(4,128)S(1)} %slot_places.1.places, ...), custom_call_target="tpu_custom_call" | custom-call | flops 1000000000 | tf_op jit(solution)/shard_map/top_carry/pallas_call | solution.py:157
  64.3 1.3 %collective-permute-start.25 = (f32[4,64,128]{2,1,0:T(8,128)S(1)}, f32[4,64,128]{2,1,0:T(8,128)S(1)}, u32[]{:S(2)}, u32[]{:S(2)}) collective-permute-start(f32[4,64,128]{2,1,0:T(8,128)S(1)} %get-tuple-element.110), channel_id=1, source_target_pairs={{0,4},{2,6},{4,0},{6,2},{8,12},{10,14},{12,8},{14,10},{16,20},{18,... | collective-permute-start | bytes 393224 | tf_op jit(solution)/shard_map/ppermute | solution.py:463
  66.3 2.1 %collective-permute-start.29 = (f32[4,64,128]{2,1,0:T(8,128)S(1)}, f32[4,64,128]{2,1,0:T(8,128)S(1)}, u32[]{:S(2)}, u32[]{:S(2)}) collective-permute-start(f32[4,64,128]{2,1,0:T(8,128)S(1)} %get-tuple-element.114), channel_id=1, source_target_pairs={{0,8},{2,10},{4,12},{6,14},{8,0},{10,2},{12,4},{14,6},{16,24},{18,... | collective-permute-start | bytes 393224 | tf_op jit(solution)/shard_map/ppermute | solution.py:463
  69.3 3.8 %collective-permute-start.26 = (f32[4,64,128]{2,1,0:T(8,128)S(1)}, f32[4,64,128]{2,1,0:T(8,128)S(1)}, u32[]{:S(2)}, u32[]{:S(2)}) collective-permute-start(f32[4,64,128]{2,1,0:T(8,128)S(1)} %add.38), channel_id=1, source_target_pairs={{0,16},{2,18},{4,20},{6,22},{8,24},{10,26},{12,28},{14,30},{16,0},... | collective-permute-start | bytes 393224 | tf_op jit(solution)/shard_map/ppermute | solution.py:463
  73.2 1.6 %collective-permute-start.28 = (f32[4,64,128]{2,1,0:T(8,128)S(1)}, f32[4,64,128]{2,1,0:T(8,128)S(1)}, u32[]{:S(2)}, u32[]{:S(2)}) collective-permute-start(f32[4,64,128]{2,1,0:T(8,128)S(1)} %add.40), channel_id=1, source_target_pairs={{0,4},{2,6},{4,0},{6,2},{8,16},{10,18},{12,20},{14,22},{16,8},{18,... | collective-permute-start | bytes 393224 | tf_op jit(solution)/shard_map/ppermute | solution.py:474
  75.3 3.0 %collective-permute-done.26 = f32[4,64,128]{2,1,0:T(8,128)S(1)} collective-permute-done((f32[4,64,128]{2,1,0:T(8,128)S(1)}, f32[4,64,128]{2,1,0:T(8,128)S(1)}, u32[]{:S(2)}, u32[]{:S(2)}) %collective-permute-start.26) | collective-permute-done | bytes 131104 | tf_op jit(solution)/shard_map/ppermute | solution.py:463
  78.3 1.4 %collective-permute-done.30 = f32[4,64,128]{2,1,0:T(8,128)S(1)} collective-permute-done((f32[4,64,128]{2,1,0:T(8,128)S(1)}, f32[4,64,128]{2,1,0:T(8,128)S(1)}, u32[]{:S(2)}, u32[]{:S(2)}) %collective-permute-start.30) | collective-permute-done | bytes 131104 | tf_op jit(solution)/shard_map/ppermute | solution.py:463
  79.8 1.6 %collective-permute-start.31 = (f32[4,64,128]{2,1,0:T(8,128)S(1)}, f32[4,64,128]{2,1,0:T(8,128)S(1)}, u32[]{:S(2)}, u32[]{:S(2)}) collective-permute-start(f32[4,64,128]{2,1,0:T(8,128)S(1)} %add_subtract_fusion.own), channel_id=1, source_target_pairs={{0,1},{1,0},{2,3},{3,2},{4,5},{5,4},{6,7},{7,6},{8,9},{9,8},{10,11... | collective-permute-start | bytes 393224 | tf_op jit(solution)/shard_map/ppermute | solution.py:460
  81.4 1.9 %diag_by_tiles.1 = (bf16[2,256,1024]{2,1,0:T(8,128)(2,1)S(1)}, bf16[2,256,1024]{2,1,0:T(8,128)(2,1)S(1)}, bf16[2,256,1024]{2,1,0:T(8,128)(2,1)S(1)}, bf16[2,256,1024]{2,1,0:T(8,128)(2,1)S(1)}) custom-call(f32[3,2,128,256]{3,2,1,0:T(8,128)S(1)} %copy-done, f32[3,2,128,256]{3,2,1,0:T(8,128)S(1)} %collective-permute-done.2.refs_5_.d1.d_partner, ...), custom_call_target="tpu_custom_call" | custom-call | flops 3000000000 | tf_op jit(solution)/shard_map/diag_by_tiles/pallas_call | solution.py:157
  83.3 1.7 %lowest_carry.1 = (f32[32,64,128]{2,1,0:T(8,128)S(1)}, f32[2,64,128]{2,1,0:T(8,128)S(1)}, f32[2,64,128]{2,1,0:T(8,128)S(1)}) custom-call(s32[3,16]{1,0:T(4,128)S(1)} %slot_places.1.places, s32[3,16]{1,0:T(4,128)S(1)} %collective-permute-done.places_partner, f32[4,64,256]{2,1,0:T(8,128)S(1)} %get-tuple-element.124.residual, ...), custom_call_target="tpu_custom_call" | custom-call | flops 2000000000 | tf_op jit(solution)/shard_map/lowest_carry/pallas_call | solution.py:157
  85.0 1.7 %middle_carry.1 = (f32[2,64,128]{2,1,0:T(8,128)S(1)}, f32[2,64,128]{2,1,0:T(8,128)S(1)}, f32[4,64,128]{2,1,0:T(8,128)S(1)}, f32[4,64,128]{2,1,0:T(8,128)S(1)}, f...) custom-call(s32[3,16]{1,0:T(4,128)S(1)} %slot_places.1.places, ...), custom_call_target="tpu_custom_call" | custom-call | flops 1000000000 | tf_op jit(solution)/shard_map/middle_carry/pallas_call | solution.py:157
  87.3 1.5 %collective-permute-start.35 = (f32[4,64,128]{2,1,0:T(8,128)S(1)}, f32[4,64,128]{2,1,0:T(8,128)S(1)}, u32[]{:S(2)}, u32[]{:S(2)}) collective-permute-start(f32[4,64,128]{2,1,0:T(8,128)S(1)} %get-tuple-element.132), channel_id=1, source_target_pairs={{0,4},{2,6},{4,0},{6,2},{8,12},{10,14},{12,8},{14,10},{16,20},{18,... | collective-permute-start | bytes 393224 | tf_op jit(solution)/shard_map/ppermute | solution.py:463
  89.4 1.5 %collective-permute-start.32 = (f32[4,64,128]{2,1,0:T(8,128)S(1)}, f32[4,64,128]{2,1,0:T(8,128)S(1)}, u32[]{:S(2)}, u32[]{:S(2)}) collective-permute-start(f32[4,64,128]{2,1,0:T(8,128)S(1)} %get-tuple-element.128), channel_id=1, source_target_pairs={{0,8},{2,10},{4,12},{6,14},{8,0},{10,2},{12,4},{14,6},{16,24},{18,... | collective-permute-start | bytes 393224 | tf_op jit(solution)/shard_map/ppermute | solution.py:463
  91.8 1.4 %collective-permute-start.38 = (f32[4,64,128]{2,1,0:T(8,128)S(1)}, f32[4,64,128]{2,1,0:T(8,128)S(1)}, u32[]{:S(2)}, u32[]{:S(2)}) collective-permute-start(f32[4,64,128]{2,1,0:T(8,128)S(1)} %add.46), channel_id=1, source_target_pairs={{0,4},{2,6},{4,0},{6,2},{8,12},{10,14},{12,8},{14,10},{16,20},{18,... | collective-permute-start | bytes 393224 | tf_op jit(solution)/shard_map/ppermute | solution.py:463
  93.2 1.3 %collective-permute-start.36 = (f32[4,64,128]{2,1,0:T(8,128)S(1)}, f32[4,64,128]{2,1,0:T(8,128)S(1)}, u32[]{:S(2)}, u32[]{:S(2)}) collective-permute-start(f32[4,64,128]{2,1,0:T(8,128)S(1)} %add.45), channel_id=1, source_target_pairs={{0,4},{2,6},{4,0},{6,2},{8,16},{10,18},{12,20},{14,22},{16,8},{18,... | collective-permute-start | bytes 393224 | tf_op jit(solution)/shard_map/ppermute | solution.py:474
  94.5 1.9 %collective-permute-start.34 = (f32[4,64,128]{2,1,0:T(8,128)S(1)}, f32[4,64,128]{2,1,0:T(8,128)S(1)}, u32[]{:S(2)}, u32[]{:S(2)}) collective-permute-start(f32[4,64,128]{2,1,0:T(8,128)S(1)} %add.44), channel_id=1, source_target_pairs={{0,16},{2,18},{4,20},{6,22},{8,24},{10,26},{12,28},{14,30},{16,0},... | collective-permute-start | bytes 393224 | tf_op jit(solution)/shard_map/ppermute | solution.py:463
  96.8 1.4 %collective-permute-done.36.d = f32[4,64,128]{2,1,0:T(8,128)S(1)} collective-permute-done((f32[4,64,128]{2,1,0:T(8,128)S(1)}, f32[4,64,128]{2,1,0:T(8,128)S(1)}, u32[]{:S(2)}, u32[]{:S(2)}) %collective-permute-start.36) | collective-permute-done | bytes 131104 | tf_op jit(solution)/shard_map/ppermute | solution.py:474
  98.2 3.6 %collective-permute-done.34.c = f32[4,64,128]{2,1,0:T(8,128)S(1)} collective-permute-done((f32[4,64,128]{2,1,0:T(8,128)S(1)}, f32[4,64,128]{2,1,0:T(8,128)S(1)}, u32[]{:S(2)}, u32[]{:S(2)}) %collective-permute-start.34) | collective-permute-done | bytes 131104 | tf_op jit(solution)/shard_map/ppermute | solution.py:463
  103.7 1.6 %collective-permute-start.40 = (f32[2,128,128]{2,1,0:T(8,128)S(1)}, f32[2,128,128]{2,1,0:T(8,128)S(1)}, u32[]{:S(2)}, u32[]{:S(2)}) collective-permute-start(f32[2,128,128]{2,1,0:T(8,128)S(1)} %get-tuple-element.138), channel_id=1, source_target_pairs={{0,1},{1,0},{2,3},{3,2},{4,5},{5,4},{6,7},{7,6},{8,9},{9,8},{10,11... | collective-permute-start | bytes 393224 | tf_op jit(solution)/shard_map/ppermute | solution.py:460
  105.5 3.9 %collective-permute-done.40 = f32[2,128,128]{2,1,0:T(8,128)S(1)} collective-permute-done((f32[2,128,128]{2,1,0:T(8,128)S(1)}, f32[2,128,128]{2,1,0:T(8,128)S(1)}, u32[]{:S(2)}, u32[]{:S(2)}) %collective-permute-start.40) | collective-permute-done | bytes 131104 | tf_op jit(solution)/shard_map/ppermute | solution.py:460
  (76 shorter events, 16.0 us)
Async XLA Ops:
  0.0 11.3 %copy-start.1 = (f32[3,2,128,128]{3,2,1,0:T(8,128)S(1)}, f32[3,2,128,128]{3,2,1,0:T(8,128)}, u32[]{:S(2)}) copy-start(f32[3,2,128,128]{3,2,1,0:T(8,128)} %rhs) | copy-start | bytes 1179652
  0.0 9.7 %collective-permute-start.1 = (f32[2,2,8,128,256]{4,3,2,1,0:T(8,128)}, f32[2,2,8,128,256]{4,3,2,1,0:T(8,128)S(1)}, u32[]{:S(2)}, u32[]{:S(2)}) collective-permute-start(f32[2,2,8,128,256]{4,3,2,1,0:T(8,128)} %own.2), channel_id=1, source_target_pairs={{0,2},{2,0},{4,6},{6,4},{8,10},{10,8},{12,14},{14,12},{16,18},{18,... | collective-permute-start | bytes 12582920 | tf_op jit(solution)/shard_map/ppermute | solution.py:463
  0.5 9.3 %collective-permute-start.2 = (f32[3,2,128,256]{3,2,1,0:T(8,128)}, f32[3,2,128,256]{3,2,1,0:T(8,128)S(1)}, u32[]{:S(2)}, u32[]{:S(2)}) collective-permute-start(f32[3,2,128,256]{3,2,1,0:T(8,128)} %d_own.1), channel_id=1, source_target_pairs={{0,2},{2,0},{4,6},{6,4},{8,10},{10,8},{12,14},{14,12},{16,18},{18,... | collective-permute-start | bytes 2359304 | tf_op jit(solution)/shard_map/ppermute | solution.py:463
  1.4 8.3 %collective-permute-start.3 = (f32[2,128,128]{2,1,0:T(8,128)S(1)}, f32[2,128,128]{2,1,0:T(8,128)S(1)}, u32[]{:S(2)}, u32[]{:S(2)}) collective-permute-start(f32[2,128,128]{2,1,0:T(8,128)S(1)} %slice_bitcast_fusion.rhs_own), channel_id=1, source_target_pairs={{0,1},{1,0},{2,3},{3,2},{4,5},{5,4},{6,7},{7,6},{8,9},{9,8},{10,11... | collective-permute-start | bytes 393224 | tf_op jit(solution)/shard_map/ppermute | solution.py:460
  5.5 13.9 %collective-permute-start.6 = (f32[2,2,128,256]{3,2,1,0:T(8,128)S(1)}, f32[2,2,128,256]{3,2,1,0:T(8,128)S(1)}, u32[]{:S(2)}, u32[]{:S(2)}) collective-permute-start(f32[2,2,128,256]{3,2,1,0:T(8,128)S(1)} %slice.7), channel_id=1, source_target_pairs={{0,1},{1,0},{2,3},{3,2},{4,5},{5,4},{6,7},{7,6},{8,9},{9,8},{10,11... | collective-permute-start | bytes 1572872 | tf_op jit(solution)/shard_map/ppermute | solution.py:460
  5.6 0.7 copy-start.2
  6.3 0.7 copy-start.3
  8.5 1.2 %collective-permute-start = (s32[3,16]{1,0:T(4,128)S(1)}, s32[3,16]{1,0:T(4,128)S(1)}, u32[]{:S(2)}, u32[]{:S(2)}) collective-permute-start(s32[3,16]{1,0:T(4,128)S(1)} %slot_places.1.places), channel_id=1, source_target_pairs={{0,2},{2,0},{4,6},{6,4},{8,10},{10,8},{12,14},{14,12},{16,18},{18,... | collective-permute-start | bytes 584 | tf_op jit(solution)/shard_map/ppermute | solution.py:463
  11.0 1.3 %collective-permute-start.4 = (f32[2,64,128]{2,1,0:T(8,128)S(1)}, f32[2,64,128]{2,1,0:T(8,128)S(1)}, u32[]{:S(2)}, u32[]{:S(2)}) collective-permute-start(f32[2,64,128]{2,1,0:T(8,128)S(1)} %get-tuple-element.78), channel_id=1, source_target_pairs={{0,2},{2,0},{4,6},{6,4},{8,10},{10,8},{12,14},{14,12},{16,18},{18,... | collective-permute-start | bytes 196616 | tf_op jit(solution)/shard_map/ppermute | solution.py:463
  12.3 8.9 %collective-permute-start.7 = (f32[4,64,128]{2,1,0:T(8,128)S(1)}, f32[4,64,128]{2,1,0:T(8,128)S(1)}, u32[]{:S(2)}, u32[]{:S(2)}) collective-permute-start(f32[4,64,128]{2,1,0:T(8,128)S(1)} %constant_dynamic-update-slice_fusion.refs_8_.refs_4_.values), channel_id=1, source_target_pairs={{0,4},{2,6},{4,0},{6,2},{8,12},{10,14},{12,8},{14,10},{16,20},{18,... | collective-permute-start | bytes 393224 | tf_op jit(solution)/shard_map/ppermute | solution.py:463
  14.3 16.9 %copy-start = (f32[3,2,128,256]{3,2,1,0:T(8,128)S(1)}, f32[3,2,128,256]{3,2,1,0:T(8,128)}, u32[]{:S(2)}) copy-start(f32[3,2,128,256]{3,2,1,0:T(8,128)} %d_own.1) | copy-start | bytes 2359300
  14.3 8.4 %collective-permute-start.5 = (f32[2,2,64,128]{3,2,1,0:T(8,128)S(1)}, f32[2,2,64,128]{3,2,1,0:T(8,128)S(1)}, u32[]{:S(2)}, u32[]{:S(2)}) collective-permute-start(f32[2,2,64,128]{3,2,1,0:T(8,128)S(1)} %get-tuple-element.83), channel_id=1, source_target_pairs={{0,2},{2,0},{4,6},{6,4},{8,10},{10,8},{12,14},{14,12},{16,18},{18,... | collective-permute-start | bytes 393224 | tf_op jit(solution)/shard_map/ppermute | solution.py:463
  14.3 10.1 %collective-permute-start.10 = (f32[4,64,128]{2,1,0:T(8,128)S(1)}, f32[4,64,128]{2,1,0:T(8,128)S(1)}, u32[]{:S(2)}, u32[]{:S(2)}) collective-permute-start(f32[4,64,128]{2,1,0:T(8,128)S(1)} %constant_dynamic-update-slice_fusion.refs_8_.refs_4_.values), channel_id=1, source_target_pairs={{0,16},{2,18},{4,20},{6,22},{8,24},{10,26},{12,28},{14,30},{16,0},... | collective-permute-start | bytes 393224 | tf_op jit(solution)/shard_map/ppermute | solution.py:463
  16.9 10.8 %collective-permute-start.12 = (f32[4,64,128]{2,1,0:T(8,128)S(1)}, f32[4,64,128]{2,1,0:T(8,128)S(1)}, u32[]{:S(2)}, u32[]{:S(2)}) collective-permute-start(f32[4,64,128]{2,1,0:T(8,128)S(1)} %constant_dynamic-update-slice_fusion.refs_8_.refs_4_.values), channel_id=1, source_target_pairs={{0,4},{2,6},{4,0},{6,2},{8,16},{10,18},{12,20},{14,22},{16,8},{18,... | collective-permute-start | bytes 393224 | tf_op jit(solution)/shard_map/ppermute | solution.py:474
  19.4 8.3 %collective-permute-start.8 = (f32[4,64,128]{2,1,0:T(8,128)S(1)}, f32[4,64,128]{2,1,0:T(8,128)S(1)}, u32[]{:S(2)}, u32[]{:S(2)}) collective-permute-start(f32[4,64,128]{2,1,0:T(8,128)S(1)} %constant_dynamic-update-slice_fusion.refs_8_.refs_4_.values), channel_id=1, source_target_pairs={{0,8},{2,10},{4,12},{6,14},{8,0},{10,2},{12,4},{14,6},{16,24},{18,... | collective-permute-start | bytes 393224 | tf_op jit(solution)/shard_map/ppermute | solution.py:463
  21.2 6.5 %collective-permute-start.13 = (f32[4,64,128]{2,1,0:T(8,128)S(1)}, f32[4,64,128]{2,1,0:T(8,128)S(1)}, u32[]{:S(2)}, u32[]{:S(2)}) collective-permute-start(f32[4,64,128]{2,1,0:T(8,128)S(1)} %collective-permute-done.7.refs_9_.refs_5_), channel_id=1, source_target_pairs={{0,4},{2,6},{4,0},{6,2},{8,16},{10,18},{12,20},{14,22},{16,8},{18,... | collective-permute-start | bytes 393224 | tf_op jit(solution)/shard_map/ppermute | solution.py:474
  22.7 6.0 %collective-permute-start.9 = (f32[4,64,128]{2,1,0:T(8,128)S(1)}, f32[4,64,128]{2,1,0:T(8,128)S(1)}, u32[]{:S(2)}, u32[]{:S(2)}) collective-permute-start(f32[4,64,128]{2,1,0:T(8,128)S(1)} %collective-permute-done.7.refs_9_.refs_5_), channel_id=1, source_target_pairs={{0,8},{2,10},{4,12},{6,14},{8,0},{10,2},{12,4},{14,6},{16,24},{18,... | collective-permute-start | bytes 393224 | tf_op jit(solution)/shard_map/ppermute | solution.py:463
  24.4 5.0 %collective-permute-start.11 = (f32[4,64,128]{2,1,0:T(8,128)S(1)}, f32[4,64,128]{2,1,0:T(8,128)S(1)}, u32[]{:S(2)}, u32[]{:S(2)}) collective-permute-start(f32[4,64,128]{2,1,0:T(8,128)S(1)} %collective-permute-done.10.refs_12_.refs_8_), channel_id=1, source_target_pairs={{0,4},{2,6},{4,0},{6,2},{8,12},{10,14},{12,8},{14,10},{16,20},{18,... | collective-permute-start | bytes 393224 | tf_op jit(solution)/shard_map/ppermute | solution.py:463
  29.4 1.9 %collective-permute-start.14 = (f32[2,2,128,256]{3,2,1,0:T(8,128)S(1)}, f32[2,2,128,256]{3,2,1,0:T(8,128)S(1)}, u32[]{:S(2)}, u32[]{:S(2)}) collective-permute-start(f32[2,2,128,256]{3,2,1,0:T(8,128)S(1)} %collective-permute-done.6.refs_6_.d2), channel_id=1, source_target_pairs={{0,2},{2,0},{4,6},{6,4},{8,10},{10,8},{12,14},{14,12},{16,18},{18,... | collective-permute-start | bytes 1572872 | tf_op jit(solution)/shard_map/ppermute | solution.py:463
  33.9 5.6 %collective-permute-start.15 = (f32[4,64,128]{2,1,0:T(8,128)S(1)}, f32[4,64,128]{2,1,0:T(8,128)S(1)}, u32[]{:S(2)}, u32[]{:S(2)}) collective-permute-start(f32[4,64,128]{2,1,0:T(8,128)S(1)} %get-tuple-element.93), channel_id=1, source_target_pairs={{0,1},{1,0},{2,3},{3,2},{4,5},{5,4},{6,7},{7,6},{8,9},{9,8},{10,11... | collective-permute-start | bytes 393224 | tf_op jit(solution)/shard_map/ppermute | solution.py:460
  39.6 6.4 %collective-permute-start.16 = (f32[4,64,128]{2,1,0:T(8,128)S(1)}, f32[4,64,128]{2,1,0:T(8,128)S(1)}, u32[]{:S(2)}, u32[]{:S(2)}) collective-permute-start(f32[4,64,128]{2,1,0:T(8,128)S(1)} %add.36.refs_5_), channel_id=1, source_target_pairs={{0,4},{2,6},{4,0},{6,2},{8,12},{10,14},{12,8},{14,10},{16,20},{18,... | collective-permute-start | bytes 393224 | tf_op jit(solution)/shard_map/ppermute | solution.py:463
  41.1 8.7 %collective-permute-start.19 = (f32[4,64,128]{2,1,0:T(8,128)S(1)}, f32[4,64,128]{2,1,0:T(8,128)S(1)}, u32[]{:S(2)}, u32[]{:S(2)}) collective-permute-start(f32[4,64,128]{2,1,0:T(8,128)S(1)} %add.36.refs_5_), channel_id=1, source_target_pairs={{0,16},{2,18},{4,20},{6,22},{8,24},{10,26},{12,28},{14,30},{16,0},... | collective-permute-start | bytes 393224 | tf_op jit(solution)/shard_map/ppermute | solution.py:463
  43.0 11.6 %collective-permute-start.17 = (f32[4,64,128]{2,1,0:T(8,128)S(1)}, f32[4,64,128]{2,1,0:T(8,128)S(1)}, u32[]{:S(2)}, u32[]{:S(2)}) collective-permute-start(f32[4,64,128]{2,1,0:T(8,128)S(1)} %add.36.refs_5_), channel_id=1, source_target_pairs={{0,8},{2,10},{4,12},{6,14},{8,0},{10,2},{12,4},{14,6},{16,24},{18,... | collective-permute-start | bytes 393224 | tf_op jit(solution)/shard_map/ppermute | solution.py:463
  44.4 10.1 %collective-permute-start.21 = (f32[4,64,128]{2,1,0:T(8,128)S(1)}, f32[4,64,128]{2,1,0:T(8,128)S(1)}, u32[]{:S(2)}, u32[]{:S(2)}) collective-permute-start(f32[4,64,128]{2,1,0:T(8,128)S(1)} %add.36.refs_5_), channel_id=1, source_target_pairs={{0,4},{2,6},{4,0},{6,2},{8,16},{10,18},{12,20},{14,22},{16,8},{18,... | collective-permute-start | bytes 393224 | tf_op jit(solution)/shard_map/ppermute | solution.py:474
  45.9 8.6 %collective-permute-start.18 = (f32[4,64,128]{2,1,0:T(8,128)S(1)}, f32[4,64,128]{2,1,0:T(8,128)S(1)}, u32[]{:S(2)}, u32[]{:S(2)}) collective-permute-start(f32[4,64,128]{2,1,0:T(8,128)S(1)} %collective-permute-done.16.refs_6_), channel_id=1, source_target_pairs={{0,8},{2,10},{4,12},{6,14},{8,0},{10,2},{12,4},{14,6},{16,24},{18,... | collective-permute-start | bytes 393224 | tf_op jit(solution)/shard_map/ppermute | solution.py:463
  45.9 8.8 %collective-permute-start.22 = (f32[4,64,128]{2,1,0:T(8,128)S(1)}, f32[4,64,128]{2,1,0:T(8,128)S(1)}, u32[]{:S(2)}, u32[]{:S(2)}) collective-permute-start(f32[4,64,128]{2,1,0:T(8,128)S(1)} %collective-permute-done.16.refs_6_), channel_id=1, source_target_pairs={{0,4},{2,6},{4,0},{6,2},{8,16},{10,18},{12,20},{14,22},{16,8},{18,... | collective-permute-start | bytes 393224 | tf_op jit(solution)/shard_map/ppermute | solution.py:474
  49.8 5.0 %collective-permute-start.20 = (f32[4,64,128]{2,1,0:T(8,128)S(1)}, f32[4,64,128]{2,1,0:T(8,128)S(1)}, u32[]{:S(2)}, u32[]{:S(2)}) collective-permute-start(f32[4,64,128]{2,1,0:T(8,128)S(1)} %collective-permute-done.19.refs_9_), channel_id=1, source_target_pairs={{0,4},{2,6},{4,0},{6,2},{8,12},{10,14},{12,8},{14,10},{16,20},{18,... | collective-permute-start | bytes 393224 | tf_op jit(solution)/shard_map/ppermute | solution.py:463
  56.3 6.4 %collective-permute-start.23 = (f32[4,64,256]{2,1,0:T(8,128)S(1)}, f32[4,64,256]{2,1,0:T(8,128)S(1)}, u32[]{:S(2)}, u32[]{:S(2)}) collective-permute-start(f32[4,64,256]{2,1,0:T(8,128)S(1)} %update_top.1.mine), channel_id=1, source_target_pairs={{0,1},{1,0},{2,3},{3,2},{4,5},{5,4},{6,7},{7,6},{8,9},{9,8},{10,11... | collective-permute-start | bytes 786440 | tf_op jit(solution)/shard_map/ppermute | solution.py:460
  64.3 5.0 %collective-permute-start.25 = (f32[4,64,128]{2,1,0:T(8,128)S(1)}, f32[4,64,128]{2,1,0:T(8,128)S(1)}, u32[]{:S(2)}, u32[]{:S(2)}) collective-permute-start(f32[4,64,128]{2,1,0:T(8,128)S(1)} %get-tuple-element.110), channel_id=1, source_target_pairs={{0,4},{2,6},{4,0},{6,2},{8,12},{10,14},{12,8},{14,10},{16,20},{18,... | collective-permute-start | bytes 393224 | tf_op jit(solution)/shard_map/ppermute | solution.py:463
  65.6 7.6 %collective-permute-start.27 = (f32[4,64,128]{2,1,0:T(8,128)S(1)}, f32[4,64,128]{2,1,0:T(8,128)S(1)}, u32[]{:S(2)}, u32[]{:S(2)}) collective-permute-start(f32[4,64,128]{2,1,0:T(8,128)S(1)} %get-tuple-element.112), channel_id=1, source_target_pairs={{0,4},{2,6},{4,0},{6,2},{8,12},{10,14},{12,8},{14,10},{16,20},{18,... | collective-permute-start | bytes 393224 | tf_op jit(solution)/shard_map/ppermute | solution.py:463
  66.3 8.4 %collective-permute-start.29 = (f32[4,64,128]{2,1,0:T(8,128)S(1)}, f32[4,64,128]{2,1,0:T(8,128)S(1)}, u32[]{:S(2)}, u32[]{:S(2)}) collective-permute-start(f32[4,64,128]{2,1,0:T(8,128)S(1)} %get-tuple-element.114), channel_id=1, source_target_pairs={{0,8},{2,10},{4,12},{6,14},{8,0},{10,2},{12,4},{14,6},{16,24},{18,... | collective-permute-start | bytes 393224 | tf_op jit(solution)/shard_map/ppermute | solution.py:463
  68.4 6.9 %collective-permute-start.24 = (f32[4,64,128]{2,1,0:T(8,128)S(1)}, f32[4,64,128]{2,1,0:T(8,128)S(1)}, u32[]{:S(2)}, u32[]{:S(2)}) collective-permute-start(f32[4,64,128]{2,1,0:T(8,128)S(1)} %get-tuple-element.108), channel_id=1, source_target_pairs={{0,8},{2,10},{4,12},{6,14},{8,0},{10,2},{12,4},{14,6},{16,24},{18,... | collective-permute-start | bytes 393224 | tf_op jit(solution)/shard_map/ppermute | solution.py:463
  69.3 9.0 %collective-permute-start.26 = (f32[4,64,128]{2,1,0:T(8,128)S(1)}, f32[4,64,128]{2,1,0:T(8,128)S(1)}, u32[]{:S(2)}, u32[]{:S(2)}) collective-permute-start(f32[4,64,128]{2,1,0:T(8,128)S(1)} %add.38), channel_id=1, source_target_pairs={{0,16},{2,18},{4,20},{6,22},{8,24},{10,26},{12,28},{14,30},{16,0},... | collective-permute-start | bytes 393224 | tf_op jit(solution)/shard_map/ppermute | solution.py:463
  73.2 5.2 %collective-permute-start.28 = (f32[4,64,128]{2,1,0:T(8,128)S(1)}, f32[4,64,128]{2,1,0:T(8,128)S(1)}, u32[]{:S(2)}, u32[]{:S(2)}) collective-permute-start(f32[4,64,128]{2,1,0:T(8,128)S(1)} %add.40), channel_id=1, source_target_pairs={{0,4},{2,6},{4,0},{6,2},{8,16},{10,18},{12,20},{14,22},{16,8},{18,... | collective-permute-start | bytes 393224 | tf_op jit(solution)/shard_map/ppermute | solution.py:474
  74.7 5.0 %collective-permute-start.30 = (f32[4,64,128]{2,1,0:T(8,128)S(1)}, f32[4,64,128]{2,1,0:T(8,128)S(1)}, u32[]{:S(2)}, u32[]{:S(2)}) collective-permute-start(f32[4,64,128]{2,1,0:T(8,128)S(1)} %add.42), channel_id=1, source_target_pairs={{0,4},{2,6},{4,0},{6,2},{8,12},{10,14},{12,8},{14,10},{16,20},{18,... | collective-permute-start | bytes 393224 | tf_op jit(solution)/shard_map/ppermute | solution.py:463
  79.8 5.1 %collective-permute-start.31 = (f32[4,64,128]{2,1,0:T(8,128)S(1)}, f32[4,64,128]{2,1,0:T(8,128)S(1)}, u32[]{:S(2)}, u32[]{:S(2)}) collective-permute-start(f32[4,64,128]{2,1,0:T(8,128)S(1)} %add_subtract_fusion.own), channel_id=1, source_target_pairs={{0,1},{1,0},{2,3},{3,2},{4,5},{5,4},{6,7},{7,6},{8,9},{9,8},{10,11... | collective-permute-start | bytes 393224 | tf_op jit(solution)/shard_map/ppermute | solution.py:460
  86.7 5.0 %collective-permute-start.37 = (f32[4,64,128]{2,1,0:T(8,128)S(1)}, f32[4,64,128]{2,1,0:T(8,128)S(1)}, u32[]{:S(2)}, u32[]{:S(2)}) collective-permute-start(f32[4,64,128]{2,1,0:T(8,128)S(1)} %get-tuple-element.134), channel_id=1, source_target_pairs={{0,8},{2,10},{4,12},{6,14},{8,0},{10,2},{12,4},{14,6},{16,24},{18,... | collective-permute-start | bytes 393224 | tf_op jit(solution)/shard_map/ppermute | solution.py:463
  87.3 5.8 %collective-permute-start.35 = (f32[4,64,128]{2,1,0:T(8,128)S(1)}, f32[4,64,128]{2,1,0:T(8,128)S(1)}, u32[]{:S(2)}, u32[]{:S(2)}) collective-permute-start(f32[4,64,128]{2,1,0:T(8,128)S(1)} %get-tuple-element.132), channel_id=1, source_target_pairs={{0,4},{2,6},{4,0},{6,2},{8,12},{10,14},{12,8},{14,10},{16,20},{18,... | collective-permute-start | bytes 393224 | tf_op jit(solution)/shard_map/ppermute | solution.py:463
  88.8 5.7 %collective-permute-start.33 = (f32[4,64,128]{2,1,0:T(8,128)S(1)}, f32[4,64,128]{2,1,0:T(8,128)S(1)}, u32[]{:S(2)}, u32[]{:S(2)}) collective-permute-start(f32[4,64,128]{2,1,0:T(8,128)S(1)} %get-tuple-element.130), channel_id=1, source_target_pairs={{0,4},{2,6},{4,0},{6,2},{8,12},{10,14},{12,8},{14,10},{16,20},{18,... | collective-permute-start | bytes 393224 | tf_op jit(solution)/shard_map/ppermute | solution.py:463
  89.4 7.1 %collective-permute-start.32 = (f32[4,64,128]{2,1,0:T(8,128)S(1)}, f32[4,64,128]{2,1,0:T(8,128)S(1)}, u32[]{:S(2)}, u32[]{:S(2)}) collective-permute-start(f32[4,64,128]{2,1,0:T(8,128)S(1)} %get-tuple-element.128), channel_id=1, source_target_pairs={{0,8},{2,10},{4,12},{6,14},{8,0},{10,2},{12,4},{14,6},{16,24},{18,... | collective-permute-start | bytes 393224 | tf_op jit(solution)/shard_map/ppermute | solution.py:463
  91.8 5.0 %collective-permute-start.38 = (f32[4,64,128]{2,1,0:T(8,128)S(1)}, f32[4,64,128]{2,1,0:T(8,128)S(1)}, u32[]{:S(2)}, u32[]{:S(2)}) collective-permute-start(f32[4,64,128]{2,1,0:T(8,128)S(1)} %add.46), channel_id=1, source_target_pairs={{0,4},{2,6},{4,0},{6,2},{8,12},{10,14},{12,8},{14,10},{16,20},{18,... | collective-permute-start | bytes 393224 | tf_op jit(solution)/shard_map/ppermute | solution.py:463
  93.2 5.0 %collective-permute-start.36 = (f32[4,64,128]{2,1,0:T(8,128)S(1)}, f32[4,64,128]{2,1,0:T(8,128)S(1)}, u32[]{:S(2)}, u32[]{:S(2)}) collective-permute-start(f32[4,64,128]{2,1,0:T(8,128)S(1)} %add.45), channel_id=1, source_target_pairs={{0,4},{2,6},{4,0},{6,2},{8,16},{10,18},{12,20},{14,22},{16,8},{18,... | collective-permute-start | bytes 393224 | tf_op jit(solution)/shard_map/ppermute | solution.py:474
  94.5 7.3 %collective-permute-start.34 = (f32[4,64,128]{2,1,0:T(8,128)S(1)}, f32[4,64,128]{2,1,0:T(8,128)S(1)}, u32[]{:S(2)}, u32[]{:S(2)}) collective-permute-start(f32[4,64,128]{2,1,0:T(8,128)S(1)} %add.44), channel_id=1, source_target_pairs={{0,16},{2,18},{4,20},{6,22},{8,24},{10,26},{12,28},{14,30},{16,0},... | collective-permute-start | bytes 393224 | tf_op jit(solution)/shard_map/ppermute | solution.py:463
  102.2 1.4 %collective-permute-start.39 = (f32[2,64,256]{2,1,0:T(8,128)S(1)}, f32[2,64,256]{2,1,0:T(8,128)S(1)}, u32[]{:S(2)}, u32[]{:S(2)}) collective-permute-start(f32[2,64,256]{2,1,0:T(8,128)S(1)} %get-tuple-element.136), channel_id=1, source_target_pairs={{0,2},{2,0},{4,6},{6,4},{8,10},{10,8},{12,14},{14,12},{16,18},{18,... | collective-permute-start | bytes 393224 | tf_op jit(solution)/shard_map/ppermute | solution.py:463
  102.2 3.1 %collective-permute-start.41 = (f32[2,64,128]{2,1,0:T(8,128)S(1)}, f32[2,64,128]{2,1,0:T(8,128)S(1)}, u32[]{:S(2)}, u32[]{:S(2)}) collective-permute-start(f32[2,64,128]{2,1,0:T(8,128)S(1)} %get-tuple-element.142), channel_id=1, source_target_pairs={{0,2},{2,0},{4,6},{6,4},{8,10},{10,8},{12,14},{14,12},{16,18},{18,... | collective-permute-start | bytes 196616 | tf_op jit(solution)/shard_map/ppermute | solution.py:463
  102.7 2.6 %collective-permute-start.42 = (f32[2,64,128]{2,1,0:T(8,128)S(1)}, f32[2,64,128]{2,1,0:T(8,128)S(1)}, u32[]{:S(2)}, u32[]{:S(2)}) collective-permute-start(f32[2,64,128]{2,1,0:T(8,128)S(1)} %get-tuple-element.144), channel_id=1, source_target_pairs={{0,2},{2,0},{4,6},{6,4},{8,10},{10,8},{12,14},{14,12},{16,18},{18,... | collective-permute-start | bytes 196616 | tf_op jit(solution)/shard_map/ppermute | solution.py:463
  103.7 5.6 %collective-permute-start.40 = (f32[2,128,128]{2,1,0:T(8,128)S(1)}, f32[2,128,128]{2,1,0:T(8,128)S(1)}, u32[]{:S(2)}, u32[]{:S(2)}) collective-permute-start(f32[2,128,128]{2,1,0:T(8,128)S(1)} %get-tuple-element.138), channel_id=1, source_target_pairs={{0,1},{1,0},{2,3},{3,2},{4,5},{5,4},{6,7},{7,6},{8,9},{9,8},{10,11... | collective-permute-start | bytes 393224 | tf_op jit(solution)/shard_map/ppermute | solution.py:460

commit v5 on v4

--- a/solution.py
+++ b/solution.py
@@ -319,34 +319,22 @@
     return mine[level - 1, s] if s < half else partner[level - 1, s % half]
 
 
-def lower_residuals(index, level, places, rhs, tiles, pieces, window):
+def update_lower(index, level, places, places_partner, rhs, rhs_partner, *refs):
+    tiles, pieces, (out, window) = refs[:4], refs[4:-2], refs[-2:]
     col = lax.axis_index("cols")
-    for s, left in enumerate(gathered(index, places, pieces, window)):
-        right = upper_of(level, *rhs, s)
+    for s, left in enumerate(gathered(index, (places, places_partner), pieces, window)):
+        right = upper_of(level, rhs, rhs_partner, s)
         zero = jnp.zeros_like(right)
         base = jnp.concatenate([jnp.where(col == 0, right, zero), jnp.where(col == 0, zero, right)], 1)
-        yield base - dot3(left, part_of(tiles, s), NN)
-
-
-def update_middle(places, places_partner, rhs, rhs_partner, *refs):
-    tiles, diags, pieces, (own, other, window) = refs[:4], refs[4:8], refs[8:-3], refs[-3:]
+        out[s] = base - dot3(left, part_of(tiles, s), NN)
+
+
+def middle_values(residual, d0, d1, d2, d3, own, other):
     depth = own.shape[2]
-    residuals = lower_residuals(
-        0, 1, (places, places_partner), (rhs, rhs_partner), tiles, pieces, window
-    )
-    for s, residual in enumerate(residuals):
-        values = dot3(residual, whole_diag(1, diags, s), NT)
+    for s in range(own.shape[0]):
+        values = dot3(residual[s], whole_diag(1, (d0, d1, d2, d3), s), NT)
         own[s] = values[:, :depth]
         other[s] = values[:, depth:]
-
-
-def update_top_low(places, places_partner, rhs, rhs_partner, *refs):
-    tiles, pieces, (out, window) = refs[:4], refs[4:-2], refs[-2:]
-    residuals = lower_residuals(
-        1, 2, (places, places_partner), (rhs, rhs_partner), tiles, pieces, window
-    )
-    for s, residual in enumerate(residuals):
-        out[s] = residual
 
 
 def update_top(places, places_partner, *refs):
@@ -482,12 +470,19 @@
             value, beside, near, swap_rows(beside, 4), far, swap_x(far), mid, swap_mid(beside)
         ]
 
-    def scatter_pieces(p):
+    def scatter_upper(p):
         far = swap_rows(p[4] + swap_x(p[5]), 8)
-        mid = swap_mid(p[6] + swap_x(p[7]))
-        beside = swap_x(p[1] + swap_rows(p[3], 4))
+        beside = swap_x(p[1] + (swap_mid(p[7]) + swap_rows(p[3], 4)))
+        mid = swap_mid(p[6])
         near = swap_rows(p[2], 4)
-        return [p[0], near, far, mid, beside]
+        return [p[0], far, beside, mid, near]
+
+    def scatter_lowest(p):
+        far = swap_rows(p[4] + swap_x(p[5]), 8)
+        beside = swap_x(p[1] + (swap_mid(p[7]) + swap_rows(p[3], 4)))
+        mid = swap_mid(p[6])
+        near = swap_rows(p[2], 4)
+        return [p[0], near, mid, beside, far]
 
     rhs0 = rhs[0]
     rhs0_other = swap_cols(rhs0)
@@ -521,16 +516,17 @@
     scratch = [pltpu.VMEM(window, F32)]
     d_other, _ = after((d_other, (low_tiles, uppers, pieces0)))
     diags = [diag_inv, d_partner, d_other, swap_core(d_other)]
-    own, other = call(
-        update_middle, "update_middle", [piece] * 2,
-        [*places, *uppers, *low_tiles, *diags, *pieces0], 2, scratch,
-    )
+    partial = call(
+        functools.partial(update_lower, 0, 1), "update_middle", [full],
+        [*places, *uppers, *low_tiles, *pieces0], 2, scratch,
+    )[0]
+    own, other = call(middle_values, "middle_values", [piece] * 2, [partial, *diags], 0)
     values1 = own + swap_cols(other)
     pieces1 = gather_pieces(values1)
     tiles, _ = after((factor_tiles, values1))
     top_tiles = split_tiles(1, tiles, tiles_partner)
     base = call(
-        update_top_low, "update_top_low", [full],
+        functools.partial(update_lower, 1, 2), "update_top_low", [full],
         [*places, *uppers, *top_tiles, *pieces0], 2, scratch,
     )[0]
 
@@ -546,7 +542,7 @@
         top_carry, "top_carry", [full] + [piece] * PIECES,
         [*places, partial, swap_cols(partial), *top_turned], 2, scratch,
     )
-    carried = values1 - functools.reduce(jnp.add, scatter_pieces(out))
+    carried = values1 - functools.reduce(jnp.add, scatter_upper(out))
     residual, low_ready, _ = after((residual, low_tiles, carried))
     low_turned = call(diag_by_tiles, "diag_by_tiles", wide, [*diags, *low_ready], 0, cost=3000)
     lowest, mine2, partner2 = call(
@@ -562,7 +558,7 @@
 
     mine, partner = call(
         last_product, "last_product", [(owned, half_columns, block)] * 2,
-        [values0, *scatter_pieces(out), diag_inv, d_partner], 0,
+        [values0, *scatter_lowest(out), diag_inv, d_partner], 0,
     )
     own, other = call(
         turned_solution, "turned_solution", [(owned, share_rows, columns)] * 2,

time: 110 us -> 106 us (0.964)
  waiting for transfers between devices: 33.5 us -> 31.6 us
  Pallas kernels: 22.5 us -> 21.4 us
  starting transfers between devices: 49.6 us -> 48.5 us
    ppermute x6 -> x8, waiting for transfers between devices: 1.42 us -> 0.02 us  [swap_mid(): return lax.ppermute(value, 'rows', pairs)]
    ppermute x31 -> x29, starting transfers between devices: 33.1 us -> 31.9 us  [swap_rows(): lax.ppermute(value, 'rows', [(r, r ^ bits) for r in range(rows_total)])]
    ppermute x31 -> x29, waiting for transfers between devices: 20 us -> 19.1 us  [swap_rows(): lax.ppermute(value, 'rows', [(r, r ^ bits) for r in range(rows_total)])]
    pallas_call x12 -> x13, Pallas kernels: 15.8 us -> 14.9 us  [call(): pl.pallas_call(kernel, out_shape=[jax.ShapeDtypeStruct(*out) if isinstanc...]
    ppermute x6 -> x8, starting transfers between devices: 6.99 us -> 7.55 us  [swap_mid(): return lax.ppermute(value, 'rows', pairs)]
  transfers between devices with their start and end apart: 43 -> 43, of which waited for: 19 -> 17; matrix products, arithmetic and copies ran while one was open for 2% -> 2% of each run, Pallas kernels for 13% -> 15%
where the time goes in v5:
time: 106 us
  starting transfers between devices  48.5 us (46%)
  waiting for transfers between devices  31.6 us (30%)
  Pallas kernels  21.4 us (20%)
  local copies, waits for them, and re-layouts  3.36 us (3%)
    ppermute x29, starting transfers between devices, swap_rows(): lax.ppermute(value, 'rows', [(r, r ^ bits) for r in range(rows_total)])  31.9 us
    ppermute x29, waiting for transfers between devices, swap_rows(): lax.ppermute(value, 'rows', [(r, r ^ bits) for r in range(rows_total)])  19.1 us
    pallas_call x13, Pallas kernels, call(): pl.pallas_call(kernel, out_shape=[jax.ShapeDtypeStruct(*out) if isinstanc...  14.9 us
    ppermute x6, waiting for transfers between devices, swap_cols(): return lax.ppermute(value, 'cols', [(0, 1), (1, 0)])  12.5 us
    ppermute x6, starting transfers between devices, swap_cols(): return lax.ppermute(value, 'cols', [(0, 1), (1, 0)])  9.04 us
    ppermute x8, starting transfers between devices, swap_mid(): return lax.ppermute(value, 'rows', pairs)  7.55 us
    pallas_call x2, Pallas kernels, split_tiles(): pl.pallas_call(split_kernel, grid=(owned,), out_shape=[jax.ShapeDtypeStru...  3.67 us
  transfers between devices with their start and end apart: 43, of which 17 were waited for; matrix products, arithmetic and copies ran while one was open for 2% of the time, Pallas kernels for 15%

profile of v5, /device:TPU:0, one launch (start us, length us, event | category | flops | bytes accessed | tf_op | source)
XLA Modules:
  0.0 106.0 jit_solution(2122597267479211420)
XLA Ops:
  1.4 3.0 %collective-permute-start.3 = (f32[2,128,128]{2,1,0:T(8,128)S(1)}, f32[2,128,128]{2,1,0:T(8,128)S(1)}, u32[]{:S(2)}, u32[]{:S(2)}) collective-permute-start(f32[2,128,128]{2,1,0:T(8,128)S(1)} %slice_bitcast_fusion.rhs_own), channel_id=1, source_target_pairs={{0,1},{1,0},{2,3},{3,2},{4,5},{5,4},{6,7},{7,6},{8,9},{9,8},{10,11... | collective-permute-start | bytes 393224 | tf_op jit(solution)/shard_map/ppermute | solution.py:448
  4.5 1.1 %slice.7 = f32[2,2,128,256]{3,2,1,0:T(8,128)S(1)} slice(f32[3,2,128,256]{3,2,1,0:T(8,128)} %d_own.1), slice={[1:3], [0:2], [0:128], [0:256]} | slice | bytes 1048576 | tf_op jit(solution)/shard_map/slice | solution.py:501
  7.0 1.5 %slot_places.1.places = s32[3,16]{1,0:T(4,128)S(1)} custom-call(s32[2,2,8]{2,1,0:T(2,128)S(1)} %copy-done.2, s32[2,2]{1,0:T(2,128)S(1)} %copy-done.3), custom_call_target="tpu_custom_call" | custom-call | flops 500000000 | tf_op jit(solution)/shard_map/slot_places/pallas_call | solution.py:491
  8.6 1.1 %collective-permute-done.places_partner = s32[3,16]{1,0:T(4,128)S(1)} collective-permute-done((s32[3,16]{1,0:T(4,128)S(1)}, s32[3,16]{1,0:T(4,128)S(1)}, u32[]{:S(2)}, u32[]{:S(2)}) %collective-permute-start) | collective-permute-done | bytes 224 | tf_op jit(solution)/shard_map/ppermute | solution.py:451
  9.7 1.3 %first_values.1 = (f32[2,64,128]{2,1,0:T(8,128)S(1)}, f32[2,64,128]{2,1,0:T(8,128)S(1)}) custom-call(f32[2,128,128]{2,1,0:T(8,128)S(1)} %slice_bitcast_fusion.rhs_own, f32[2,128,128]{2,1,0:T(8,128)S(1)} %collective-permute-done.3.rhs_other, f32[3,2,128,256]{3,2,1,0:T(8,128)} %d_own.1), custom_call_target="tpu_custom_call" | custom-call | flops 500000000 | tf_op jit(solution)/shard_map/first_values/pallas_call | solution.py:249
  12.3 2.0 %collective-permute-start.6 = (f32[4,64,128]{2,1,0:T(8,128)S(1)}, f32[4,64,128]{2,1,0:T(8,128)S(1)}, u32[]{:S(2)}, u32[]{:S(2)}) collective-permute-start(f32[4,64,128]{2,1,0:T(8,128)S(1)} %constant_dynamic-update-slice_fusion.refs_4_.values), channel_id=1, source_target_pairs={{0,4},{2,6},{4,0},{6,2},{8,12},{10,14},{12,8},{14,10},{16,20},{18,... | collective-permute-start | bytes 393224 | tf_op jit(solution)/shard_map/ppermute | solution.py:451
  14.3 2.6 %collective-permute-start.9 = (f32[4,64,128]{2,1,0:T(8,128)S(1)}, f32[4,64,128]{2,1,0:T(8,128)S(1)}, u32[]{:S(2)}, u32[]{:S(2)}) collective-permute-start(f32[4,64,128]{2,1,0:T(8,128)S(1)} %constant_dynamic-update-slice_fusion.refs_4_.values), channel_id=1, source_target_pairs={{0,16},{2,18},{4,20},{6,22},{8,24},{10,26},{12,28},{14,30},{16,0},... | collective-permute-start | bytes 393224 | tf_op jit(solution)/shard_map/ppermute | solution.py:451
  17.4 2.0 %collective-permute-done.13.d2 = f32[2,2,128,256]{3,2,1,0:T(8,128)S(1)} collective-permute-done((f32[2,2,128,256]{3,2,1,0:T(8,128)S(1)}, f32[2,2,128,256]{3,2,1,0:T(8,128)S(1)}, u32[]{:S(2)}, u32[]{:S(2)}) %collective-permute-start.13) | collective-permute-done | bytes 524320 | tf_op jit(solution)/shard_map/ppermute | solution.py:448
  19.4 1.8 %collective-permute-start.7 = (f32[4,64,128]{2,1,0:T(8,128)S(1)}, f32[4,64,128]{2,1,0:T(8,128)S(1)}, u32[]{:S(2)}, u32[]{:S(2)}) collective-permute-start(f32[4,64,128]{2,1,0:T(8,128)S(1)} %constant_dynamic-update-slice_fusion.refs_4_.values), channel_id=1, source_target_pairs={{0,8},{2,10},{4,12},{6,14},{8,0},{10,2},{12,4},{14,6},{16,24},{18,... | collective-permute-start | bytes 393224 | tf_op jit(solution)/shard_map/ppermute | solution.py:451
  21.2 1.5 %collective-permute-start.12 = (f32[4,64,128]{2,1,0:T(8,128)S(1)}, f32[4,64,128]{2,1,0:T(8,128)S(1)}, u32[]{:S(2)}, u32[]{:S(2)}) collective-permute-start(f32[4,64,128]{2,1,0:T(8,128)S(1)} %collective-permute-done.6.refs_5_), channel_id=1, source_target_pairs={{0,4},{2,6},{4,0},{6,2},{8,16},{10,18},{12,20},{14,22},{16,8},{18,... | collective-permute-start | bytes 393224 | tf_op jit(solution)/shard_map/ppermute | solution.py:462
  22.7 1.7 %collective-permute-start.8 = (f32[4,64,128]{2,1,0:T(8,128)S(1)}, f32[4,64,128]{2,1,0:T(8,128)S(1)}, u32[]{:S(2)}, u32[]{:S(2)}) collective-permute-start(f32[4,64,128]{2,1,0:T(8,128)S(1)} %collective-permute-done.6.refs_5_), channel_id=1, source_target_pairs={{0,8},{2,10},{4,12},{6,14},{8,0},{10,2},{12,4},{14,6},{16,24},{18,... | collective-permute-start | bytes 393224 | tf_op jit(solution)/shard_map/ppermute | solution.py:451
  24.4 1.5 %collective-permute-start.10 = (f32[4,64,128]{2,1,0:T(8,128)S(1)}, f32[4,64,128]{2,1,0:T(8,128)S(1)}, u32[]{:S(2)}, u32[]{:S(2)}) collective-permute-start(f32[4,64,128]{2,1,0:T(8,128)S(1)} %collective-permute-done.9.refs_8_), channel_id=1, source_target_pairs={{0,4},{2,6},{4,0},{6,2},{8,12},{10,14},{12,8},{14,10},{16,20},{18,... | collective-permute-start | bytes 393224 | tf_op jit(solution)/shard_map/ppermute | solution.py:451
  25.9 1.8 %split_tiles.2 = (bf16[2,1024,256]{2,1,0:T(8,128)(2,1)S(1)}, bf16[2,1024,256]{2,1,0:T(8,128)(2,1)S(1)}, bf16[2,1024,256]{2,1,0:T(8,128)(2,1)S(1)}, bf16[2,1024,256]{2,1,0:T(8,128)(2,1)S(1)}) custom-call(f32[2,2,8,128,256]{4,3,2,1,0:T(8,128)} %own.2, f32[2,2,8,128,256]{4,3,2,1,0:T(8,128)S(1)} %collective-permute-done.1.partner), custom_call_target="tpu_custom_call" | custom-call | flops 2000000000 | tf_op jit(solution)/shard_map/split_tiles/pallas_call | solution.py:187
  29.4 1.4 %update_middle.1.residual = f32[4,64,256]{2,1,0:T(8,128)S(1)} custom-call(s32[3,16]{1,0:T(4,128)S(1)} %slot_places.1.places, s32[3,16]{1,0:T(4,128)S(1)} %collective-permute-done.places_partner, f32[2,2,64,128]{3,2,1,0:T(8,128)S(1)} %get-tuple-element.82.rhs, f32[2,2,64,128]{3,2,1,0:T(8,128)S(1)} %collective-permute-done.5.rhs_partner, ...), custom_call_target="tpu_custom_call" | custom-call | flops 1000000000 | tf_op jit(solution)/shard_map/update_middle/pallas_call | solution.py:157
  31.7 1.6 %collective-permute-start.15 = (f32[4,64,128]{2,1,0:T(8,128)S(1)}, f32[4,64,128]{2,1,0:T(8,128)S(1)}, u32[]{:S(2)}, u32[]{:S(2)}) collective-permute-start(f32[4,64,128]{2,1,0:T(8,128)S(1)} %get-tuple-element.93), channel_id=1, source_target_pairs={{0,1},{1,0},{2,3},{3,2},{4,5},{5,4},{6,7},{7,6},{8,9},{9,8},{10,11... | collective-permute-start | bytes 393224 | tf_op jit(solution)/shard_map/ppermute | solution.py:448
  33.3 4.0 %collective-permute-done.15 = f32[4,64,128]{2,1,0:T(8,128)S(1)} collective-permute-done((f32[4,64,128]{2,1,0:T(8,128)S(1)}, f32[4,64,128]{2,1,0:T(8,128)S(1)}, u32[]{:S(2)}, u32[]{:S(2)}) %collective-permute-start.15) | collective-permute-done | bytes 131104 | tf_op jit(solution)/shard_map/ppermute | solution.py:448
  37.3 1.6 %collective-permute-start.16 = (f32[4,64,128]{2,1,0:T(8,128)S(1)}, f32[4,64,128]{2,1,0:T(8,128)S(1)}, u32[]{:S(2)}, u32[]{:S(2)}) collective-permute-start(f32[4,64,128]{2,1,0:T(8,128)S(1)} %add.36.refs_5_), channel_id=1, source_target_pairs={{0,4},{2,6},{4,0},{6,2},{8,12},{10,14},{12,8},{14,10},{16,20},{18,... | collective-permute-start | bytes 393224 | tf_op jit(solution)/shard_map/ppermute | solution.py:451
  38.9 1.8 %collective-permute-start.19 = (f32[4,64,128]{2,1,0:T(8,128)S(1)}, f32[4,64,128]{2,1,0:T(8,128)S(1)}, u32[]{:S(2)}, u32[]{:S(2)}) collective-permute-start(f32[4,64,128]{2,1,0:T(8,128)S(1)} %add.36.refs_5_), channel_id=1, source_target_pairs={{0,16},{2,18},{4,20},{6,22},{8,24},{10,26},{12,28},{14,30},{16,0},... | collective-permute-start | bytes 393224 | tf_op jit(solution)/shard_map/ppermute | solution.py:451
  40.7 1.5 %collective-permute-start.17 = (f32[4,64,128]{2,1,0:T(8,128)S(1)}, f32[4,64,128]{2,1,0:T(8,128)S(1)}, u32[]{:S(2)}, u32[]{:S(2)}) collective-permute-start(f32[4,64,128]{2,1,0:T(8,128)S(1)} %add.36.refs_5_), channel_id=1, source_target_pairs={{0,8},{2,10},{4,12},{6,14},{8,0},{10,2},{12,4},{14,6},{16,24},{18,... | collective-permute-start | bytes 393224 | tf_op jit(solution)/shard_map/ppermute | solution.py:451
  42.2 1.5 %collective-permute-start.21 = (f32[4,64,128]{2,1,0:T(8,128)S(1)}, f32[4,64,128]{2,1,0:T(8,128)S(1)}, u32[]{:S(2)}, u32[]{:S(2)}) collective-permute-start(f32[4,64,128]{2,1,0:T(8,128)S(1)} %add.36.refs_5_), channel_id=1, source_target_pairs={{0,4},{2,6},{4,0},{6,2},{8,16},{10,18},{12,20},{14,22},{16,8},{18,... | collective-permute-start | bytes 393224 | tf_op jit(solution)/shard_map/ppermute | solution.py:462
  44.3 3.3 %collective-permute-done.19.refs_9_ = f32[4,64,128]{2,1,0:T(8,128)S(1)} collective-permute-done((f32[4,64,128]{2,1,0:T(8,128)S(1)}, f32[4,64,128]{2,1,0:T(8,128)S(1)}, u32[]{:S(2)}, u32[]{:S(2)}) %collective-permute-start.19) | collective-permute-done | bytes 131104 | tf_op jit(solution)/shard_map/ppermute | solution.py:451
  47.6 1.2 %collective-permute-start.20 = (f32[4,64,128]{2,1,0:T(8,128)S(1)}, f32[4,64,128]{2,1,0:T(8,128)S(1)}, u32[]{:S(2)}, u32[]{:S(2)}) collective-permute-start(f32[4,64,128]{2,1,0:T(8,128)S(1)} %collective-permute-done.19.refs_9_), channel_id=1, source_target_pairs={{0,4},{2,6},{4,0},{6,2},{8,12},{10,14},{12,8},{14,10},{16,20},{18,... | collective-permute-start | bytes 393224 | tf_op jit(solution)/shard_map/ppermute | solution.py:451
  48.8 1.8 %split_tiles.3 = (bf16[2,1024,256]{2,1,0:T(8,128)(2,1)S(1)}, bf16[2,1024,256]{2,1,0:T(8,128)(2,1)S(1)}, bf16[2,1024,256]{2,1,0:T(8,128)(2,1)S(1)}, bf16[2,1024,256]{2,1,0:T(8,128)(2,1)S(1)}) custom-call(f32[2,2,8,128,256]{4,3,2,1,0:T(8,128)} %own.2, f32[2,2,8,128,256]{4,3,2,1,0:T(8,128)S(1)} %collective-permute-done.1.partner), custom_call_target="tpu_custom_call" | custom-call | flops 2000000000 | tf_op jit(solution)/shard_map/split_tiles/pallas_call | solution.py:187
  50.6 1.5 %update_top_low.1.refs_4_ = f32[4,64,256]{2,1,0:T(8,128)S(1)} custom-call(s32[3,16]{1,0:T(4,128)S(1)} %slot_places.1.places, s32[3,16]{1,0:T(4,128)S(1)} %collective-permute-done.places_partner, f32[2,2,64,128]{3,2,1,0:T(8,128)S(1)} %get-tuple-element.82.rhs, f32[2,2,64,128]{3,2,1,0:T(8,128)S(1)} %collective-permute-done.5.rhs_partner, ...), custom_call_target="tpu_custom_call" | custom-call | flops 1000000000 | tf_op jit(solution)/shard_map/update_top_low/pallas_call | solution.py:157
  52.6 1.5 %update_top.1.mine = f32[4,64,256]{2,1,0:T(8,128)S(1)} custom-call(s32[3,16]{1,0:T(4,128)S(1)} %slot_places.1.places, s32[3,16]{1,0:T(4,128)S(1)} %collective-permute-done.places_partner, bf16[2,1024,256]{2,1,0:T(8,128)(2,1)S(1)} %get-tuple-element.99.refs_0_, bf16[2,1024,256]{2,1,0:T(8,128)(2,1)S(1)} %get-tuple-element.100.refs_1_, ...), custom_call_target="tpu_custom_call" | custom-call | flops 1000000000 | tf_op jit(solution)/shard_map/update_top/pallas_call | solution.py:157
  54.0 1.6 %collective-permute-start.23 = (f32[4,64,256]{2,1,0:T(8,128)S(1)}, f32[4,64,256]{2,1,0:T(8,128)S(1)}, u32[]{:S(2)}, u32[]{:S(2)}) collective-permute-start(f32[4,64,256]{2,1,0:T(8,128)S(1)} %update_top.1.mine), channel_id=1, source_target_pairs={{0,1},{1,0},{2,3},{3,2},{4,5},{5,4},{6,7},{7,6},{8,9},{9,8},{10,11... | collective-permute-start | bytes 786440 | tf_op jit(solution)/shard_map/ppermute | solution.py:448
  55.6 2.7 %gram_by_tiles.1 = (f32[4,256,256]{2,1,0:T(8,128)S(1)}, bf16[2,256,1024]{2,1,0:T(8,128)(2,1)S(1)}, bf16[2,256,1024]{2,1,0:T(8,128)(2,1)S(1)}, bf16[2,256,1024]{2,1,0:T(8,128)(2,1)S(1)}, bf16[2,256,1024]{2,1,0:T(8,128)(2,1)S(1)}) custom-call(f32[3,2,128,256]{3,2,1,0:T(8,128)S(1)} %copy-done, f32[3,2,128,256]{3,2,1,0:T(8,128)S(1)} %collective-permute-done.2.d1.d_partner, ...), custom_call_target="tpu_custom_call" | custom-call | flops 3000000000 | tf_op jit(solution)/shard_map/gram_by_tiles/pallas_call | solution.py:157
  58.3 2.2 %collective-permute-done.23.theirs = f32[4,64,256]{2,1,0:T(8,128)S(1)} collective-permute-done((f32[4,64,256]{2,1,0:T(8,128)S(1)}, f32[4,64,256]{2,1,0:T(8,128)S(1)}, u32[]{:S(2)}, u32[]{:S(2)}) %collective-permute-start.23) | collective-permute-done | bytes 262176 | tf_op jit(solution)/shard_map/ppermute | solution.py:448
  60.4 1.6 %top_carry.1 = (f32[4,64,256]{2,1,0:T(8,128)S(1)}, f32[4,64,128]{2,1,0:T(8,128)S(1)}, f32[4,64,128]{2,1,0:T(8,128)S(1)}, f32[4,64,128]{2,1,0:T(8,128)S(1)}, f32[...) custom-call(s32[3,16]{1,0:T(4,128)S(1)} %slot_places.1.places, ...), custom_call_target="tpu_custom_call" | custom-call | flops 1000000000 | tf_op jit(solution)/shard_map/top_carry/pallas_call | solution.py:157
  62.0 1.3 %collective-permute-start.24 = (f32[4,64,128]{2,1,0:T(8,128)S(1)}, f32[4,64,128]{2,1,0:T(8,128)S(1)}, u32[]{:S(2)}, u32[]{:S(2)}) collective-permute-start(f32[4,64,128]{2,1,0:T(8,128)S(1)} %get-tuple-element.109), channel_id=1, source_target_pairs={{0,4},{2,6},{4,0},{6,2},{8,12},{10,14},{12,8},{14,10},{16,20},{18,... | collective-permute-start | bytes 393224 | tf_op jit(solution)/shard_map/ppermute | solution.py:451
  64.1 3.3 %collective-permute-start.27 = (f32[4,64,128]{2,1,0:T(8,128)S(1)}, f32[4,64,128]{2,1,0:T(8,128)S(1)}, u32[]{:S(2)}, u32[]{:S(2)}) collective-permute-start(f32[4,64,128]{2,1,0:T(8,128)S(1)} %get-tuple-element.112), channel_id=1, source_target_pairs={{0,8},{2,10},{4,12},{6,14},{8,0},{10,2},{12,4},{14,6},{16,24},{18,... | collective-permute-start | bytes 393224 | tf_op jit(solution)/shard_map/ppermute | solution.py:451
  68.4 2.0 %collective-permute-start.25 = (f32[4,64,128]{2,1,0:T(8,128)S(1)}, f32[4,64,128]{2,1,0:T(8,128)S(1)}, u32[]{:S(2)}, u32[]{:S(2)}) collective-permute-start(f32[4,64,128]{2,1,0:T(8,128)S(1)} %add.37), channel_id=1, source_target_pairs={{0,16},{2,18},{4,20},{6,22},{8,24},{10,26},{12,28},{14,30},{16,0},... | collective-permute-start | bytes 393224 | tf_op jit(solution)/shard_map/ppermute | solution.py:451
  70.4 1.2 %collective-permute-done.27 = f32[4,64,128]{2,1,0:T(8,128)S(1)} collective-permute-done((f32[4,64,128]{2,1,0:T(8,128)S(1)}, f32[4,64,128]{2,1,0:T(8,128)S(1)}, u32[]{:S(2)}, u32[]{:S(2)}) %collective-permute-start.27) | collective-permute-done | bytes 131104 | tf_op jit(solution)/shard_map/ppermute | solution.py:451
  71.6 1.7 %collective-permute-start.28 = (f32[4,64,128]{2,1,0:T(8,128)S(1)}, f32[4,64,128]{2,1,0:T(8,128)S(1)}, u32[]{:S(2)}, u32[]{:S(2)}) collective-permute-start(f32[4,64,128]{2,1,0:T(8,128)S(1)} %add_add_fusion.1), channel_id=1, source_target_pairs={{0,4},{2,6},{4,0},{6,2},{8,12},{10,14},{12,8},{14,10},{16,20},{18,... | collective-permute-start | bytes 393224 | tf_op jit(solution)/shard_map/ppermute | solution.py:451
  73.6 3.7 %collective-permute-done.25 = f32[4,64,128]{2,1,0:T(8,128)S(1)} collective-permute-done((f32[4,64,128]{2,1,0:T(8,128)S(1)}, f32[4,64,128]{2,1,0:T(8,128)S(1)}, u32[]{:S(2)}, u32[]{:S(2)}) %collective-permute-start.25) | collective-permute-done | bytes 131104 | tf_op jit(solution)/shard_map/ppermute | solution.py:451
  77.4 1.6 %collective-permute-start.31 = (f32[4,64,128]{2,1,0:T(8,128)S(1)}, f32[4,64,128]{2,1,0:T(8,128)S(1)}, u32[]{:S(2)}, u32[]{:S(2)}) collective-permute-start(f32[4,64,128]{2,1,0:T(8,128)S(1)} %add_subtract_fusion.own), channel_id=1, source_target_pairs={{0,1},{1,0},{2,3},{3,2},{4,5},{5,4},{6,7},{7,6},{8,9},{9,8},{10,11... | collective-permute-start | bytes 393224 | tf_op jit(solution)/shard_map/ppermute | solution.py:448
  79.0 1.9 %diag_by_tiles.1 = (bf16[2,256,1024]{2,1,0:T(8,128)(2,1)S(1)}, bf16[2,256,1024]{2,1,0:T(8,128)(2,1)S(1)}, bf16[2,256,1024]{2,1,0:T(8,128)(2,1)S(1)}, bf16[2,256,1024]{2,1,0:T(8,128)(2,1)S(1)}) custom-call(f32[3,2,128,256]{3,2,1,0:T(8,128)S(1)} %copy-done, f32[3,2,128,256]{3,2,1,0:T(8,128)S(1)} %collective-permute-done.2.d1.d_partner, ...), custom_call_target="tpu_custom_call" | custom-call | flops 3000000000 | tf_op jit(solution)/shard_map/diag_by_tiles/pallas_call | solution.py:157
  80.8 1.7 %lowest_carry.1 = (f32[32,64,128]{2,1,0:T(8,128)S(1)}, f32[2,64,128]{2,1,0:T(8,128)S(1)}, f32[2,64,128]{2,1,0:T(8,128)S(1)}) custom-call(s32[3,16]{1,0:T(4,128)S(1)} %slot_places.1.places, s32[3,16]{1,0:T(4,128)S(1)} %collective-permute-done.places_partner, f32[4,64,256]{2,1,0:T(8,128)S(1)} %get-tuple-element.124.residual, ...), custom_call_target="tpu_custom_call" | custom-call | flops 2000000000 | tf_op jit(solution)/shard_map/lowest_carry/pallas_call | solution.py:157
  82.5 1.7 %middle_carry.1 = (f32[2,64,128]{2,1,0:T(8,128)S(1)}, f32[2,64,128]{2,1,0:T(8,128)S(1)}, f32[4,64,128]{2,1,0:T(8,128)S(1)}, f32[4,64,128]{2,1,0:T(8,128)S(1)}, f...) custom-call(s32[3,16]{1,0:T(4,128)S(1)} %slot_places.1.places, ...), custom_call_target="tpu_custom_call" | custom-call | flops 1000000000 | tf_op jit(solution)/shard_map/middle_carry/pallas_call | solution.py:157
  84.2 1.1 %collective-permute-start.37 = (f32[4,64,128]{2,1,0:T(8,128)S(1)}, f32[4,64,128]{2,1,0:T(8,128)S(1)}, u32[]{:S(2)}, u32[]{:S(2)}) collective-permute-start(f32[4,64,128]{2,1,0:T(8,128)S(1)} %get-tuple-element.134), channel_id=1, source_target_pairs={{0,4},{2,6},{4,0},{6,2},{8,12},{10,14},{12,8},{14,10},{16,20},{18,... | collective-permute-start | bytes 393224 | tf_op jit(solution)/shard_map/ppermute | solution.py:451
  85.3 1.0 collective-permute-start.34
  86.3 1.2 %collective-permute-start.35 = (f32[4,64,128]{2,1,0:T(8,128)S(1)}, f32[4,64,128]{2,1,0:T(8,128)S(1)}, u32[]{:S(2)}, u32[]{:S(2)}) collective-permute-start(f32[4,64,128]{2,1,0:T(8,128)S(1)} %get-tuple-element.132), channel_id=1, source_target_pairs={{0,8},{2,10},{4,12},{6,14},{8,0},{10,2},{12,4},{14,6},{16,24},{18,... | collective-permute-start | bytes 393224 | tf_op jit(solution)/shard_map/ppermute | solution.py:451
  89.4 1.0 collective-permute-done.37
  90.4 1.8 %collective-permute-start.38 = (f32[4,64,128]{2,1,0:T(8,128)S(1)}, f32[4,64,128]{2,1,0:T(8,128)S(1)}, u32[]{:S(2)}, u32[]{:S(2)}) collective-permute-start(f32[4,64,128]{2,1,0:T(8,128)S(1)} %add.46), channel_id=1, source_target_pairs={{0,16},{2,18},{4,20},{6,22},{8,24},{10,26},{12,28},{14,30},{16,0},... | collective-permute-start | bytes 393224 | tf_op jit(solution)/shard_map/ppermute | solution.py:451
  92.3 1.2 %collective-permute-start.36 = (f32[4,64,128]{2,1,0:T(8,128)S(1)}, f32[4,64,128]{2,1,0:T(8,128)S(1)}, u32[]{:S(2)}, u32[]{:S(2)}) collective-permute-start(f32[4,64,128]{2,1,0:T(8,128)S(1)} %add_add_fusion), channel_id=1, source_target_pairs={{0,4},{2,6},{4,0},{6,2},{8,12},{10,14},{12,8},{14,10},{16,20},{18,... | collective-permute-start | bytes 393224 | tf_op jit(solution)/shard_map/ppermute | solution.py:451
  93.5 4.3 %collective-permute-done.38.e = f32[4,64,128]{2,1,0:T(8,128)S(1)} collective-permute-done((f32[4,64,128]{2,1,0:T(8,128)S(1)}, f32[4,64,128]{2,1,0:T(8,128)S(1)}, u32[]{:S(2)}, u32[]{:S(2)}) %collective-permute-start.38) | collective-permute-done | bytes 131104 | tf_op jit(solution)/shard_map/ppermute | solution.py:451
  99.6 1.2 %collective-permute-start.40 = (f32[2,128,128]{2,1,0:T(8,128)S(1)}, f32[2,128,128]{2,1,0:T(8,128)S(1)}, u32[]{:S(2)}, u32[]{:S(2)}) collective-permute-start(f32[2,128,128]{2,1,0:T(8,128)S(1)} %get-tuple-element.138), channel_id=1, source_target_pairs={{0,1},{1,0},{2,3},{3,2},{4,5},{5,4},{6,7},{7,6},{8,9},{9,8},{10,11... | collective-permute-start | bytes 393224 | tf_op jit(solution)/shard_map/ppermute | solution.py:448
  101.0 4.3 %collective-permute-done.40 = f32[2,128,128]{2,1,0:T(8,128)S(1)} collective-permute-done((f32[2,128,128]{2,1,0:T(8,128)S(1)}, f32[2,128,128]{2,1,0:T(8,128)S(1)}, u32[]{:S(2)}, u32[]{:S(2)}) %collective-permute-start.40) | collective-permute-done | bytes 131104 | tf_op jit(solution)/shard_map/ppermute | solution.py:448
  (75 shorter events, 15.3 us)
Async XLA Ops:
  0.0 11.3 %copy-start.1 = (f32[3,2,128,128]{3,2,1,0:T(8,128)S(1)}, f32[3,2,128,128]{3,2,1,0:T(8,128)}, u32[]{:S(2)}) copy-start(f32[3,2,128,128]{3,2,1,0:T(8,128)} %rhs) | copy-start | bytes 1179652
  0.0 9.7 %collective-permute-start.1 = (f32[2,2,8,128,256]{4,3,2,1,0:T(8,128)}, f32[2,2,8,128,256]{4,3,2,1,0:T(8,128)S(1)}, u32[]{:S(2)}, u32[]{:S(2)}) collective-permute-start(f32[2,2,8,128,256]{4,3,2,1,0:T(8,128)} %own.2), channel_id=1, source_target_pairs={{0,2},{2,0},{4,6},{6,4},{8,10},{10,8},{12,14},{14,12},{16,18},{18,... | collective-permute-start | bytes 12582920 | tf_op jit(solution)/shard_map/ppermute | solution.py:451
  0.5 9.3 %collective-permute-start.2 = (f32[3,2,128,256]{3,2,1,0:T(8,128)}, f32[3,2,128,256]{3,2,1,0:T(8,128)S(1)}, u32[]{:S(2)}, u32[]{:S(2)}) collective-permute-start(f32[3,2,128,256]{3,2,1,0:T(8,128)} %d_own.1), channel_id=1, source_target_pairs={{0,2},{2,0},{4,6},{6,4},{8,10},{10,8},{12,14},{14,12},{16,18},{18,... | collective-permute-start | bytes 2359304 | tf_op jit(solution)/shard_map/ppermute | solution.py:451
  1.4 8.3 %collective-permute-start.3 = (f32[2,128,128]{2,1,0:T(8,128)S(1)}, f32[2,128,128]{2,1,0:T(8,128)S(1)}, u32[]{:S(2)}, u32[]{:S(2)}) collective-permute-start(f32[2,128,128]{2,1,0:T(8,128)S(1)} %slice_bitcast_fusion.rhs_own), channel_id=1, source_target_pairs={{0,1},{1,0},{2,3},{3,2},{4,5},{5,4},{6,7},{7,6},{8,9},{9,8},{10,11... | collective-permute-start | bytes 393224 | tf_op jit(solution)/shard_map/ppermute | solution.py:448
  5.5 13.9 %collective-permute-start.13 = (f32[2,2,128,256]{3,2,1,0:T(8,128)S(1)}, f32[2,2,128,256]{3,2,1,0:T(8,128)S(1)}, u32[]{:S(2)}, u32[]{:S(2)}) collective-permute-start(f32[2,2,128,256]{3,2,1,0:T(8,128)S(1)} %slice.7), channel_id=1, source_target_pairs={{0,1},{1,0},{2,3},{3,2},{4,5},{5,4},{6,7},{7,6},{8,9},{9,8},{10,11... | collective-permute-start | bytes 1572872 | tf_op jit(solution)/shard_map/ppermute | solution.py:448
  5.6 0.7 copy-start.2
  6.3 0.7 copy-start.3
  8.5 1.2 %collective-permute-start = (s32[3,16]{1,0:T(4,128)S(1)}, s32[3,16]{1,0:T(4,128)S(1)}, u32[]{:S(2)}, u32[]{:S(2)}) collective-permute-start(s32[3,16]{1,0:T(4,128)S(1)} %slot_places.1.places), channel_id=1, source_target_pairs={{0,2},{2,0},{4,6},{6,4},{8,10},{10,8},{12,14},{14,12},{16,18},{18,... | collective-permute-start | bytes 584 | tf_op jit(solution)/shard_map/ppermute | solution.py:451
  11.0 1.3 %collective-permute-start.4 = (f32[2,64,128]{2,1,0:T(8,128)S(1)}, f32[2,64,128]{2,1,0:T(8,128)S(1)}, u32[]{:S(2)}, u32[]{:S(2)}) collective-permute-start(f32[2,64,128]{2,1,0:T(8,128)S(1)} %get-tuple-element.78), channel_id=1, source_target_pairs={{0,2},{2,0},{4,6},{6,4},{8,10},{10,8},{12,14},{14,12},{16,18},{18,... | collective-permute-start | bytes 196616 | tf_op jit(solution)/shard_map/ppermute | solution.py:451
  12.3 8.9 %collective-permute-start.6 = (f32[4,64,128]{2,1,0:T(8,128)S(1)}, f32[4,64,128]{2,1,0:T(8,128)S(1)}, u32[]{:S(2)}, u32[]{:S(2)}) collective-permute-start(f32[4,64,128]{2,1,0:T(8,128)S(1)} %constant_dynamic-update-slice_fusion.refs_4_.values), channel_id=1, source_target_pairs={{0,4},{2,6},{4,0},{6,2},{8,12},{10,14},{12,8},{14,10},{16,20},{18,... | collective-permute-start | bytes 393224 | tf_op jit(solution)/shard_map/ppermute | solution.py:451
  14.3 8.4 %collective-permute-start.5 = (f32[2,2,64,128]{3,2,1,0:T(8,128)S(1)}, f32[2,2,64,128]{3,2,1,0:T(8,128)S(1)}, u32[]{:S(2)}, u32[]{:S(2)}) collective-permute-start(f32[2,2,64,128]{3,2,1,0:T(8,128)S(1)} %get-tuple-element.83), channel_id=1, source_target_pairs={{0,2},{2,0},{4,6},{6,4},{8,10},{10,8},{12,14},{14,12},{16,18},{18,... | collective-permute-start | bytes 393224 | tf_op jit(solution)/shard_map/ppermute | solution.py:451
  14.3 10.1 %collective-permute-start.9 = (f32[4,64,128]{2,1,0:T(8,128)S(1)}, f32[4,64,128]{2,1,0:T(8,128)S(1)}, u32[]{:S(2)}, u32[]{:S(2)}) collective-permute-start(f32[4,64,128]{2,1,0:T(8,128)S(1)} %constant_dynamic-update-slice_fusion.refs_4_.values), channel_id=1, source_target_pairs={{0,16},{2,18},{4,20},{6,22},{8,24},{10,26},{12,28},{14,30},{16,0},... | collective-permute-start | bytes 393224 | tf_op jit(solution)/shard_map/ppermute | solution.py:451
  16.9 10.8 %collective-permute-start.11 = (f32[4,64,128]{2,1,0:T(8,128)S(1)}, f32[4,64,128]{2,1,0:T(8,128)S(1)}, u32[]{:S(2)}, u32[]{:S(2)}) collective-permute-start(f32[4,64,128]{2,1,0:T(8,128)S(1)} %constant_dynamic-update-slice_fusion.refs_4_.values), channel_id=1, source_target_pairs={{0,4},{2,6},{4,0},{6,2},{8,16},{10,18},{12,20},{14,22},{16,8},{18,... | collective-permute-start | bytes 393224 | tf_op jit(solution)/shard_map/ppermute | solution.py:462
  19.4 8.3 %collective-permute-start.7 = (f32[4,64,128]{2,1,0:T(8,128)S(1)}, f32[4,64,128]{2,1,0:T(8,128)S(1)}, u32[]{:S(2)}, u32[]{:S(2)}) collective-permute-start(f32[4,64,128]{2,1,0:T(8,128)S(1)} %constant_dynamic-update-slice_fusion.refs_4_.values), channel_id=1, source_target_pairs={{0,8},{2,10},{4,12},{6,14},{8,0},{10,2},{12,4},{14,6},{16,24},{18,... | collective-permute-start | bytes 393224 | tf_op jit(solution)/shard_map/ppermute | solution.py:451
  21.2 6.5 %collective-permute-start.12 = (f32[4,64,128]{2,1,0:T(8,128)S(1)}, f32[4,64,128]{2,1,0:T(8,128)S(1)}, u32[]{:S(2)}, u32[]{:S(2)}) collective-permute-start(f32[4,64,128]{2,1,0:T(8,128)S(1)} %collective-permute-done.6.refs_5_), channel_id=1, source_target_pairs={{0,4},{2,6},{4,0},{6,2},{8,16},{10,18},{12,20},{14,22},{16,8},{18,... | collective-permute-start | bytes 393224 | tf_op jit(solution)/shard_map/ppermute | solution.py:462
  22.7 6.0 %collective-permute-start.8 = (f32[4,64,128]{2,1,0:T(8,128)S(1)}, f32[4,64,128]{2,1,0:T(8,128)S(1)}, u32[]{:S(2)}, u32[]{:S(2)}) collective-permute-start(f32[4,64,128]{2,1,0:T(8,128)S(1)} %collective-permute-done.6.refs_5_), channel_id=1, source_target_pairs={{0,8},{2,10},{4,12},{6,14},{8,0},{10,2},{12,4},{14,6},{16,24},{18,... | collective-permute-start | bytes 393224 | tf_op jit(solution)/shard_map/ppermute | solution.py:451
  24.4 5.0 %collective-permute-start.10 = (f32[4,64,128]{2,1,0:T(8,128)S(1)}, f32[4,64,128]{2,1,0:T(8,128)S(1)}, u32[]{:S(2)}, u32[]{:S(2)}) collective-permute-start(f32[4,64,128]{2,1,0:T(8,128)S(1)} %collective-permute-done.9.refs_8_), channel_id=1, source_target_pairs={{0,4},{2,6},{4,0},{6,2},{8,12},{10,14},{12,8},{14,10},{16,20},{18,... | collective-permute-start | bytes 393224 | tf_op jit(solution)/shard_map/ppermute | solution.py:451
  27.7 3.5 %copy-start = (f32[3,2,128,256]{3,2,1,0:T(8,128)S(1)}, f32[3,2,128,256]{3,2,1,0:T(8,128)}, u32[]{:S(2)}) copy-start(f32[3,2,128,256]{3,2,1,0:T(8,128)} %d_own.1) | copy-start | bytes 2359300
  29.4 1.9 %collective-permute-start.14 = (f32[2,2,128,256]{3,2,1,0:T(8,128)S(1)}, f32[2,2,128,256]{3,2,1,0:T(8,128)S(1)}, u32[]{:S(2)}, u32[]{:S(2)}) collective-permute-start(f32[2,2,128,256]{3,2,1,0:T(8,128)S(1)} %collective-permute-done.13.d2), channel_id=1, source_target_pairs={{0,2},{2,0},{4,6},{6,4},{8,10},{10,8},{12,14},{14,12},{16,18},{18,... | collective-permute-start | bytes 1572872 | tf_op jit(solution)/shard_map/ppermute | solution.py:451
  31.7 5.6 %collective-permute-start.15 = (f32[4,64,128]{2,1,0:T(8,128)S(1)}, f32[4,64,128]{2,1,0:T(8,128)S(1)}, u32[]{:S(2)}, u32[]{:S(2)}) collective-permute-start(f32[4,64,128]{2,1,0:T(8,128)S(1)} %get-tuple-element.93), channel_id=1, source_target_pairs={{0,1},{1,0},{2,3},{3,2},{4,5},{5,4},{6,7},{7,6},{8,9},{9,8},{10,11... | collective-permute-start | bytes 393224 | tf_op jit(solution)/shard_map/ppermute | solution.py:448
  37.3 6.4 %collective-permute-start.16 = (f32[4,64,128]{2,1,0:T(8,128)S(1)}, f32[4,64,128]{2,1,0:T(8,128)S(1)}, u32[]{:S(2)}, u32[]{:S(2)}) collective-permute-start(f32[4,64,128]{2,1,0:T(8,128)S(1)} %add.36.refs_5_), channel_id=1, source_target_pairs={{0,4},{2,6},{4,0},{6,2},{8,12},{10,14},{12,8},{14,10},{16,20},{18,... | collective-permute-start | bytes 393224 | tf_op jit(solution)/shard_map/ppermute | solution.py:451
  38.9 8.7 %collective-permute-start.19 = (f32[4,64,128]{2,1,0:T(8,128)S(1)}, f32[4,64,128]{2,1,0:T(8,128)S(1)}, u32[]{:S(2)}, u32[]{:S(2)}) collective-permute-start(f32[4,64,128]{2,1,0:T(8,128)S(1)} %add.36.refs_5_), channel_id=1, source_target_pairs={{0,16},{2,18},{4,20},{6,22},{8,24},{10,26},{12,28},{14,30},{16,0},... | collective-permute-start | bytes 393224 | tf_op jit(solution)/shard_map/ppermute | solution.py:451
  40.7 11.4 %collective-permute-start.17 = (f32[4,64,128]{2,1,0:T(8,128)S(1)}, f32[4,64,128]{2,1,0:T(8,128)S(1)}, u32[]{:S(2)}, u32[]{:S(2)}) collective-permute-start(f32[4,64,128]{2,1,0:T(8,128)S(1)} %add.36.refs_5_), channel_id=1, source_target_pairs={{0,8},{2,10},{4,12},{6,14},{8,0},{10,2},{12,4},{14,6},{16,24},{18,... | collective-permute-start | bytes 393224 | tf_op jit(solution)/shard_map/ppermute | solution.py:451
  42.2 9.9 %collective-permute-start.21 = (f32[4,64,128]{2,1,0:T(8,128)S(1)}, f32[4,64,128]{2,1,0:T(8,128)S(1)}, u32[]{:S(2)}, u32[]{:S(2)}) collective-permute-start(f32[4,64,128]{2,1,0:T(8,128)S(1)} %add.36.refs_5_), channel_id=1, source_target_pairs={{0,4},{2,6},{4,0},{6,2},{8,16},{10,18},{12,20},{14,22},{16,8},{18,... | collective-permute-start | bytes 393224 | tf_op jit(solution)/shard_map/ppermute | solution.py:462
  43.7 8.4 %collective-permute-start.18 = (f32[4,64,128]{2,1,0:T(8,128)S(1)}, f32[4,64,128]{2,1,0:T(8,128)S(1)}, u32[]{:S(2)}, u32[]{:S(2)}) collective-permute-start(f32[4,64,128]{2,1,0:T(8,128)S(1)} %collective-permute-done.16.refs_6_), channel_id=1, source_target_pairs={{0,8},{2,10},{4,12},{6,14},{8,0},{10,2},{12,4},{14,6},{16,24},{18,... | collective-permute-start | bytes 393224 | tf_op jit(solution)/shard_map/ppermute | solution.py:451
  43.7 8.8 %collective-permute-start.22 = (f32[4,64,128]{2,1,0:T(8,128)S(1)}, f32[4,64,128]{2,1,0:T(8,128)S(1)}, u32[]{:S(2)}, u32[]{:S(2)}) collective-permute-start(f32[4,64,128]{2,1,0:T(8,128)S(1)} %collective-permute-done.16.refs_6_), channel_id=1, source_target_pairs={{0,4},{2,6},{4,0},{6,2},{8,16},{10,18},{12,20},{14,22},{16,8},{18,... | collective-permute-start | bytes 393224 | tf_op jit(solution)/shard_map/ppermute | solution.py:462
  47.6 5.0 %collective-permute-start.20 = (f32[4,64,128]{2,1,0:T(8,128)S(1)}, f32[4,64,128]{2,1,0:T(8,128)S(1)}, u32[]{:S(2)}, u32[]{:S(2)}) collective-permute-start(f32[4,64,128]{2,1,0:T(8,128)S(1)} %collective-permute-done.19.refs_9_), channel_id=1, source_target_pairs={{0,4},{2,6},{4,0},{6,2},{8,12},{10,14},{12,8},{14,10},{16,20},{18,... | collective-permute-start | bytes 393224 | tf_op jit(solution)/shard_map/ppermute | solution.py:451
  54.0 6.4 %collective-permute-start.23 = (f32[4,64,256]{2,1,0:T(8,128)S(1)}, f32[4,64,256]{2,1,0:T(8,128)S(1)}, u32[]{:S(2)}, u32[]{:S(2)}) collective-permute-start(f32[4,64,256]{2,1,0:T(8,128)S(1)} %update_top.1.mine), channel_id=1, source_target_pairs={{0,1},{1,0},{2,3},{3,2},{4,5},{5,4},{6,7},{7,6},{8,9},{9,8},{10,11... | collective-permute-start | bytes 786440 | tf_op jit(solution)/shard_map/ppermute | solution.py:448
  62.0 6.4 %collective-permute-start.24 = (f32[4,64,128]{2,1,0:T(8,128)S(1)}, f32[4,64,128]{2,1,0:T(8,128)S(1)}, u32[]{:S(2)}, u32[]{:S(2)}) collective-permute-start(f32[4,64,128]{2,1,0:T(8,128)S(1)} %get-tuple-element.109), channel_id=1, source_target_pairs={{0,4},{2,6},{4,0},{6,2},{8,12},{10,14},{12,8},{14,10},{16,20},{18,... | collective-permute-start | bytes 393224 | tf_op jit(solution)/shard_map/ppermute | solution.py:451
  63.3 7.2 %collective-permute-start.26 = (f32[4,64,128]{2,1,0:T(8,128)S(1)}, f32[4,64,128]{2,1,0:T(8,128)S(1)}, u32[]{:S(2)}, u32[]{:S(2)}) collective-permute-start(f32[4,64,128]{2,1,0:T(8,128)S(1)} %get-tuple-element.111), channel_id=1, source_target_pairs={{0,4},{2,6},{4,0},{6,2},{8,16},{10,18},{12,20},{14,22},{16,8},{18,... | collective-permute-start | bytes 393224 | tf_op jit(solution)/shard_map/ppermute | solution.py:462
  64.1 7.5 %collective-permute-start.27 = (f32[4,64,128]{2,1,0:T(8,128)S(1)}, f32[4,64,128]{2,1,0:T(8,128)S(1)}, u32[]{:S(2)}, u32[]{:S(2)}) collective-permute-start(f32[4,64,128]{2,1,0:T(8,128)S(1)} %get-tuple-element.112), channel_id=1, source_target_pairs={{0,8},{2,10},{4,12},{6,14},{8,0},{10,2},{12,4},{14,6},{16,24},{18,... | collective-permute-start | bytes 393224 | tf_op jit(solution)/shard_map/ppermute | solution.py:451
  67.4 5.9 %collective-permute-start.29 = (f32[4,64,128]{2,1,0:T(8,128)S(1)}, f32[4,64,128]{2,1,0:T(8,128)S(1)}, u32[]{:S(2)}, u32[]{:S(2)}) collective-permute-start(f32[4,64,128]{2,1,0:T(8,128)S(1)} %get-tuple-element.113), channel_id=1, source_target_pairs={{0,4},{2,6},{4,0},{6,2},{8,16},{10,18},{12,20},{14,22},{16,8},{18,... | collective-permute-start | bytes 393224 | tf_op jit(solution)/shard_map/ppermute | solution.py:462
  68.0 5.7 %collective-permute-start.30 = (f32[4,64,128]{2,1,0:T(8,128)S(1)}, f32[4,64,128]{2,1,0:T(8,128)S(1)}, u32[]{:S(2)}, u32[]{:S(2)}) collective-permute-start(f32[4,64,128]{2,1,0:T(8,128)S(1)} %get-tuple-element.114), channel_id=1, source_target_pairs={{0,8},{2,10},{4,12},{6,14},{8,0},{10,2},{12,4},{14,6},{16,24},{18,... | collective-permute-start | bytes 393224 | tf_op jit(solution)/shard_map/ppermute | solution.py:451
  68.4 8.9 %collective-permute-start.25 = (f32[4,64,128]{2,1,0:T(8,128)S(1)}, f32[4,64,128]{2,1,0:T(8,128)S(1)}, u32[]{:S(2)}, u32[]{:S(2)}) collective-permute-start(f32[4,64,128]{2,1,0:T(8,128)S(1)} %add.37), channel_id=1, source_target_pairs={{0,16},{2,18},{4,20},{6,22},{8,24},{10,26},{12,28},{14,30},{16,0},... | collective-permute-start | bytes 393224 | tf_op jit(solution)/shard_map/ppermute | solution.py:451
  71.6 5.7 %collective-permute-start.28 = (f32[4,64,128]{2,1,0:T(8,128)S(1)}, f32[4,64,128]{2,1,0:T(8,128)S(1)}, u32[]{:S(2)}, u32[]{:S(2)}) collective-permute-start(f32[4,64,128]{2,1,0:T(8,128)S(1)} %add_add_fusion.1), channel_id=1, source_target_pairs={{0,4},{2,6},{4,0},{6,2},{8,12},{10,14},{12,8},{14,10},{16,20},{18,... | collective-permute-start | bytes 393224 | tf_op jit(solution)/shard_map/ppermute | solution.py:451
  77.4 5.1 %collective-permute-start.31 = (f32[4,64,128]{2,1,0:T(8,128)S(1)}, f32[4,64,128]{2,1,0:T(8,128)S(1)}, u32[]{:S(2)}, u32[]{:S(2)}) collective-permute-start(f32[4,64,128]{2,1,0:T(8,128)S(1)} %add_subtract_fusion.own), channel_id=1, source_target_pairs={{0,1},{1,0},{2,3},{3,2},{4,5},{5,4},{6,7},{7,6},{8,9},{9,8},{10,11... | collective-permute-start | bytes 393224 | tf_op jit(solution)/shard_map/ppermute | solution.py:448
  84.2 6.2 %collective-permute-start.37 = (f32[4,64,128]{2,1,0:T(8,128)S(1)}, f32[4,64,128]{2,1,0:T(8,128)S(1)}, u32[]{:S(2)}, u32[]{:S(2)}) collective-permute-start(f32[4,64,128]{2,1,0:T(8,128)S(1)} %get-tuple-element.134), channel_id=1, source_target_pairs={{0,4},{2,6},{4,0},{6,2},{8,12},{10,14},{12,8},{14,10},{16,20},{18,... | collective-permute-start | bytes 393224 | tf_op jit(solution)/shard_map/ppermute | solution.py:451
  85.3 7.0 %collective-permute-start.34 = (f32[4,64,128]{2,1,0:T(8,128)S(1)}, f32[4,64,128]{2,1,0:T(8,128)S(1)}, u32[]{:S(2)}, u32[]{:S(2)}) collective-permute-start(f32[4,64,128]{2,1,0:T(8,128)S(1)} %get-tuple-element.131), channel_id=1, source_target_pairs={{0,4},{2,6},{4,0},{6,2},{8,16},{10,18},{12,20},{14,22},{16,8},{18,... | collective-permute-start | bytes 393224 | tf_op jit(solution)/shard_map/ppermute | solution.py:462
  86.3 6.0 %collective-permute-start.35 = (f32[4,64,128]{2,1,0:T(8,128)S(1)}, f32[4,64,128]{2,1,0:T(8,128)S(1)}, u32[]{:S(2)}, u32[]{:S(2)}) collective-permute-start(f32[4,64,128]{2,1,0:T(8,128)S(1)} %get-tuple-element.132), channel_id=1, source_target_pairs={{0,8},{2,10},{4,12},{6,14},{8,0},{10,2},{12,4},{14,6},{16,24},{18,... | collective-permute-start | bytes 393224 | tf_op jit(solution)/shard_map/ppermute | solution.py:451
  87.5 6.0 %collective-permute-start.32 = (f32[4,64,128]{2,1,0:T(8,128)S(1)}, f32[4,64,128]{2,1,0:T(8,128)S(1)}, u32[]{:S(2)}, u32[]{:S(2)}) collective-permute-start(f32[4,64,128]{2,1,0:T(8,128)S(1)} %get-tuple-element.128), channel_id=1, source_target_pairs={{0,8},{2,10},{4,12},{6,14},{8,0},{10,2},{12,4},{14,6},{16,24},{18,... | collective-permute-start | bytes 393224 | tf_op jit(solution)/shard_map/ppermute | solution.py:451
  88.4 5.2 %collective-permute-start.33 = (f32[4,64,128]{2,1,0:T(8,128)S(1)}, f32[4,64,128]{2,1,0:T(8,128)S(1)}, u32[]{:S(2)}, u32[]{:S(2)}) collective-permute-start(f32[4,64,128]{2,1,0:T(8,128)S(1)} %get-tuple-element.129), channel_id=1, source_target_pairs={{0,4},{2,6},{4,0},{6,2},{8,16},{10,18},{12,20},{14,22},{16,8},{18,... | collective-permute-start | bytes 393224 | tf_op jit(solution)/shard_map/ppermute | solution.py:462
  90.4 7.3 %collective-permute-start.38 = (f32[4,64,128]{2,1,0:T(8,128)S(1)}, f32[4,64,128]{2,1,0:T(8,128)S(1)}, u32[]{:S(2)}, u32[]{:S(2)}) collective-permute-start(f32[4,64,128]{2,1,0:T(8,128)S(1)} %add.46), channel_id=1, source_target_pairs={{0,16},{2,18},{4,20},{6,22},{8,24},{10,26},{12,28},{14,30},{16,0},... | collective-permute-start | bytes 393224 | tf_op jit(solution)/shard_map/ppermute | solution.py:451
  92.3 5.5 %collective-permute-start.36 = (f32[4,64,128]{2,1,0:T(8,128)S(1)}, f32[4,64,128]{2,1,0:T(8,128)S(1)}, u32[]{:S(2)}, u32[]{:S(2)}) collective-permute-start(f32[4,64,128]{2,1,0:T(8,128)S(1)} %add_add_fusion), channel_id=1, source_target_pairs={{0,4},{2,6},{4,0},{6,2},{8,12},{10,14},{12,8},{14,10},{16,20},{18,... | collective-permute-start | bytes 393224 | tf_op jit(solution)/shard_map/ppermute | solution.py:451
  98.1 1.4 %collective-permute-start.39 = (f32[2,64,256]{2,1,0:T(8,128)S(1)}, f32[2,64,256]{2,1,0:T(8,128)S(1)}, u32[]{:S(2)}, u32[]{:S(2)}) collective-permute-start(f32[2,64,256]{2,1,0:T(8,128)S(1)} %get-tuple-element.136), channel_id=1, source_target_pairs={{0,2},{2,0},{4,6},{6,4},{8,10},{10,8},{12,14},{14,12},{16,18},{18,... | collective-permute-start | bytes 393224 | tf_op jit(solution)/shard_map/ppermute | solution.py:451
  98.1 2.7 %collective-permute-start.41 = (f32[2,64,128]{2,1,0:T(8,128)S(1)}, f32[2,64,128]{2,1,0:T(8,128)S(1)}, u32[]{:S(2)}, u32[]{:S(2)}) collective-permute-start(f32[2,64,128]{2,1,0:T(8,128)S(1)} %get-tuple-element.142), channel_id=1, source_target_pairs={{0,2},{2,0},{4,6},{6,4},{8,10},{10,8},{12,14},{14,12},{16,18},{18,... | collective-permute-start | bytes 196616 | tf_op jit(solution)/shard_map/ppermute | solution.py:451
  98.6 2.2 %collective-permute-start.42 = (f32[2,64,128]{2,1,0:T(8,128)S(1)}, f32[2,64,128]{2,1,0:T(8,128)S(1)}, u32[]{:S(2)}, u32[]{:S(2)}) collective-permute-start(f32[2,64,128]{2,1,0:T(8,128)S(1)} %get-tuple-element.144), channel_id=1, source_target_pairs={{0,2},{2,0},{4,6},{6,4},{8,10},{10,8},{12,14},{14,12},{16,18},{18,... | collective-permute-start | bytes 196616 | tf_op jit(solution)/shard_map/ppermute | solution.py:451
  99.6 5.6 %collective-permute-start.40 = (f32[2,128,128]{2,1,0:T(8,128)S(1)}, f32[2,128,128]{2,1,0:T(8,128)S(1)}, u32[]{:S(2)}, u32[]{:S(2)}) collective-permute-start(f32[2,128,128]{2,1,0:T(8,128)S(1)} %get-tuple-element.138), channel_id=1, source_target_pairs={{0,1},{1,0},{2,3},{3,2},{4,5},{5,4},{6,7},{7,6},{8,9},{9,8},{10,11... | collective-permute-start | bytes 393224 | tf_op jit(solution)/shard_map/ppermute | solution.py:448

commit v6 on v5

--- a/solution.py
+++ b/solution.py
@@ -127,10 +127,10 @@
 
 
 def dot3(left, right, dims):
-    left_high, left_low = halves(left)
+    left_high, left_low = left if isinstance(left, tuple) else halves(left)
     right_high, right_low = right if isinstance(right, tuple) else halves(right)
     dot = functools.partial(lax.dot_general, dimension_numbers=dims, preferred_element_type=F32)
-    rows = left.shape[0]
+    rows = left_high.shape[0]
     both = dot(jnp.concatenate([left_high, left_low], 0), right_high)
     return both[:rows] + both[rows:] + dot(left_high, right_low)
 
@@ -231,33 +231,33 @@
     return tuple(part[s % half] for part in chosen)
 
 
-def first_values(rhs_own, rhs_other, diag, mine, partner):
+def split_first(diag, high, low):
+    for s in range(high.shape[0]):
+        put_halves(diag[0, s], high, low, s)
+
+
+def first_values(rhs_own, rhs_other, diag_high, diag_low, mine, partner):
     core, col = lax.axis_index("rows") % 2, lax.axis_index("cols")
     half = mine.shape[1]
     for s in range(rhs_own.shape[0]):
         rows = ordered(rhs_own[s], rhs_other[s], col, 0)
-        values = dot3(diag[0, s], rows, NN).T
+        values = dot3((diag_high[s], diag_low[s]), rows, NN).T
         low, high = values[:half], values[half:]
         mine[s] = jnp.where(core == 0, low, high)
         partner[s] = jnp.where(core == 0, high, low)
 
 
-def first_call(rhs_own, rhs_other, diag):
-    owned, depth, columns = rhs_own.shape
-    whole = pl.BlockSpec((owned, depth, columns), lambda i: (0, 0, 0))
-    half = pl.BlockSpec((owned, columns // 2, depth), lambda i: (0, 0, 0))
+def split_diag(diag):
+    shape = diag.shape[1:]
     return pl.pallas_call(
-        first_values,
+        split_first,
         grid=(1,),
-        out_shape=[jax.ShapeDtypeStruct((owned, columns // 2, depth), F32)] * 2,
-        in_specs=[
-            whole, whole,
-            pl.BlockSpec((1,) + diag.shape[1:], lambda i: (0, 0, 0, 0)),
-        ],
-        out_specs=[half, half],
-        name="first_values",
+        out_shape=[jax.ShapeDtypeStruct(shape, BF16)] * 2,
+        in_specs=[pl.BlockSpec((1,) + shape, lambda i: (0, 0, 0, 0))],
+        out_specs=[pl.BlockSpec(shape, lambda i: (0, 0, 0))] * 2,
+        name="split_diag",
         **options(500),
-    )(rhs_own, rhs_other, pltpu.with_memory_space_constraint(diag, pltpu.HBM))
+    )(pltpu.with_memory_space_constraint(diag, pltpu.HBM))
 
 
 def slot_places(sources, counts, places):
@@ -488,6 +488,10 @@
     rhs0_other = swap_cols(rhs0)
     d_partner = swap_core(diag_inv)
     tiles_partner = swap_core(factor_tiles)
+    d_low = split_diag(diag_inv)
+    upper_diag = diag_inv[1:]
+    d_other = swap_cols(upper_diag)
+    tile_source, upper_diag, rhs0 = after((tile_source, upper_diag, rhs0))
     own_places = pl.pallas_call(
         slot_places,
         out_shape=jax.ShapeDtypeStruct((levels, owned * slots), jnp.int32),
@@ -497,20 +501,20 @@
         **options(500),
     )(tile_source, tile_count)
     places = [own_places, swap_core(own_places)]
-    diag, rhs0 = after((diag_inv, rhs0))
-    d_other = swap_cols(diag[1:])
-    rhs0, places, tiles_partner, d_partner = after((rhs0, places, tiles_partner, d_partner))
-    mine, partner = first_call(rhs0, rhs0_other, diag_inv)
+    rhs0, places, tiles_partner, d_partner, d_low = after(
+        (rhs0, places, tiles_partner, d_partner, d_low)
+    )
+    mine, partner = call(first_values, "first_values", [shared] * 2, [rhs0, rhs0_other, *d_low], 0)
     values0 = jnp.concatenate([mine, swap_core(partner)], 0)
+    upper, upper_partner = call(
+        turned_rhs, "turned_rhs", [(levels - 1, owned, half_columns, share_rows)] * 2, [rhs], 0
+    )
+    uppers = [upper, swap_core(upper_partner)]
+    values0, uppers = after((values0, uppers))
     pieces0 = gather_pieces(values0)
 
     reach = slots * share_rows
     wide = [((owned, block, reach), BF16)] * 4
-    rhs, _ = after((rhs, partner))
-    upper, partner = call(
-        turned_rhs, "turned_rhs", [(levels - 1, owned, half_columns, share_rows)] * 2, [rhs], 0
-    )
-    uppers = [upper, swap_core(partner)]
     low_tiles = split_tiles(0, factor_tiles, tiles_partner)
     full = (sups, half_columns, block)
     scratch = [pltpu.VMEM(window, F32)]

time: 106 us -> 105 us (level)
  starting transfers between devices: 48.5 us -> 46.2 us
  waiting for transfers between devices: 31.6 us -> 32.7 us
    ppermute x29, waiting for transfers between devices: 19.1 us -> 21.8 us  [swap_rows(): lax.ppermute(value, 'rows', [(r, r ^ bits) for r in range(rows_total)])]
    ppermute x29, starting transfers between devices: 31.9 us -> 29.2 us  [swap_rows(): lax.ppermute(value, 'rows', [(r, r ^ bits) for r in range(rows_total)])]
    ppermute x6, waiting for transfers between devices: 12.5 us -> 10.9 us  [swap_cols(): return lax.ppermute(value, 'cols', [(0, 1), (1, 0)])]
    pallas_call x13 -> x14, Pallas kernels: 14.9 us -> 15.3 us  [call(): pl.pallas_call(kernel, out_shape=[jax.ShapeDtypeStruct(*out) if isinstanc...]
where the time goes in v6:
time: 105 us
  starting transfers between devices  46.2 us (44%)
  waiting for transfers between devices  32.7 us (31%)
  Pallas kernels  21.4 us (20%)
  local copies, waits for them, and re-layouts  3.36 us (3%)
    ppermute x29, starting transfers between devices, swap_rows(): lax.ppermute(value, 'rows', [(r, r ^ bits) for r in range(rows_total)])  29.2 us
    ppermute x29, waiting for transfers between devices, swap_rows(): lax.ppermute(value, 'rows', [(r, r ^ bits) for r in range(rows_total)])  21.8 us
    pallas_call x14, Pallas kernels, call(): pl.pallas_call(kernel, out_shape=[jax.ShapeDtypeStruct(*out) if isinstanc...  15.3 us
    ppermute x6, waiting for transfers between devices, swap_cols(): return lax.ppermute(value, 'cols', [(0, 1), (1, 0)])  10.9 us
    ppermute x6, starting transfers between devices, swap_cols(): return lax.ppermute(value, 'cols', [(0, 1), (1, 0)])  9.16 us
    ppermute x8, starting transfers between devices, swap_mid(): return lax.ppermute(value, 'rows', pairs)  7.85 us
    pallas_call x2, Pallas kernels, split_tiles(): pl.pallas_call(split_kernel, grid=(owned,), out_shape=[jax.ShapeDtypeStru...  3.67 us
  transfers between devices with their start and end apart: 43, of which 17 were waited for; matrix products, arithmetic and copies ran while one was open for 2% of the time, Pallas kernels for 15%

profile of v6, /device:TPU:0, one launch (start us, length us, event | category | flops | bytes accessed | tf_op | source)
XLA Modules:
  0.0 105.0 jit_solution(14353858694048830024)
XLA Ops:
  0.5 0.9 slice_bitcast_fusion.rhs_own
  1.4 3.0 %collective-permute-start.3 = (f32[2,128,128]{2,1,0:T(8,128)S(1)}, f32[2,128,128]{2,1,0:T(8,128)S(1)}, u32[]{:S(2)}, u32[]{:S(2)}) collective-permute-start(f32[2,128,128]{2,1,0:T(8,128)S(1)} %slice_bitcast_fusion.rhs_own), channel_id=1, source_target_pairs={{0,1},{1,0},{2,3},{3,2},{4,5},{5,4},{6,7},{7,6},{8,9},{9,8},{10,11... | collective-permute-start | bytes 393224 | tf_op jit(solution)/shard_map/ppermute | solution.py:448
  4.5 1.1 %slice.6 = f32[2,2,128,256]{3,2,1,0:T(8,128)S(1)} slice(f32[3,2,128,256]{3,2,1,0:T(8,128)} %d_own.1), slice={[1:3], [0:2], [0:128], [0:256]} | slice | bytes 1048576 | tf_op jit(solution)/shard_map/slice | solution.py:492
  7.0 1.5 %slot_places.1.places = s32[3,16]{1,0:T(4,128)S(1)} custom-call(s32[2,2,8]{2,1,0:T(2,128)S(1)} %copy-done.2, s32[2,2]{1,0:T(2,128)S(1)} %copy-done.3), custom_call_target="tpu_custom_call" | custom-call | flops 500000000 | tf_op jit(solution)/shard_map/slot_places/pallas_call | solution.py:495
  8.6 1.0 split_diag.1
  12.1 1.9 %collective-permute-start.6 = (f32[4,64,128]{2,1,0:T(8,128)S(1)}, f32[4,64,128]{2,1,0:T(8,128)S(1)}, u32[]{:S(2)}, u32[]{:S(2)}) collective-permute-start(f32[4,64,128]{2,1,0:T(8,128)S(1)} %pad_maximum_fusion.1.refs_4_.values), channel_id=1, source_target_pairs={{0,4},{2,6},{4,0},{6,2},{8,12},{10,14},{12,8},{14,10},{16,20},{18,... | collective-permute-start | bytes 393224 | tf_op jit(solution)/shard_map/ppermute | solution.py:451
  14.0 2.6 %collective-permute-start.9 = (f32[4,64,128]{2,1,0:T(8,128)S(1)}, f32[4,64,128]{2,1,0:T(8,128)S(1)}, u32[]{:S(2)}, u32[]{:S(2)}) collective-permute-start(f32[4,64,128]{2,1,0:T(8,128)S(1)} %pad_maximum_fusion.1.refs_4_.values), channel_id=1, source_target_pairs={{0,16},{2,18},{4,20},{6,22},{8,24},{10,26},{12,28},{14,30},{16,0},... | collective-permute-start | bytes 393224 | tf_op jit(solution)/shard_map/ppermute | solution.py:451
  17.2 1.0 collective-permute-start.7
  18.2 1.6 %collective-permute-start.12 = (f32[4,64,128]{2,1,0:T(8,128)S(1)}, f32[4,64,128]{2,1,0:T(8,128)S(1)}, u32[]{:S(2)}, u32[]{:S(2)}) collective-permute-start(f32[4,64,128]{2,1,0:T(8,128)S(1)} %collective-permute-done.6.refs_5_), channel_id=1, source_target_pairs={{0,4},{2,6},{4,0},{6,2},{8,16},{10,18},{12,20},{14,22},{16,8},{18,... | collective-permute-start | bytes 393224 | tf_op jit(solution)/shard_map/ppermute | solution.py:462
  19.8 1.5 %collective-permute-start.8 = (f32[4,64,128]{2,1,0:T(8,128)S(1)}, f32[4,64,128]{2,1,0:T(8,128)S(1)}, u32[]{:S(2)}, u32[]{:S(2)}) collective-permute-start(f32[4,64,128]{2,1,0:T(8,128)S(1)} %collective-permute-done.6.refs_5_), channel_id=1, source_target_pairs={{0,8},{2,10},{4,12},{6,14},{8,0},{10,2},{12,4},{14,6},{16,24},{18,... | collective-permute-start | bytes 393224 | tf_op jit(solution)/shard_map/ppermute | solution.py:451
  21.3 2.9 %collective-permute-done.9.refs_8_ = f32[4,64,128]{2,1,0:T(8,128)S(1)} collective-permute-done((f32[4,64,128]{2,1,0:T(8,128)S(1)}, f32[4,64,128]{2,1,0:T(8,128)S(1)}, u32[]{:S(2)}, u32[]{:S(2)}) %collective-permute-start.9) | collective-permute-done | bytes 131104 | tf_op jit(solution)/shard_map/ppermute | solution.py:451
  24.3 1.8 %split_tiles.2 = (bf16[2,1024,256]{2,1,0:T(8,128)(2,1)S(1)}, bf16[2,1024,256]{2,1,0:T(8,128)(2,1)S(1)}, bf16[2,1024,256]{2,1,0:T(8,128)(2,1)S(1)}, bf16[2,1024,256]{2,1,0:T(8,128)(2,1)S(1)}) custom-call(f32[2,2,8,128,256]{4,3,2,1,0:T(8,128)} %own.2, f32[2,2,8,128,256]{4,3,2,1,0:T(8,128)S(1)} %collective-permute-done.1.partner), custom_call_target="tpu_custom_call" | custom-call | flops 2000000000 | tf_op jit(solution)/shard_map/split_tiles/pallas_call | solution.py:187
  26.6 2.4 %collective-permute-done.10.refs_9_ = f32[4,64,128]{2,1,0:T(8,128)S(1)} collective-permute-done((f32[4,64,128]{2,1,0:T(8,128)S(1)}, f32[4,64,128]{2,1,0:T(8,128)S(1)}, u32[]{:S(2)}, u32[]{:S(2)}) %collective-permute-start.10) | collective-permute-done | bytes 131104 | tf_op jit(solution)/shard_map/ppermute | solution.py:451
  29.1 1.4 %update_middle.1.residual = f32[4,64,256]{2,1,0:T(8,128)S(1)} custom-call(s32[3,16]{1,0:T(4,128)S(1)} %slot_places.1.places, s32[3,16]{1,0:T(4,128)S(1)} %collective-permute-done.places_partner, f32[2,2,64,128]{3,2,1,0:T(8,128)S(1)} %get-tuple-element.95.rhs, f32[2,2,64,128]{3,2,1,0:T(8,128)S(1)} %collective-permute-done.5.rhs_partner, ...), custom_call_target="tpu_custom_call" | custom-call | flops 1000000000 | tf_op jit(solution)/shard_map/update_middle/pallas_call | solution.py:157
  31.5 1.6 %collective-permute-start.15 = (f32[4,64,128]{2,1,0:T(8,128)S(1)}, f32[4,64,128]{2,1,0:T(8,128)S(1)}, u32[]{:S(2)}, u32[]{:S(2)}) collective-permute-start(f32[4,64,128]{2,1,0:T(8,128)S(1)} %get-tuple-element.105), channel_id=1, source_target_pairs={{0,1},{1,0},{2,3},{3,2},{4,5},{5,4},{6,7},{7,6},{8,9},{9,8},{10,11... | collective-permute-start | bytes 393224 | tf_op jit(solution)/shard_map/ppermute | solution.py:448
  33.0 4.0 %collective-permute-done.15 = f32[4,64,128]{2,1,0:T(8,128)S(1)} collective-permute-done((f32[4,64,128]{2,1,0:T(8,128)S(1)}, f32[4,64,128]{2,1,0:T(8,128)S(1)}, u32[]{:S(2)}, u32[]{:S(2)}) %collective-permute-start.15) | collective-permute-done | bytes 131104 | tf_op jit(solution)/shard_map/ppermute | solution.py:448
  37.5 2.4 %collective-permute-start.19 = (f32[4,64,128]{2,1,0:T(8,128)S(1)}, f32[4,64,128]{2,1,0:T(8,128)S(1)}, u32[]{:S(2)}, u32[]{:S(2)}) collective-permute-start(f32[4,64,128]{2,1,0:T(8,128)S(1)} %add.36.refs_5_), channel_id=1, source_target_pairs={{0,16},{2,18},{4,20},{6,22},{8,24},{10,26},{12,28},{14,30},{16,0},... | collective-permute-start | bytes 393224 | tf_op jit(solution)/shard_map/ppermute | solution.py:451
  39.9 1.3 %collective-permute-start.17 = (f32[4,64,128]{2,1,0:T(8,128)S(1)}, f32[4,64,128]{2,1,0:T(8,128)S(1)}, u32[]{:S(2)}, u32[]{:S(2)}) collective-permute-start(f32[4,64,128]{2,1,0:T(8,128)S(1)} %add.36.refs_5_), channel_id=1, source_target_pairs={{0,8},{2,10},{4,12},{6,14},{8,0},{10,2},{12,4},{14,6},{16,24},{18,... | collective-permute-start | bytes 393224 | tf_op jit(solution)/shard_map/ppermute | solution.py:451
  41.1 1.5 %collective-permute-start.21 = (f32[4,64,128]{2,1,0:T(8,128)S(1)}, f32[4,64,128]{2,1,0:T(8,128)S(1)}, u32[]{:S(2)}, u32[]{:S(2)}) collective-permute-start(f32[4,64,128]{2,1,0:T(8,128)S(1)} %add.36.refs_5_), channel_id=1, source_target_pairs={{0,4},{2,6},{4,0},{6,2},{8,16},{10,18},{12,20},{14,22},{16,8},{18,... | collective-permute-start | bytes 393224 | tf_op jit(solution)/shard_map/ppermute | solution.py:462
  43.4 2.8 %collective-permute-done.19.refs_9_ = f32[4,64,128]{2,1,0:T(8,128)S(1)} collective-permute-done((f32[4,64,128]{2,1,0:T(8,128)S(1)}, f32[4,64,128]{2,1,0:T(8,128)S(1)}, u32[]{:S(2)}, u32[]{:S(2)}) %collective-permute-start.19) | collective-permute-done | bytes 131104 | tf_op jit(solution)/shard_map/ppermute | solution.py:451
  46.2 1.7 %collective-permute-start.20 = (f32[4,64,128]{2,1,0:T(8,128)S(1)}, f32[4,64,128]{2,1,0:T(8,128)S(1)}, u32[]{:S(2)}, u32[]{:S(2)}) collective-permute-start(f32[4,64,128]{2,1,0:T(8,128)S(1)} %collective-permute-done.19.refs_9_), channel_id=1, source_target_pairs={{0,4},{2,6},{4,0},{6,2},{8,12},{10,14},{12,8},{14,10},{16,20},{18,... | collective-permute-start | bytes 393224 | tf_op jit(solution)/shard_map/ppermute | solution.py:451
  47.9 1.8 %split_tiles.3 = (bf16[2,1024,256]{2,1,0:T(8,128)(2,1)S(1)}, bf16[2,1024,256]{2,1,0:T(8,128)(2,1)S(1)}, bf16[2,1024,256]{2,1,0:T(8,128)(2,1)S(1)}, bf16[2,1024,256]{2,1,0:T(8,128)(2,1)S(1)}) custom-call(f32[2,2,8,128,256]{4,3,2,1,0:T(8,128)} %own.2, f32[2,2,8,128,256]{4,3,2,1,0:T(8,128)S(1)} %collective-permute-done.1.partner), custom_call_target="tpu_custom_call" | custom-call | flops 2000000000 | tf_op jit(solution)/shard_map/split_tiles/pallas_call | solution.py:187
  49.8 1.5 %update_top_low.1.refs_4_ = f32[4,64,256]{2,1,0:T(8,128)S(1)} custom-call(s32[3,16]{1,0:T(4,128)S(1)} %slot_places.1.places, s32[3,16]{1,0:T(4,128)S(1)} %collective-permute-done.places_partner, f32[2,2,64,128]{3,2,1,0:T(8,128)S(1)} %get-tuple-element.95.rhs, f32[2,2,64,128]{3,2,1,0:T(8,128)S(1)} %collective-permute-done.5.rhs_partner, ...), custom_call_target="tpu_custom_call" | custom-call | flops 1000000000 | tf_op jit(solution)/shard_map/update_top_low/pallas_call | solution.py:157
  51.3 1.5 %update_top.1.mine = f32[4,64,256]{2,1,0:T(8,128)S(1)} custom-call(s32[3,16]{1,0:T(4,128)S(1)} %slot_places.1.places, s32[3,16]{1,0:T(4,128)S(1)} %collective-permute-done.places_partner, bf16[2,1024,256]{2,1,0:T(8,128)(2,1)S(1)} %get-tuple-element.111.refs_0_, bf16[2,1024,256]{2,1,0:T(8,128)(2,1)S(1)} %get-tuple-element.112.refs_1_, ...), custom_call_target="tpu_custom_call" | custom-call | flops 1000000000 | tf_op jit(solution)/shard_map/update_top/pallas_call | solution.py:157
  52.7 1.7 %collective-permute-start.23 = (f32[4,64,256]{2,1,0:T(8,128)S(1)}, f32[4,64,256]{2,1,0:T(8,128)S(1)}, u32[]{:S(2)}, u32[]{:S(2)}) collective-permute-start(f32[4,64,256]{2,1,0:T(8,128)S(1)} %update_top.1.mine), channel_id=1, source_target_pairs={{0,1},{1,0},{2,3},{3,2},{4,5},{5,4},{6,7},{7,6},{8,9},{9,8},{10,11... | collective-permute-start | bytes 786440 | tf_op jit(solution)/shard_map/ppermute | solution.py:448
  54.4 2.7 %gram_by_tiles.1 = (f32[4,256,256]{2,1,0:T(8,128)S(1)}, bf16[2,256,1024]{2,1,0:T(8,128)(2,1)S(1)}, bf16[2,256,1024]{2,1,0:T(8,128)(2,1)S(1)}, bf16[2,256,1024]{2,1,0:T(8,128)(2,1)S(1)}, bf16[2,256,1024]{2,1,0:T(8,128)(2,1)S(1)}) custom-call(f32[3,2,128,256]{3,2,1,0:T(8,128)S(1)} %copy-done, f32[3,2,128,256]{3,2,1,0:T(8,128)S(1)} %collective-permute-done.2.d1.d_partner, ...), custom_call_target="tpu_custom_call" | custom-call | flops 3000000000 | tf_op jit(solution)/shard_map/gram_by_tiles/pallas_call | solution.py:157
  57.1 2.5 %collective-permute-done.23.theirs = f32[4,64,256]{2,1,0:T(8,128)S(1)} collective-permute-done((f32[4,64,256]{2,1,0:T(8,128)S(1)}, f32[4,64,256]{2,1,0:T(8,128)S(1)}, u32[]{:S(2)}, u32[]{:S(2)}) %collective-permute-start.23) | collective-permute-done | bytes 262176 | tf_op jit(solution)/shard_map/ppermute | solution.py:448
  59.6 1.6 %top_carry.1 = (f32[4,64,256]{2,1,0:T(8,128)S(1)}, f32[4,64,128]{2,1,0:T(8,128)S(1)}, f32[4,64,128]{2,1,0:T(8,128)S(1)}, f32[4,64,128]{2,1,0:T(8,128)S(1)}, f32[...) custom-call(s32[3,16]{1,0:T(4,128)S(1)} %slot_places.1.places, ...), custom_call_target="tpu_custom_call" | custom-call | flops 1000000000 | tf_op jit(solution)/shard_map/top_carry/pallas_call | solution.py:157
  61.2 1.2 %collective-permute-start.24 = (f32[4,64,128]{2,1,0:T(8,128)S(1)}, f32[4,64,128]{2,1,0:T(8,128)S(1)}, u32[]{:S(2)}, u32[]{:S(2)}) collective-permute-start(f32[4,64,128]{2,1,0:T(8,128)S(1)} %get-tuple-element.121), channel_id=1, source_target_pairs={{0,4},{2,6},{4,0},{6,2},{8,12},{10,14},{12,8},{14,10},{16,20},{18,... | collective-permute-start | bytes 393224 | tf_op jit(solution)/shard_map/ppermute | solution.py:451
  63.3 3.1 %collective-permute-start.27 = (f32[4,64,128]{2,1,0:T(8,128)S(1)}, f32[4,64,128]{2,1,0:T(8,128)S(1)}, u32[]{:S(2)}, u32[]{:S(2)}) collective-permute-start(f32[4,64,128]{2,1,0:T(8,128)S(1)} %get-tuple-element.124), channel_id=1, source_target_pairs={{0,8},{2,10},{4,12},{6,14},{8,0},{10,2},{12,4},{14,6},{16,24},{18,... | collective-permute-start | bytes 393224 | tf_op jit(solution)/shard_map/ppermute | solution.py:451
  67.3 2.0 %collective-permute-start.25 = (f32[4,64,128]{2,1,0:T(8,128)S(1)}, f32[4,64,128]{2,1,0:T(8,128)S(1)}, u32[]{:S(2)}, u32[]{:S(2)}) collective-permute-start(f32[4,64,128]{2,1,0:T(8,128)S(1)} %add.37), channel_id=1, source_target_pairs={{0,16},{2,18},{4,20},{6,22},{8,24},{10,26},{12,28},{14,30},{16,0},... | collective-permute-start | bytes 393224 | tf_op jit(solution)/shard_map/ppermute | solution.py:451
  69.3 1.2 %collective-permute-done.27 = f32[4,64,128]{2,1,0:T(8,128)S(1)} collective-permute-done((f32[4,64,128]{2,1,0:T(8,128)S(1)}, f32[4,64,128]{2,1,0:T(8,128)S(1)}, u32[]{:S(2)}, u32[]{:S(2)}) %collective-permute-start.27) | collective-permute-done | bytes 131104 | tf_op jit(solution)/shard_map/ppermute | solution.py:451
  70.6 1.7 %collective-permute-start.28 = (f32[4,64,128]{2,1,0:T(8,128)S(1)}, f32[4,64,128]{2,1,0:T(8,128)S(1)}, u32[]{:S(2)}, u32[]{:S(2)}) collective-permute-start(f32[4,64,128]{2,1,0:T(8,128)S(1)} %add_add_fusion.1), channel_id=1, source_target_pairs={{0,4},{2,6},{4,0},{6,2},{8,12},{10,14},{12,8},{14,10},{16,20},{18,... | collective-permute-start | bytes 393224 | tf_op jit(solution)/shard_map/ppermute | solution.py:451
  72.6 3.7 %collective-permute-done.25 = f32[4,64,128]{2,1,0:T(8,128)S(1)} collective-permute-done((f32[4,64,128]{2,1,0:T(8,128)S(1)}, f32[4,64,128]{2,1,0:T(8,128)S(1)}, u32[]{:S(2)}, u32[]{:S(2)}) %collective-permute-start.25) | collective-permute-done | bytes 131104 | tf_op jit(solution)/shard_map/ppermute | solution.py:451
  76.3 1.6 %collective-permute-start.31 = (f32[4,64,128]{2,1,0:T(8,128)S(1)}, f32[4,64,128]{2,1,0:T(8,128)S(1)}, u32[]{:S(2)}, u32[]{:S(2)}) collective-permute-start(f32[4,64,128]{2,1,0:T(8,128)S(1)} %add_subtract_fusion.own), channel_id=1, source_target_pairs={{0,1},{1,0},{2,3},{3,2},{4,5},{5,4},{6,7},{7,6},{8,9},{9,8},{10,11... | collective-permute-start | bytes 393224 | tf_op jit(solution)/shard_map/ppermute | solution.py:448
  77.9 1.9 %diag_by_tiles.1 = (bf16[2,256,1024]{2,1,0:T(8,128)(2,1)S(1)}, bf16[2,256,1024]{2,1,0:T(8,128)(2,1)S(1)}, bf16[2,256,1024]{2,1,0:T(8,128)(2,1)S(1)}, bf16[2,256,1024]{2,1,0:T(8,128)(2,1)S(1)}) custom-call(f32[3,2,128,256]{3,2,1,0:T(8,128)S(1)} %copy-done, f32[3,2,128,256]{3,2,1,0:T(8,128)S(1)} %collective-permute-done.2.d1.d_partner, ...), custom_call_target="tpu_custom_call" | custom-call | flops 3000000000 | tf_op jit(solution)/shard_map/diag_by_tiles/pallas_call | solution.py:157
  79.7 1.7 %lowest_carry.1 = (f32[32,64,128]{2,1,0:T(8,128)S(1)}, f32[2,64,128]{2,1,0:T(8,128)S(1)}, f32[2,64,128]{2,1,0:T(8,128)S(1)}) custom-call(s32[3,16]{1,0:T(4,128)S(1)} %slot_places.1.places, s32[3,16]{1,0:T(4,128)S(1)} %collective-permute-done.places_partner, f32[4,64,256]{2,1,0:T(8,128)S(1)} %get-tuple-element.136.residual, ...), custom_call_target="tpu_custom_call" | custom-call | flops 2000000000 | tf_op jit(solution)/shard_map/lowest_carry/pallas_call | solution.py:157
  81.4 1.7 %middle_carry.1 = (f32[2,64,128]{2,1,0:T(8,128)S(1)}, f32[2,64,128]{2,1,0:T(8,128)S(1)}, f32[4,64,128]{2,1,0:T(8,128)S(1)}, f32[4,64,128]{2,1,0:T(8,128)S(1)}, f...) custom-call(s32[3,16]{1,0:T(4,128)S(1)} %slot_places.1.places, ...), custom_call_target="tpu_custom_call" | custom-call | flops 1000000000 | tf_op jit(solution)/shard_map/middle_carry/pallas_call | solution.py:157
  83.2 1.0 collective-permute-start.37
  84.2 1.1 %collective-permute-start.34 = (f32[4,64,128]{2,1,0:T(8,128)S(1)}, f32[4,64,128]{2,1,0:T(8,128)S(1)}, u32[]{:S(2)}, u32[]{:S(2)}) collective-permute-start(f32[4,64,128]{2,1,0:T(8,128)S(1)} %get-tuple-element.143), channel_id=1, source_target_pairs={{0,4},{2,6},{4,0},{6,2},{8,16},{10,18},{12,20},{14,22},{16,8},{18,... | collective-permute-start | bytes 393224 | tf_op jit(solution)/shard_map/ppermute | solution.py:462
  85.3 1.2 %collective-permute-start.35 = (f32[4,64,128]{2,1,0:T(8,128)S(1)}, f32[4,64,128]{2,1,0:T(8,128)S(1)}, u32[]{:S(2)}, u32[]{:S(2)}) collective-permute-start(f32[4,64,128]{2,1,0:T(8,128)S(1)} %get-tuple-element.144), channel_id=1, source_target_pairs={{0,8},{2,10},{4,12},{6,14},{8,0},{10,2},{12,4},{14,6},{16,24},{18,... | collective-permute-start | bytes 393224 | tf_op jit(solution)/shard_map/ppermute | solution.py:451
  87.3 1.0 collective-permute-start.33
  88.3 1.1 %collective-permute-done.37 = f32[4,64,128]{2,1,0:T(8,128)S(1)} collective-permute-done((f32[4,64,128]{2,1,0:T(8,128)S(1)}, f32[4,64,128]{2,1,0:T(8,128)S(1)}, u32[]{:S(2)}, u32[]{:S(2)}) %collective-permute-start.37) | collective-permute-done | bytes 131104 | tf_op jit(solution)/shard_map/ppermute | solution.py:451
  89.4 1.8 %collective-permute-start.38 = (f32[4,64,128]{2,1,0:T(8,128)S(1)}, f32[4,64,128]{2,1,0:T(8,128)S(1)}, u32[]{:S(2)}, u32[]{:S(2)}) collective-permute-start(f32[4,64,128]{2,1,0:T(8,128)S(1)} %add.46), channel_id=1, source_target_pairs={{0,16},{2,18},{4,20},{6,22},{8,24},{10,26},{12,28},{14,30},{16,0},... | collective-permute-start | bytes 393224 | tf_op jit(solution)/shard_map/ppermute | solution.py:451
  91.2 1.2 %collective-permute-start.36 = (f32[4,64,128]{2,1,0:T(8,128)S(1)}, f32[4,64,128]{2,1,0:T(8,128)S(1)}, u32[]{:S(2)}, u32[]{:S(2)}) collective-permute-start(f32[4,64,128]{2,1,0:T(8,128)S(1)} %add_add_fusion), channel_id=1, source_target_pairs={{0,4},{2,6},{4,0},{6,2},{8,12},{10,14},{12,8},{14,10},{16,20},{18,... | collective-permute-start | bytes 393224 | tf_op jit(solution)/shard_map/ppermute | solution.py:451
  92.4 4.3 %collective-permute-done.38.e = f32[4,64,128]{2,1,0:T(8,128)S(1)} collective-permute-done((f32[4,64,128]{2,1,0:T(8,128)S(1)}, f32[4,64,128]{2,1,0:T(8,128)S(1)}, u32[]{:S(2)}, u32[]{:S(2)}) %collective-permute-start.38) | collective-permute-done | bytes 131104 | tf_op jit(solution)/shard_map/ppermute | solution.py:451
  98.6 1.1 %collective-permute-start.40 = (f32[2,128,128]{2,1,0:T(8,128)S(1)}, f32[2,128,128]{2,1,0:T(8,128)S(1)}, u32[]{:S(2)}, u32[]{:S(2)}) collective-permute-start(f32[2,128,128]{2,1,0:T(8,128)S(1)} %get-tuple-element.150), channel_id=1, source_target_pairs={{0,1},{1,0},{2,3},{3,2},{4,5},{5,4},{6,7},{7,6},{8,9},{9,8},{10,11... | collective-permute-start | bytes 393224 | tf_op jit(solution)/shard_map/ppermute | solution.py:448
  99.9 4.3 %collective-permute-done.40 = f32[2,128,128]{2,1,0:T(8,128)S(1)} collective-permute-done((f32[2,128,128]{2,1,0:T(8,128)S(1)}, f32[2,128,128]{2,1,0:T(8,128)S(1)}, u32[]{:S(2)}, u32[]{:S(2)}) %collective-permute-start.40) | collective-permute-done | bytes 131104 | tf_op jit(solution)/shard_map/ppermute | solution.py:448
  (75 shorter events, 13.8 us)
Async XLA Ops:
  0.0 9.8 %collective-permute-start.1 = (f32[2,2,8,128,256]{4,3,2,1,0:T(8,128)}, f32[2,2,8,128,256]{4,3,2,1,0:T(8,128)S(1)}, u32[]{:S(2)}, u32[]{:S(2)}) collective-permute-start(f32[2,2,8,128,256]{4,3,2,1,0:T(8,128)} %own.2), channel_id=1, source_target_pairs={{0,2},{2,0},{4,6},{6,4},{8,10},{10,8},{12,14},{14,12},{16,18},{18,... | collective-permute-start | bytes 12582920 | tf_op jit(solution)/shard_map/ppermute | solution.py:451
  0.5 9.3 %collective-permute-start.2 = (f32[3,2,128,256]{3,2,1,0:T(8,128)}, f32[3,2,128,256]{3,2,1,0:T(8,128)S(1)}, u32[]{:S(2)}, u32[]{:S(2)}) collective-permute-start(f32[3,2,128,256]{3,2,1,0:T(8,128)} %d_own.1), channel_id=1, source_target_pairs={{0,2},{2,0},{4,6},{6,4},{8,10},{10,8},{12,14},{14,12},{16,18},{18,... | collective-permute-start | bytes 2359304 | tf_op jit(solution)/shard_map/ppermute | solution.py:451
  1.4 9.1 %copy-start.1 = (f32[3,2,128,128]{3,2,1,0:T(8,128)S(1)}, f32[3,2,128,128]{3,2,1,0:T(8,128)}, u32[]{:S(2)}) copy-start(f32[3,2,128,128]{3,2,1,0:T(8,128)} %rhs.1) | copy-start | bytes 1179652
  1.4 8.3 %collective-permute-start.3 = (f32[2,128,128]{2,1,0:T(8,128)S(1)}, f32[2,128,128]{2,1,0:T(8,128)S(1)}, u32[]{:S(2)}, u32[]{:S(2)}) collective-permute-start(f32[2,128,128]{2,1,0:T(8,128)S(1)} %slice_bitcast_fusion.rhs_own), channel_id=1, source_target_pairs={{0,1},{1,0},{2,3},{3,2},{4,5},{5,4},{6,7},{7,6},{8,9},{9,8},{10,11... | collective-permute-start | bytes 393224 | tf_op jit(solution)/shard_map/ppermute | solution.py:448
  5.6 14.2 %collective-permute-start.13 = (f32[2,2,128,256]{3,2,1,0:T(8,128)S(1)}, f32[2,2,128,256]{3,2,1,0:T(8,128)S(1)}, u32[]{:S(2)}, u32[]{:S(2)}) collective-permute-start(f32[2,2,128,256]{3,2,1,0:T(8,128)S(1)} %slice.6), channel_id=1, source_target_pairs={{0,1},{1,0},{2,3},{3,2},{4,5},{5,4},{6,7},{7,6},{8,9},{9,8},{10,11... | collective-permute-start | bytes 1572872 | tf_op jit(solution)/shard_map/ppermute | solution.py:448
  5.7 0.7 copy-start.2
  6.3 0.7 copy-start.3
  8.5 1.2 %collective-permute-start = (s32[3,16]{1,0:T(4,128)S(1)}, s32[3,16]{1,0:T(4,128)S(1)}, u32[]{:S(2)}, u32[]{:S(2)}) collective-permute-start(s32[3,16]{1,0:T(4,128)S(1)} %slot_places.1.places), channel_id=1, source_target_pairs={{0,2},{2,0},{4,6},{6,4},{8,10},{10,8},{12,14},{14,12},{16,18},{18,... | collective-permute-start | bytes 584 | tf_op jit(solution)/shard_map/ppermute | solution.py:451
  10.1 1.3 %collective-permute-start.4 = (f32[2,64,128]{2,1,0:T(8,128)S(1)}, f32[2,64,128]{2,1,0:T(8,128)S(1)}, u32[]{:S(2)}, u32[]{:S(2)}) collective-permute-start(f32[2,64,128]{2,1,0:T(8,128)S(1)} %get-tuple-element.89), channel_id=1, source_target_pairs={{0,2},{2,0},{4,6},{6,4},{8,10},{10,8},{12,14},{14,12},{16,18},{18,... | collective-permute-start | bytes 196616 | tf_op jit(solution)/shard_map/ppermute | solution.py:451
  10.7 1.4 %collective-permute-start.5 = (f32[2,2,64,128]{3,2,1,0:T(8,128)S(1)}, f32[2,2,64,128]{3,2,1,0:T(8,128)S(1)}, u32[]{:S(2)}, u32[]{:S(2)}) collective-permute-start(f32[2,2,64,128]{3,2,1,0:T(8,128)S(1)} %get-tuple-element.91), channel_id=1, source_target_pairs={{0,2},{2,0},{4,6},{6,4},{8,10},{10,8},{12,14},{14,12},{16,18},{18,... | collective-permute-start | bytes 393224 | tf_op jit(solution)/shard_map/ppermute | solution.py:451
  12.1 6.1 %collective-permute-start.6 = (f32[4,64,128]{2,1,0:T(8,128)S(1)}, f32[4,64,128]{2,1,0:T(8,128)S(1)}, u32[]{:S(2)}, u32[]{:S(2)}) collective-permute-start(f32[4,64,128]{2,1,0:T(8,128)S(1)} %pad_maximum_fusion.1.refs_4_.values), channel_id=1, source_target_pairs={{0,4},{2,6},{4,0},{6,2},{8,12},{10,14},{12,8},{14,10},{16,20},{18,... | collective-permute-start | bytes 393224 | tf_op jit(solution)/shard_map/ppermute | solution.py:451
  14.0 10.1 %collective-permute-start.9 = (f32[4,64,128]{2,1,0:T(8,128)S(1)}, f32[4,64,128]{2,1,0:T(8,128)S(1)}, u32[]{:S(2)}, u32[]{:S(2)}) collective-permute-start(f32[4,64,128]{2,1,0:T(8,128)S(1)} %pad_maximum_fusion.1.refs_4_.values), channel_id=1, source_target_pairs={{0,16},{2,18},{4,20},{6,22},{8,24},{10,26},{12,28},{14,30},{16,0},... | collective-permute-start | bytes 393224 | tf_op jit(solution)/shard_map/ppermute | solution.py:451
  16.6 9.5 %collective-permute-start.11 = (f32[4,64,128]{2,1,0:T(8,128)S(1)}, f32[4,64,128]{2,1,0:T(8,128)S(1)}, u32[]{:S(2)}, u32[]{:S(2)}) collective-permute-start(f32[4,64,128]{2,1,0:T(8,128)S(1)} %pad_maximum_fusion.1.refs_4_.values), channel_id=1, source_target_pairs={{0,4},{2,6},{4,0},{6,2},{8,16},{10,18},{12,20},{14,22},{16,8},{18,... | collective-permute-start | bytes 393224 | tf_op jit(solution)/shard_map/ppermute | solution.py:462
  17.2 9.0 %collective-permute-start.7 = (f32[4,64,128]{2,1,0:T(8,128)S(1)}, f32[4,64,128]{2,1,0:T(8,128)S(1)}, u32[]{:S(2)}, u32[]{:S(2)}) collective-permute-start(f32[4,64,128]{2,1,0:T(8,128)S(1)} %pad_maximum_fusion.1.refs_4_.values), channel_id=1, source_target_pairs={{0,8},{2,10},{4,12},{6,14},{8,0},{10,2},{12,4},{14,6},{16,24},{18,... | collective-permute-start | bytes 393224 | tf_op jit(solution)/shard_map/ppermute | solution.py:451
  18.2 8.0 %collective-permute-start.12 = (f32[4,64,128]{2,1,0:T(8,128)S(1)}, f32[4,64,128]{2,1,0:T(8,128)S(1)}, u32[]{:S(2)}, u32[]{:S(2)}) collective-permute-start(f32[4,64,128]{2,1,0:T(8,128)S(1)} %collective-permute-done.6.refs_5_), channel_id=1, source_target_pairs={{0,4},{2,6},{4,0},{6,2},{8,16},{10,18},{12,20},{14,22},{16,8},{18,... | collective-permute-start | bytes 393224 | tf_op jit(solution)/shard_map/ppermute | solution.py:462
  19.8 6.9 %collective-permute-start.8 = (f32[4,64,128]{2,1,0:T(8,128)S(1)}, f32[4,64,128]{2,1,0:T(8,128)S(1)}, u32[]{:S(2)}, u32[]{:S(2)}) collective-permute-start(f32[4,64,128]{2,1,0:T(8,128)S(1)} %collective-permute-done.6.refs_5_), channel_id=1, source_target_pairs={{0,8},{2,10},{4,12},{6,14},{8,0},{10,2},{12,4},{14,6},{16,24},{18,... | collective-permute-start | bytes 393224 | tf_op jit(solution)/shard_map/ppermute | solution.py:451
  24.1 5.0 %collective-permute-start.10 = (f32[4,64,128]{2,1,0:T(8,128)S(1)}, f32[4,64,128]{2,1,0:T(8,128)S(1)}, u32[]{:S(2)}, u32[]{:S(2)}) collective-permute-start(f32[4,64,128]{2,1,0:T(8,128)S(1)} %collective-permute-done.9.refs_8_), channel_id=1, source_target_pairs={{0,4},{2,6},{4,0},{6,2},{8,12},{10,14},{12,8},{14,10},{16,20},{18,... | collective-permute-start | bytes 393224 | tf_op jit(solution)/shard_map/ppermute | solution.py:451
  26.1 4.9 %copy-start = (f32[3,2,128,256]{3,2,1,0:T(8,128)S(1)}, f32[3,2,128,256]{3,2,1,0:T(8,128)}, u32[]{:S(2)}) copy-start(f32[3,2,128,256]{3,2,1,0:T(8,128)} %d_own.1) | copy-start | bytes 2359300
  29.1 1.9 %collective-permute-start.14 = (f32[2,2,128,256]{3,2,1,0:T(8,128)S(1)}, f32[2,2,128,256]{3,2,1,0:T(8,128)S(1)}, u32[]{:S(2)}, u32[]{:S(2)}) collective-permute-start(f32[2,2,128,256]{3,2,1,0:T(8,128)S(1)} %collective-permute-done.13.d2), channel_id=1, source_target_pairs={{0,2},{2,0},{4,6},{6,4},{8,10},{10,8},{12,14},{14,12},{16,18},{18,... | collective-permute-start | bytes 1572872 | tf_op jit(solution)/shard_map/ppermute | solution.py:451
  31.5 5.6 %collective-permute-start.15 = (f32[4,64,128]{2,1,0:T(8,128)S(1)}, f32[4,64,128]{2,1,0:T(8,128)S(1)}, u32[]{:S(2)}, u32[]{:S(2)}) collective-permute-start(f32[4,64,128]{2,1,0:T(8,128)S(1)} %get-tuple-element.105), channel_id=1, source_target_pairs={{0,1},{1,0},{2,3},{3,2},{4,5},{5,4},{6,7},{7,6},{8,9},{9,8},{10,11... | collective-permute-start | bytes 393224 | tf_op jit(solution)/shard_map/ppermute | solution.py:448
  37.1 5.5 %collective-permute-start.16 = (f32[4,64,128]{2,1,0:T(8,128)S(1)}, f32[4,64,128]{2,1,0:T(8,128)S(1)}, u32[]{:S(2)}, u32[]{:S(2)}) collective-permute-start(f32[4,64,128]{2,1,0:T(8,128)S(1)} %add.36.refs_5_), channel_id=1, source_target_pairs={{0,4},{2,6},{4,0},{6,2},{8,12},{10,14},{12,8},{14,10},{16,20},{18,... | collective-permute-start | bytes 393224 | tf_op jit(solution)/shard_map/ppermute | solution.py:451
  37.5 8.8 %collective-permute-start.19 = (f32[4,64,128]{2,1,0:T(8,128)S(1)}, f32[4,64,128]{2,1,0:T(8,128)S(1)}, u32[]{:S(2)}, u32[]{:S(2)}) collective-permute-start(f32[4,64,128]{2,1,0:T(8,128)S(1)} %add.36.refs_5_), channel_id=1, source_target_pairs={{0,16},{2,18},{4,20},{6,22},{8,24},{10,26},{12,28},{14,30},{16,0},... | collective-permute-start | bytes 393224 | tf_op jit(solution)/shard_map/ppermute | solution.py:451
  39.9 11.3 %collective-permute-start.17 = (f32[4,64,128]{2,1,0:T(8,128)S(1)}, f32[4,64,128]{2,1,0:T(8,128)S(1)}, u32[]{:S(2)}, u32[]{:S(2)}) collective-permute-start(f32[4,64,128]{2,1,0:T(8,128)S(1)} %add.36.refs_5_), channel_id=1, source_target_pairs={{0,8},{2,10},{4,12},{6,14},{8,0},{10,2},{12,4},{14,6},{16,24},{18,... | collective-permute-start | bytes 393224 | tf_op jit(solution)/shard_map/ppermute | solution.py:451
  41.1 10.1 %collective-permute-start.21 = (f32[4,64,128]{2,1,0:T(8,128)S(1)}, f32[4,64,128]{2,1,0:T(8,128)S(1)}, u32[]{:S(2)}, u32[]{:S(2)}) collective-permute-start(f32[4,64,128]{2,1,0:T(8,128)S(1)} %add.36.refs_5_), channel_id=1, source_target_pairs={{0,4},{2,6},{4,0},{6,2},{8,16},{10,18},{12,20},{14,22},{16,8},{18,... | collective-permute-start | bytes 393224 | tf_op jit(solution)/shard_map/ppermute | solution.py:462
  42.6 8.6 %collective-permute-start.18 = (f32[4,64,128]{2,1,0:T(8,128)S(1)}, f32[4,64,128]{2,1,0:T(8,128)S(1)}, u32[]{:S(2)}, u32[]{:S(2)}) collective-permute-start(f32[4,64,128]{2,1,0:T(8,128)S(1)} %collective-permute-done.16.refs_6_), channel_id=1, source_target_pairs={{0,8},{2,10},{4,12},{6,14},{8,0},{10,2},{12,4},{14,6},{16,24},{18,... | collective-permute-start | bytes 393224 | tf_op jit(solution)/shard_map/ppermute | solution.py:451
  42.6 8.6 %collective-permute-start.22 = (f32[4,64,128]{2,1,0:T(8,128)S(1)}, f32[4,64,128]{2,1,0:T(8,128)S(1)}, u32[]{:S(2)}, u32[]{:S(2)}) collective-permute-start(f32[4,64,128]{2,1,0:T(8,128)S(1)} %collective-permute-done.16.refs_6_), channel_id=1, source_target_pairs={{0,4},{2,6},{4,0},{6,2},{8,16},{10,18},{12,20},{14,22},{16,8},{18,... | collective-permute-start | bytes 393224 | tf_op jit(solution)/shard_map/ppermute | solution.py:462
  46.2 5.0 %collective-permute-start.20 = (f32[4,64,128]{2,1,0:T(8,128)S(1)}, f32[4,64,128]{2,1,0:T(8,128)S(1)}, u32[]{:S(2)}, u32[]{:S(2)}) collective-permute-start(f32[4,64,128]{2,1,0:T(8,128)S(1)} %collective-permute-done.19.refs_9_), channel_id=1, source_target_pairs={{0,4},{2,6},{4,0},{6,2},{8,12},{10,14},{12,8},{14,10},{16,20},{18,... | collective-permute-start | bytes 393224 | tf_op jit(solution)/shard_map/ppermute | solution.py:451
  52.7 6.9 %collective-permute-start.23 = (f32[4,64,256]{2,1,0:T(8,128)S(1)}, f32[4,64,256]{2,1,0:T(8,128)S(1)}, u32[]{:S(2)}, u32[]{:S(2)}) collective-permute-start(f32[4,64,256]{2,1,0:T(8,128)S(1)} %update_top.1.mine), channel_id=1, source_target_pairs={{0,1},{1,0},{2,3},{3,2},{4,5},{5,4},{6,7},{7,6},{8,9},{9,8},{10,11... | collective-permute-start | bytes 786440 | tf_op jit(solution)/shard_map/ppermute | solution.py:448
  61.2 6.1 %collective-permute-start.24 = (f32[4,64,128]{2,1,0:T(8,128)S(1)}, f32[4,64,128]{2,1,0:T(8,128)S(1)}, u32[]{:S(2)}, u32[]{:S(2)}) collective-permute-start(f32[4,64,128]{2,1,0:T(8,128)S(1)} %get-tuple-element.121), channel_id=1, source_target_pairs={{0,4},{2,6},{4,0},{6,2},{8,12},{10,14},{12,8},{14,10},{16,20},{18,... | collective-permute-start | bytes 393224 | tf_op jit(solution)/shard_map/ppermute | solution.py:451
  62.4 6.9 %collective-permute-start.26 = (f32[4,64,128]{2,1,0:T(8,128)S(1)}, f32[4,64,128]{2,1,0:T(8,128)S(1)}, u32[]{:S(2)}, u32[]{:S(2)}) collective-permute-start(f32[4,64,128]{2,1,0:T(8,128)S(1)} %get-tuple-element.123), channel_id=1, source_target_pairs={{0,4},{2,6},{4,0},{6,2},{8,16},{10,18},{12,20},{14,22},{16,8},{18,... | collective-permute-start | bytes 393224 | tf_op jit(solution)/shard_map/ppermute | solution.py:462
  63.3 7.2 %collective-permute-start.27 = (f32[4,64,128]{2,1,0:T(8,128)S(1)}, f32[4,64,128]{2,1,0:T(8,128)S(1)}, u32[]{:S(2)}, u32[]{:S(2)}) collective-permute-start(f32[4,64,128]{2,1,0:T(8,128)S(1)} %get-tuple-element.124), channel_id=1, source_target_pairs={{0,8},{2,10},{4,12},{6,14},{8,0},{10,2},{12,4},{14,6},{16,24},{18,... | collective-permute-start | bytes 393224 | tf_op jit(solution)/shard_map/ppermute | solution.py:451
  66.3 5.9 %collective-permute-start.29 = (f32[4,64,128]{2,1,0:T(8,128)S(1)}, f32[4,64,128]{2,1,0:T(8,128)S(1)}, u32[]{:S(2)}, u32[]{:S(2)}) collective-permute-start(f32[4,64,128]{2,1,0:T(8,128)S(1)} %get-tuple-element.125), channel_id=1, source_target_pairs={{0,4},{2,6},{4,0},{6,2},{8,16},{10,18},{12,20},{14,22},{16,8},{18,... | collective-permute-start | bytes 393224 | tf_op jit(solution)/shard_map/ppermute | solution.py:462
  66.9 5.7 %collective-permute-start.30 = (f32[4,64,128]{2,1,0:T(8,128)S(1)}, f32[4,64,128]{2,1,0:T(8,128)S(1)}, u32[]{:S(2)}, u32[]{:S(2)}) collective-permute-start(f32[4,64,128]{2,1,0:T(8,128)S(1)} %get-tuple-element.126), channel_id=1, source_target_pairs={{0,8},{2,10},{4,12},{6,14},{8,0},{10,2},{12,4},{14,6},{16,24},{18,... | collective-permute-start | bytes 393224 | tf_op jit(solution)/shard_map/ppermute | solution.py:451
  67.3 8.9 %collective-permute-start.25 = (f32[4,64,128]{2,1,0:T(8,128)S(1)}, f32[4,64,128]{2,1,0:T(8,128)S(1)}, u32[]{:S(2)}, u32[]{:S(2)}) collective-permute-start(f32[4,64,128]{2,1,0:T(8,128)S(1)} %add.37), channel_id=1, source_target_pairs={{0,16},{2,18},{4,20},{6,22},{8,24},{10,26},{12,28},{14,30},{16,0},... | collective-permute-start | bytes 393224 | tf_op jit(solution)/shard_map/ppermute | solution.py:451
  70.6 5.7 %collective-permute-start.28 = (f32[4,64,128]{2,1,0:T(8,128)S(1)}, f32[4,64,128]{2,1,0:T(8,128)S(1)}, u32[]{:S(2)}, u32[]{:S(2)}) collective-permute-start(f32[4,64,128]{2,1,0:T(8,128)S(1)} %add_add_fusion.1), channel_id=1, source_target_pairs={{0,4},{2,6},{4,0},{6,2},{8,12},{10,14},{12,8},{14,10},{16,20},{18,... | collective-permute-start | bytes 393224 | tf_op jit(solution)/shard_map/ppermute | solution.py:451
  76.3 5.1 %collective-permute-start.31 = (f32[4,64,128]{2,1,0:T(8,128)S(1)}, f32[4,64,128]{2,1,0:T(8,128)S(1)}, u32[]{:S(2)}, u32[]{:S(2)}) collective-permute-start(f32[4,64,128]{2,1,0:T(8,128)S(1)} %add_subtract_fusion.own), channel_id=1, source_target_pairs={{0,1},{1,0},{2,3},{3,2},{4,5},{5,4},{6,7},{7,6},{8,9},{9,8},{10,11... | collective-permute-start | bytes 393224 | tf_op jit(solution)/shard_map/ppermute | solution.py:448
  83.2 6.2 %collective-permute-start.37 = (f32[4,64,128]{2,1,0:T(8,128)S(1)}, f32[4,64,128]{2,1,0:T(8,128)S(1)}, u32[]{:S(2)}, u32[]{:S(2)}) collective-permute-start(f32[4,64,128]{2,1,0:T(8,128)S(1)} %get-tuple-element.146), channel_id=1, source_target_pairs={{0,4},{2,6},{4,0},{6,2},{8,12},{10,14},{12,8},{14,10},{16,20},{18,... | collective-permute-start | bytes 393224 | tf_op jit(solution)/shard_map/ppermute | solution.py:451
  84.2 7.0 %collective-permute-start.34 = (f32[4,64,128]{2,1,0:T(8,128)S(1)}, f32[4,64,128]{2,1,0:T(8,128)S(1)}, u32[]{:S(2)}, u32[]{:S(2)}) collective-permute-start(f32[4,64,128]{2,1,0:T(8,128)S(1)} %get-tuple-element.143), channel_id=1, source_target_pairs={{0,4},{2,6},{4,0},{6,2},{8,16},{10,18},{12,20},{14,22},{16,8},{18,... | collective-permute-start | bytes 393224 | tf_op jit(solution)/shard_map/ppermute | solution.py:462
  85.3 6.0 %collective-permute-start.35 = (f32[4,64,128]{2,1,0:T(8,128)S(1)}, f32[4,64,128]{2,1,0:T(8,128)S(1)}, u32[]{:S(2)}, u32[]{:S(2)}) collective-permute-start(f32[4,64,128]{2,1,0:T(8,128)S(1)} %get-tuple-element.144), channel_id=1, source_target_pairs={{0,8},{2,10},{4,12},{6,14},{8,0},{10,2},{12,4},{14,6},{16,24},{18,... | collective-permute-start | bytes 393224 | tf_op jit(solution)/shard_map/ppermute | solution.py:451
  86.4 6.0 %collective-permute-start.32 = (f32[4,64,128]{2,1,0:T(8,128)S(1)}, f32[4,64,128]{2,1,0:T(8,128)S(1)}, u32[]{:S(2)}, u32[]{:S(2)}) collective-permute-start(f32[4,64,128]{2,1,0:T(8,128)S(1)} %get-tuple-element.140), channel_id=1, source_target_pairs={{0,8},{2,10},{4,12},{6,14},{8,0},{10,2},{12,4},{14,6},{16,24},{18,... | collective-permute-start | bytes 393224 | tf_op jit(solution)/shard_map/ppermute | solution.py:451
  87.3 5.1 %collective-permute-start.33 = (f32[4,64,128]{2,1,0:T(8,128)S(1)}, f32[4,64,128]{2,1,0:T(8,128)S(1)}, u32[]{:S(2)}, u32[]{:S(2)}) collective-permute-start(f32[4,64,128]{2,1,0:T(8,128)S(1)} %get-tuple-element.141), channel_id=1, source_target_pairs={{0,4},{2,6},{4,0},{6,2},{8,16},{10,18},{12,20},{14,22},{16,8},{18,... | collective-permute-start | bytes 393224 | tf_op jit(solution)/shard_map/ppermute | solution.py:462
  89.4 7.3 %collective-permute-start.38 = (f32[4,64,128]{2,1,0:T(8,128)S(1)}, f32[4,64,128]{2,1,0:T(8,128)S(1)}, u32[]{:S(2)}, u32[]{:S(2)}) collective-permute-start(f32[4,64,128]{2,1,0:T(8,128)S(1)} %add.46), channel_id=1, source_target_pairs={{0,16},{2,18},{4,20},{6,22},{8,24},{10,26},{12,28},{14,30},{16,0},... | collective-permute-start | bytes 393224 | tf_op jit(solution)/shard_map/ppermute | solution.py:451
  91.2 5.5 %collective-permute-start.36 = (f32[4,64,128]{2,1,0:T(8,128)S(1)}, f32[4,64,128]{2,1,0:T(8,128)S(1)}, u32[]{:S(2)}, u32[]{:S(2)}) collective-permute-start(f32[4,64,128]{2,1,0:T(8,128)S(1)} %add_add_fusion), channel_id=1, source_target_pairs={{0,4},{2,6},{4,0},{6,2},{8,12},{10,14},{12,8},{14,10},{16,20},{18,... | collective-permute-start | bytes 393224 | tf_op jit(solution)/shard_map/ppermute | solution.py:451
  97.0 1.4 %collective-permute-start.39 = (f32[2,64,256]{2,1,0:T(8,128)S(1)}, f32[2,64,256]{2,1,0:T(8,128)S(1)}, u32[]{:S(2)}, u32[]{:S(2)}) collective-permute-start(f32[2,64,256]{2,1,0:T(8,128)S(1)} %get-tuple-element.148), channel_id=1, source_target_pairs={{0,2},{2,0},{4,6},{6,4},{8,10},{10,8},{12,14},{14,12},{16,18},{18,... | collective-permute-start | bytes 393224 | tf_op jit(solution)/shard_map/ppermute | solution.py:451
  97.1 2.6 %collective-permute-start.41 = (f32[2,64,128]{2,1,0:T(8,128)S(1)}, f32[2,64,128]{2,1,0:T(8,128)S(1)}, u32[]{:S(2)}, u32[]{:S(2)}) collective-permute-start(f32[2,64,128]{2,1,0:T(8,128)S(1)} %get-tuple-element.154), channel_id=1, source_target_pairs={{0,2},{2,0},{4,6},{6,4},{8,10},{10,8},{12,14},{14,12},{16,18},{18,... | collective-permute-start | bytes 196616 | tf_op jit(solution)/shard_map/ppermute | solution.py:451
  97.6 2.1 %collective-permute-start.42 = (f32[2,64,128]{2,1,0:T(8,128)S(1)}, f32[2,64,128]{2,1,0:T(8,128)S(1)}, u32[]{:S(2)}, u32[]{:S(2)}) collective-permute-start(f32[2,64,128]{2,1,0:T(8,128)S(1)} %get-tuple-element.156), channel_id=1, source_target_pairs={{0,2},{2,0},{4,6},{6,4},{8,10},{10,8},{12,14},{14,12},{16,18},{18,... | collective-permute-start | bytes 196616 | tf_op jit(solution)/shard_map/ppermute | solution.py:451
  98.6 5.6 %collective-permute-start.40 = (f32[2,128,128]{2,1,0:T(8,128)S(1)}, f32[2,128,128]{2,1,0:T(8,128)S(1)}, u32[]{:S(2)}, u32[]{:S(2)}) collective-permute-start(f32[2,128,128]{2,1,0:T(8,128)S(1)} %get-tuple-element.150), channel_id=1, source_target_pairs={{0,1},{1,0},{2,3},{3,2},{4,5},{5,4},{6,7},{7,6},{8,9},{9,8},{10,11... | collective-permute-start | bytes 393224 | tf_op jit(solution)/shard_map/ppermute | solution.py:448

commit v7 on v6

--- a/solution.py
+++ b/solution.py
@@ -525,6 +525,9 @@
         [*places, *uppers, *low_tiles, *pieces0], 2, scratch,
     )[0]
     own, other = call(middle_values, "middle_values", [piece] * 2, [partial, *diags], 0)
+    low_ready, _ = after((low_tiles, other))
+    low_turned = call(diag_by_tiles, "diag_by_tiles", wide, [*diags, *low_ready], 0, cost=3000)
+    own, low_turned = after((own, low_turned))
     values1 = own + swap_cols(other)
     pieces1 = gather_pieces(values1)
     tiles, _ = after((factor_tiles, values1))
@@ -547,8 +550,7 @@
         [*places, partial, swap_cols(partial), *top_turned], 2, scratch,
     )
     carried = values1 - functools.reduce(jnp.add, scatter_upper(out))
-    residual, low_ready, _ = after((residual, low_tiles, carried))
-    low_turned = call(diag_by_tiles, "diag_by_tiles", wide, [*diags, *low_ready], 0, cost=3000)
+    residual, _ = after((residual, carried))
     lowest, mine2, partner2 = call(
         lowest_carry, "lowest_carry", [window, shared, shared],
         [*places, residual, *top_turned, grams], 2, cost=2000,

time: 105 us -> 105 us (level)
  transfers between devices with their start and end apart: 43 -> 43, of which waited for: 17 -> 19; matrix products, arithmetic and copies ran while one was open for 2% -> 2% of each run, Pallas kernels for 15% -> 15%
where the time goes in v7:
time: 105 us
  starting transfers between devices  46.6 us (44%)
  waiting for transfers between devices  32 us (30%)
  Pallas kernels  21.4 us (20%)
  local copies, waits for them, and re-layouts  3.36 us (3%)
    ppermute x29, starting transfers between devices, swap_rows(): lax.ppermute(value, 'rows', [(r, r ^ bits) for r in range(rows_total)])  29.1 us
    ppermute x29, waiting for transfers between devices, swap_rows(): lax.ppermute(value, 'rows', [(r, r ^ bits) for r in range(rows_total)])  21.3 us
    pallas_call x14, Pallas kernels, call(): pl.pallas_call(kernel, out_shape=[jax.ShapeDtypeStruct(*out) if isinstanc...  15.3 us
    ppermute x6, waiting for transfers between devices, swap_cols(): return lax.ppermute(value, 'cols', [(0, 1), (1, 0)])  10.4 us
    ppermute x6, starting transfers between devices, swap_cols(): return lax.ppermute(value, 'cols', [(0, 1), (1, 0)])  9.59 us
    ppermute x8, starting transfers between devices, swap_mid(): return lax.ppermute(value, 'rows', pairs)  7.88 us
    pallas_call x2, Pallas kernels, split_tiles(): pl.pallas_call(split_kernel, grid=(owned,), out_shape=[jax.ShapeDtypeStru...  3.67 us
  transfers between devices with their start and end apart: 43, of which 19 were waited for; matrix products, arithmetic and copies ran while one was open for 2% of the time, Pallas kernels for 15%

profile of v7, /device:TPU:0, one launch (start us, length us, event | category | flops | bytes accessed | tf_op | source)
XLA Modules:
  0.0 104.6 jit_solution(13819558264588827058)
XLA Ops:
  0.5 0.9 slice_bitcast_fusion.rhs_own
  1.4 3.0 %collective-permute-start.3 = (f32[2,128,128]{2,1,0:T(8,128)S(1)}, f32[2,128,128]{2,1,0:T(8,128)S(1)}, u32[]{:S(2)}, u32[]{:S(2)}) collective-permute-start(f32[2,128,128]{2,1,0:T(8,128)S(1)} %slice_bitcast_fusion.rhs_own), channel_id=1, source_target_pairs={{0,1},{1,0},{2,3},{3,2},{4,5},{5,4},{6,7},{7,6},{8,9},{9,8},{10,11... | collective-permute-start | bytes 393224 | tf_op jit(solution)/shard_map/ppermute | solution.py:448
  4.5 1.1 %slice.6 = f32[2,2,128,256]{3,2,1,0:T(8,128)S(1)} slice(f32[3,2,128,256]{3,2,1,0:T(8,128)} %d_own.1), slice={[1:3], [0:2], [0:128], [0:256]} | slice | bytes 1048576 | tf_op jit(solution)/shard_map/slice | solution.py:492
  7.0 1.5 %slot_places.1.places = s32[3,16]{1,0:T(4,128)S(1)} custom-call(s32[2,2,8]{2,1,0:T(2,128)S(1)} %copy-done.2, s32[2,2]{1,0:T(2,128)S(1)} %copy-done.3), custom_call_target="tpu_custom_call" | custom-call | flops 500000000 | tf_op jit(solution)/shard_map/slot_places/pallas_call | solution.py:495
  8.6 1.0 split_diag.1
  12.1 1.9 %collective-permute-start.6 = (f32[4,64,128]{2,1,0:T(8,128)S(1)}, f32[4,64,128]{2,1,0:T(8,128)S(1)}, u32[]{:S(2)}, u32[]{:S(2)}) collective-permute-start(f32[4,64,128]{2,1,0:T(8,128)S(1)} %pad_maximum_fusion.1.refs_4_.values), channel_id=1, source_target_pairs={{0,4},{2,6},{4,0},{6,2},{8,12},{10,14},{12,8},{14,10},{16,20},{18,... | collective-permute-start | bytes 393224 | tf_op jit(solution)/shard_map/ppermute | solution.py:451
  14.0 2.6 %collective-permute-start.9 = (f32[4,64,128]{2,1,0:T(8,128)S(1)}, f32[4,64,128]{2,1,0:T(8,128)S(1)}, u32[]{:S(2)}, u32[]{:S(2)}) collective-permute-start(f32[4,64,128]{2,1,0:T(8,128)S(1)} %pad_maximum_fusion.1.refs_4_.values), channel_id=1, source_target_pairs={{0,16},{2,18},{4,20},{6,22},{8,24},{10,26},{12,28},{14,30},{16,0},... | collective-permute-start | bytes 393224 | tf_op jit(solution)/shard_map/ppermute | solution.py:451
  17.2 1.0 collective-permute-start.7
  18.2 1.6 %collective-permute-start.12 = (f32[4,64,128]{2,1,0:T(8,128)S(1)}, f32[4,64,128]{2,1,0:T(8,128)S(1)}, u32[]{:S(2)}, u32[]{:S(2)}) collective-permute-start(f32[4,64,128]{2,1,0:T(8,128)S(1)} %collective-permute-done.6.refs_5_), channel_id=1, source_target_pairs={{0,4},{2,6},{4,0},{6,2},{8,16},{10,18},{12,20},{14,22},{16,8},{18,... | collective-permute-start | bytes 393224 | tf_op jit(solution)/shard_map/ppermute | solution.py:462
  19.8 1.5 %collective-permute-start.8 = (f32[4,64,128]{2,1,0:T(8,128)S(1)}, f32[4,64,128]{2,1,0:T(8,128)S(1)}, u32[]{:S(2)}, u32[]{:S(2)}) collective-permute-start(f32[4,64,128]{2,1,0:T(8,128)S(1)} %collective-permute-done.6.refs_5_), channel_id=1, source_target_pairs={{0,8},{2,10},{4,12},{6,14},{8,0},{10,2},{12,4},{14,6},{16,24},{18,... | collective-permute-start | bytes 393224 | tf_op jit(solution)/shard_map/ppermute | solution.py:451
  21.3 2.9 %collective-permute-done.9.refs_8_ = f32[4,64,128]{2,1,0:T(8,128)S(1)} collective-permute-done((f32[4,64,128]{2,1,0:T(8,128)S(1)}, f32[4,64,128]{2,1,0:T(8,128)S(1)}, u32[]{:S(2)}, u32[]{:S(2)}) %collective-permute-start.9) | collective-permute-done | bytes 131104 | tf_op jit(solution)/shard_map/ppermute | solution.py:451
  24.3 1.8 %split_tiles.2 = (bf16[2,1024,256]{2,1,0:T(8,128)(2,1)S(1)}, bf16[2,1024,256]{2,1,0:T(8,128)(2,1)S(1)}, bf16[2,1024,256]{2,1,0:T(8,128)(2,1)S(1)}, bf16[2,1024,256]{2,1,0:T(8,128)(2,1)S(1)}) custom-call(f32[2,2,8,128,256]{4,3,2,1,0:T(8,128)} %own.2, f32[2,2,8,128,256]{4,3,2,1,0:T(8,128)S(1)} %collective-permute-done.1.partner), custom_call_target="tpu_custom_call" | custom-call | flops 2000000000 | tf_op jit(solution)/shard_map/split_tiles/pallas_call | solution.py:187
  26.6 2.4 %collective-permute-done.10.refs_9_ = f32[4,64,128]{2,1,0:T(8,128)S(1)} collective-permute-done((f32[4,64,128]{2,1,0:T(8,128)S(1)}, f32[4,64,128]{2,1,0:T(8,128)S(1)}, u32[]{:S(2)}, u32[]{:S(2)}) %collective-permute-start.10) | collective-permute-done | bytes 131104 | tf_op jit(solution)/shard_map/ppermute | solution.py:451
  29.1 1.4 %update_middle.1.residual = f32[4,64,256]{2,1,0:T(8,128)S(1)} custom-call(s32[3,16]{1,0:T(4,128)S(1)} %slot_places.1.places, s32[3,16]{1,0:T(4,128)S(1)} %collective-permute-done.places_partner, f32[2,2,64,128]{3,2,1,0:T(8,128)S(1)} %get-tuple-element.100.rhs, f32[2,2,64,128]{3,2,1,0:T(8,128)S(1)} %collective-permute-done.5.rhs_partner, ...), custom_call_target="tpu_custom_call" | custom-call | flops 1000000000 | tf_op jit(solution)/shard_map/update_middle/pallas_call | solution.py:157
  31.5 1.6 %collective-permute-start.15 = (f32[4,64,128]{2,1,0:T(8,128)S(1)}, f32[4,64,128]{2,1,0:T(8,128)S(1)}, u32[]{:S(2)}, u32[]{:S(2)}) collective-permute-start(f32[4,64,128]{2,1,0:T(8,128)S(1)} %get-tuple-element.110), channel_id=1, source_target_pairs={{0,1},{1,0},{2,3},{3,2},{4,5},{5,4},{6,7},{7,6},{8,9},{9,8},{10,11... | collective-permute-start | bytes 393224 | tf_op jit(solution)/shard_map/ppermute | solution.py:448
  33.0 1.9 %diag_by_tiles.1 = (bf16[2,256,1024]{2,1,0:T(8,128)(2,1)S(1)}, bf16[2,256,1024]{2,1,0:T(8,128)(2,1)S(1)}, bf16[2,256,1024]{2,1,0:T(8,128)(2,1)S(1)}, bf16[2,256,1024]{2,1,0:T(8,128)(2,1)S(1)}) custom-call(f32[3,2,128,256]{3,2,1,0:T(8,128)S(1)} %copy-done, f32[3,2,128,256]{3,2,1,0:T(8,128)S(1)} %collective-permute-done.2.d1.d_partner, ...), custom_call_target="tpu_custom_call" | custom-call | flops 3000000000 | tf_op jit(solution)/shard_map/diag_by_tiles/pallas_call | solution.py:157
  34.9 2.2 %collective-permute-done.15 = f32[4,64,128]{2,1,0:T(8,128)S(1)} collective-permute-done((f32[4,64,128]{2,1,0:T(8,128)S(1)}, f32[4,64,128]{2,1,0:T(8,128)S(1)}, u32[]{:S(2)}, u32[]{:S(2)}) %collective-permute-start.15) | collective-permute-done | bytes 131104 | tf_op jit(solution)/shard_map/ppermute | solution.py:448
  37.5 2.4 %collective-permute-start.19 = (f32[4,64,128]{2,1,0:T(8,128)S(1)}, f32[4,64,128]{2,1,0:T(8,128)S(1)}, u32[]{:S(2)}, u32[]{:S(2)}) collective-permute-start(f32[4,64,128]{2,1,0:T(8,128)S(1)} %add.36.refs_5_), channel_id=1, source_target_pairs={{0,16},{2,18},{4,20},{6,22},{8,24},{10,26},{12,28},{14,30},{16,0},... | collective-permute-start | bytes 393224 | tf_op jit(solution)/shard_map/ppermute | solution.py:451
  39.9 1.3 %collective-permute-start.17 = (f32[4,64,128]{2,1,0:T(8,128)S(1)}, f32[4,64,128]{2,1,0:T(8,128)S(1)}, u32[]{:S(2)}, u32[]{:S(2)}) collective-permute-start(f32[4,64,128]{2,1,0:T(8,128)S(1)} %add.36.refs_5_), channel_id=1, source_target_pairs={{0,8},{2,10},{4,12},{6,14},{8,0},{10,2},{12,4},{14,6},{16,24},{18,... | collective-permute-start | bytes 393224 | tf_op jit(solution)/shard_map/ppermute | solution.py:451
  41.1 1.5 %collective-permute-start.21 = (f32[4,64,128]{2,1,0:T(8,128)S(1)}, f32[4,64,128]{2,1,0:T(8,128)S(1)}, u32[]{:S(2)}, u32[]{:S(2)}) collective-permute-start(f32[4,64,128]{2,1,0:T(8,128)S(1)} %add.36.refs_5_), channel_id=1, source_target_pairs={{0,4},{2,6},{4,0},{6,2},{8,16},{10,18},{12,20},{14,22},{16,8},{18,... | collective-permute-start | bytes 393224 | tf_op jit(solution)/shard_map/ppermute | solution.py:462
  43.4 2.8 %collective-permute-done.19.refs_9_ = f32[4,64,128]{2,1,0:T(8,128)S(1)} collective-permute-done((f32[4,64,128]{2,1,0:T(8,128)S(1)}, f32[4,64,128]{2,1,0:T(8,128)S(1)}, u32[]{:S(2)}, u32[]{:S(2)}) %collective-permute-start.19) | collective-permute-done | bytes 131104 | tf_op jit(solution)/shard_map/ppermute | solution.py:451
  46.2 1.7 %collective-permute-start.20 = (f32[4,64,128]{2,1,0:T(8,128)S(1)}, f32[4,64,128]{2,1,0:T(8,128)S(1)}, u32[]{:S(2)}, u32[]{:S(2)}) collective-permute-start(f32[4,64,128]{2,1,0:T(8,128)S(1)} %collective-permute-done.19.refs_9_), channel_id=1, source_target_pairs={{0,4},{2,6},{4,0},{6,2},{8,12},{10,14},{12,8},{14,10},{16,20},{18,... | collective-permute-start | bytes 393224 | tf_op jit(solution)/shard_map/ppermute | solution.py:451
  47.9 1.8 %split_tiles.3 = (bf16[2,1024,256]{2,1,0:T(8,128)(2,1)S(1)}, bf16[2,1024,256]{2,1,0:T(8,128)(2,1)S(1)}, bf16[2,1024,256]{2,1,0:T(8,128)(2,1)S(1)}, bf16[2,1024,256]{2,1,0:T(8,128)(2,1)S(1)}) custom-call(f32[2,2,8,128,256]{4,3,2,1,0:T(8,128)} %own.2, f32[2,2,8,128,256]{4,3,2,1,0:T(8,128)S(1)} %collective-permute-done.1.partner), custom_call_target="tpu_custom_call" | custom-call | flops 2000000000 | tf_op jit(solution)/shard_map/split_tiles/pallas_call | solution.py:187
  49.8 1.5 %update_top_low.1.refs_4_ = f32[4,64,256]{2,1,0:T(8,128)S(1)} custom-call(s32[3,16]{1,0:T(4,128)S(1)} %slot_places.1.places, s32[3,16]{1,0:T(4,128)S(1)} %collective-permute-done.places_partner, f32[2,2,64,128]{3,2,1,0:T(8,128)S(1)} %get-tuple-element.100.rhs, f32[2,2,64,128]{3,2,1,0:T(8,128)S(1)} %collective-permute-done.5.rhs_partner, ...), custom_call_target="tpu_custom_call" | custom-call | flops 1000000000 | tf_op jit(solution)/shard_map/update_top_low/pallas_call | solution.py:157
  51.3 1.5 %update_top.1.mine = f32[4,64,256]{2,1,0:T(8,128)S(1)} custom-call(s32[3,16]{1,0:T(4,128)S(1)} %slot_places.1.places, s32[3,16]{1,0:T(4,128)S(1)} %collective-permute-done.places_partner, bf16[2,1024,256]{2,1,0:T(8,128)(2,1)S(1)} %get-tuple-element.125.refs_0_, bf16[2,1024,256]{2,1,0:T(8,128)(2,1)S(1)} %get-tuple-element.126.refs_1_, ...), custom_call_target="tpu_custom_call" | custom-call | flops 1000000000 | tf_op jit(solution)/shard_map/update_top/pallas_call | solution.py:157
  52.7 1.7 %collective-permute-start.23 = (f32[4,64,256]{2,1,0:T(8,128)S(1)}, f32[4,64,256]{2,1,0:T(8,128)S(1)}, u32[]{:S(2)}, u32[]{:S(2)}) collective-permute-start(f32[4,64,256]{2,1,0:T(8,128)S(1)} %update_top.1.mine), channel_id=1, source_target_pairs={{0,1},{1,0},{2,3},{3,2},{4,5},{5,4},{6,7},{7,6},{8,9},{9,8},{10,11... | collective-permute-start | bytes 786440 | tf_op jit(solution)/shard_map/ppermute | solution.py:448
  54.4 2.7 %gram_by_tiles.1 = (f32[4,256,256]{2,1,0:T(8,128)S(1)}, bf16[2,256,1024]{2,1,0:T(8,128)(2,1)S(1)}, bf16[2,256,1024]{2,1,0:T(8,128)(2,1)S(1)}, bf16[2,256,1024]{2,1,0:T(8,128)(2,1)S(1)}, bf16[2,256,1024]{2,1,0:T(8,128)(2,1)S(1)}) custom-call(f32[3,2,128,256]{3,2,1,0:T(8,128)S(1)} %copy-done, f32[3,2,128,256]{3,2,1,0:T(8,128)S(1)} %collective-permute-done.2.d1.d_partner, ...), custom_call_target="tpu_custom_call" | custom-call | flops 3000000000 | tf_op jit(solution)/shard_map/gram_by_tiles/pallas_call | solution.py:157
  57.1 2.5 %collective-permute-done.23.theirs = f32[4,64,256]{2,1,0:T(8,128)S(1)} collective-permute-done((f32[4,64,256]{2,1,0:T(8,128)S(1)}, f32[4,64,256]{2,1,0:T(8,128)S(1)}, u32[]{:S(2)}, u32[]{:S(2)}) %collective-permute-start.23) | collective-permute-done | bytes 262176 | tf_op jit(solution)/shard_map/ppermute | solution.py:448
  59.6 1.6 %top_carry.1 = (f32[4,64,256]{2,1,0:T(8,128)S(1)}, f32[4,64,128]{2,1,0:T(8,128)S(1)}, f32[4,64,128]{2,1,0:T(8,128)S(1)}, f32[4,64,128]{2,1,0:T(8,128)S(1)}, f32[...) custom-call(s32[3,16]{1,0:T(4,128)S(1)} %slot_places.1.places, ...), custom_call_target="tpu_custom_call" | custom-call | flops 1000000000 | tf_op jit(solution)/shard_map/top_carry/pallas_call | solution.py:157
  61.2 1.2 %collective-permute-start.24 = (f32[4,64,128]{2,1,0:T(8,128)S(1)}, f32[4,64,128]{2,1,0:T(8,128)S(1)}, u32[]{:S(2)}, u32[]{:S(2)}) collective-permute-start(f32[4,64,128]{2,1,0:T(8,128)S(1)} %get-tuple-element.135), channel_id=1, source_target_pairs={{0,4},{2,6},{4,0},{6,2},{8,12},{10,14},{12,8},{14,10},{16,20},{18,... | collective-permute-start | bytes 393224 | tf_op jit(solution)/shard_map/ppermute | solution.py:451
  63.3 3.1 %collective-permute-start.27 = (f32[4,64,128]{2,1,0:T(8,128)S(1)}, f32[4,64,128]{2,1,0:T(8,128)S(1)}, u32[]{:S(2)}, u32[]{:S(2)}) collective-permute-start(f32[4,64,128]{2,1,0:T(8,128)S(1)} %get-tuple-element.138), channel_id=1, source_target_pairs={{0,8},{2,10},{4,12},{6,14},{8,0},{10,2},{12,4},{14,6},{16,24},{18,... | collective-permute-start | bytes 393224 | tf_op jit(solution)/shard_map/ppermute | solution.py:451
  67.3 2.0 %collective-permute-start.25 = (f32[4,64,128]{2,1,0:T(8,128)S(1)}, f32[4,64,128]{2,1,0:T(8,128)S(1)}, u32[]{:S(2)}, u32[]{:S(2)}) collective-permute-start(f32[4,64,128]{2,1,0:T(8,128)S(1)} %add.37), channel_id=1, source_target_pairs={{0,16},{2,18},{4,20},{6,22},{8,24},{10,26},{12,28},{14,30},{16,0},... | collective-permute-start | bytes 393224 | tf_op jit(solution)/shard_map/ppermute | solution.py:451
  69.3 1.2 %collective-permute-done.27 = f32[4,64,128]{2,1,0:T(8,128)S(1)} collective-permute-done((f32[4,64,128]{2,1,0:T(8,128)S(1)}, f32[4,64,128]{2,1,0:T(8,128)S(1)}, u32[]{:S(2)}, u32[]{:S(2)}) %collective-permute-start.27) | collective-permute-done | bytes 131104 | tf_op jit(solution)/shard_map/ppermute | solution.py:451
  70.6 1.7 %collective-permute-start.28 = (f32[4,64,128]{2,1,0:T(8,128)S(1)}, f32[4,64,128]{2,1,0:T(8,128)S(1)}, u32[]{:S(2)}, u32[]{:S(2)}) collective-permute-start(f32[4,64,128]{2,1,0:T(8,128)S(1)} %add_add_fusion.1), channel_id=1, source_target_pairs={{0,4},{2,6},{4,0},{6,2},{8,12},{10,14},{12,8},{14,10},{16,20},{18,... | collective-permute-start | bytes 393224 | tf_op jit(solution)/shard_map/ppermute | solution.py:451
  72.6 3.7 %collective-permute-done.25 = f32[4,64,128]{2,1,0:T(8,128)S(1)} collective-permute-done((f32[4,64,128]{2,1,0:T(8,128)S(1)}, f32[4,64,128]{2,1,0:T(8,128)S(1)}, u32[]{:S(2)}, u32[]{:S(2)}) %collective-permute-start.25) | collective-permute-done | bytes 131104 | tf_op jit(solution)/shard_map/ppermute | solution.py:451
  76.3 1.6 %collective-permute-start.31 = (f32[4,64,128]{2,1,0:T(8,128)S(1)}, f32[4,64,128]{2,1,0:T(8,128)S(1)}, u32[]{:S(2)}, u32[]{:S(2)}) collective-permute-start(f32[4,64,128]{2,1,0:T(8,128)S(1)} %add_subtract_fusion.own), channel_id=1, source_target_pairs={{0,1},{1,0},{2,3},{3,2},{4,5},{5,4},{6,7},{7,6},{8,9},{9,8},{10,11... | collective-permute-start | bytes 393224 | tf_op jit(solution)/shard_map/ppermute | solution.py:448
  77.9 1.7 %lowest_carry.1 = (f32[32,64,128]{2,1,0:T(8,128)S(1)}, f32[2,64,128]{2,1,0:T(8,128)S(1)}, f32[2,64,128]{2,1,0:T(8,128)S(1)}) custom-call(s32[3,16]{1,0:T(4,128)S(1)} %slot_places.1.places, s32[3,16]{1,0:T(4,128)S(1)} %collective-permute-done.places_partner, f32[4,64,256]{2,1,0:T(8,128)S(1)} %get-tuple-element.146.residual, ...), custom_call_target="tpu_custom_call" | custom-call | flops 2000000000 | tf_op jit(solution)/shard_map/lowest_carry/pallas_call | solution.py:157
  79.5 1.8 %collective-permute-done.31.other = f32[4,64,128]{2,1,0:T(8,128)S(1)} collective-permute-done((f32[4,64,128]{2,1,0:T(8,128)S(1)}, f32[4,64,128]{2,1,0:T(8,128)S(1)}, u32[]{:S(2)}, u32[]{:S(2)}) %collective-permute-start.31) | collective-permute-done | bytes 131104 | tf_op jit(solution)/shard_map/ppermute | solution.py:448
  81.3 1.7 %middle_carry.1 = (f32[2,64,128]{2,1,0:T(8,128)S(1)}, f32[2,64,128]{2,1,0:T(8,128)S(1)}, f32[4,64,128]{2,1,0:T(8,128)S(1)}, f32[4,64,128]{2,1,0:T(8,128)S(1)}, f...) custom-call(s32[3,16]{1,0:T(4,128)S(1)} %slot_places.1.places, ...), custom_call_target="tpu_custom_call" | custom-call | flops 1000000000 | tf_op jit(solution)/shard_map/middle_carry/pallas_call | solution.py:157
  83.1 1.0 collective-permute-start.37
  84.1 1.1 %collective-permute-start.34 = (f32[4,64,128]{2,1,0:T(8,128)S(1)}, f32[4,64,128]{2,1,0:T(8,128)S(1)}, u32[]{:S(2)}, u32[]{:S(2)}) collective-permute-start(f32[4,64,128]{2,1,0:T(8,128)S(1)} %get-tuple-element.153), channel_id=1, source_target_pairs={{0,4},{2,6},{4,0},{6,2},{8,16},{10,18},{12,20},{14,22},{16,8},{18,... | collective-permute-start | bytes 393224 | tf_op jit(solution)/shard_map/ppermute | solution.py:462
  85.1 1.2 %collective-permute-start.35 = (f32[4,64,128]{2,1,0:T(8,128)S(1)}, f32[4,64,128]{2,1,0:T(8,128)S(1)}, u32[]{:S(2)}, u32[]{:S(2)}) collective-permute-start(f32[4,64,128]{2,1,0:T(8,128)S(1)} %get-tuple-element.154), channel_id=1, source_target_pairs={{0,8},{2,10},{4,12},{6,14},{8,0},{10,2},{12,4},{14,6},{16,24},{18,... | collective-permute-start | bytes 393224 | tf_op jit(solution)/shard_map/ppermute | solution.py:451
  87.2 1.0 collective-permute-start.33
  89.0 1.7 %collective-permute-start.38 = (f32[4,64,128]{2,1,0:T(8,128)S(1)}, f32[4,64,128]{2,1,0:T(8,128)S(1)}, u32[]{:S(2)}, u32[]{:S(2)}) collective-permute-start(f32[4,64,128]{2,1,0:T(8,128)S(1)} %add.46), channel_id=1, source_target_pairs={{0,16},{2,18},{4,20},{6,22},{8,24},{10,26},{12,28},{14,30},{16,0},... | collective-permute-start | bytes 393224 | tf_op jit(solution)/shard_map/ppermute | solution.py:451
  90.7 1.2 %collective-permute-start.36 = (f32[4,64,128]{2,1,0:T(8,128)S(1)}, f32[4,64,128]{2,1,0:T(8,128)S(1)}, u32[]{:S(2)}, u32[]{:S(2)}) collective-permute-start(f32[4,64,128]{2,1,0:T(8,128)S(1)} %add_add_fusion), channel_id=1, source_target_pairs={{0,4},{2,6},{4,0},{6,2},{8,12},{10,14},{12,8},{14,10},{16,20},{18,... | collective-permute-start | bytes 393224 | tf_op jit(solution)/shard_map/ppermute | solution.py:451
  92.1 4.2 %collective-permute-done.38.e = f32[4,64,128]{2,1,0:T(8,128)S(1)} collective-permute-done((f32[4,64,128]{2,1,0:T(8,128)S(1)}, f32[4,64,128]{2,1,0:T(8,128)S(1)}, u32[]{:S(2)}, u32[]{:S(2)}) %collective-permute-start.38) | collective-permute-done | bytes 131104 | tf_op jit(solution)/shard_map/ppermute | solution.py:451
  98.2 1.6 %collective-permute-start.40 = (f32[2,128,128]{2,1,0:T(8,128)S(1)}, f32[2,128,128]{2,1,0:T(8,128)S(1)}, u32[]{:S(2)}, u32[]{:S(2)}) collective-permute-start(f32[2,128,128]{2,1,0:T(8,128)S(1)} %get-tuple-element.160), channel_id=1, source_target_pairs={{0,1},{1,0},{2,3},{3,2},{4,5},{5,4},{6,7},{7,6},{8,9},{9,8},{10,11... | collective-permute-start | bytes 393224 | tf_op jit(solution)/shard_map/ppermute | solution.py:448
  99.9 3.9 %collective-permute-done.40 = f32[2,128,128]{2,1,0:T(8,128)S(1)} collective-permute-done((f32[2,128,128]{2,1,0:T(8,128)S(1)}, f32[2,128,128]{2,1,0:T(8,128)S(1)}, u32[]{:S(2)}, u32[]{:S(2)}) %collective-permute-start.40) | collective-permute-done | bytes 131104 | tf_op jit(solution)/shard_map/ppermute | solution.py:448
  (75 shorter events, 14.8 us)
Async XLA Ops:
  0.0 9.8 %collective-permute-start.1 = (f32[2,2,8,128,256]{4,3,2,1,0:T(8,128)}, f32[2,2,8,128,256]{4,3,2,1,0:T(8,128)S(1)}, u32[]{:S(2)}, u32[]{:S(2)}) collective-permute-start(f32[2,2,8,128,256]{4,3,2,1,0:T(8,128)} %own.2), channel_id=1, source_target_pairs={{0,2},{2,0},{4,6},{6,4},{8,10},{10,8},{12,14},{14,12},{16,18},{18,... | collective-permute-start | bytes 12582920 | tf_op jit(solution)/shard_map/ppermute | solution.py:451
  0.5 9.3 %collective-permute-start.2 = (f32[3,2,128,256]{3,2,1,0:T(8,128)}, f32[3,2,128,256]{3,2,1,0:T(8,128)S(1)}, u32[]{:S(2)}, u32[]{:S(2)}) collective-permute-start(f32[3,2,128,256]{3,2,1,0:T(8,128)} %d_own.1), channel_id=1, source_target_pairs={{0,2},{2,0},{4,6},{6,4},{8,10},{10,8},{12,14},{14,12},{16,18},{18,... | collective-permute-start | bytes 2359304 | tf_op jit(solution)/shard_map/ppermute | solution.py:451
  1.4 9.1 %copy-start.1 = (f32[3,2,128,128]{3,2,1,0:T(8,128)S(1)}, f32[3,2,128,128]{3,2,1,0:T(8,128)}, u32[]{:S(2)}) copy-start(f32[3,2,128,128]{3,2,1,0:T(8,128)} %rhs.1) | copy-start | bytes 1179652
  1.4 8.3 %collective-permute-start.3 = (f32[2,128,128]{2,1,0:T(8,128)S(1)}, f32[2,128,128]{2,1,0:T(8,128)S(1)}, u32[]{:S(2)}, u32[]{:S(2)}) collective-permute-start(f32[2,128,128]{2,1,0:T(8,128)S(1)} %slice_bitcast_fusion.rhs_own), channel_id=1, source_target_pairs={{0,1},{1,0},{2,3},{3,2},{4,5},{5,4},{6,7},{7,6},{8,9},{9,8},{10,11... | collective-permute-start | bytes 393224 | tf_op jit(solution)/shard_map/ppermute | solution.py:448
  5.6 14.2 %collective-permute-start.13 = (f32[2,2,128,256]{3,2,1,0:T(8,128)S(1)}, f32[2,2,128,256]{3,2,1,0:T(8,128)S(1)}, u32[]{:S(2)}, u32[]{:S(2)}) collective-permute-start(f32[2,2,128,256]{3,2,1,0:T(8,128)S(1)} %slice.6), channel_id=1, source_target_pairs={{0,1},{1,0},{2,3},{3,2},{4,5},{5,4},{6,7},{7,6},{8,9},{9,8},{10,11... | collective-permute-start | bytes 1572872 | tf_op jit(solution)/shard_map/ppermute | solution.py:448
  5.7 0.7 copy-start.2
  6.3 0.7 copy-start.3
  8.5 1.2 %collective-permute-start = (s32[3,16]{1,0:T(4,128)S(1)}, s32[3,16]{1,0:T(4,128)S(1)}, u32[]{:S(2)}, u32[]{:S(2)}) collective-permute-start(s32[3,16]{1,0:T(4,128)S(1)} %slot_places.1.places), channel_id=1, source_target_pairs={{0,2},{2,0},{4,6},{6,4},{8,10},{10,8},{12,14},{14,12},{16,18},{18,... | collective-permute-start | bytes 584 | tf_op jit(solution)/shard_map/ppermute | solution.py:451
  10.1 1.3 %collective-permute-start.4 = (f32[2,64,128]{2,1,0:T(8,128)S(1)}, f32[2,64,128]{2,1,0:T(8,128)S(1)}, u32[]{:S(2)}, u32[]{:S(2)}) collective-permute-start(f32[2,64,128]{2,1,0:T(8,128)S(1)} %get-tuple-element.94), channel_id=1, source_target_pairs={{0,2},{2,0},{4,6},{6,4},{8,10},{10,8},{12,14},{14,12},{16,18},{18,... | collective-permute-start | bytes 196616 | tf_op jit(solution)/shard_map/ppermute | solution.py:451
  10.7 1.4 %collective-permute-start.5 = (f32[2,2,64,128]{3,2,1,0:T(8,128)S(1)}, f32[2,2,64,128]{3,2,1,0:T(8,128)S(1)}, u32[]{:S(2)}, u32[]{:S(2)}) collective-permute-start(f32[2,2,64,128]{3,2,1,0:T(8,128)S(1)} %get-tuple-element.96), channel_id=1, source_target_pairs={{0,2},{2,0},{4,6},{6,4},{8,10},{10,8},{12,14},{14,12},{16,18},{18,... | collective-permute-start | bytes 393224 | tf_op jit(solution)/shard_map/ppermute | solution.py:451
  12.1 6.1 %collective-permute-start.6 = (f32[4,64,128]{2,1,0:T(8,128)S(1)}, f32[4,64,128]{2,1,0:T(8,128)S(1)}, u32[]{:S(2)}, u32[]{:S(2)}) collective-permute-start(f32[4,64,128]{2,1,0:T(8,128)S(1)} %pad_maximum_fusion.1.refs_4_.values), channel_id=1, source_target_pairs={{0,4},{2,6},{4,0},{6,2},{8,12},{10,14},{12,8},{14,10},{16,20},{18,... | collective-permute-start | bytes 393224 | tf_op jit(solution)/shard_map/ppermute | solution.py:451
  14.0 10.1 %collective-permute-start.9 = (f32[4,64,128]{2,1,0:T(8,128)S(1)}, f32[4,64,128]{2,1,0:T(8,128)S(1)}, u32[]{:S(2)}, u32[]{:S(2)}) collective-permute-start(f32[4,64,128]{2,1,0:T(8,128)S(1)} %pad_maximum_fusion.1.refs_4_.values), channel_id=1, source_target_pairs={{0,16},{2,18},{4,20},{6,22},{8,24},{10,26},{12,28},{14,30},{16,0},... | collective-permute-start | bytes 393224 | tf_op jit(solution)/shard_map/ppermute | solution.py:451
  16.6 9.5 %collective-permute-start.11 = (f32[4,64,128]{2,1,0:T(8,128)S(1)}, f32[4,64,128]{2,1,0:T(8,128)S(1)}, u32[]{:S(2)}, u32[]{:S(2)}) collective-permute-start(f32[4,64,128]{2,1,0:T(8,128)S(1)} %pad_maximum_fusion.1.refs_4_.values), channel_id=1, source_target_pairs={{0,4},{2,6},{4,0},{6,2},{8,16},{10,18},{12,20},{14,22},{16,8},{18,... | collective-permute-start | bytes 393224 | tf_op jit(solution)/shard_map/ppermute | solution.py:462
  17.2 9.0 %collective-permute-start.7 = (f32[4,64,128]{2,1,0:T(8,128)S(1)}, f32[4,64,128]{2,1,0:T(8,128)S(1)}, u32[]{:S(2)}, u32[]{:S(2)}) collective-permute-start(f32[4,64,128]{2,1,0:T(8,128)S(1)} %pad_maximum_fusion.1.refs_4_.values), channel_id=1, source_target_pairs={{0,8},{2,10},{4,12},{6,14},{8,0},{10,2},{12,4},{14,6},{16,24},{18,... | collective-permute-start | bytes 393224 | tf_op jit(solution)/shard_map/ppermute | solution.py:451
  18.2 8.0 %collective-permute-start.12 = (f32[4,64,128]{2,1,0:T(8,128)S(1)}, f32[4,64,128]{2,1,0:T(8,128)S(1)}, u32[]{:S(2)}, u32[]{:S(2)}) collective-permute-start(f32[4,64,128]{2,1,0:T(8,128)S(1)} %collective-permute-done.6.refs_5_), channel_id=1, source_target_pairs={{0,4},{2,6},{4,0},{6,2},{8,16},{10,18},{12,20},{14,22},{16,8},{18,... | collective-permute-start | bytes 393224 | tf_op jit(solution)/shard_map/ppermute | solution.py:462
  19.8 6.9 %collective-permute-start.8 = (f32[4,64,128]{2,1,0:T(8,128)S(1)}, f32[4,64,128]{2,1,0:T(8,128)S(1)}, u32[]{:S(2)}, u32[]{:S(2)}) collective-permute-start(f32[4,64,128]{2,1,0:T(8,128)S(1)} %collective-permute-done.6.refs_5_), channel_id=1, source_target_pairs={{0,8},{2,10},{4,12},{6,14},{8,0},{10,2},{12,4},{14,6},{16,24},{18,... | collective-permute-start | bytes 393224 | tf_op jit(solution)/shard_map/ppermute | solution.py:451
  24.1 5.0 %collective-permute-start.10 = (f32[4,64,128]{2,1,0:T(8,128)S(1)}, f32[4,64,128]{2,1,0:T(8,128)S(1)}, u32[]{:S(2)}, u32[]{:S(2)}) collective-permute-start(f32[4,64,128]{2,1,0:T(8,128)S(1)} %collective-permute-done.9.refs_8_), channel_id=1, source_target_pairs={{0,4},{2,6},{4,0},{6,2},{8,12},{10,14},{12,8},{14,10},{16,20},{18,... | collective-permute-start | bytes 393224 | tf_op jit(solution)/shard_map/ppermute | solution.py:451
  26.1 4.9 %copy-start = (f32[3,2,128,256]{3,2,1,0:T(8,128)S(1)}, f32[3,2,128,256]{3,2,1,0:T(8,128)}, u32[]{:S(2)}) copy-start(f32[3,2,128,256]{3,2,1,0:T(8,128)} %d_own.1) | copy-start | bytes 2359300
  29.1 1.9 %collective-permute-start.14 = (f32[2,2,128,256]{3,2,1,0:T(8,128)S(1)}, f32[2,2,128,256]{3,2,1,0:T(8,128)S(1)}, u32[]{:S(2)}, u32[]{:S(2)}) collective-permute-start(f32[2,2,128,256]{3,2,1,0:T(8,128)S(1)} %collective-permute-done.13.d2), channel_id=1, source_target_pairs={{0,2},{2,0},{4,6},{6,4},{8,10},{10,8},{12,14},{14,12},{16,18},{18,... | collective-permute-start | bytes 1572872 | tf_op jit(solution)/shard_map/ppermute | solution.py:451
  31.5 5.6 %collective-permute-start.15 = (f32[4,64,128]{2,1,0:T(8,128)S(1)}, f32[4,64,128]{2,1,0:T(8,128)S(1)}, u32[]{:S(2)}, u32[]{:S(2)}) collective-permute-start(f32[4,64,128]{2,1,0:T(8,128)S(1)} %get-tuple-element.110), channel_id=1, source_target_pairs={{0,1},{1,0},{2,3},{3,2},{4,5},{5,4},{6,7},{7,6},{8,9},{9,8},{10,11... | collective-permute-start | bytes 393224 | tf_op jit(solution)/shard_map/ppermute | solution.py:448
  37.1 5.5 %collective-permute-start.16 = (f32[4,64,128]{2,1,0:T(8,128)S(1)}, f32[4,64,128]{2,1,0:T(8,128)S(1)}, u32[]{:S(2)}, u32[]{:S(2)}) collective-permute-start(f32[4,64,128]{2,1,0:T(8,128)S(1)} %add.36.refs_5_), channel_id=1, source_target_pairs={{0,4},{2,6},{4,0},{6,2},{8,12},{10,14},{12,8},{14,10},{16,20},{18,... | collective-permute-start | bytes 393224 | tf_op jit(solution)/shard_map/ppermute | solution.py:451
  37.5 8.8 %collective-permute-start.19 = (f32[4,64,128]{2,1,0:T(8,128)S(1)}, f32[4,64,128]{2,1,0:T(8,128)S(1)}, u32[]{:S(2)}, u32[]{:S(2)}) collective-permute-start(f32[4,64,128]{2,1,0:T(8,128)S(1)} %add.36.refs_5_), channel_id=1, source_target_pairs={{0,16},{2,18},{4,20},{6,22},{8,24},{10,26},{12,28},{14,30},{16,0},... | collective-permute-start | bytes 393224 | tf_op jit(solution)/shard_map/ppermute | solution.py:451
  39.9 11.3 %collective-permute-start.17 = (f32[4,64,128]{2,1,0:T(8,128)S(1)}, f32[4,64,128]{2,1,0:T(8,128)S(1)}, u32[]{:S(2)}, u32[]{:S(2)}) collective-permute-start(f32[4,64,128]{2,1,0:T(8,128)S(1)} %add.36.refs_5_), channel_id=1, source_target_pairs={{0,8},{2,10},{4,12},{6,14},{8,0},{10,2},{12,4},{14,6},{16,24},{18,... | collective-permute-start | bytes 393224 | tf_op jit(solution)/shard_map/ppermute | solution.py:451
  41.1 10.1 %collective-permute-start.21 = (f32[4,64,128]{2,1,0:T(8,128)S(1)}, f32[4,64,128]{2,1,0:T(8,128)S(1)}, u32[]{:S(2)}, u32[]{:S(2)}) collective-permute-start(f32[4,64,128]{2,1,0:T(8,128)S(1)} %add.36.refs_5_), channel_id=1, source_target_pairs={{0,4},{2,6},{4,0},{6,2},{8,16},{10,18},{12,20},{14,22},{16,8},{18,... | collective-permute-start | bytes 393224 | tf_op jit(solution)/shard_map/ppermute | solution.py:462
  42.6 8.6 %collective-permute-start.18 = (f32[4,64,128]{2,1,0:T(8,128)S(1)}, f32[4,64,128]{2,1,0:T(8,128)S(1)}, u32[]{:S(2)}, u32[]{:S(2)}) collective-permute-start(f32[4,64,128]{2,1,0:T(8,128)S(1)} %collective-permute-done.16.refs_6_), channel_id=1, source_target_pairs={{0,8},{2,10},{4,12},{6,14},{8,0},{10,2},{12,4},{14,6},{16,24},{18,... | collective-permute-start | bytes 393224 | tf_op jit(solution)/shard_map/ppermute | solution.py:451
  42.6 8.6 %collective-permute-start.22 = (f32[4,64,128]{2,1,0:T(8,128)S(1)}, f32[4,64,128]{2,1,0:T(8,128)S(1)}, u32[]{:S(2)}, u32[]{:S(2)}) collective-permute-start(f32[4,64,128]{2,1,0:T(8,128)S(1)} %collective-permute-done.16.refs_6_), channel_id=1, source_target_pairs={{0,4},{2,6},{4,0},{6,2},{8,16},{10,18},{12,20},{14,22},{16,8},{18,... | collective-permute-start | bytes 393224 | tf_op jit(solution)/shard_map/ppermute | solution.py:462
  46.2 5.0 %collective-permute-start.20 = (f32[4,64,128]{2,1,0:T(8,128)S(1)}, f32[4,64,128]{2,1,0:T(8,128)S(1)}, u32[]{:S(2)}, u32[]{:S(2)}) collective-permute-start(f32[4,64,128]{2,1,0:T(8,128)S(1)} %collective-permute-done.19.refs_9_), channel_id=1, source_target_pairs={{0,4},{2,6},{4,0},{6,2},{8,12},{10,14},{12,8},{14,10},{16,20},{18,... | collective-permute-start | bytes 393224 | tf_op jit(solution)/shard_map/ppermute | solution.py:451
  52.7 6.9 %collective-permute-start.23 = (f32[4,64,256]{2,1,0:T(8,128)S(1)}, f32[4,64,256]{2,1,0:T(8,128)S(1)}, u32[]{:S(2)}, u32[]{:S(2)}) collective-permute-start(f32[4,64,256]{2,1,0:T(8,128)S(1)} %update_top.1.mine), channel_id=1, source_target_pairs={{0,1},{1,0},{2,3},{3,2},{4,5},{5,4},{6,7},{7,6},{8,9},{9,8},{10,11... | collective-permute-start | bytes 786440 | tf_op jit(solution)/shard_map/ppermute | solution.py:448
  61.2 6.1 %collective-permute-start.24 = (f32[4,64,128]{2,1,0:T(8,128)S(1)}, f32[4,64,128]{2,1,0:T(8,128)S(1)}, u32[]{:S(2)}, u32[]{:S(2)}) collective-permute-start(f32[4,64,128]{2,1,0:T(8,128)S(1)} %get-tuple-element.135), channel_id=1, source_target_pairs={{0,4},{2,6},{4,0},{6,2},{8,12},{10,14},{12,8},{14,10},{16,20},{18,... | collective-permute-start | bytes 393224 | tf_op jit(solution)/shard_map/ppermute | solution.py:451
  62.4 6.9 %collective-permute-start.26 = (f32[4,64,128]{2,1,0:T(8,128)S(1)}, f32[4,64,128]{2,1,0:T(8,128)S(1)}, u32[]{:S(2)}, u32[]{:S(2)}) collective-permute-start(f32[4,64,128]{2,1,0:T(8,128)S(1)} %get-tuple-element.137), channel_id=1, source_target_pairs={{0,4},{2,6},{4,0},{6,2},{8,16},{10,18},{12,20},{14,22},{16,8},{18,... | collective-permute-start | bytes 393224 | tf_op jit(solution)/shard_map/ppermute | solution.py:462
  63.3 7.2 %collective-permute-start.27 = (f32[4,64,128]{2,1,0:T(8,128)S(1)}, f32[4,64,128]{2,1,0:T(8,128)S(1)}, u32[]{:S(2)}, u32[]{:S(2)}) collective-permute-start(f32[4,64,128]{2,1,0:T(8,128)S(1)} %get-tuple-element.138), channel_id=1, source_target_pairs={{0,8},{2,10},{4,12},{6,14},{8,0},{10,2},{12,4},{14,6},{16,24},{18,... | collective-permute-start | bytes 393224 | tf_op jit(solution)/shard_map/ppermute | solution.py:451
  66.3 5.9 %collective-permute-start.29 = (f32[4,64,128]{2,1,0:T(8,128)S(1)}, f32[4,64,128]{2,1,0:T(8,128)S(1)}, u32[]{:S(2)}, u32[]{:S(2)}) collective-permute-start(f32[4,64,128]{2,1,0:T(8,128)S(1)} %get-tuple-element.139), channel_id=1, source_target_pairs={{0,4},{2,6},{4,0},{6,2},{8,16},{10,18},{12,20},{14,22},{16,8},{18,... | collective-permute-start | bytes 393224 | tf_op jit(solution)/shard_map/ppermute | solution.py:462
  66.9 5.7 %collective-permute-start.30 = (f32[4,64,128]{2,1,0:T(8,128)S(1)}, f32[4,64,128]{2,1,0:T(8,128)S(1)}, u32[]{:S(2)}, u32[]{:S(2)}) collective-permute-start(f32[4,64,128]{2,1,0:T(8,128)S(1)} %get-tuple-element.140), channel_id=1, source_target_pairs={{0,8},{2,10},{4,12},{6,14},{8,0},{10,2},{12,4},{14,6},{16,24},{18,... | collective-permute-start | bytes 393224 | tf_op jit(solution)/shard_map/ppermute | solution.py:451
  67.3 8.9 %collective-permute-start.25 = (f32[4,64,128]{2,1,0:T(8,128)S(1)}, f32[4,64,128]{2,1,0:T(8,128)S(1)}, u32[]{:S(2)}, u32[]{:S(2)}) collective-permute-start(f32[4,64,128]{2,1,0:T(8,128)S(1)} %add.37), channel_id=1, source_target_pairs={{0,16},{2,18},{4,20},{6,22},{8,24},{10,26},{12,28},{14,30},{16,0},... | collective-permute-start | bytes 393224 | tf_op jit(solution)/shard_map/ppermute | solution.py:451
  70.6 5.7 %collective-permute-start.28 = (f32[4,64,128]{2,1,0:T(8,128)S(1)}, f32[4,64,128]{2,1,0:T(8,128)S(1)}, u32[]{:S(2)}, u32[]{:S(2)}) collective-permute-start(f32[4,64,128]{2,1,0:T(8,128)S(1)} %add_add_fusion.1), channel_id=1, source_target_pairs={{0,4},{2,6},{4,0},{6,2},{8,12},{10,14},{12,8},{14,10},{16,20},{18,... | collective-permute-start | bytes 393224 | tf_op jit(solution)/shard_map/ppermute | solution.py:451
  76.3 5.0 %collective-permute-start.31 = (f32[4,64,128]{2,1,0:T(8,128)S(1)}, f32[4,64,128]{2,1,0:T(8,128)S(1)}, u32[]{:S(2)}, u32[]{:S(2)}) collective-permute-start(f32[4,64,128]{2,1,0:T(8,128)S(1)} %add_subtract_fusion.own), channel_id=1, source_target_pairs={{0,1},{1,0},{2,3},{3,2},{4,5},{5,4},{6,7},{7,6},{8,9},{9,8},{10,11... | collective-permute-start | bytes 393224 | tf_op jit(solution)/shard_map/ppermute | solution.py:448
  83.1 5.9 %collective-permute-start.37 = (f32[4,64,128]{2,1,0:T(8,128)S(1)}, f32[4,64,128]{2,1,0:T(8,128)S(1)}, u32[]{:S(2)}, u32[]{:S(2)}) collective-permute-start(f32[4,64,128]{2,1,0:T(8,128)S(1)} %get-tuple-element.156), channel_id=1, source_target_pairs={{0,4},{2,6},{4,0},{6,2},{8,12},{10,14},{12,8},{14,10},{16,20},{18,... | collective-permute-start | bytes 393224 | tf_op jit(solution)/shard_map/ppermute | solution.py:451
  84.1 6.6 %collective-permute-start.34 = (f32[4,64,128]{2,1,0:T(8,128)S(1)}, f32[4,64,128]{2,1,0:T(8,128)S(1)}, u32[]{:S(2)}, u32[]{:S(2)}) collective-permute-start(f32[4,64,128]{2,1,0:T(8,128)S(1)} %get-tuple-element.153), channel_id=1, source_target_pairs={{0,4},{2,6},{4,0},{6,2},{8,16},{10,18},{12,20},{14,22},{16,8},{18,... | collective-permute-start | bytes 393224 | tf_op jit(solution)/shard_map/ppermute | solution.py:462
  85.1 5.5 %collective-permute-start.35 = (f32[4,64,128]{2,1,0:T(8,128)S(1)}, f32[4,64,128]{2,1,0:T(8,128)S(1)}, u32[]{:S(2)}, u32[]{:S(2)}) collective-permute-start(f32[4,64,128]{2,1,0:T(8,128)S(1)} %get-tuple-element.154), channel_id=1, source_target_pairs={{0,8},{2,10},{4,12},{6,14},{8,0},{10,2},{12,4},{14,6},{16,24},{18,... | collective-permute-start | bytes 393224 | tf_op jit(solution)/shard_map/ppermute | solution.py:451
  86.3 5.5 %collective-permute-start.32 = (f32[4,64,128]{2,1,0:T(8,128)S(1)}, f32[4,64,128]{2,1,0:T(8,128)S(1)}, u32[]{:S(2)}, u32[]{:S(2)}) collective-permute-start(f32[4,64,128]{2,1,0:T(8,128)S(1)} %get-tuple-element.150), channel_id=1, source_target_pairs={{0,8},{2,10},{4,12},{6,14},{8,0},{10,2},{12,4},{14,6},{16,24},{18,... | collective-permute-start | bytes 393224 | tf_op jit(solution)/shard_map/ppermute | solution.py:451
  87.2 5.0 %collective-permute-start.33 = (f32[4,64,128]{2,1,0:T(8,128)S(1)}, f32[4,64,128]{2,1,0:T(8,128)S(1)}, u32[]{:S(2)}, u32[]{:S(2)}) collective-permute-start(f32[4,64,128]{2,1,0:T(8,128)S(1)} %get-tuple-element.151), channel_id=1, source_target_pairs={{0,4},{2,6},{4,0},{6,2},{8,16},{10,18},{12,20},{14,22},{16,8},{18,... | collective-permute-start | bytes 393224 | tf_op jit(solution)/shard_map/ppermute | solution.py:462
  89.0 7.3 %collective-permute-start.38 = (f32[4,64,128]{2,1,0:T(8,128)S(1)}, f32[4,64,128]{2,1,0:T(8,128)S(1)}, u32[]{:S(2)}, u32[]{:S(2)}) collective-permute-start(f32[4,64,128]{2,1,0:T(8,128)S(1)} %add.46), channel_id=1, source_target_pairs={{0,16},{2,18},{4,20},{6,22},{8,24},{10,26},{12,28},{14,30},{16,0},... | collective-permute-start | bytes 393224 | tf_op jit(solution)/shard_map/ppermute | solution.py:451
  90.7 5.6 %collective-permute-start.36 = (f32[4,64,128]{2,1,0:T(8,128)S(1)}, f32[4,64,128]{2,1,0:T(8,128)S(1)}, u32[]{:S(2)}, u32[]{:S(2)}) collective-permute-start(f32[4,64,128]{2,1,0:T(8,128)S(1)} %add_add_fusion), channel_id=1, source_target_pairs={{0,4},{2,6},{4,0},{6,2},{8,12},{10,14},{12,8},{14,10},{16,20},{18,... | collective-permute-start | bytes 393224 | tf_op jit(solution)/shard_map/ppermute | solution.py:451
  96.6 1.4 %collective-permute-start.39 = (f32[2,64,256]{2,1,0:T(8,128)S(1)}, f32[2,64,256]{2,1,0:T(8,128)S(1)}, u32[]{:S(2)}, u32[]{:S(2)}) collective-permute-start(f32[2,64,256]{2,1,0:T(8,128)S(1)} %get-tuple-element.158), channel_id=1, source_target_pairs={{0,2},{2,0},{4,6},{6,4},{8,10},{10,8},{12,14},{14,12},{16,18},{18,... | collective-permute-start | bytes 393224 | tf_op jit(solution)/shard_map/ppermute | solution.py:451
  96.7 3.1 %collective-permute-start.41 = (f32[2,64,128]{2,1,0:T(8,128)S(1)}, f32[2,64,128]{2,1,0:T(8,128)S(1)}, u32[]{:S(2)}, u32[]{:S(2)}) collective-permute-start(f32[2,64,128]{2,1,0:T(8,128)S(1)} %get-tuple-element.164), channel_id=1, source_target_pairs={{0,2},{2,0},{4,6},{6,4},{8,10},{10,8},{12,14},{14,12},{16,18},{18,... | collective-permute-start | bytes 196616 | tf_op jit(solution)/shard_map/ppermute | solution.py:451
  97.2 2.6 %collective-permute-start.42 = (f32[2,64,128]{2,1,0:T(8,128)S(1)}, f32[2,64,128]{2,1,0:T(8,128)S(1)}, u32[]{:S(2)}, u32[]{:S(2)}) collective-permute-start(f32[2,64,128]{2,1,0:T(8,128)S(1)} %get-tuple-element.166), channel_id=1, source_target_pairs={{0,2},{2,0},{4,6},{6,4},{8,10},{10,8},{12,14},{14,12},{16,18},{18,... | collective-permute-start | bytes 196616 | tf_op jit(solution)/shard_map/ppermute | solution.py:451
  98.2 5.6 %collective-permute-start.40 = (f32[2,128,128]{2,1,0:T(8,128)S(1)}, f32[2,128,128]{2,1,0:T(8,128)S(1)}, u32[]{:S(2)}, u32[]{:S(2)}) collective-permute-start(f32[2,128,128]{2,1,0:T(8,128)S(1)} %get-tuple-element.160), channel_id=1, source_target_pairs={{0,1},{1,0},{2,3},{3,2},{4,5},{5,4},{6,7},{7,6},{8,9},{9,8},{10,11... | collective-permute-start | bytes 393224 | tf_op jit(solution)/shard_map/ppermute | solution.py:448

commit v8 on v7

--- a/solution.py
+++ b/solution.py
@@ -482,7 +482,7 @@
         beside = swap_x(p[1] + (swap_mid(p[7]) + swap_rows(p[3], 4)))
         mid = swap_mid(p[6])
         near = swap_rows(p[2], 4)
-        return [p[0], near, mid, beside, far]
+        return [p[0], mid, near, beside, far]
 
     rhs0 = rhs[0]
     rhs0_other = swap_cols(rhs0)

time: 105 us -> 105 us (level)
  transfers between devices with their start and end apart: 43 -> 43, of which waited for: 19 -> 20; matrix products, arithmetic and copies ran while one was open for 2% -> 2% of each run, Pallas kernels for 15% -> 15%
where the time goes in v8:
time: 105 us
  starting transfers between devices  47 us (45%)
  waiting for transfers between devices  31.6 us (30%)
  Pallas kernels  21.4 us (20%)
  local copies, waits for them, and re-layouts  3.36 us (3%)
    ppermute x29, starting transfers between devices, swap_rows(): lax.ppermute(value, 'rows', [(r, r ^ bits) for r in range(rows_total)])  28.7 us
    ppermute x29, waiting for transfers between devices, swap_rows(): lax.ppermute(value, 'rows', [(r, r ^ bits) for r in range(rows_total)])  21 us
    pallas_call x14, Pallas kernels, call(): pl.pallas_call(kernel, out_shape=[jax.ShapeDtypeStruct(*out) if isinstanc...  15.2 us
    ppermute x6, waiting for transfers between devices, swap_cols(): return lax.ppermute(value, 'cols', [(0, 1), (1, 0)])  10.4 us
    ppermute x6, starting transfers between devices, swap_cols(): return lax.ppermute(value, 'cols', [(0, 1), (1, 0)])  9.6 us
    ppermute x8, starting transfers between devices, swap_mid(): return lax.ppermute(value, 'rows', pairs)  8.67 us
    pallas_call x2, Pallas kernels, split_tiles(): pl.pallas_call(split_kernel, grid=(owned,), out_shape=[jax.ShapeDtypeStru...  3.67 us
  transfers between devices with their start and end apart: 43, of which 20 were waited for; matrix products, arithmetic and copies ran while one was open for 2% of the time, Pallas kernels for 15%

profile of v8, /device:TPU:0, one launch (start us, length us, event | category | flops | bytes accessed | tf_op | source)
XLA Modules:
  0.0 104.6 jit_solution(11993299951586017746)
XLA Ops:
  0.5 0.9 slice_bitcast_fusion.rhs_own
  1.4 3.0 %collective-permute-start.3 = (f32[2,128,128]{2,1,0:T(8,128)S(1)}, f32[2,128,128]{2,1,0:T(8,128)S(1)}, u32[]{:S(2)}, u32[]{:S(2)}) collective-permute-start(f32[2,128,128]{2,1,0:T(8,128)S(1)} %slice_bitcast_fusion.rhs_own), channel_id=1, source_target_pairs={{0,1},{1,0},{2,3},{3,2},{4,5},{5,4},{6,7},{7,6},{8,9},{9,8},{10,11... | collective-permute-start | bytes 393224 | tf_op jit(solution)/shard_map/ppermute | solution.py:448
  4.5 1.1 %slice.6 = f32[2,2,128,256]{3,2,1,0:T(8,128)S(1)} slice(f32[3,2,128,256]{3,2,1,0:T(8,128)} %d_own.1), slice={[1:3], [0:2], [0:128], [0:256]} | slice | bytes 1048576 | tf_op jit(solution)/shard_map/slice | solution.py:492
  7.0 1.5 %slot_places.1.places = s32[3,16]{1,0:T(4,128)S(1)} custom-call(s32[2,2,8]{2,1,0:T(2,128)S(1)} %copy-done.2, s32[2,2]{1,0:T(2,128)S(1)} %copy-done.3), custom_call_target="tpu_custom_call" | custom-call | flops 500000000 | tf_op jit(solution)/shard_map/slot_places/pallas_call | solution.py:495
  8.6 1.0 split_diag.1
  12.1 1.9 %collective-permute-start.6 = (f32[4,64,128]{2,1,0:T(8,128)S(1)}, f32[4,64,128]{2,1,0:T(8,128)S(1)}, u32[]{:S(2)}, u32[]{:S(2)}) collective-permute-start(f32[4,64,128]{2,1,0:T(8,128)S(1)} %pad_maximum_fusion.1.refs_4_.values), channel_id=1, source_target_pairs={{0,4},{2,6},{4,0},{6,2},{8,12},{10,14},{12,8},{14,10},{16,20},{18,... | collective-permute-start | bytes 393224 | tf_op jit(solution)/shard_map/ppermute | solution.py:451
  14.0 2.6 %collective-permute-start.9 = (f32[4,64,128]{2,1,0:T(8,128)S(1)}, f32[4,64,128]{2,1,0:T(8,128)S(1)}, u32[]{:S(2)}, u32[]{:S(2)}) collective-permute-start(f32[4,64,128]{2,1,0:T(8,128)S(1)} %pad_maximum_fusion.1.refs_4_.values), channel_id=1, source_target_pairs={{0,16},{2,18},{4,20},{6,22},{8,24},{10,26},{12,28},{14,30},{16,0},... | collective-permute-start | bytes 393224 | tf_op jit(solution)/shard_map/ppermute | solution.py:451
  17.2 1.0 collective-permute-start.7
  18.2 1.6 %collective-permute-start.12 = (f32[4,64,128]{2,1,0:T(8,128)S(1)}, f32[4,64,128]{2,1,0:T(8,128)S(1)}, u32[]{:S(2)}, u32[]{:S(2)}) collective-permute-start(f32[4,64,128]{2,1,0:T(8,128)S(1)} %collective-permute-done.6.refs_5_), channel_id=1, source_target_pairs={{0,4},{2,6},{4,0},{6,2},{8,16},{10,18},{12,20},{14,22},{16,8},{18,... | collective-permute-start | bytes 393224 | tf_op jit(solution)/shard_map/ppermute | solution.py:462
  19.8 1.5 %collective-permute-start.8 = (f32[4,64,128]{2,1,0:T(8,128)S(1)}, f32[4,64,128]{2,1,0:T(8,128)S(1)}, u32[]{:S(2)}, u32[]{:S(2)}) collective-permute-start(f32[4,64,128]{2,1,0:T(8,128)S(1)} %collective-permute-done.6.refs_5_), channel_id=1, source_target_pairs={{0,8},{2,10},{4,12},{6,14},{8,0},{10,2},{12,4},{14,6},{16,24},{18,... | collective-permute-start | bytes 393224 | tf_op jit(solution)/shard_map/ppermute | solution.py:451
  21.3 2.9 %collective-permute-done.9.refs_8_ = f32[4,64,128]{2,1,0:T(8,128)S(1)} collective-permute-done((f32[4,64,128]{2,1,0:T(8,128)S(1)}, f32[4,64,128]{2,1,0:T(8,128)S(1)}, u32[]{:S(2)}, u32[]{:S(2)}) %collective-permute-start.9) | collective-permute-done | bytes 131104 | tf_op jit(solution)/shard_map/ppermute | solution.py:451
  24.3 1.8 %split_tiles.2 = (bf16[2,1024,256]{2,1,0:T(8,128)(2,1)S(1)}, bf16[2,1024,256]{2,1,0:T(8,128)(2,1)S(1)}, bf16[2,1024,256]{2,1,0:T(8,128)(2,1)S(1)}, bf16[2,1024,256]{2,1,0:T(8,128)(2,1)S(1)}) custom-call(f32[2,2,8,128,256]{4,3,2,1,0:T(8,128)} %own.2, f32[2,2,8,128,256]{4,3,2,1,0:T(8,128)S(1)} %collective-permute-done.1.partner), custom_call_target="tpu_custom_call" | custom-call | flops 2000000000 | tf_op jit(solution)/shard_map/split_tiles/pallas_call | solution.py:187
  26.6 2.4 %collective-permute-done.10.refs_9_ = f32[4,64,128]{2,1,0:T(8,128)S(1)} collective-permute-done((f32[4,64,128]{2,1,0:T(8,128)S(1)}, f32[4,64,128]{2,1,0:T(8,128)S(1)}, u32[]{:S(2)}, u32[]{:S(2)}) %collective-permute-start.10) | collective-permute-done | bytes 131104 | tf_op jit(solution)/shard_map/ppermute | solution.py:451
  29.1 1.4 %update_middle.1.residual = f32[4,64,256]{2,1,0:T(8,128)S(1)} custom-call(s32[3,16]{1,0:T(4,128)S(1)} %slot_places.1.places, s32[3,16]{1,0:T(4,128)S(1)} %collective-permute-done.places_partner, f32[2,2,64,128]{3,2,1,0:T(8,128)S(1)} %get-tuple-element.100.rhs, f32[2,2,64,128]{3,2,1,0:T(8,128)S(1)} %collective-permute-done.5.rhs_partner, ...), custom_call_target="tpu_custom_call" | custom-call | flops 1000000000 | tf_op jit(solution)/shard_map/update_middle/pallas_call | solution.py:157
  31.5 1.6 %collective-permute-start.15 = (f32[4,64,128]{2,1,0:T(8,128)S(1)}, f32[4,64,128]{2,1,0:T(8,128)S(1)}, u32[]{:S(2)}, u32[]{:S(2)}) collective-permute-start(f32[4,64,128]{2,1,0:T(8,128)S(1)} %get-tuple-element.110), channel_id=1, source_target_pairs={{0,1},{1,0},{2,3},{3,2},{4,5},{5,4},{6,7},{7,6},{8,9},{9,8},{10,11... | collective-permute-start | bytes 393224 | tf_op jit(solution)/shard_map/ppermute | solution.py:448
  33.0 1.9 %diag_by_tiles.1 = (bf16[2,256,1024]{2,1,0:T(8,128)(2,1)S(1)}, bf16[2,256,1024]{2,1,0:T(8,128)(2,1)S(1)}, bf16[2,256,1024]{2,1,0:T(8,128)(2,1)S(1)}, bf16[2,256,1024]{2,1,0:T(8,128)(2,1)S(1)}) custom-call(f32[3,2,128,256]{3,2,1,0:T(8,128)S(1)} %copy-done, f32[3,2,128,256]{3,2,1,0:T(8,128)S(1)} %collective-permute-done.2.d1.d_partner, ...), custom_call_target="tpu_custom_call" | custom-call | flops 3000000000 | tf_op jit(solution)/shard_map/diag_by_tiles/pallas_call | solution.py:157
  34.9 2.2 %collective-permute-done.15 = f32[4,64,128]{2,1,0:T(8,128)S(1)} collective-permute-done((f32[4,64,128]{2,1,0:T(8,128)S(1)}, f32[4,64,128]{2,1,0:T(8,128)S(1)}, u32[]{:S(2)}, u32[]{:S(2)}) %collective-permute-start.15) | collective-permute-done | bytes 131104 | tf_op jit(solution)/shard_map/ppermute | solution.py:448
  37.5 2.4 %collective-permute-start.19 = (f32[4,64,128]{2,1,0:T(8,128)S(1)}, f32[4,64,128]{2,1,0:T(8,128)S(1)}, u32[]{:S(2)}, u32[]{:S(2)}) collective-permute-start(f32[4,64,128]{2,1,0:T(8,128)S(1)} %add.36.refs_5_), channel_id=1, source_target_pairs={{0,16},{2,18},{4,20},{6,22},{8,24},{10,26},{12,28},{14,30},{16,0},... | collective-permute-start | bytes 393224 | tf_op jit(solution)/shard_map/ppermute | solution.py:451
  39.9 1.3 %collective-permute-start.17 = (f32[4,64,128]{2,1,0:T(8,128)S(1)}, f32[4,64,128]{2,1,0:T(8,128)S(1)}, u32[]{:S(2)}, u32[]{:S(2)}) collective-permute-start(f32[4,64,128]{2,1,0:T(8,128)S(1)} %add.36.refs_5_), channel_id=1, source_target_pairs={{0,8},{2,10},{4,12},{6,14},{8,0},{10,2},{12,4},{14,6},{16,24},{18,... | collective-permute-start | bytes 393224 | tf_op jit(solution)/shard_map/ppermute | solution.py:451
  41.1 1.5 %collective-permute-start.21 = (f32[4,64,128]{2,1,0:T(8,128)S(1)}, f32[4,64,128]{2,1,0:T(8,128)S(1)}, u32[]{:S(2)}, u32[]{:S(2)}) collective-permute-start(f32[4,64,128]{2,1,0:T(8,128)S(1)} %add.36.refs_5_), channel_id=1, source_target_pairs={{0,4},{2,6},{4,0},{6,2},{8,16},{10,18},{12,20},{14,22},{16,8},{18,... | collective-permute-start | bytes 393224 | tf_op jit(solution)/shard_map/ppermute | solution.py:462
  43.4 2.8 %collective-permute-done.19.refs_9_ = f32[4,64,128]{2,1,0:T(8,128)S(1)} collective-permute-done((f32[4,64,128]{2,1,0:T(8,128)S(1)}, f32[4,64,128]{2,1,0:T(8,128)S(1)}, u32[]{:S(2)}, u32[]{:S(2)}) %collective-permute-start.19) | collective-permute-done | bytes 131104 | tf_op jit(solution)/shard_map/ppermute | solution.py:451
  46.2 1.7 %collective-permute-start.20 = (f32[4,64,128]{2,1,0:T(8,128)S(1)}, f32[4,64,128]{2,1,0:T(8,128)S(1)}, u32[]{:S(2)}, u32[]{:S(2)}) collective-permute-start(f32[4,64,128]{2,1,0:T(8,128)S(1)} %collective-permute-done.19.refs_9_), channel_id=1, source_target_pairs={{0,4},{2,6},{4,0},{6,2},{8,12},{10,14},{12,8},{14,10},{16,20},{18,... | collective-permute-start | bytes 393224 | tf_op jit(solution)/shard_map/ppermute | solution.py:451
  47.9 1.8 %split_tiles.3 = (bf16[2,1024,256]{2,1,0:T(8,128)(2,1)S(1)}, bf16[2,1024,256]{2,1,0:T(8,128)(2,1)S(1)}, bf16[2,1024,256]{2,1,0:T(8,128)(2,1)S(1)}, bf16[2,1024,256]{2,1,0:T(8,128)(2,1)S(1)}) custom-call(f32[2,2,8,128,256]{4,3,2,1,0:T(8,128)} %own.2, f32[2,2,8,128,256]{4,3,2,1,0:T(8,128)S(1)} %collective-permute-done.1.partner), custom_call_target="tpu_custom_call" | custom-call | flops 2000000000 | tf_op jit(solution)/shard_map/split_tiles/pallas_call | solution.py:187
  49.8 1.5 %update_top_low.1.refs_4_ = f32[4,64,256]{2,1,0:T(8,128)S(1)} custom-call(s32[3,16]{1,0:T(4,128)S(1)} %slot_places.1.places, s32[3,16]{1,0:T(4,128)S(1)} %collective-permute-done.places_partner, f32[2,2,64,128]{3,2,1,0:T(8,128)S(1)} %get-tuple-element.100.rhs, f32[2,2,64,128]{3,2,1,0:T(8,128)S(1)} %collective-permute-done.5.rhs_partner, ...), custom_call_target="tpu_custom_call" | custom-call | flops 1000000000 | tf_op jit(solution)/shard_map/update_top_low/pallas_call | solution.py:157
  51.3 1.5 %update_top.1.mine = f32[4,64,256]{2,1,0:T(8,128)S(1)} custom-call(s32[3,16]{1,0:T(4,128)S(1)} %slot_places.1.places, s32[3,16]{1,0:T(4,128)S(1)} %collective-permute-done.places_partner, bf16[2,1024,256]{2,1,0:T(8,128)(2,1)S(1)} %get-tuple-element.125.refs_0_, bf16[2,1024,256]{2,1,0:T(8,128)(2,1)S(1)} %get-tuple-element.126.refs_1_, ...), custom_call_target="tpu_custom_call" | custom-call | flops 1000000000 | tf_op jit(solution)/shard_map/update_top/pallas_call | solution.py:157
  52.7 1.7 %collective-permute-start.23 = (f32[4,64,256]{2,1,0:T(8,128)S(1)}, f32[4,64,256]{2,1,0:T(8,128)S(1)}, u32[]{:S(2)}, u32[]{:S(2)}) collective-permute-start(f32[4,64,256]{2,1,0:T(8,128)S(1)} %update_top.1.mine), channel_id=1, source_target_pairs={{0,1},{1,0},{2,3},{3,2},{4,5},{5,4},{6,7},{7,6},{8,9},{9,8},{10,11... | collective-permute-start | bytes 786440 | tf_op jit(solution)/shard_map/ppermute | solution.py:448
  54.4 2.7 %gram_by_tiles.1 = (f32[4,256,256]{2,1,0:T(8,128)S(1)}, bf16[2,256,1024]{2,1,0:T(8,128)(2,1)S(1)}, bf16[2,256,1024]{2,1,0:T(8,128)(2,1)S(1)}, bf16[2,256,1024]{2,1,0:T(8,128)(2,1)S(1)}, bf16[2,256,1024]{2,1,0:T(8,128)(2,1)S(1)}) custom-call(f32[3,2,128,256]{3,2,1,0:T(8,128)S(1)} %copy-done, f32[3,2,128,256]{3,2,1,0:T(8,128)S(1)} %collective-permute-done.2.d1.d_partner, ...), custom_call_target="tpu_custom_call" | custom-call | flops 3000000000 | tf_op jit(solution)/shard_map/gram_by_tiles/pallas_call | solution.py:157
  57.1 2.5 %collective-permute-done.23.theirs = f32[4,64,256]{2,1,0:T(8,128)S(1)} collective-permute-done((f32[4,64,256]{2,1,0:T(8,128)S(1)}, f32[4,64,256]{2,1,0:T(8,128)S(1)}, u32[]{:S(2)}, u32[]{:S(2)}) %collective-permute-start.23) | collective-permute-done | bytes 262176 | tf_op jit(solution)/shard_map/ppermute | solution.py:448
  59.6 1.5 %top_carry.1 = (f32[4,64,256]{2,1,0:T(8,128)S(1)}, f32[4,64,128]{2,1,0:T(8,128)S(1)}, f32[4,64,128]{2,1,0:T(8,128)S(1)}, f32[4,64,128]{2,1,0:T(8,128)S(1)}, f32[...) custom-call(s32[3,16]{1,0:T(4,128)S(1)} %slot_places.1.places, ...), custom_call_target="tpu_custom_call" | custom-call | flops 1000000000 | tf_op jit(solution)/shard_map/top_carry/pallas_call | solution.py:157
  61.2 1.2 %collective-permute-start.24 = (f32[4,64,128]{2,1,0:T(8,128)S(1)}, f32[4,64,128]{2,1,0:T(8,128)S(1)}, u32[]{:S(2)}, u32[]{:S(2)}) collective-permute-start(f32[4,64,128]{2,1,0:T(8,128)S(1)} %get-tuple-element.135), channel_id=1, source_target_pairs={{0,4},{2,6},{4,0},{6,2},{8,12},{10,14},{12,8},{14,10},{16,20},{18,... | collective-permute-start | bytes 393224 | tf_op jit(solution)/shard_map/ppermute | solution.py:451
  63.3 3.1 %collective-permute-start.27 = (f32[4,64,128]{2,1,0:T(8,128)S(1)}, f32[4,64,128]{2,1,0:T(8,128)S(1)}, u32[]{:S(2)}, u32[]{:S(2)}) collective-permute-start(f32[4,64,128]{2,1,0:T(8,128)S(1)} %get-tuple-element.138), channel_id=1, source_target_pairs={{0,8},{2,10},{4,12},{6,14},{8,0},{10,2},{12,4},{14,6},{16,24},{18,... | collective-permute-start | bytes 393224 | tf_op jit(solution)/shard_map/ppermute | solution.py:451
  67.3 2.0 %collective-permute-start.25 = (f32[4,64,128]{2,1,0:T(8,128)S(1)}, f32[4,64,128]{2,1,0:T(8,128)S(1)}, u32[]{:S(2)}, u32[]{:S(2)}) collective-permute-start(f32[4,64,128]{2,1,0:T(8,128)S(1)} %add.37), channel_id=1, source_target_pairs={{0,16},{2,18},{4,20},{6,22},{8,24},{10,26},{12,28},{14,30},{16,0},... | collective-permute-start | bytes 393224 | tf_op jit(solution)/shard_map/ppermute | solution.py:451
  69.3 1.2 %collective-permute-done.27 = f32[4,64,128]{2,1,0:T(8,128)S(1)} collective-permute-done((f32[4,64,128]{2,1,0:T(8,128)S(1)}, f32[4,64,128]{2,1,0:T(8,128)S(1)}, u32[]{:S(2)}, u32[]{:S(2)}) %collective-permute-start.27) | collective-permute-done | bytes 131104 | tf_op jit(solution)/shard_map/ppermute | solution.py:451
  70.6 1.7 %collective-permute-start.28 = (f32[4,64,128]{2,1,0:T(8,128)S(1)}, f32[4,64,128]{2,1,0:T(8,128)S(1)}, u32[]{:S(2)}, u32[]{:S(2)}) collective-permute-start(f32[4,64,128]{2,1,0:T(8,128)S(1)} %add_add_fusion.1), channel_id=1, source_target_pairs={{0,4},{2,6},{4,0},{6,2},{8,12},{10,14},{12,8},{14,10},{16,20},{18,... | collective-permute-start | bytes 393224 | tf_op jit(solution)/shard_map/ppermute | solution.py:451
  72.6 3.7 %collective-permute-done.25 = f32[4,64,128]{2,1,0:T(8,128)S(1)} collective-permute-done((f32[4,64,128]{2,1,0:T(8,128)S(1)}, f32[4,64,128]{2,1,0:T(8,128)S(1)}, u32[]{:S(2)}, u32[]{:S(2)}) %collective-permute-start.25) | collective-permute-done | bytes 131104 | tf_op jit(solution)/shard_map/ppermute | solution.py:451
  76.3 1.6 %collective-permute-start.31 = (f32[4,64,128]{2,1,0:T(8,128)S(1)}, f32[4,64,128]{2,1,0:T(8,128)S(1)}, u32[]{:S(2)}, u32[]{:S(2)}) collective-permute-start(f32[4,64,128]{2,1,0:T(8,128)S(1)} %add_subtract_fusion.own), channel_id=1, source_target_pairs={{0,1},{1,0},{2,3},{3,2},{4,5},{5,4},{6,7},{7,6},{8,9},{9,8},{10,11... | collective-permute-start | bytes 393224 | tf_op jit(solution)/shard_map/ppermute | solution.py:448
  77.9 1.7 %lowest_carry.1 = (f32[32,64,128]{2,1,0:T(8,128)S(1)}, f32[2,64,128]{2,1,0:T(8,128)S(1)}, f32[2,64,128]{2,1,0:T(8,128)S(1)}) custom-call(s32[3,16]{1,0:T(4,128)S(1)} %slot_places.1.places, s32[3,16]{1,0:T(4,128)S(1)} %collective-permute-done.places_partner, f32[4,64,256]{2,1,0:T(8,128)S(1)} %get-tuple-element.146.residual, ...), custom_call_target="tpu_custom_call" | custom-call | flops 2000000000 | tf_op jit(solution)/shard_map/lowest_carry/pallas_call | solution.py:157
  79.6 1.8 %collective-permute-done.31.other = f32[4,64,128]{2,1,0:T(8,128)S(1)} collective-permute-done((f32[4,64,128]{2,1,0:T(8,128)S(1)}, f32[4,64,128]{2,1,0:T(8,128)S(1)}, u32[]{:S(2)}, u32[]{:S(2)}) %collective-permute-start.31) | collective-permute-done | bytes 131104 | tf_op jit(solution)/shard_map/ppermute | solution.py:448
  81.3 1.7 %middle_carry.1 = (f32[2,64,128]{2,1,0:T(8,128)S(1)}, f32[2,64,128]{2,1,0:T(8,128)S(1)}, f32[4,64,128]{2,1,0:T(8,128)S(1)}, f32[4,64,128]{2,1,0:T(8,128)S(1)}, f...) custom-call(s32[3,16]{1,0:T(4,128)S(1)} %slot_places.1.places, ...), custom_call_target="tpu_custom_call" | custom-call | flops 1000000000 | tf_op jit(solution)/shard_map/middle_carry/pallas_call | solution.py:157
  83.1 1.0 collective-permute-start.37
  84.1 1.1 %collective-permute-start.34 = (f32[4,64,128]{2,1,0:T(8,128)S(1)}, f32[4,64,128]{2,1,0:T(8,128)S(1)}, u32[]{:S(2)}, u32[]{:S(2)}) collective-permute-start(f32[4,64,128]{2,1,0:T(8,128)S(1)} %get-tuple-element.153), channel_id=1, source_target_pairs={{0,4},{2,6},{4,0},{6,2},{8,16},{10,18},{12,20},{14,22},{16,8},{18,... | collective-permute-start | bytes 393224 | tf_op jit(solution)/shard_map/ppermute | solution.py:462
  85.1 1.2 %collective-permute-start.35 = (f32[4,64,128]{2,1,0:T(8,128)S(1)}, f32[4,64,128]{2,1,0:T(8,128)S(1)}, u32[]{:S(2)}, u32[]{:S(2)}) collective-permute-start(f32[4,64,128]{2,1,0:T(8,128)S(1)} %get-tuple-element.154), channel_id=1, source_target_pairs={{0,8},{2,10},{4,12},{6,14},{8,0},{10,2},{12,4},{14,6},{16,24},{18,... | collective-permute-start | bytes 393224 | tf_op jit(solution)/shard_map/ppermute | solution.py:451
  86.3 1.8 %collective-permute-start.32 = (f32[4,64,128]{2,1,0:T(8,128)S(1)}, f32[4,64,128]{2,1,0:T(8,128)S(1)}, u32[]{:S(2)}, u32[]{:S(2)}) collective-permute-start(f32[4,64,128]{2,1,0:T(8,128)S(1)} %get-tuple-element.150), channel_id=1, source_target_pairs={{0,4},{2,6},{4,0},{6,2},{8,16},{10,18},{12,20},{14,22},{16,8},{18,... | collective-permute-start | bytes 393224 | tf_op jit(solution)/shard_map/ppermute | solution.py:462
  89.0 1.7 %collective-permute-start.38 = (f32[4,64,128]{2,1,0:T(8,128)S(1)}, f32[4,64,128]{2,1,0:T(8,128)S(1)}, u32[]{:S(2)}, u32[]{:S(2)}) collective-permute-start(f32[4,64,128]{2,1,0:T(8,128)S(1)} %add.46), channel_id=1, source_target_pairs={{0,16},{2,18},{4,20},{6,22},{8,24},{10,26},{12,28},{14,30},{16,0},... | collective-permute-start | bytes 393224 | tf_op jit(solution)/shard_map/ppermute | solution.py:451
  91.8 1.4 %collective-permute-done.33.c = f32[4,64,128]{2,1,0:T(8,128)S(1)} collective-permute-done((f32[4,64,128]{2,1,0:T(8,128)S(1)}, f32[4,64,128]{2,1,0:T(8,128)S(1)}, u32[]{:S(2)}, u32[]{:S(2)}) %collective-permute-start.33) | collective-permute-done | bytes 131104 | tf_op jit(solution)/shard_map/ppermute | solution.py:451
  93.1 3.2 %collective-permute-done.38.e = f32[4,64,128]{2,1,0:T(8,128)S(1)} collective-permute-done((f32[4,64,128]{2,1,0:T(8,128)S(1)}, f32[4,64,128]{2,1,0:T(8,128)S(1)}, u32[]{:S(2)}, u32[]{:S(2)}) %collective-permute-start.38) | collective-permute-done | bytes 131104 | tf_op jit(solution)/shard_map/ppermute | solution.py:451
  98.1 1.6 %collective-permute-start.40 = (f32[2,128,128]{2,1,0:T(8,128)S(1)}, f32[2,128,128]{2,1,0:T(8,128)S(1)}, u32[]{:S(2)}, u32[]{:S(2)}) collective-permute-start(f32[2,128,128]{2,1,0:T(8,128)S(1)} %get-tuple-element.160), channel_id=1, source_target_pairs={{0,1},{1,0},{2,3},{3,2},{4,5},{5,4},{6,7},{7,6},{8,9},{9,8},{10,11... | collective-permute-start | bytes 393224 | tf_op jit(solution)/shard_map/ppermute | solution.py:448
  99.9 3.9 %collective-permute-done.40 = f32[2,128,128]{2,1,0:T(8,128)S(1)} collective-permute-done((f32[2,128,128]{2,1,0:T(8,128)S(1)}, f32[2,128,128]{2,1,0:T(8,128)S(1)}, u32[]{:S(2)}, u32[]{:S(2)}) %collective-permute-start.40) | collective-permute-done | bytes 131104 | tf_op jit(solution)/shard_map/ppermute | solution.py:448
  (75 shorter events, 14.8 us)
Async XLA Ops:
  0.0 9.8 %collective-permute-start.1 = (f32[2,2,8,128,256]{4,3,2,1,0:T(8,128)}, f32[2,2,8,128,256]{4,3,2,1,0:T(8,128)S(1)}, u32[]{:S(2)}, u32[]{:S(2)}) collective-permute-start(f32[2,2,8,128,256]{4,3,2,1,0:T(8,128)} %own.2), channel_id=1, source_target_pairs={{0,2},{2,0},{4,6},{6,4},{8,10},{10,8},{12,14},{14,12},{16,18},{18,... | collective-permute-start | bytes 12582920 | tf_op jit(solution)/shard_map/ppermute | solution.py:451
  0.5 9.3 %collective-permute-start.2 = (f32[3,2,128,256]{3,2,1,0:T(8,128)}, f32[3,2,128,256]{3,2,1,0:T(8,128)S(1)}, u32[]{:S(2)}, u32[]{:S(2)}) collective-permute-start(f32[3,2,128,256]{3,2,1,0:T(8,128)} %d_own.1), channel_id=1, source_target_pairs={{0,2},{2,0},{4,6},{6,4},{8,10},{10,8},{12,14},{14,12},{16,18},{18,... | collective-permute-start | bytes 2359304 | tf_op jit(solution)/shard_map/ppermute | solution.py:451
  1.4 9.1 %copy-start.1 = (f32[3,2,128,128]{3,2,1,0:T(8,128)S(1)}, f32[3,2,128,128]{3,2,1,0:T(8,128)}, u32[]{:S(2)}) copy-start(f32[3,2,128,128]{3,2,1,0:T(8,128)} %rhs.1) | copy-start | bytes 1179652
  1.4 8.3 %collective-permute-start.3 = (f32[2,128,128]{2,1,0:T(8,128)S(1)}, f32[2,128,128]{2,1,0:T(8,128)S(1)}, u32[]{:S(2)}, u32[]{:S(2)}) collective-permute-start(f32[2,128,128]{2,1,0:T(8,128)S(1)} %slice_bitcast_fusion.rhs_own), channel_id=1, source_target_pairs={{0,1},{1,0},{2,3},{3,2},{4,5},{5,4},{6,7},{7,6},{8,9},{9,8},{10,11... | collective-permute-start | bytes 393224 | tf_op jit(solution)/shard_map/ppermute | solution.py:448
  5.6 14.2 %collective-permute-start.13 = (f32[2,2,128,256]{3,2,1,0:T(8,128)S(1)}, f32[2,2,128,256]{3,2,1,0:T(8,128)S(1)}, u32[]{:S(2)}, u32[]{:S(2)}) collective-permute-start(f32[2,2,128,256]{3,2,1,0:T(8,128)S(1)} %slice.6), channel_id=1, source_target_pairs={{0,1},{1,0},{2,3},{3,2},{4,5},{5,4},{6,7},{7,6},{8,9},{9,8},{10,11... | collective-permute-start | bytes 1572872 | tf_op jit(solution)/shard_map/ppermute | solution.py:448
  5.7 0.7 copy-start.2
  6.3 0.7 copy-start.3
  8.5 1.2 %collective-permute-start = (s32[3,16]{1,0:T(4,128)S(1)}, s32[3,16]{1,0:T(4,128)S(1)}, u32[]{:S(2)}, u32[]{:S(2)}) collective-permute-start(s32[3,16]{1,0:T(4,128)S(1)} %slot_places.1.places), channel_id=1, source_target_pairs={{0,2},{2,0},{4,6},{6,4},{8,10},{10,8},{12,14},{14,12},{16,18},{18,... | collective-permute-start | bytes 584 | tf_op jit(solution)/shard_map/ppermute | solution.py:451
  10.1 1.3 %collective-permute-start.4 = (f32[2,64,128]{2,1,0:T(8,128)S(1)}, f32[2,64,128]{2,1,0:T(8,128)S(1)}, u32[]{:S(2)}, u32[]{:S(2)}) collective-permute-start(f32[2,64,128]{2,1,0:T(8,128)S(1)} %get-tuple-element.94), channel_id=1, source_target_pairs={{0,2},{2,0},{4,6},{6,4},{8,10},{10,8},{12,14},{14,12},{16,18},{18,... | collective-permute-start | bytes 196616 | tf_op jit(solution)/shard_map/ppermute | solution.py:451
  10.7 1.4 %collective-permute-start.5 = (f32[2,2,64,128]{3,2,1,0:T(8,128)S(1)}, f32[2,2,64,128]{3,2,1,0:T(8,128)S(1)}, u32[]{:S(2)}, u32[]{:S(2)}) collective-permute-start(f32[2,2,64,128]{3,2,1,0:T(8,128)S(1)} %get-tuple-element.96), channel_id=1, source_target_pairs={{0,2},{2,0},{4,6},{6,4},{8,10},{10,8},{12,14},{14,12},{16,18},{18,... | collective-permute-start | bytes 393224 | tf_op jit(solution)/shard_map/ppermute | solution.py:451
  12.1 6.1 %collective-permute-start.6 = (f32[4,64,128]{2,1,0:T(8,128)S(1)}, f32[4,64,128]{2,1,0:T(8,128)S(1)}, u32[]{:S(2)}, u32[]{:S(2)}) collective-permute-start(f32[4,64,128]{2,1,0:T(8,128)S(1)} %pad_maximum_fusion.1.refs_4_.values), channel_id=1, source_target_pairs={{0,4},{2,6},{4,0},{6,2},{8,12},{10,14},{12,8},{14,10},{16,20},{18,... | collective-permute-start | bytes 393224 | tf_op jit(solution)/shard_map/ppermute | solution.py:451
  14.0 10.1 %collective-permute-start.9 = (f32[4,64,128]{2,1,0:T(8,128)S(1)}, f32[4,64,128]{2,1,0:T(8,128)S(1)}, u32[]{:S(2)}, u32[]{:S(2)}) collective-permute-start(f32[4,64,128]{2,1,0:T(8,128)S(1)} %pad_maximum_fusion.1.refs_4_.values), channel_id=1, source_target_pairs={{0,16},{2,18},{4,20},{6,22},{8,24},{10,26},{12,28},{14,30},{16,0},... | collective-permute-start | bytes 393224 | tf_op jit(solution)/shard_map/ppermute | solution.py:451
  16.6 9.5 %collective-permute-start.11 = (f32[4,64,128]{2,1,0:T(8,128)S(1)}, f32[4,64,128]{2,1,0:T(8,128)S(1)}, u32[]{:S(2)}, u32[]{:S(2)}) collective-permute-start(f32[4,64,128]{2,1,0:T(8,128)S(1)} %pad_maximum_fusion.1.refs_4_.values), channel_id=1, source_target_pairs={{0,4},{2,6},{4,0},{6,2},{8,16},{10,18},{12,20},{14,22},{16,8},{18,... | collective-permute-start | bytes 393224 | tf_op jit(solution)/shard_map/ppermute | solution.py:462
  17.2 9.0 %collective-permute-start.7 = (f32[4,64,128]{2,1,0:T(8,128)S(1)}, f32[4,64,128]{2,1,0:T(8,128)S(1)}, u32[]{:S(2)}, u32[]{:S(2)}) collective-permute-start(f32[4,64,128]{2,1,0:T(8,128)S(1)} %pad_maximum_fusion.1.refs_4_.values), channel_id=1, source_target_pairs={{0,8},{2,10},{4,12},{6,14},{8,0},{10,2},{12,4},{14,6},{16,24},{18,... | collective-permute-start | bytes 393224 | tf_op jit(solution)/shard_map/ppermute | solution.py:451
  18.2 8.0 %collective-permute-start.12 = (f32[4,64,128]{2,1,0:T(8,128)S(1)}, f32[4,64,128]{2,1,0:T(8,128)S(1)}, u32[]{:S(2)}, u32[]{:S(2)}) collective-permute-start(f32[4,64,128]{2,1,0:T(8,128)S(1)} %collective-permute-done.6.refs_5_), channel_id=1, source_target_pairs={{0,4},{2,6},{4,0},{6,2},{8,16},{10,18},{12,20},{14,22},{16,8},{18,... | collective-permute-start | bytes 393224 | tf_op jit(solution)/shard_map/ppermute | solution.py:462
  19.8 6.9 %collective-permute-start.8 = (f32[4,64,128]{2,1,0:T(8,128)S(1)}, f32[4,64,128]{2,1,0:T(8,128)S(1)}, u32[]{:S(2)}, u32[]{:S(2)}) collective-permute-start(f32[4,64,128]{2,1,0:T(8,128)S(1)} %collective-permute-done.6.refs_5_), channel_id=1, source_target_pairs={{0,8},{2,10},{4,12},{6,14},{8,0},{10,2},{12,4},{14,6},{16,24},{18,... | collective-permute-start | bytes 393224 | tf_op jit(solution)/shard_map/ppermute | solution.py:451
  24.1 5.0 %collective-permute-start.10 = (f32[4,64,128]{2,1,0:T(8,128)S(1)}, f32[4,64,128]{2,1,0:T(8,128)S(1)}, u32[]{:S(2)}, u32[]{:S(2)}) collective-permute-start(f32[4,64,128]{2,1,0:T(8,128)S(1)} %collective-permute-done.9.refs_8_), channel_id=1, source_target_pairs={{0,4},{2,6},{4,0},{6,2},{8,12},{10,14},{12,8},{14,10},{16,20},{18,... | collective-permute-start | bytes 393224 | tf_op jit(solution)/shard_map/ppermute | solution.py:451
  26.1 4.9 %copy-start = (f32[3,2,128,256]{3,2,1,0:T(8,128)S(1)}, f32[3,2,128,256]{3,2,1,0:T(8,128)}, u32[]{:S(2)}) copy-start(f32[3,2,128,256]{3,2,1,0:T(8,128)} %d_own.1) | copy-start | bytes 2359300
  29.1 1.9 %collective-permute-start.14 = (f32[2,2,128,256]{3,2,1,0:T(8,128)S(1)}, f32[2,2,128,256]{3,2,1,0:T(8,128)S(1)}, u32[]{:S(2)}, u32[]{:S(2)}) collective-permute-start(f32[2,2,128,256]{3,2,1,0:T(8,128)S(1)} %collective-permute-done.13.d2), channel_id=1, source_target_pairs={{0,2},{2,0},{4,6},{6,4},{8,10},{10,8},{12,14},{14,12},{16,18},{18,... | collective-permute-start | bytes 1572872 | tf_op jit(solution)/shard_map/ppermute | solution.py:451
  31.5 5.6 %collective-permute-start.15 = (f32[4,64,128]{2,1,0:T(8,128)S(1)}, f32[4,64,128]{2,1,0:T(8,128)S(1)}, u32[]{:S(2)}, u32[]{:S(2)}) collective-permute-start(f32[4,64,128]{2,1,0:T(8,128)S(1)} %get-tuple-element.110), channel_id=1, source_target_pairs={{0,1},{1,0},{2,3},{3,2},{4,5},{5,4},{6,7},{7,6},{8,9},{9,8},{10,11... | collective-permute-start | bytes 393224 | tf_op jit(solution)/shard_map/ppermute | solution.py:448
  37.1 5.5 %collective-permute-start.16 = (f32[4,64,128]{2,1,0:T(8,128)S(1)}, f32[4,64,128]{2,1,0:T(8,128)S(1)}, u32[]{:S(2)}, u32[]{:S(2)}) collective-permute-start(f32[4,64,128]{2,1,0:T(8,128)S(1)} %add.36.refs_5_), channel_id=1, source_target_pairs={{0,4},{2,6},{4,0},{6,2},{8,12},{10,14},{12,8},{14,10},{16,20},{18,... | collective-permute-start | bytes 393224 | tf_op jit(solution)/shard_map/ppermute | solution.py:451
  37.5 8.8 %collective-permute-start.19 = (f32[4,64,128]{2,1,0:T(8,128)S(1)}, f32[4,64,128]{2,1,0:T(8,128)S(1)}, u32[]{:S(2)}, u32[]{:S(2)}) collective-permute-start(f32[4,64,128]{2,1,0:T(8,128)S(1)} %add.36.refs_5_), channel_id=1, source_target_pairs={{0,16},{2,18},{4,20},{6,22},{8,24},{10,26},{12,28},{14,30},{16,0},... | collective-permute-start | bytes 393224 | tf_op jit(solution)/shard_map/ppermute | solution.py:451
  39.9 11.3 %collective-permute-start.17 = (f32[4,64,128]{2,1,0:T(8,128)S(1)}, f32[4,64,128]{2,1,0:T(8,128)S(1)}, u32[]{:S(2)}, u32[]{:S(2)}) collective-permute-start(f32[4,64,128]{2,1,0:T(8,128)S(1)} %add.36.refs_5_), channel_id=1, source_target_pairs={{0,8},{2,10},{4,12},{6,14},{8,0},{10,2},{12,4},{14,6},{16,24},{18,... | collective-permute-start | bytes 393224 | tf_op jit(solution)/shard_map/ppermute | solution.py:451
  41.1 10.1 %collective-permute-start.21 = (f32[4,64,128]{2,1,0:T(8,128)S(1)}, f32[4,64,128]{2,1,0:T(8,128)S(1)}, u32[]{:S(2)}, u32[]{:S(2)}) collective-permute-start(f32[4,64,128]{2,1,0:T(8,128)S(1)} %add.36.refs_5_), channel_id=1, source_target_pairs={{0,4},{2,6},{4,0},{6,2},{8,16},{10,18},{12,20},{14,22},{16,8},{18,... | collective-permute-start | bytes 393224 | tf_op jit(solution)/shard_map/ppermute | solution.py:462
  42.6 8.6 %collective-permute-start.18 = (f32[4,64,128]{2,1,0:T(8,128)S(1)}, f32[4,64,128]{2,1,0:T(8,128)S(1)}, u32[]{:S(2)}, u32[]{:S(2)}) collective-permute-start(f32[4,64,128]{2,1,0:T(8,128)S(1)} %collective-permute-done.16.refs_6_), channel_id=1, source_target_pairs={{0,8},{2,10},{4,12},{6,14},{8,0},{10,2},{12,4},{14,6},{16,24},{18,... | collective-permute-start | bytes 393224 | tf_op jit(solution)/shard_map/ppermute | solution.py:451
  42.6 8.6 %collective-permute-start.22 = (f32[4,64,128]{2,1,0:T(8,128)S(1)}, f32[4,64,128]{2,1,0:T(8,128)S(1)}, u32[]{:S(2)}, u32[]{:S(2)}) collective-permute-start(f32[4,64,128]{2,1,0:T(8,128)S(1)} %collective-permute-done.16.refs_6_), channel_id=1, source_target_pairs={{0,4},{2,6},{4,0},{6,2},{8,16},{10,18},{12,20},{14,22},{16,8},{18,... | collective-permute-start | bytes 393224 | tf_op jit(solution)/shard_map/ppermute | solution.py:462
  46.2 5.0 %collective-permute-start.20 = (f32[4,64,128]{2,1,0:T(8,128)S(1)}, f32[4,64,128]{2,1,0:T(8,128)S(1)}, u32[]{:S(2)}, u32[]{:S(2)}) collective-permute-start(f32[4,64,128]{2,1,0:T(8,128)S(1)} %collective-permute-done.19.refs_9_), channel_id=1, source_target_pairs={{0,4},{2,6},{4,0},{6,2},{8,12},{10,14},{12,8},{14,10},{16,20},{18,... | collective-permute-start | bytes 393224 | tf_op jit(solution)/shard_map/ppermute | solution.py:451
  52.7 6.9 %collective-permute-start.23 = (f32[4,64,256]{2,1,0:T(8,128)S(1)}, f32[4,64,256]{2,1,0:T(8,128)S(1)}, u32[]{:S(2)}, u32[]{:S(2)}) collective-permute-start(f32[4,64,256]{2,1,0:T(8,128)S(1)} %update_top.1.mine), channel_id=1, source_target_pairs={{0,1},{1,0},{2,3},{3,2},{4,5},{5,4},{6,7},{7,6},{8,9},{9,8},{10,11... | collective-permute-start | bytes 786440 | tf_op jit(solution)/shard_map/ppermute | solution.py:448
  61.2 6.1 %collective-permute-start.24 = (f32[4,64,128]{2,1,0:T(8,128)S(1)}, f32[4,64,128]{2,1,0:T(8,128)S(1)}, u32[]{:S(2)}, u32[]{:S(2)}) collective-permute-start(f32[4,64,128]{2,1,0:T(8,128)S(1)} %get-tuple-element.135), channel_id=1, source_target_pairs={{0,4},{2,6},{4,0},{6,2},{8,12},{10,14},{12,8},{14,10},{16,20},{18,... | collective-permute-start | bytes 393224 | tf_op jit(solution)/shard_map/ppermute | solution.py:451
  62.4 6.9 %collective-permute-start.26 = (f32[4,64,128]{2,1,0:T(8,128)S(1)}, f32[4,64,128]{2,1,0:T(8,128)S(1)}, u32[]{:S(2)}, u32[]{:S(2)}) collective-permute-start(f32[4,64,128]{2,1,0:T(8,128)S(1)} %get-tuple-element.137), channel_id=1, source_target_pairs={{0,4},{2,6},{4,0},{6,2},{8,16},{10,18},{12,20},{14,22},{16,8},{18,... | collective-permute-start | bytes 393224 | tf_op jit(solution)/shard_map/ppermute | solution.py:462
  63.3 7.2 %collective-permute-start.27 = (f32[4,64,128]{2,1,0:T(8,128)S(1)}, f32[4,64,128]{2,1,0:T(8,128)S(1)}, u32[]{:S(2)}, u32[]{:S(2)}) collective-permute-start(f32[4,64,128]{2,1,0:T(8,128)S(1)} %get-tuple-element.138), channel_id=1, source_target_pairs={{0,8},{2,10},{4,12},{6,14},{8,0},{10,2},{12,4},{14,6},{16,24},{18,... | collective-permute-start | bytes 393224 | tf_op jit(solution)/shard_map/ppermute | solution.py:451
  66.3 5.9 %collective-permute-start.29 = (f32[4,64,128]{2,1,0:T(8,128)S(1)}, f32[4,64,128]{2,1,0:T(8,128)S(1)}, u32[]{:S(2)}, u32[]{:S(2)}) collective-permute-start(f32[4,64,128]{2,1,0:T(8,128)S(1)} %get-tuple-element.139), channel_id=1, source_target_pairs={{0,4},{2,6},{4,0},{6,2},{8,16},{10,18},{12,20},{14,22},{16,8},{18,... | collective-permute-start | bytes 393224 | tf_op jit(solution)/shard_map/ppermute | solution.py:462
  66.9 5.7 %collective-permute-start.30 = (f32[4,64,128]{2,1,0:T(8,128)S(1)}, f32[4,64,128]{2,1,0:T(8,128)S(1)}, u32[]{:S(2)}, u32[]{:S(2)}) collective-permute-start(f32[4,64,128]{2,1,0:T(8,128)S(1)} %get-tuple-element.140), channel_id=1, source_target_pairs={{0,8},{2,10},{4,12},{6,14},{8,0},{10,2},{12,4},{14,6},{16,24},{18,... | collective-permute-start | bytes 393224 | tf_op jit(solution)/shard_map/ppermute | solution.py:451
  67.3 8.9 %collective-permute-start.25 = (f32[4,64,128]{2,1,0:T(8,128)S(1)}, f32[4,64,128]{2,1,0:T(8,128)S(1)}, u32[]{:S(2)}, u32[]{:S(2)}) collective-permute-start(f32[4,64,128]{2,1,0:T(8,128)S(1)} %add.37), channel_id=1, source_target_pairs={{0,16},{2,18},{4,20},{6,22},{8,24},{10,26},{12,28},{14,30},{16,0},... | collective-permute-start | bytes 393224 | tf_op jit(solution)/shard_map/ppermute | solution.py:451
  70.6 5.7 %collective-permute-start.28 = (f32[4,64,128]{2,1,0:T(8,128)S(1)}, f32[4,64,128]{2,1,0:T(8,128)S(1)}, u32[]{:S(2)}, u32[]{:S(2)}) collective-permute-start(f32[4,64,128]{2,1,0:T(8,128)S(1)} %add_add_fusion.1), channel_id=1, source_target_pairs={{0,4},{2,6},{4,0},{6,2},{8,12},{10,14},{12,8},{14,10},{16,20},{18,... | collective-permute-start | bytes 393224 | tf_op jit(solution)/shard_map/ppermute | solution.py:451
  76.3 5.0 %collective-permute-start.31 = (f32[4,64,128]{2,1,0:T(8,128)S(1)}, f32[4,64,128]{2,1,0:T(8,128)S(1)}, u32[]{:S(2)}, u32[]{:S(2)}) collective-permute-start(f32[4,64,128]{2,1,0:T(8,128)S(1)} %add_subtract_fusion.own), channel_id=1, source_target_pairs={{0,1},{1,0},{2,3},{3,2},{4,5},{5,4},{6,7},{7,6},{8,9},{9,8},{10,11... | collective-permute-start | bytes 393224 | tf_op jit(solution)/shard_map/ppermute | solution.py:448
  83.1 5.9 %collective-permute-start.37 = (f32[4,64,128]{2,1,0:T(8,128)S(1)}, f32[4,64,128]{2,1,0:T(8,128)S(1)}, u32[]{:S(2)}, u32[]{:S(2)}) collective-permute-start(f32[4,64,128]{2,1,0:T(8,128)S(1)} %get-tuple-element.156), channel_id=1, source_target_pairs={{0,4},{2,6},{4,0},{6,2},{8,12},{10,14},{12,8},{14,10},{16,20},{18,... | collective-permute-start | bytes 393224 | tf_op jit(solution)/shard_map/ppermute | solution.py:451
  84.1 6.5 %collective-permute-start.34 = (f32[4,64,128]{2,1,0:T(8,128)S(1)}, f32[4,64,128]{2,1,0:T(8,128)S(1)}, u32[]{:S(2)}, u32[]{:S(2)}) collective-permute-start(f32[4,64,128]{2,1,0:T(8,128)S(1)} %get-tuple-element.153), channel_id=1, source_target_pairs={{0,4},{2,6},{4,0},{6,2},{8,16},{10,18},{12,20},{14,22},{16,8},{18,... | collective-permute-start | bytes 393224 | tf_op jit(solution)/shard_map/ppermute | solution.py:462
  85.1 5.5 %collective-permute-start.35 = (f32[4,64,128]{2,1,0:T(8,128)S(1)}, f32[4,64,128]{2,1,0:T(8,128)S(1)}, u32[]{:S(2)}, u32[]{:S(2)}) collective-permute-start(f32[4,64,128]{2,1,0:T(8,128)S(1)} %get-tuple-element.154), channel_id=1, source_target_pairs={{0,8},{2,10},{4,12},{6,14},{8,0},{10,2},{12,4},{14,6},{16,24},{18,... | collective-permute-start | bytes 393224 | tf_op jit(solution)/shard_map/ppermute | solution.py:451
  86.3 5.4 %collective-permute-start.32 = (f32[4,64,128]{2,1,0:T(8,128)S(1)}, f32[4,64,128]{2,1,0:T(8,128)S(1)}, u32[]{:S(2)}, u32[]{:S(2)}) collective-permute-start(f32[4,64,128]{2,1,0:T(8,128)S(1)} %get-tuple-element.150), channel_id=1, source_target_pairs={{0,4},{2,6},{4,0},{6,2},{8,16},{10,18},{12,20},{14,22},{16,8},{18,... | collective-permute-start | bytes 393224 | tf_op jit(solution)/shard_map/ppermute | solution.py:462
  88.2 5.0 %collective-permute-start.33 = (f32[4,64,128]{2,1,0:T(8,128)S(1)}, f32[4,64,128]{2,1,0:T(8,128)S(1)}, u32[]{:S(2)}, u32[]{:S(2)}) collective-permute-start(f32[4,64,128]{2,1,0:T(8,128)S(1)} %get-tuple-element.151), channel_id=1, source_target_pairs={{0,8},{2,10},{4,12},{6,14},{8,0},{10,2},{12,4},{14,6},{16,24},{18,... | collective-permute-start | bytes 393224 | tf_op jit(solution)/shard_map/ppermute | solution.py:451
  89.0 7.3 %collective-permute-start.38 = (f32[4,64,128]{2,1,0:T(8,128)S(1)}, f32[4,64,128]{2,1,0:T(8,128)S(1)}, u32[]{:S(2)}, u32[]{:S(2)}) collective-permute-start(f32[4,64,128]{2,1,0:T(8,128)S(1)} %add.46), channel_id=1, source_target_pairs={{0,16},{2,18},{4,20},{6,22},{8,24},{10,26},{12,28},{14,30},{16,0},... | collective-permute-start | bytes 393224 | tf_op jit(solution)/shard_map/ppermute | solution.py:451
  90.7 5.7 %collective-permute-start.36 = (f32[4,64,128]{2,1,0:T(8,128)S(1)}, f32[4,64,128]{2,1,0:T(8,128)S(1)}, u32[]{:S(2)}, u32[]{:S(2)}) collective-permute-start(f32[4,64,128]{2,1,0:T(8,128)S(1)} %add_add_fusion), channel_id=1, source_target_pairs={{0,4},{2,6},{4,0},{6,2},{8,12},{10,14},{12,8},{14,10},{16,20},{18,... | collective-permute-start | bytes 393224 | tf_op jit(solution)/shard_map/ppermute | solution.py:451
  96.6 1.4 %collective-permute-start.39 = (f32[2,64,256]{2,1,0:T(8,128)S(1)}, f32[2,64,256]{2,1,0:T(8,128)S(1)}, u32[]{:S(2)}, u32[]{:S(2)}) collective-permute-start(f32[2,64,256]{2,1,0:T(8,128)S(1)} %get-tuple-element.158), channel_id=1, source_target_pairs={{0,2},{2,0},{4,6},{6,4},{8,10},{10,8},{12,14},{14,12},{16,18},{18,... | collective-permute-start | bytes 393224 | tf_op jit(solution)/shard_map/ppermute | solution.py:451
  96.7 3.1 %collective-permute-start.41 = (f32[2,64,128]{2,1,0:T(8,128)S(1)}, f32[2,64,128]{2,1,0:T(8,128)S(1)}, u32[]{:S(2)}, u32[]{:S(2)}) collective-permute-start(f32[2,64,128]{2,1,0:T(8,128)S(1)} %get-tuple-element.164), channel_id=1, source_target_pairs={{0,2},{2,0},{4,6},{6,4},{8,10},{10,8},{12,14},{14,12},{16,18},{18,... | collective-permute-start | bytes 196616 | tf_op jit(solution)/shard_map/ppermute | solution.py:451
  97.2 2.6 %collective-permute-start.42 = (f32[2,64,128]{2,1,0:T(8,128)S(1)}, f32[2,64,128]{2,1,0:T(8,128)S(1)}, u32[]{:S(2)}, u32[]{:S(2)}) collective-permute-start(f32[2,64,128]{2,1,0:T(8,128)S(1)} %get-tuple-element.166), channel_id=1, source_target_pairs={{0,2},{2,0},{4,6},{6,4},{8,10},{10,8},{12,14},{14,12},{16,18},{18,... | collective-permute-start | bytes 196616 | tf_op jit(solution)/shard_map/ppermute | solution.py:451
  98.1 5.6 %collective-permute-start.40 = (f32[2,128,128]{2,1,0:T(8,128)S(1)}, f32[2,128,128]{2,1,0:T(8,128)S(1)}, u32[]{:S(2)}, u32[]{:S(2)}) collective-permute-start(f32[2,128,128]{2,1,0:T(8,128)S(1)} %get-tuple-element.160), channel_id=1, source_target_pairs={{0,1},{1,0},{2,3},{3,2},{4,5},{5,4},{6,7},{7,6},{8,9},{9,8},{10,11... | collective-permute-start | bytes 393224 | tf_op jit(solution)/shard_map/ppermute | solution.py:448
